TPU v7x, 32 devices: a whole 2x2x4 slice. The times are simulated.
32 devices in a mesh: rows: 8 (over y, x, core), cols: 4 (over z).
Axes of the slice: x: 2, y: 2, z: 4, core: 2. Of those that a mesh axis runs over, the one named last changes fastest.
Arguments:
- features: bfloat16 [4, 64, 160, 256], P(None, 'rows', 'cols'), may hold values from -6 to 6
- occupancy: int32 [4, 64, 160], P(None, 'rows', 'cols'), may hold values from 0 to 1, as said below
- cotangent: bfloat16 [4, 64, 160, 256], P(None, 'rows', 'cols'), may hold values from -6 to 6
- conv_weights: float32 [2, 589824], replicated, may hold values from -0.125 to 0.125
- conv_first: float32 [2, 589824], P(None, ('rows', 'cols')), may hold values from -128 to 128
- conv_second: float32 [2, 589824], P(None, ('rows', 'cols')), may hold values from 20.48 to 327.68
- norm_scale_bias: float32 [4, 256], replicated, may hold values from 0.5 to 1.5
- norm_first: float32 [4, 256], replicated, may hold values from -128 to 128
- norm_second: float32 [4, 256], replicated, may hold values from 20.48 to 327.68
Outputs:
- block_out: bfloat16 [4, 64, 160, 256], P(None, 'rows', 'cols')
- grad_input: float32 [4, 64, 160, 256], P(None, 'rows', 'cols')
- conv_grads: float32 [2, 589824], P(None, ('rows', 'cols'))
- conv_new: float32 [2, 589824], P(None, ('rows', 'cols'))
- conv_first_new: float32 [2, 589824], P(None, ('rows', 'cols'))
- conv_second_new: float32 [2, 589824], P(None, ('rows', 'cols'))
- norm_grads: float32 [4, 256], replicated
- norm_new: float32 [4, 256], replicated
- norm_first_new: float32 [4, 256], replicated
- norm_second_new: float32 [4, 256], replicated
Inputs may be any that keep to these rules, and one draw needn't show every extreme that they name: `occupancy`: 0 or 1; the share of ones differs from one 8 x 40 tile to another, the same in every scene.
All inputs are finite; a program needn't handle non-finite values.
Results may differ from a plain program's by a relative error of at most 0.0033.
The roundings to bfloat16 on the way count: a program that leaves them out, or rounds other values in their place, can miss the bound.
Values may be sent and summed in bfloat16 or wider, within the bound.
No kernel may reach another device: no remote copies, remote signals or barrier semaphores. Data moves between devices by JAX's collectives and lax.ppermute only.
A program may use at most 64 MiB of HBM per device.

v0:
```python
import functools
import math

import jax
import jax.numpy as jnp
from jax import lax
from jax.experimental import pallas as pl
from jax.experimental.pallas import tpu as pltpu
from jax.sharding import PartitionSpec as P

STEP = 5
BOTH = ("rows", "cols")
RIM = 4
F32, BF16 = jnp.float32, jnp.bfloat16


def shape_of(shape, dtype):
    return jax.ShapeDtypeStruct(shape, dtype)


def kernel_call(body, out_shape, flops, smem=(), scratch=(), limit=40):
    def call(*operands):
        specs = [
            pl.BlockSpec(memory_space=pltpu.SMEM if i in smem else pltpu.VMEM)
            for i in range(len(operands))
        ]
        return pl.pallas_call(
            body,
            out_shape=out_shape,
            in_specs=specs,
            out_specs=[pl.BlockSpec(memory_space=pltpu.VMEM)] * len(out_shape),
            scratch_shapes=list(scratch),
            compiler_params=pltpu.CompilerParams(vmem_limit_bytes=limit << 20),
            cost_estimate=pl.CostEstimate(
                flops=int(flops), bytes_accessed=4 << 20, transcendentals=0
            ),
        )(*operands)

    return call


def dot(a, b):
    return jnp.dot(a, b, preferred_element_type=F32)


def dot_nt(a, b):
    return lax.dot_general(a, b, (((1,), (1,)), ((), ())), preferred_element_type=F32)


def total_of(ref):
    count = ref.shape[0]
    total = ref[0]
    for i in range(1, count):
        total = total + ref[i]
    return total


def to_all(ref, parts):
    value = jnp.concatenate(parts, axis=0)
    for i in range(ref.shape[0]):
        ref[i] = value


def store_shifted(ref, start, row):
    width, chans = row.shape
    ref[start : start + width, 0:chans] = pltpu.roll(row, 1, 0).astype(BF16)
    ref[start : start + width, chans : 2 * chans] = row.astype(BF16)
    ref[start : start + width, 2 * chans : 3 * chans] = pltpu.roll(row, width - 1, 0).astype(BF16)


class Geometry:
    def __init__(self, scenes, height, width, chans):
        self.s, self.h, self.w, self.c = scenes, height, width, chans
        self.wp = width + 2 * RIM


def in_grid(row, r, g, lo, hi, edge):
    row = jnp.concatenate([row[: g.w], row[g.w :] * edge], axis=0)
    if r < RIM:
        row = row * lo
    elif r >= RIM + g.h:
        row = row * hi
    return row


def edge_mask(bounds, g):
    place = lax.broadcasted_iota(jnp.int32, (2 * RIM, g.c), 0)
    return jnp.where(place < RIM, bounds[2].astype(F32), bounds[3].astype(F32))


def sum_rows(value):
    rows, chans = value.shape
    return jnp.sum(value.reshape(rows // 8, 8, chans), axis=0)


def prepare_kernel(w_ref, one_ref, two_ref):
    chans = one_ref.shape[1]
    lanes = w_ref.shape[1]
    per = chans // lanes
    taps = one_ref.shape[0] // chans

    def tap(t, carry):
        for k, out in enumerate((one_ref, two_ref)):
            parts = [
                w_ref[pl.ds(t * chans * per * 2 + 2 * half + k, chans, stride=2 * per), :]
                for half in range(per)
            ]
            out[pl.ds(pl.multiple_of(t * chans, chans), chans), :] = jnp.concatenate(
                parts, axis=1
            ).astype(BF16)
        return carry

    lax.fori_loop(0, taps, tap, 0)


def first_conv_kernel(g, chunk, up, top, bottom, down, edges, w, x_ref, z_ref, st_ref):
    half = g.h // 2
    rows_in, rows_out = g.h + 2 * RIM, g.h + 2 * RIM - 2
    s1 = jnp.zeros((8, g.c), F32)
    s2 = jnp.zeros((8, g.c), F32)
    for s in range(g.s):
        for r in range(rows_in):
            source, place = (
                (up, r)
                if r < RIM
                else (top, r - RIM)
                if r < RIM + half
                else (bottom, r - RIM - half)
                if r < RIM + g.h
                else (down, r - RIM - g.h)
            )
            row = jnp.concatenate(
                [source[s, place].astype(F32), edges[s, r].astype(F32)], axis=0
            )
            store_shifted(x_ref, (s * rows_in + r) * g.wp, row)
        for r in range(0, rows_out, chunk):
            base = (s * rows_in + r) * g.wp
            size = chunk * g.wp
            lhs = jnp.concatenate(
                [x_ref[base + a * g.wp : base + a * g.wp + size, :] for a in range(3)], axis=1
            )
            acc = dot(lhs, w[...])
            z_ref[(s * rows_out + r) * g.wp : (s * rows_out + r) * g.wp + size, :] = acc
            for i in range(chunk):
                if RIM <= r + i + 1 < RIM + g.h:
                    own = acc[i * g.wp : i * g.wp + g.w]
                    s1 = s1 + sum_rows(own)
                    s2 = s2 + sum_rows(own * own)
    to_all(st_ref, [jnp.sum(s1, 0, keepdims=True), jnp.sum(s2, 0, keepdims=True)])


def stats_of(total, count):
    mean = total[0:1] / count
    var = total[1:2] / count - mean * mean
    return mean, lax.rsqrt(var + 1e-05)


def second_conv_kernel(
    g, chunk, count, bounds, z1, st, params, w, cot, h_ref, z_ref, st_ref
):
    rows_in, rows_out = g.h + 2 * RIM - 2, g.h + 2 * RIM - 4
    mean, rstd = stats_of(total_of(st), count)
    scale = params[0:1] * rstd
    shift = params[1:2] - mean * scale
    lo, hi = bounds[0].astype(F32), bounds[1].astype(F32)
    edge = edge_mask(bounds, g)
    sums = [jnp.zeros((8, g.c), F32) for _ in range(4)]
    for s in range(g.s):
        for r in range(rows_in):
            start = (s * rows_in + r) * g.wp
            row = jnp.maximum(z1[start : start + g.wp, :] * scale + shift, 0.0)
            store_shifted(h_ref, start, in_grid(row, r + 1, g, lo, hi, edge))
        for r in range(0, rows_out, chunk):
            base = (s * rows_in + r) * g.wp
            size = chunk * g.wp
            lhs = jnp.concatenate(
                [h_ref[base + a * g.wp : base + a * g.wp + size, :] for a in range(3)], axis=1
            )
            acc = dot(lhs, w[...])
            z_ref[(s * rows_out + r) * g.wp : (s * rows_out + r) * g.wp + size, :] = acc
            for i in range(chunk):
                if RIM <= r + i + 2 < RIM + g.h:
                    own = acc[i * g.wp : i * g.wp + g.w]
                    dn = cot[s, r + i + 2 - RIM].astype(F32)
                    for k, v in enumerate((own, own * own, dn, dn * own)):
                        sums[k] = sums[k] + sum_rows(v)
    to_all(st_ref, [jnp.sum(v, 0, keepdims=True) for v in sums])


def kernel_gradient(g, core, field, rows_field, first_row, dt_ref, keep, send):
    chans, half = g.c, g.c // 2
    mine = pl.multiple_of(core * half, half)
    other = pl.multiple_of((1 - core) * half, half)
    span = g.h * g.wp
    for a in range(3):
        acc = None
        for s in range(g.s):
            lanes = slice(s * span, (s + 1) * span)
            lhs = jnp.concatenate(
                [dt_ref[pl.ds(mine, half), lanes], dt_ref[pl.ds(other, half), lanes]], axis=0
            )
            start = (s * rows_field + first_row + a) * g.wp
            term = dot(lhs, field[start : start + span, :])
            acc = term if acc is None else acc + term
        for b in range(3):
            keep[a * 3 + b] = acc[0:half, b * chans : (b + 1) * chans]
            send[a * 3 + b] = acc[half:, b * chans : (b + 1) * chans]


def second_gradient_kernel(
    g, count, bounds, z2, st, params, cot_up, cot, cot_down, cot_edges, x, h,
    out_ref, d_ref, keep, send, dt_ref
):
    rows = g.h + 2 * RIM - 4
    total = total_of(st)
    mean, rstd = stats_of(total, count)
    scale, shift = params[2:3], params[3:4]
    sum_dn = total[2:3]
    sum_dx = rstd * (total[3:4] - mean * sum_dn)
    k0 = scale * rstd
    k1 = k0 * (sum_dn / count)
    k2 = k0 * rstd * (sum_dx / count)
    out_scale = scale * rstd
    lo, hi = bounds[0].astype(F32), bounds[1].astype(F32)
    edge = edge_mask(bounds, g)
    x_rows = g.h + 2 * RIM
    rim = RIM - 2
    for s in range(g.s):
        for i in range(rows):
            r = i + 2
            start = (s * rows + i) * g.wp
            source, place = (
                (cot_up, i)
                if i < rim
                else (cot, i - rim)
                if i < rim + g.h
                else (cot_down, i - rim - g.h)
            )
            dn = jnp.concatenate(
                [source[s, place].astype(F32), cot_edges[s, i].astype(F32)], axis=0
            )
            centred = z2[start : start + g.wp, :] - mean
            d = in_grid(k0 * dn - k1 - centred * k2, r, g, lo, hi, edge)
            store_shifted(d_ref, start, d)
            if RIM <= r < RIM + g.h:
                centre = (s * x_rows + r) * g.wp
                masked = x[centre : centre + g.wp, g.c : 2 * g.c].astype(F32)[: g.w]
                out_ref[s, r - RIM] = (
                    masked + (centred[: g.w] * out_scale + shift)
                ).astype(BF16)
                own = jnp.concatenate(
                    [d[: g.w], jnp.zeros((g.wp - g.w, g.c), F32)], axis=0
                )
                at = (s * g.h + r - RIM) * g.wp
                dt_ref[:, at : at + g.wp] = own.astype(BF16).T if False else own.T.astype(BF16)
    kernel_gradient(g, bounds[4], h, g.h + 2 * RIM - 2, RIM - 2, dt_ref, keep, send)


def transposed_conv(g, d_ref, w, s, rows_in, r, chunk):
    acc = None
    size = chunk * g.wp
    for a in range(3):
        start = (s * rows_in + r + a) * g.wp
        for b in range(3):
            tap = (2 - a) * 3 + (2 - b)
            term = dot_nt(
                d_ref[start : start + size, b * g.c : (b + 1) * g.c],
                w[tap * g.c : (tap + 1) * g.c, :],
            )
            acc = term if acc is None else acc + term
    return acc


def hidden_gradient_kernel(g, chunk, count, d, w, z1, st, params, dn_ref, st_ref):
    rows_in, rows_out, z_rows = g.h + 2 * RIM - 4, g.h + 2 * RIM - 6, g.h + 2 * RIM - 2
    mean, rstd = stats_of(total_of(st), count)
    scale = params[0:1] * rstd
    shift = params[1:2] - mean * scale
    s0 = jnp.zeros((8, g.c), F32)
    s1 = jnp.zeros((8, g.c), F32)
    for s in range(g.s):
        for r in range(0, rows_out, chunk):
            acc = transposed_conv(g, d, w, s, rows_in, r, chunk)
            at = (s * z_rows + r + 2) * g.wp
            z = z1[at : at + chunk * g.wp, :]
            dn = jnp.where(z * scale + shift > 0, acc, 0.0)
            dn_ref[(s * rows_out + r) * g.wp : (s * rows_out + r + chunk) * g.wp, :] = dn
            for i in range(chunk):
                if RIM <= r + i + 3 < RIM + g.h:
                    own = dn[i * g.wp : i * g.wp + g.w]
                    s0 = s0 + sum_rows(own)
                    s1 = s1 + sum_rows(own * (z[i * g.wp : i * g.wp + g.w] - mean))
    to_all(
        st_ref, [jnp.sum(s0, 0, keepdims=True), jnp.sum(s1, 0, keepdims=True) * rstd]
    )


def first_gradient_kernel(
    g, count, bounds, dn_ref, z1, st, st3, params, x, e_ref, keep, send, dt_ref
):
    rows, z_rows = g.h + 2 * RIM - 6, g.h + 2 * RIM - 2
    mean, rstd = stats_of(total_of(st), count)
    total = total_of(st3)
    k0 = params[0:1] * rstd
    k1 = k0 * (total[0:1] / count)
    k2 = k0 * rstd * (total[1:2] / count)
    lo, hi = bounds[0].astype(F32), bounds[1].astype(F32)
    edge = edge_mask(bounds, g)
    for s in range(g.s):
        for i in range(rows):
            r = i + 3
            start = (s * rows + i) * g.wp
            at = (s * z_rows + i + 2) * g.wp
            centred = z1[at : at + g.wp, :] - mean
            d = k0 * dn_ref[start : start + g.wp, :] - k1 - centred * k2
            d = in_grid(d, r, g, lo, hi, edge)
            store_shifted(e_ref, start, d)
            if RIM <= r < RIM + g.h:
                own = jnp.concatenate(
                    [d[: g.w], jnp.zeros((g.wp - g.w, g.c), F32)], axis=0
                )
                place = (s * g.h + r - RIM) * g.wp
                dt_ref[:, place : place + g.wp] = own.T.astype(BF16)
    kernel_gradient(g, bounds[4], x, g.h + 2 * RIM, RIM - 1, dt_ref, keep, send)


def input_gradient_kernel(g, chunk, e, w, cot, mask, out_ref):
    rows_in = g.h + 2 * RIM - 6
    for s in range(g.s):
        for r in range(0, g.h, chunk):
            acc = transposed_conv(g, e, w, s, rows_in, r, chunk)
            for i in range(chunk):
                own = acc[i * g.wp : i * g.wp + g.w]
                out_ref[s, r + i] = (cot[s, r + i].astype(F32) + own) * mask[
                    s, r + i
                ].astype(F32)


def pair_sum_kernel(keep, got, out_ref):
    taps, half, chans = keep.shape
    for t in range(taps):
        total = keep[t] + got[t]
        out_ref[t * chans : (t + 1) * chans, :] = total.T.astype(BF16)


def adamw(weight, grad, first, second, rate):
    first_new = 0.9 * first + 0.1 * grad
    second_new = 0.999 * second + 0.001 * grad * grad
    first_hat = first_new / (1.0 - 0.9**STEP)
    second_hat = second_new / (1.0 - 0.999**STEP)
    weight_new = weight - rate * (first_hat / (jnp.sqrt(second_hat) + 1e-08) + 0.01 * weight)
    return (weight_new, first_new, second_new)


def adamw_kernel(ncols, one, two, w, first, second, grad_ref, w_ref, first_ref, second_ref):
    devices, rows, lanes = one.shape
    for k, part in enumerate((one, two)):
        for half in range(2):
            grad = None
            for source in range(devices):
                if (source // ncols) % 2 == half:
                    term = part[source].astype(F32)
                    grad = term if grad is None else grad + term
            at = pl.ds(2 * half + k, rows, stride=4)
            new = adamw(w[at, :], grad, first[at, :], second[at, :], 0.02)
            grad_ref[at, :] = grad
            w_ref[at, :], first_ref[at, :], second_ref[at, :] = new


def shifted(block, axis, step):
    count = lax.axis_size(axis)
    pairs = [(i, i + step) for i in range(count) if 0 <= i + step < count]
    return lax.ppermute(block, axis, pairs)


def to_chunks(flat):
    return flat.reshape(2, -1, 128).transpose(1, 0, 2).reshape(-1, 128)


def from_chunks(rows):
    return rows.reshape(-1, 2, 128).transpose(1, 0, 2).reshape(2, -1)


def exchange(parts):
    return lax.all_to_all(parts, BOTH, 0, 0, tiled=True)


def body(
    features,
    occupancy,
    cotangent,
    conv_weights,
    conv_first,
    conv_second,
    norm_scale_bias,
    norm_first,
    norm_second,
):
    scenes, height, width, chans = features.shape
    g = Geometry(scenes, height, width, chans)
    wp = g.wp
    nrows, ncols = lax.axis_size("rows"), lax.axis_size("cols")
    devices = nrows * ncols
    count = float(scenes * height * width * devices)
    row, col = lax.axis_index("rows"), lax.axis_index("cols")
    bounds = jnp.stack(
        [row > 0, row < nrows - 1, col < ncols - 1, col > 0, row % 2 == 1]
    ).astype(jnp.int32)
    half = height // 2

    maskb = jnp.broadcast_to(occupancy.astype(BF16)[..., None], features.shape)
    top = features[:, :half] * occupancy[:, :half].astype(BF16)[..., None]
    bottom = features[:, half:] * occupancy[:, half:].astype(BF16)[..., None]
    up = shifted(bottom, "rows", 1)
    down = shifted(top, "rows", -1)
    tall = jnp.concatenate([up, top, bottom, down], axis=1)
    right = shifted(tall[:, :, :RIM], "cols", -1)
    left = shifted(tall[:, :, width - RIM :], "cols", 1)
    edges = jnp.concatenate([right, left], axis=2)

    rim = RIM - 2
    cot_up = shifted(cotangent[:, height - rim :], "rows", 1)
    cot_down = shifted(cotangent[:, :rim], "rows", -1)
    cot_tall = jnp.concatenate([cot_up, cotangent, cot_down], axis=1)
    cot_right = shifted(cot_tall[:, :, :rim], "cols", -1)
    cot_left = shifted(cot_tall[:, :, width - rim :], "cols", 1)
    gap = jnp.zeros((scenes, height + 2 * rim, 2 * RIM - 2 * rim, chans), BF16)
    cot_edges = jnp.concatenate([cot_right, gap, cot_left], axis=2)

    chunked = to_chunks(conv_weights)
    taps = 9 * chans
    w1, w2 = kernel_call(
        prepare_kernel, [shape_of((taps, chans), BF16)] * 2, 0
    )(chunked)

    rows1, rows2, rows3 = height + 2 * RIM - 2, height + 2 * RIM - 4, height + 2 * RIM - 6
    n0, n1, n2, n3 = (
        scenes * wp * r for r in (height + 2 * RIM, rows1, rows2, rows3)
    )

    def conv_flops(n):
        return 2 * n * taps * chans

    x, z1, st = kernel_call(
        functools.partial(first_conv_kernel, g, 7),
        [
            shape_of((n0, 3 * chans), BF16),
            shape_of((n1, chans), F32),
            shape_of((devices, 2, chans), F32),
        ],
        conv_flops(n1),
    )(up, top, bottom, down, edges, w1)
    st1 = exchange(st)
    h, z2, st = kernel_call(
        functools.partial(second_conv_kernel, g, 6, count),
        [
            shape_of((n1, 3 * chans), BF16),
            shape_of((n2, chans), F32),
            shape_of((devices, 4, chans), F32),
        ],
        conv_flops(n2),
        smem=(0,),
    )(bounds, z1, st1, norm_scale_bias, w2, cotangent)
    st2 = exchange(st)
    grad_shape = shape_of((9, chans // 2, chans), F32)
    own_pixels = scenes * height * wp
    block_out, d, keep2, send2 = kernel_call(
        functools.partial(second_gradient_kernel, g, count),
        [
            shape_of(features.shape, BF16),
            shape_of((n2, 3 * chans), BF16),
            grad_shape,
            grad_shape,
        ],
        conv_flops(own_pixels),
        smem=(0,),
        scratch=[pltpu.VMEM((chans, own_pixels), BF16)],
    )(bounds, z2, st2, norm_scale_bias, cot_up, cotangent, cot_down, cot_edges, x, h)
    pairs = [(i, i ^ 1) for i in range(nrows)]
    got2 = lax.ppermute(send2, "rows", pairs)
    dn1, st = kernel_call(
        functools.partial(hidden_gradient_kernel, g, 5, count),
        [shape_of((n3, chans), F32), shape_of((devices, 2, chans), F32)],
        conv_flops(n3),
    )(d, w2, z1, st1, norm_scale_bias)
    st3 = exchange(st)
    add_pair = kernel_call(pair_sum_kernel, [shape_of((taps, chans // 2), BF16)], 0)
    (part2,) = add_pair(keep2, got2)
    share_rows = taps // devices
    parts2 = exchange(part2.reshape(devices, share_rows, chans // 2))
    e, keep1, send1 = kernel_call(
        functools.partial(first_gradient_kernel, g, count),
        [shape_of((n3, 3 * chans), BF16), grad_shape, grad_shape],
        conv_flops(own_pixels),
        smem=(0,),
        scratch=[pltpu.VMEM((chans, own_pixels), BF16)],
    )(bounds, dn1, z1, st1, st3, norm_scale_bias, x)
    got1 = lax.ppermute(send1, "rows", pairs)
    (part1,) = add_pair(keep1, got1)
    parts1 = exchange(part1.reshape(devices, share_rows, chans // 2))
    (grad_input,) = kernel_call(
        functools.partial(input_gradient_kernel, g, 8),
        [shape_of(features.shape, F32)],
        conv_flops(own_pixels),
    )(e, w1, cotangent, maskb)

    share = conv_first.shape[1]
    start = (row * ncols + col) * (share // 64)
    own_weights = lax.dynamic_slice_in_dim(chunked, start, share // 64, 0)
    chunk_shape = shape_of((share // 64, 128), F32)
    updated = kernel_call(
        functools.partial(adamw_kernel, ncols), [chunk_shape] * 4, 0
    )(parts1, parts2, own_weights, to_chunks(conv_first), to_chunks(conv_second))
    conv_grads, conv_new, conv_first_new, conv_second_new = map(from_chunks, updated)

    total2, total3 = jnp.sum(st2, 0), jnp.sum(st3, 0)
    mean2 = total2[0] / count
    rstd2 = lax.rsqrt(total2[1] / count - mean2 * mean2 + 1e-05)
    norm_grads = jnp.stack(
        [total3[1], total3[0], rstd2 * (total2[3] - mean2 * total2[2]), total2[2]]
    )
    norm_new, norm_first_new, norm_second_new = adamw(
        norm_scale_bias, norm_grads, norm_first, norm_second, 0.75
    )
    return (
        block_out,
        grad_input,
        conv_grads,
        conv_new,
        conv_first_new,
        conv_second_new,
        norm_grads,
        norm_new,
        norm_first_new,
        norm_second_new,
    )


def solution(mesh):
    tile = P(None, "rows", "cols", None)
    share = P(None, ("rows", "cols"))
    return jax.shard_map(
        body,
        mesh=mesh,
        in_specs=(tile, P(None, "rows", "cols"), tile, P(), share, share, P(), P(), P()),
        out_specs=(tile, tile, share, share, share, share, P(), P(), P(), P()),
        check_vma=False,
    )
```

profile of v0, /device:TPU:1, one launch (start us, length us, event | category | flops | bytes accessed | tf_op | source)
XLA Modules:
  0.0 153.4 jit_solution(14894876730783811557)
XLA Ops:
  1.4 1.3 slice_multiply_fusion
  2.7 4.5 %collective-permute-start = (bf16[4,4,40,256]{3,2,1,0:T(8,128)(2,1)S(1)}, bf16[4,4,40,256]{3,2,1,0:T(8,128)(2,1)S(1)}, u32[]{:S(2)}, u32[]{:S(2)}) collective-permute-start(bf16[4,4,40,256]{3,2,1,0:T(8,128)(2,1)S(1)} %get-tuple-element.63.bottom), channel_id=1, source_target_pairs={{0,4},{4,8},{8,12},{12,16},{16,20},{20,24},{24,28},{1,5},{5,9},{9,... | collective-permute-start | bytes 983048 | tf_op jit(solution)/shard_map/ppermute | solution.py:373
  7.2 1.9 %collective-permute-start.1 = (bf16[4,4,40,256]{3,2,1,0:T(8,128)(2,1)S(1)}, bf16[4,4,40,256]{3,2,1,0:T(8,128)(2,1)S(1)}, u32[]{:S(2)}, u32[]{:S(2)}) collective-permute-start(bf16[4,4,40,256]{3,2,1,0:T(8,128)(2,1)S(1)} %get-tuple-element.62.top), channel_id=1, source_target_pairs={{4,0},{8,4},{12,8},{16,12},{20,16},{24,20},{28,24},{5,1},{9,5},{13... | collective-permute-start | bytes 983048 | tf_op jit(solution)/shard_map/ppermute | solution.py:373
  9.2 1.7 %fusion.5 = (bf16[4,2,40,256]{3,2,1,0:T(8,128)(2,1)}, bf16[4,2,40,256]{3,2,1,0:T(8,128)(2,1)}) fusion(bf16[4,8,40,256]{3,2,1,0:T(8,128)(2,1)} %cot.5), kind=kLoop, calls=%fused_computation.23 | loop fusion | bytes 655360 | tf_op jit(solution)/shard_map/slice | solution.py:423
  10.9 3.6 %collective-permute-start.4 = (bf16[4,2,40,256]{3,2,1,0:T(8,128)(2,1)}, bf16[4,2,40,256]{3,2,1,0:T(8,128)(2,1)S(1)}, u32[]{:S(2)}, u32[]{:S(2)}) collective-permute-start(bf16[4,2,40,256]{3,2,1,0:T(8,128)(2,1)} %get-tuple-element.61), channel_id=1, source_target_pairs={{0,4},{4,8},{8,12},{12,16},{16,20},{20,24},{24,28},{1,5},{5,9},{9,... | collective-permute-start | bytes 491528 | tf_op jit(solution)/shard_map/ppermute | solution.py:373
  14.5 1.9 %collective-permute-start.5 = (bf16[4,2,40,256]{3,2,1,0:T(8,128)(2,1)}, bf16[4,2,40,256]{3,2,1,0:T(8,128)(2,1)S(1)}, u32[]{:S(2)}, u32[]{:S(2)}) collective-permute-start(bf16[4,2,40,256]{3,2,1,0:T(8,128)(2,1)} %get-tuple-element.60), channel_id=1, source_target_pairs={{4,0},{8,4},{12,8},{16,12},{20,16},{24,20},{28,24},{5,1},{9,5},{13... | collective-permute-start | bytes 491528 | tf_op jit(solution)/shard_map/ppermute | solution.py:373
  16.6 2.3 %copy-done.2 = f32[2,589824]{1,0:T(2,128)S(1)} copy-done((f32[2,589824]{1,0:T(2,128)S(1)}, f32[2,589824]{1,0:T(2,128)}, u32[]{:S(2)}) %copy-start.2) | copy-done | bytes 4718616
  20.2 1.4 collective-permute-start.2
  21.6 4.0 %collective-permute-start.3 = (bf16[4,16,4,256]{3,2,1,0:T(4,128)(2,1)S(1)}, bf16[4,16,4,256]{3,2,1,0:T(4,128)(2,1)S(1)}, u32[]{:S(2)}, u32[]{:S(2)}) collective-permute-start(bf16[4,16,4,256]{3,2,1,0:T(4,128)(2,1)S(1)} %get-tuple-element.57), channel_id=1, source_target_pairs={{0,1},{1,2},{2,3},{4,5},{5,6},{6,7},{8,9},{9,10},{10,11},{12,13},{... | collective-permute-start | bytes 393224 | tf_op jit(solution)/shard_map/ppermute | solution.py:373
  28.0 1.0 copy-done.27
  29.0 1.0 copy-done.29
  30.0 4.1 %shard_map.169 = (bf16[3072,768]{1,0:T(8,128)(2,1)S(1)}, f32[2688,256]{1,0:T(8,128)S(1)}, f32[32,2,256]{2,1,0:T(2,128)}) custom-call(bf16[4,4,40,256]{3,2,1,0:T(8,128)(2,1)S(1)} %copy-done.27, bf16[4,4,40,256]{3,2,1,0:T(8,128)(2,1)S(1)} %copy-done.10, bf16[4,4,40,256]{3,2,1,0:T(8,128)(2,1)S(1)} %copy-done.12, bf16[4,4,40,256]{3,2,1,0:T(8,128)(2,1)S(1)} %copy-done.29, ...), custom_call_target="tpu_custom_call" | custom-call | flops 3170893824 | bytes 4194304 | tf_op jit(solution)/shard_map/pallas_call | solution.py:27
  34.1 2.2 %copy-done = bf16[3072,768]{1,0:T(8,128)(2,1)} copy-done((bf16[3072,768]{1,0:T(8,128)(2,1)}, bf16[3072,768]{1,0:T(8,128)(2,1)S(1)}, u32[]{:S(2)}) %copy-start) | copy-done | bytes 4718616
  36.3 8.8 %all-to-all-start = ((f32[32,2,256]{2,1,0:T(2,128)}), f32[32,2,256]{2,1,0:T(2,128)S(1)}, u32[]{:S(2)}, u32[]{:S(2)}) async-start(f32[32,2,256]{2,1,0:T(2,128)} %get-tuple-element.33), calls=%async_computation | async-start | bytes 131072 | tf_op jit(solution)/shard_map/all_to_all | solution.py:385
  45.1 1.7 %fusion.4 = (bf16[4,12,2,256]{3,2,1,0:T(2,128)(2,1)}, bf16[4,12,2,256]{3,2,1,0:T(2,128)(2,1)}) fusion(bf16[4,12,40,256]{3,2,1,0:T(8,128)(2,1)} %constant_dynamic-update-slice_fusion), kind=kLoop, calls=%fused_computation.22 | loop fusion | bytes 196608 | tf_op jit(solution)/shard_map/slice | solution.py:425
  46.8 1.3 collective-permute-start.6
  48.1 4.6 %collective-permute-start.7 = (bf16[4,12,2,256]{3,2,1,0:T(2,128)(2,1)}, bf16[4,12,2,256]{3,2,1,0:T(2,128)(2,1)}, u32[]{:S(2)}, u32[]{:S(2)}) collective-permute-start(bf16[4,12,2,256]{3,2,1,0:T(2,128)(2,1)} %get-tuple-element.59), channel_id=1, source_target_pairs={{0,1},{1,2},{2,3},{4,5},{5,6},{6,7},{8,9},{9,10},{10,11},{12,13},{... | collective-permute-start | bytes 147464 | tf_op jit(solution)/shard_map/ppermute | solution.py:373
  52.8 1.3 copy-done.37
  54.0 3.8 %shard_map.170 = (bf16[2688,768]{1,0:T(8,128)(2,1)S(1)}, f32[2304,256]{1,0:T(8,128)S(1)}, f32[32,4,256]{2,1,0:T(4,128)S(1)}) custom-call(s32[5]{0:T(128)S(1)} %convert_element_type.2.bounds, f32[2688,256]{1,0:T(8,128)S(1)} %get-tuple-element.32.z1, f32[32,2,256]{2,1,0:T(2,128)S(1)} %all-to-all-done.st, f32[4,256]{1,0:T(4,128)S(1)} %copy-done.35, ...), custom_call_target="tpu_custom_call" | custom-call | flops 2717908992 | bytes 4194304 | tf_op jit(solution)/shard_map/pallas_call | solution.py:27
  57.8 2.0 %copy-done.3 = bf16[2688,768]{1,0:T(8,128)(2,1)} copy-done((bf16[2688,768]{1,0:T(8,128)(2,1)}, bf16[2688,768]{1,0:T(8,128)(2,1)S(1)}, u32[]{:S(2)}) %copy-start.3) | copy-done | bytes 4128792
  59.8 1.4 copy-done.7
  61.9 5.4 %all-to-all-start.1 = ((f32[32,4,256]{2,1,0:T(4,128)}), f32[32,4,256]{2,1,0:T(4,128)S(1)}, u32[]{:S(2)}, u32[]{:S(2)}) async-start(f32[32,4,256]{2,1,0:T(4,128)} %copy-done.34), calls=%async_computation.1 | async-start | bytes 262144 | tf_op jit(solution)/shard_map/all_to_all | solution.py:385
  67.4 1.6 %pad_maximum_fusion.1.cot_edges = bf16[4,12,8,256]{3,2,1,0:T(8,128)(2,1)} fusion(bf16[4,12,2,256]{3,2,1,0:T(2,128)(2,1)} %collective-permute-done.7, bf16[4,12,2,256]{3,2,1,0:T(2,128)(2,1)} %collective-permute-done.6, bf16[8]{0:T(256)(128)(2,1)S(1)} %pad.5.clone), kind=kLoop, calls=%fused_computation.3 | loop fusion | flops 589824 | bytes 294928 | tf_op jit(solution)/shard_map/concatenate | solution.py:428
  69.1 5.6 %all-to-all-done.1.st = f32[32,4,256]{2,1,0:T(4,128)S(1)} async-done(((f32[32,4,256]{2,1,0:T(4,128)}), f32[32,4,256]{2,1,0:T(4,128)S(1)}, u32[]{:S(2)}, u32[]{:S(2)}) %all-to-all-start.1) | async-done | bytes 131104 | tf_op jit(solution)/shard_map/all_to_all | solution.py:385
  74.6 2.2 %copy-done.4 = bf16[2688,768]{1,0:T(8,128)(2,1)S(1)} copy-done((bf16[2688,768]{1,0:T(8,128)(2,1)S(1)}, bf16[2688,768]{1,0:T(8,128)(2,1)}, u32[]{:S(2)}) %copy-start.4) | copy-done | bytes 4128792
  76.8 1.7 %copy-done.8 = f32[2304,256]{1,0:T(8,128)S(1)} copy-done((f32[2304,256]{1,0:T(8,128)S(1)}, f32[2304,256]{1,0:T(8,128)}, u32[]{:S(2)}) %copy-start.8) | copy-done | bytes 2359320
  78.5 0.9 copy-done.19
  79.4 0.9 copy-done.21
  80.3 0.9 copy-done.23
  81.2 8.1 %shard_map.171 = (bf16[4,8,40,256]{3,2,1,0:T(8,128)(2,1)}, bf16[2304,768]{1,0:T(8,128)(2,1)S(1)}, f32[9,128,256]{2,1,0:T(8,128)S(1)}, f32[9,128,256]{2,1,0:T(8,128)S(1)}) custom-call(s32[5]{0:T(128)S(1)} %convert_element_type.2.bounds, f32[2304,256]{1,0:T(8,128)S(1)} %copy-done.8, f32[32,4,256]{2,1,0:T(4,128)S(1)} %all-to-all-done.1.st, ...), custom_call_target="tpu_custom_call" | custom-call | flops 1811939328 | bytes 4194304 | tf_op jit(solution)/shard_map/pallas_call | solution.py:27
  89.3 1.3 collective-permute-start.9
  90.7 2.8 %shard_map.172 = (f32[1920,256]{1,0:T(8,128)S(1)}, f32[32,2,256]{2,1,0:T(2,128)S(1)}) custom-call(bf16[2304,768]{1,0:T(8,128)(2,1)S(1)} %get-tuple-element.40.d, bf16[2304,256]{1,0:T(8,128)(2,1)S(1)} %copy-done.38, f32[2688,256]{1,0:T(8,128)S(1)} %get-tuple-element.32.z1, f32[32,2,256]{2,1,0:T(2,128)S(1)} %copy-done.31, f32[4,256]{1,0:T(4,128)S(1)} %copy-done.35), custom_call_target="tpu_custom_call" | custom-call | flops 2264924160 | bytes 4194304 | tf_op jit(solution)/shard_map/pallas_call | solution.py:27
  93.5 8.3 %all_to_all.25.st3 = f32[32,2,256]{2,1,0:T(2,128)S(1)} all-to-all(f32[32,2,256]{2,1,0:T(2,128)S(1)} %get-tuple-element.42), channel_id=1, replica_groups=mesh['rows'=8,'cols'=4] {'rows','cols'}, dimensions={0} | all-to-all | bytes 131072 | tf_op jit(solution)/shard_map/all_to_all | solution.py:385
  101.8 8.0 %shard_map.173 = (bf16[1920,768]{1,0:T(8,128)(2,1)S(1)}, f32[9,128,256]{2,1,0:T(8,128)S(1)}, f32[9,128,256]{2,1,0:T(8,128)}) custom-call(s32[5]{0:T(128)S(1)} %convert_element_type.2.bounds, f32[1920,256]{1,0:T(8,128)S(1)} %get-tuple-element.41.dn_ref, f32[2688,256]{1,0:T(8,128)S(1)} %get-tuple-element.32.z1, f32[32,2,256]{2,1,0:T(2,128)S(1)} %copy-done.31, ...), custom_call_target="tpu_custom_call" | custom-call | flops 1811939328 | bytes 4194304 | tf_op jit(solution)/shard_map/pallas_call | solution.py:27
  109.7 1.6 %copy-done.5 = bf16[1920,768]{1,0:T(8,128)(2,1)} copy-done((bf16[1920,768]{1,0:T(8,128)(2,1)}, bf16[1920,768]{1,0:T(8,128)(2,1)S(1)}, u32[]{:S(2)}) %copy-start.5) | copy-done | bytes 2949144
  112.2 1.1 shard_map.176
  113.3 2.4 %all-to-all-start.4 = ((bf16[32,72,128]{2,1,0:T(8,128)(2,1)}), bf16[32,72,128]{2,1,0:T(8,128)(2,1)S(1)}, u32[]{:S(2)}, u32[]{:S(2)}) async-start(bf16[32,72,128]{2,1,0:T(8,128)(2,1)} %bitcast.9), calls=%async_computation.4 | async-start | bytes 1179648 | tf_op jit(solution)/shard_map/all_to_all | solution.py:385
  115.7 1.0 copy-done.17
  116.7 1.3 copy-done.16
  118.0 1.3 copy-done.18
  119.3 1.0 shard_map.175
  120.3 12.2 %all-to-all-done.4.two = bf16[32,72,128]{2,1,0:T(8,128)(2,1)S(1)} async-done(((bf16[32,72,128]{2,1,0:T(8,128)(2,1)}), bf16[32,72,128]{2,1,0:T(8,128)(2,1)S(1)}, u32[]{:S(2)}, u32[]{:S(2)}) %all-to-all-start.4) | async-done | bytes 589856 | tf_op jit(solution)/shard_map/all_to_all | solution.py:385
  132.5 3.1 %all-to-all-start.3 = ((bf16[32,72,128]{2,1,0:T(8,128)(2,1)}), bf16[32,72,128]{2,1,0:T(8,128)(2,1)S(1)}, u32[]{:S(2)}, u32[]{:S(2)}) async-start(bf16[32,72,128]{2,1,0:T(8,128)(2,1)} %bitcast.8), calls=%async_computation.3 | async-start | bytes 1179648 | tf_op jit(solution)/shard_map/all_to_all | solution.py:385
  135.6 0.9 constant_dynamic-slice_fusion.w
  136.9 1.8 %copy-done.6 = bf16[1920,768]{1,0:T(8,128)(2,1)S(1)} copy-done((bf16[1920,768]{1,0:T(8,128)(2,1)S(1)}, bf16[1920,768]{1,0:T(8,128)(2,1)}, u32[]{:S(2)}) %copy-start.6) | copy-done | bytes 2949144
  138.8 3.1 %shard_map.174 = f32[4,8,40,256]{3,2,1,0:T(8,128)} custom-call(bf16[1920,768]{1,0:T(8,128)(2,1)S(1)} %copy-done.6, bf16[2304,256]{1,0:T(8,128)(2,1)S(1)} %copy-done.14, bf16[4,8,40,256]{3,2,1,0:T(8,128)(2,1)S(1)} %copy-done.1, bf16[4,8,40,256]{3,2,1,0:T(8,128)(2,1)S(1)} %broadcast_in_dim.5.mask), custom_call_target="tpu_custom_call" | custom-call | flops 1811939328 | bytes 4194304 | tf_op jit(solution)/shard_map/pallas_call | solution.py:27
  142.5 9.8 %all-to-all-done.3.one = bf16[32,72,128]{2,1,0:T(8,128)(2,1)S(1)} async-done(((bf16[32,72,128]{2,1,0:T(8,128)(2,1)}), bf16[32,72,128]{2,1,0:T(8,128)(2,1)S(1)}, u32[]{:S(2)}, u32[]{:S(2)}) %all-to-all-start.3) | async-done | bytes 589856 | tf_op jit(solution)/shard_map/all_to_all | solution.py:385
  152.3 1.1 shard_map.177
  (95 shorter events, 7.0 us)
Async XLA Ops:
  2.7 17.3 %copy-start.9 = (bf16[4,4,40,256]{3,2,1,0:T(8,128)(2,1)}, bf16[4,4,40,256]{3,2,1,0:T(8,128)(2,1)S(1)}, u32[]{:S(2)}) copy-start(bf16[4,4,40,256]{3,2,1,0:T(8,128)(2,1)S(1)} %get-tuple-element.62.top) | copy-start | bytes 983044
  2.7 17.3 %copy-start.11 = (bf16[4,4,40,256]{3,2,1,0:T(8,128)(2,1)}, bf16[4,4,40,256]{3,2,1,0:T(8,128)(2,1)S(1)}, u32[]{:S(2)}) copy-start(bf16[4,4,40,256]{3,2,1,0:T(8,128)(2,1)S(1)} %get-tuple-element.63.bottom) | copy-start | bytes 983044
  2.7 17.3 %collective-permute-start = (bf16[4,4,40,256]{3,2,1,0:T(8,128)(2,1)S(1)}, bf16[4,4,40,256]{3,2,1,0:T(8,128)(2,1)S(1)}, u32[]{:S(2)}, u32[]{:S(2)}) collective-permute-start(bf16[4,4,40,256]{3,2,1,0:T(8,128)(2,1)S(1)} %get-tuple-element.63.bottom), channel_id=1, source_target_pairs={{0,4},{4,8},{8,12},{12,16},{16,20},{20,24},{24,28},{1,5},{5,9},{9,... | collective-permute-start | bytes 983048 | tf_op jit(solution)/shard_map/ppermute | solution.py:373
  7.2 12.8 %collective-permute-start.1 = (bf16[4,4,40,256]{3,2,1,0:T(8,128)(2,1)S(1)}, bf16[4,4,40,256]{3,2,1,0:T(8,128)(2,1)S(1)}, u32[]{:S(2)}, u32[]{:S(2)}) collective-permute-start(bf16[4,4,40,256]{3,2,1,0:T(8,128)(2,1)S(1)} %get-tuple-element.62.top), channel_id=1, source_target_pairs={{4,0},{8,4},{12,8},{16,12},{20,16},{24,20},{28,24},{5,1},{9,5},{13... | collective-permute-start | bytes 983048 | tf_op jit(solution)/shard_map/ppermute | solution.py:373
  10.9 8.4 %collective-permute-start.4 = (bf16[4,2,40,256]{3,2,1,0:T(8,128)(2,1)}, bf16[4,2,40,256]{3,2,1,0:T(8,128)(2,1)S(1)}, u32[]{:S(2)}, u32[]{:S(2)}) collective-permute-start(bf16[4,2,40,256]{3,2,1,0:T(8,128)(2,1)} %get-tuple-element.61), channel_id=1, source_target_pairs={{0,4},{4,8},{8,12},{12,16},{16,20},{20,24},{24,28},{1,5},{5,9},{9,... | collective-permute-start | bytes 491528 | tf_op jit(solution)/shard_map/ppermute | solution.py:373
  14.5 12.0 %collective-permute-start.5 = (bf16[4,2,40,256]{3,2,1,0:T(8,128)(2,1)}, bf16[4,2,40,256]{3,2,1,0:T(8,128)(2,1)S(1)}, u32[]{:S(2)}, u32[]{:S(2)}) collective-permute-start(bf16[4,2,40,256]{3,2,1,0:T(8,128)(2,1)} %get-tuple-element.60), channel_id=1, source_target_pairs={{4,0},{8,4},{12,8},{16,12},{20,16},{24,20},{28,24},{5,1},{9,5},{13... | collective-permute-start | bytes 491528 | tf_op jit(solution)/shard_map/ppermute | solution.py:373
  16.6 2.3 %copy-start.2 = (f32[2,589824]{1,0:T(2,128)S(1)}, f32[2,589824]{1,0:T(2,128)}, u32[]{:S(2)}) copy-start(f32[2,589824]{1,0:T(2,128)} %param.12) | copy-start | bytes 14155780
  19.3 8.7 %copy-start.36 = (bf16[2304,256]{1,0:T(8,128)(2,1)}, bf16[2304,256]{1,0:T(8,128)(2,1)S(1)}, u32[]{:S(2)}) copy-start(bf16[2304,256]{1,0:T(8,128)(2,1)S(1)} %get-tuple-element.34.w) | copy-start | bytes 3538948
  19.3 8.7 %copy-start.13 = (bf16[2304,256]{1,0:T(8,128)(2,1)}, bf16[2304,256]{1,0:T(8,128)(2,1)S(1)}, u32[]{:S(2)}) copy-start(bf16[2304,256]{1,0:T(8,128)(2,1)S(1)} %get-tuple-element.31.w) | copy-start | bytes 3538948
  19.3 6.3 %copy-start.1 = (bf16[4,8,40,256]{3,2,1,0:T(8,128)(2,1)S(1)}, bf16[4,8,40,256]{3,2,1,0:T(8,128)(2,1)}, u32[]{:S(2)}) copy-start(bf16[4,8,40,256]{3,2,1,0:T(8,128)(2,1)} %cot.5) | copy-start | bytes 1966084
  19.3 8.6 %copy-start.20 = (bf16[4,2,40,256]{3,2,1,0:T(8,128)(2,1)}, bf16[4,2,40,256]{3,2,1,0:T(8,128)(2,1)S(1)}, u32[]{:S(2)}) copy-start(bf16[4,2,40,256]{3,2,1,0:T(8,128)(2,1)S(1)} %collective-permute-done.4.cot_up) | copy-start | bytes 491524
  20.0 7.9 %copy-start.26 = (bf16[4,4,40,256]{3,2,1,0:T(8,128)(2,1)}, bf16[4,4,40,256]{3,2,1,0:T(8,128)(2,1)S(1)}, u32[]{:S(2)}) copy-start(bf16[4,4,40,256]{3,2,1,0:T(8,128)(2,1)S(1)} %collective-permute-done.up) | copy-start | bytes 983044
  20.0 7.9 %copy-start.28 = (bf16[4,4,40,256]{3,2,1,0:T(8,128)(2,1)}, bf16[4,4,40,256]{3,2,1,0:T(8,128)(2,1)S(1)}, u32[]{:S(2)}) copy-start(bf16[4,4,40,256]{3,2,1,0:T(8,128)(2,1)S(1)} %collective-permute-done.1.down) | copy-start | bytes 983044
  20.2 7.8 %copy-start.10 = (bf16[4,4,40,256]{3,2,1,0:T(8,128)(2,1)S(1)}, bf16[4,4,40,256]{3,2,1,0:T(8,128)(2,1)}, u32[]{:S(2)}) copy-start(bf16[4,4,40,256]{3,2,1,0:T(8,128)(2,1)} %copy-done.9) | copy-start | bytes 983044
  20.2 7.8 %copy-start.12 = (bf16[4,4,40,256]{3,2,1,0:T(8,128)(2,1)S(1)}, bf16[4,4,40,256]{3,2,1,0:T(8,128)(2,1)}, u32[]{:S(2)}) copy-start(bf16[4,4,40,256]{3,2,1,0:T(8,128)(2,1)} %copy-done.11) | copy-start | bytes 983044
  20.2 7.1 %collective-permute-start.2 = (bf16[4,16,4,256]{3,2,1,0:T(4,128)(2,1)S(1)}, bf16[4,16,4,256]{3,2,1,0:T(4,128)(2,1)S(1)}, u32[]{:S(2)}, u32[]{:S(2)}) collective-permute-start(bf16[4,16,4,256]{3,2,1,0:T(4,128)(2,1)S(1)} %get-tuple-element.56), channel_id=1, source_target_pairs={{1,0},{2,1},{3,2},{5,4},{6,5},{7,6},{9,8},{10,9},{11,10},{13,12},{... | collective-permute-start | bytes 393224 | tf_op jit(solution)/shard_map/ppermute | solution.py:373
  21.6 6.2 %collective-permute-start.3 = (bf16[4,16,4,256]{3,2,1,0:T(4,128)(2,1)S(1)}, bf16[4,16,4,256]{3,2,1,0:T(4,128)(2,1)S(1)}, u32[]{:S(2)}, u32[]{:S(2)}) collective-permute-start(bf16[4,16,4,256]{3,2,1,0:T(4,128)(2,1)S(1)} %get-tuple-element.57), channel_id=1, source_target_pairs={{0,1},{1,2},{2,3},{4,5},{5,6},{6,7},{8,9},{9,10},{10,11},{12,13},{... | collective-permute-start | bytes 393224 | tf_op jit(solution)/shard_map/ppermute | solution.py:373
  26.5 1.5 copy-start.22
  30.0 22.8 %copy-start.35 = (f32[4,256]{1,0:T(4,128)S(1)}, f32[4,256]{1,0:T(4,128)}, u32[]{:S(2)}) copy-start(f32[4,256]{1,0:T(4,128)} %params.7) | copy-start | bytes 12292
  34.1 2.2 %copy-start = (bf16[3072,768]{1,0:T(8,128)(2,1)}, bf16[3072,768]{1,0:T(8,128)(2,1)S(1)}, u32[]{:S(2)}) copy-start(bf16[3072,768]{1,0:T(8,128)(2,1)S(1)} %get-tuple-element.37.x) | copy-start | bytes 14155780
  36.3 16.5 %all-to-all-start = ((f32[32,2,256]{2,1,0:T(2,128)}), f32[32,2,256]{2,1,0:T(2,128)S(1)}, u32[]{:S(2)}, u32[]{:S(2)}) async-start(f32[32,2,256]{2,1,0:T(2,128)} %get-tuple-element.33), calls=%async_computation | async-start | bytes 131072 | tf_op jit(solution)/shard_map/all_to_all | solution.py:385
  46.8 20.6 %collective-permute-start.6 = (bf16[4,12,2,256]{3,2,1,0:T(2,128)(2,1)}, bf16[4,12,2,256]{3,2,1,0:T(2,128)(2,1)}, u32[]{:S(2)}, u32[]{:S(2)}) collective-permute-start(bf16[4,12,2,256]{3,2,1,0:T(2,128)(2,1)} %get-tuple-element.58), channel_id=1, source_target_pairs={{1,0},{2,1},{3,2},{5,4},{6,5},{7,6},{9,8},{10,9},{11,10},{13,12},{... | collective-permute-start | bytes 147464 | tf_op jit(solution)/shard_map/ppermute | solution.py:373
  48.1 19.3 %collective-permute-start.7 = (bf16[4,12,2,256]{3,2,1,0:T(2,128)(2,1)}, bf16[4,12,2,256]{3,2,1,0:T(2,128)(2,1)}, u32[]{:S(2)}, u32[]{:S(2)}) collective-permute-start(bf16[4,12,2,256]{3,2,1,0:T(2,128)(2,1)} %get-tuple-element.59), channel_id=1, source_target_pairs={{0,1},{1,2},{2,3},{4,5},{5,6},{6,7},{8,9},{9,10},{10,11},{12,13},{... | collective-permute-start | bytes 147464 | tf_op jit(solution)/shard_map/ppermute | solution.py:373
  52.7 5.1 %copy-start.30 = (f32[32,2,256]{2,1,0:T(2,128)}, f32[32,2,256]{2,1,0:T(2,128)S(1)}, u32[]{:S(2)}) copy-start(f32[32,2,256]{2,1,0:T(2,128)S(1)} %all-to-all-done.st) | copy-start | bytes 196612
  52.8 1.3 copy-start.37
  57.8 2.0 %copy-start.3 = (bf16[2688,768]{1,0:T(8,128)(2,1)}, bf16[2688,768]{1,0:T(8,128)(2,1)S(1)}, u32[]{:S(2)}) copy-start(bf16[2688,768]{1,0:T(8,128)(2,1)S(1)} %get-tuple-element.38.h) | copy-start | bytes 12386308
  59.8 1.4 copy-start.7
  61.9 12.8 %all-to-all-start.1 = ((f32[32,4,256]{2,1,0:T(4,128)}), f32[32,4,256]{2,1,0:T(4,128)S(1)}, u32[]{:S(2)}, u32[]{:S(2)}) async-start(f32[32,4,256]{2,1,0:T(4,128)} %copy-done.34), calls=%async_computation.1 | async-start | bytes 262144 | tf_op jit(solution)/shard_map/all_to_all | solution.py:385
  74.6 2.2 %copy-start.4 = (bf16[2688,768]{1,0:T(8,128)(2,1)S(1)}, bf16[2688,768]{1,0:T(8,128)(2,1)}, u32[]{:S(2)}) copy-start(bf16[2688,768]{1,0:T(8,128)(2,1)} %copy-done.3) | copy-start | bytes 12386308
  76.8 1.7 %copy-start.8 = (f32[2304,256]{1,0:T(8,128)S(1)}, f32[2304,256]{1,0:T(8,128)}, u32[]{:S(2)}) copy-start(f32[2304,256]{1,0:T(8,128)} %copy-done.7) | copy-start | bytes 7077892
  81.2 9.4 %copy-start.31 = (f32[32,2,256]{2,1,0:T(2,128)S(1)}, f32[32,2,256]{2,1,0:T(2,128)}, u32[]{:S(2)}) copy-start(f32[32,2,256]{2,1,0:T(2,128)} %copy-done.30) | copy-start | bytes 196612
  81.2 9.4 %copy-start.38 = (bf16[2304,256]{1,0:T(8,128)(2,1)S(1)}, bf16[2304,256]{1,0:T(8,128)(2,1)}, u32[]{:S(2)}) copy-start(bf16[2304,256]{1,0:T(8,128)(2,1)} %copy-done.36) | copy-start | bytes 3538948
  89.3 22.9 %collective-permute-start.9 = (f32[9,128,256]{2,1,0:T(8,128)S(1)}, f32[9,128,256]{2,1,0:T(8,128)S(1)}, u32[]{:S(2)}, u32[]{:S(2)}) collective-permute-start(f32[9,128,256]{2,1,0:T(8,128)S(1)} %get-tuple-element.47), channel_id=1, source_target_pairs={{0,4},{4,0},{8,12},{12,8},{16,20},{20,16},{24,28},{28,24},{1,5},{5... | collective-permute-start | bytes 3538952 | tf_op jit(solution)/shard_map/ppermute | solution.py:480
  101.8 8.0 %copy-start.24 = (f32[32,2,256]{2,1,0:T(2,128)}, f32[32,2,256]{2,1,0:T(2,128)S(1)}, u32[]{:S(2)}) copy-start(f32[32,2,256]{2,1,0:T(2,128)S(1)} %all_to_all.25.st3) | copy-start | bytes 196612
  109.7 1.6 %copy-start.5 = (bf16[1920,768]{1,0:T(8,128)(2,1)}, bf16[1920,768]{1,0:T(8,128)(2,1)S(1)}, u32[]{:S(2)}) copy-start(bf16[1920,768]{1,0:T(8,128)(2,1)S(1)} %get-tuple-element.43.e) | copy-start | bytes 8847364
  111.3 2.0 %copy-start.15 = (f32[9,128,256]{2,1,0:T(8,128)}, f32[9,128,256]{2,1,0:T(8,128)S(1)}, u32[]{:S(2)}) copy-start(f32[9,128,256]{2,1,0:T(8,128)S(1)} %get-tuple-element.44.keep) | copy-start | bytes 3538948
  111.3 4.4 %collective-permute-start.8 = (f32[9,128,256]{2,1,0:T(8,128)}, f32[9,128,256]{2,1,0:T(8,128)S(1)}, u32[]{:S(2)}, u32[]{:S(2)}) collective-permute-start(f32[9,128,256]{2,1,0:T(8,128)} %get-tuple-element.45), channel_id=1, source_target_pairs={{0,4},{4,0},{8,12},{12,8},{16,20},{20,16},{24,28},{28,24},{1,5},{5... | collective-permute-start | bytes 3538952 | tf_op jit(solution)/shard_map/ppermute | solution.py:498
  113.3 19.2 %all-to-all-start.4 = ((bf16[32,72,128]{2,1,0:T(8,128)(2,1)}), bf16[32,72,128]{2,1,0:T(8,128)(2,1)S(1)}, u32[]{:S(2)}, u32[]{:S(2)}) async-start(bf16[32,72,128]{2,1,0:T(8,128)(2,1)} %bitcast.9), calls=%async_computation.4 | async-start | bytes 1179648 | tf_op jit(solution)/shard_map/all_to_all | solution.py:385
  116.7 1.3 copy-start.16
  118.0 1.3 copy-start.18
  119.3 17.4 %copy-start.25 = (f32[32,2,256]{2,1,0:T(2,128)S(1)}, f32[32,2,256]{2,1,0:T(2,128)}, u32[]{:S(2)}) copy-start(f32[32,2,256]{2,1,0:T(2,128)} %copy-done.24) | copy-start | bytes 196612
  119.3 17.7 %copy-start.14 = (bf16[2304,256]{1,0:T(8,128)(2,1)S(1)}, bf16[2304,256]{1,0:T(8,128)(2,1)}, u32[]{:S(2)}) copy-start(bf16[2304,256]{1,0:T(8,128)(2,1)} %copy-done.13) | copy-start | bytes 3538948
  132.5 19.8 %all-to-all-start.3 = ((bf16[32,72,128]{2,1,0:T(8,128)(2,1)}), bf16[32,72,128]{2,1,0:T(8,128)(2,1)S(1)}, u32[]{:S(2)}, u32[]{:S(2)}) async-start(bf16[32,72,128]{2,1,0:T(8,128)(2,1)} %bitcast.8), calls=%async_computation.3 | async-start | bytes 1179648 | tf_op jit(solution)/shard_map/all_to_all | solution.py:385
  136.9 1.8 %copy-start.6 = (bf16[1920,768]{1,0:T(8,128)(2,1)S(1)}, bf16[1920,768]{1,0:T(8,128)(2,1)}, u32[]{:S(2)}) copy-start(bf16[1920,768]{1,0:T(8,128)(2,1)} %copy-done.5) | copy-start | bytes 8847364
  138.8 3.1 %copy-start.39 = (f32[4,256]{1,0:T(4,128)S(1)}, f32[4,256]{1,0:T(4,128)}, u32[]{:S(2)}) copy-start(f32[4,256]{1,0:T(4,128)} %param.16) | copy-start | bytes 12292
  138.8 3.1 %copy-start.40 = (f32[4,256]{1,0:T(4,128)S(1)}, f32[4,256]{1,0:T(4,128)}, u32[]{:S(2)}) copy-start(f32[4,256]{1,0:T(4,128)} %param.17) | copy-start | bytes 12292
  138.8 13.5 %copy-start.32 = (f32[2,18432]{1,0:T(2,128)S(1)}, f32[2,18432]{1,0:T(2,128)}, u32[]{:S(2)}) copy-start(f32[2,18432]{1,0:T(2,128)} %param.13) | copy-start | bytes 442372
  138.8 13.5 %copy-start.33 = (f32[2,18432]{1,0:T(2,128)S(1)}, f32[2,18432]{1,0:T(2,128)}, u32[]{:S(2)}) copy-start(f32[2,18432]{1,0:T(2,128)} %param.14) | copy-start | bytes 442372
  (7 other events, 6.4 us)
where the time goes:
time: 155 us; the launch traced here: 153 us
  starting transfers between devices  45.3 us (29%)
  Pallas kernels  33.3 us (21%)
  local copies, waits for them, and re-layouts  32.5 us (21%)
  waiting for transfers between devices  28.1 us (18%)
  blocking collectives  8.29 us (5%)
  other arithmetic  4.65 us (3%)
    pallas_call x10, Pallas kernels, call(): pl.pallas_call(body, out_shape=out_shape, in_specs=specs, out_specs=[pl.B...  33.3 us
    all_to_all x4, waiting for transfers between devices, exchange(): return lax.all_to_all(parts, BOTH, 0, 0, tiled=True)  27.6 us
    unnamed x84, local copies, waits for them, and re-layouts  27 us
    ppermute x8, starting transfers between devices, shifted(): return lax.ppermute(block, axis, pairs)  23.3 us
    all_to_all x4, starting transfers between devices, exchange(): return lax.all_to_all(parts, BOTH, 0, 0, tiled=True)  19.8 us
    all_to_all x1, blocking collectives, exchange(): return lax.all_to_all(parts, BOTH, 0, 0, tiled=True)  8.29 us
  transfers between devices with their start and end apart: 14, of which 4 were waited for; matrix products, arithmetic and copies ran while one was open for 6% of the time, Pallas kernels for 13%

commit v1 on v0

v1 whole, which is shorter than its diff:
```python
import functools
import math

import jax
import jax.numpy as jnp
from jax import lax
from jax.experimental import pallas as pl
from jax.experimental.pallas import tpu as pltpu
from jax.sharding import PartitionSpec as P

STEP = 5
BOTH = ("rows", "cols")
RIM = 4
F32, BF16 = jnp.float32, jnp.bfloat16


def shape_of(shape, dtype):
    return jax.ShapeDtypeStruct(shape, dtype)


def held(shape, dtype):
    return pltpu.VMEM(shape, dtype)


def stored(shape, dtype):
    return pltpu.HBM(shape, dtype)


def kernel_call(body, out_shape, flops, far=(), far_out=(), scratch=(), limit=16, alias=None, size=4 << 20):
    def call(*operands):
        operands = [
            pltpu.with_memory_space_constraint(v, pltpu.HBM if i in far else pltpu.VMEM)
            for i, v in enumerate(operands)
        ]
        specs = [
            pl.BlockSpec(memory_space=pltpu.HBM if i in far else pltpu.VMEM)
            for i in range(len(operands))
        ]
        return pl.pallas_call(
            body,
            out_shape=out_shape,
            in_specs=specs,
            out_specs=[
                pl.BlockSpec(memory_space=pltpu.HBM if i in far_out else pltpu.VMEM)
                for i in range(len(out_shape))
            ],
            scratch_shapes=list(scratch),
            input_output_aliases=alias or {},
            compiler_params=pltpu.CompilerParams(vmem_limit_bytes=limit << 20),
            cost_estimate=pl.CostEstimate(
                flops=int(flops), bytes_accessed=size, transcendentals=0
            ),
        )(*operands)

    return call


def dot(a, b):
    return jnp.dot(a, b, preferred_element_type=F32)


def dot_nt(a, b):
    return lax.dot_general(a, b, (((1,), (1,)), ((), ())), preferred_element_type=F32)


def total_of(ref):
    count = ref.shape[0]
    total = ref[0]
    for i in range(1, count):
        total = total + ref[i]
    return total


def to_all(ref, parts):
    value = jnp.concatenate(parts, axis=0)
    for i in range(ref.shape[0]):
        ref[i] = value


def store_shifted(ref, start, row):
    width, chans = row.shape
    at = pl.ds(start if isinstance(start, int) else pl.multiple_of(start, 16), width)
    ref[at, 0:chans] = pltpu.roll(row, 1, 0).astype(BF16)
    ref[at, chans : 2 * chans] = row.astype(BF16)
    ref[at, 2 * chans : 3 * chans] = pltpu.roll(row, width - 1, 0).astype(BF16)


class Geometry:
    def __init__(self, scenes, height, width, chans):
        self.s, self.h, self.w, self.c = scenes, height, width, chans
        self.wp = width + 2 * RIM
        self.tall = height + 2 * RIM
        self.near = RIM // 2
        self.cot_tall = height + 2 * self.near
        self.side = (RIM + self.near) * height


class Place:
    def __init__(self):
        row, col = lax.axis_index("rows"), lax.axis_index("cols")
        nrows, ncols = lax.axis_size("rows"), lax.axis_size("cols")
        self.above = (row > 0).astype(F32)
        self.below = (row < nrows - 1).astype(F32)
        self.right = (col < ncols - 1).astype(F32)
        self.left = (col > 0).astype(F32)
        self.core = row % 2
        self.odd_row = row % 2 == 1
        self.odd_col = col % 2 == 1
        self.index = row * ncols + col


def wide(ref, *index):
    return ref[index].astype(F32)


def far_row(rb, rb_edge, s, k):
    return jnp.concatenate([wide(rb, s, k), wide(rb_edge, s, k)], axis=0)


def pixel_mask(occ, s):
    return occ[s].astype(F32).T


def in_grid(row, r, g, place, edge):
    row = jnp.concatenate([row[: g.w], row[g.w :] * edge], axis=0)
    if r < RIM:
        row = row * place.above
    elif r >= RIM + g.h:
        row = row * place.below
    return row


def edge_mask(place, g):
    where = lax.broadcasted_iota(jnp.int32, (2 * RIM, g.c), 0)
    return jnp.where(where < RIM, place.right, place.left)


def sum_rows(value):
    rows, chans = value.shape
    return jnp.sum(value.reshape(rows // 8, 8, chans), axis=0)


def pack_kernel(g, features, occ_far, cot, own, c_ref, d_ref, b_ref, given, seen, occ, sems):
    copies = []
    flags = pltpu.make_async_copy(occ_far, occ, sems.at[2, 0])
    flags.start()
    for s in range(g.s):
        copies.append(
            (
                pltpu.make_async_copy(features.at[s], given.at[s], sems.at[0, s]),
                pltpu.make_async_copy(cot.at[s], seen.at[s], sems.at[1, s]),
            )
        )
        for copy in copies[-1]:
            copy.start()
    odd, odd_row = Place().odd_col, Place().odd_row
    flags.wait()

    def put(s, at, rights, lefts):
        right, left = jnp.concatenate(rights, axis=0), jnp.concatenate(lefts, axis=0)
        c_ref[s, at : at + 16] = jnp.where(odd, left, right).astype(BF16)
        d_ref[s, at : at + 16] = jnp.where(odd, right, left).astype(BF16)

    for s in range(g.s):
        mask = pixel_mask(occ, s)
        for copy in copies[s]:
            copy.wait()
        rows = []
        for r in range(g.h):
            row = wide(given, s, r) * mask[:, r : r + 1]
            rows.append(row)
            own[s, r] = row.astype(BF16)
        cots = [wide(seen, s, r) for r in range(g.h)]
        for k in range(RIM):
            b_ref[s, k] = jnp.where(odd_row, rows[g.h - RIM + k], rows[k]).astype(BF16)
        for k in range(g.near):
            b_ref[s, RIM + k] = jnp.where(odd_row, cots[g.h - g.near + k], cots[k]).astype(BF16)
        for width, at, field in ((RIM, 0, rows), (g.near, RIM * g.h, cots)):
            for k in range(0, g.h, 16 // width):
                group = field[k : k + 16 // width]
                put(s, at + width * k, [v[g.w - width :] for v in group], [v[:width] for v in group])


def assemble_kernel(g, own, cot, rc, rd, ext, cot_ext, a_ref, b_edge):
    place = Place()

    def rows_of(source, s, at, width):
        gap = jnp.zeros((2 * RIM - 2 * width, g.c), F32)
        rows = []
        for first in range(0, g.h, 16 // width):
            k = at + width * first
            c, d = wide(rc, s, slice(k, k + 16)), wide(rd, s, slice(k, k + 16))
            right, left = jnp.where(place.odd_col, d, c), jnp.where(place.odd_col, c, d)
            for r in range(first, min(g.h, first + 16 // width)):
                at_row = slice(width * (r - first), width * (r - first + 1))
                parts = [wide(source, s, r), right[at_row], gap, left[at_row]]
                rows.append(jnp.concatenate([p for p in parts if p.shape[0]], axis=0))
        return rows

    odd = place.odd_row
    for s in range(g.s):
        rows = rows_of(own, s, 0, RIM)
        top, bottom = rows[:RIM], rows[g.h - RIM :]
        for r in range(g.h):
            ext[s, r] = rows[r].astype(BF16)
        for k in range(RIM):
            a_ref[s, k] = jnp.where(odd, top[k], bottom[k]).astype(BF16)
            b_edge[s, k] = jnp.where(odd, bottom[k], top[k])[g.w :].astype(BF16)
        rows = rows_of(cot, s, RIM * g.h, g.near)
        for r in range(g.h):
            cot_ext[s, r] = rows[r].astype(BF16)
        for k in range(g.near):
            top, bottom = rows[k], rows[g.h - g.near + k]
            a_ref[s, RIM + k] = jnp.where(odd, top, bottom).astype(BF16)
            b_edge[s, RIM + k] = jnp.where(odd, bottom, top)[g.w :].astype(BF16)


def prepare_kernel(w_ref, one_ref, two_ref, buffer, sems):
    chans = one_ref.shape[1]
    taps, size, lanes = buffer.shape
    per = chans // lanes
    copies = [
        pltpu.make_async_copy(w_ref.at[pl.ds(t * size, size)], buffer.at[t], sems.at[t])
        for t in range(taps)
    ]
    for copy in copies:
        copy.start()
    for t in range(taps):
        copies[t].wait()
        for k, out in enumerate((one_ref, two_ref)):
            parts = [buffer[t, pl.ds(2 * half + k, chans, stride=2 * per), :] for half in range(per)]
            out[t * chans : (t + 1) * chans, :] = jnp.concatenate(parts, axis=1).astype(BF16)


def place_shifted(ref, row_index, row):
    store_shifted(ref, row_index * row.shape[0], row)


def window_rows(g, x_ref, first, count):
    size = count * g.wp
    return jnp.concatenate(
        [x_ref[(first + a) * g.wp : (first + a) * g.wp + size, :] for a in range(3)], axis=1
    )


def own_conv_kernel(g, ext, w, z_ref, st_ref, x_ref):
    count = g.h - 2
    s1 = jnp.zeros((8, g.c), F32)
    s2 = jnp.zeros((8, g.c), F32)
    for s in range(g.s):
        for r in range(g.h):
            place_shifted(x_ref, s * g.h + r, wide(ext, s, r))
        half = count // 2
        for first in range(0, count, half):
            acc = dot(window_rows(g, x_ref, s * g.h + first, half), w[...])
            at = (s * (g.tall - 2) + RIM + first) * g.wp
            z_ref[at : at + half * g.wp, :] = acc
            for i in range(half):
                v = acc[i * g.wp : i * g.wp + g.w]
                s1 = s1 + sum_rows(v)
                s2 = s2 + sum_rows(v * v)
    st_ref[0:8] = s1
    st_ref[8:16] = s2


def rim_conv_kernel(g, ext, ra, rb, rb_edge, w, st_in, z_in, z_ref, st_ref, x_ref):
    del z_in
    odd = Place().odd_row
    s1, s2 = st_in[0:8], st_in[8:16]
    span = RIM + 2
    for s in range(g.s):
        for side in range(2):
            base = span * (2 * s + side)
            for k in range(RIM):
                near, far = wide(ra, s, k), far_row(rb, rb_edge, s, k)
                row = jnp.where(odd, near, far) if side == 0 else jnp.where(odd, far, near)
                place_shifted(x_ref, base + 2 * side + k, row)
            for j in range(2):
                own = wide(ext, s, (g.h - 2) * side + j)
                place_shifted(x_ref, base + RIM * (1 - side) + j, own)
            acc = dot(window_rows(g, x_ref, base, RIM), w[...])
            at = (s * (g.tall - 2) + (g.h + RIM - 2) * side) * g.wp
            z_ref[at : at + RIM * g.wp, :] = acc
            i = 0 if side else RIM - 1
            v = acc[i * g.wp : i * g.wp + g.w]
            s1 = s1 + sum_rows(v)
            s2 = s2 + sum_rows(v * v)
    to_all(st_ref, [jnp.sum(s1, 0, keepdims=True), jnp.sum(s2, 0, keepdims=True)])


def stats_of(total, count):
    mean = total[0:1] / count
    var = total[1:2] / count - mean * mean
    return mean, lax.rsqrt(var + 1e-05)


def second_conv_kernel(g, chunk, count, z1, st, params, w, cot, h_ref, z_ref, st_ref):
    rows_in, rows_out = g.tall - 2, g.tall - 4
    place = Place()
    mean, rstd = stats_of(total_of(st), count)
    scale = params[0:1] * rstd
    shift = params[1:2] - mean * scale
    edge = edge_mask(place, g)
    sums = [jnp.zeros((8, g.c), F32) for _ in range(4)]
    for s in range(g.s):
        for r in range(rows_in):
            start = (s * rows_in + r) * g.wp
            row = jnp.maximum(z1[start : start + g.wp, :] * scale + shift, 0.0)
            store_shifted(h_ref, start, in_grid(row, r + 1, g, place, edge))
        for r in range(0, rows_out, chunk):
            base = (s * rows_in + r) * g.wp
            size = chunk * g.wp
            lhs = jnp.concatenate(
                [h_ref[base + a * g.wp : base + a * g.wp + size, :] for a in range(3)], axis=1
            )
            acc = dot(lhs, w[...])
            z_ref[(s * rows_out + r) * g.wp : (s * rows_out + r) * g.wp + size, :] = acc
            for i in range(chunk):
                if RIM <= r + i + 2 < RIM + g.h:
                    v = acc[i * g.wp : i * g.wp + g.w]
                    dn = wide(cot, s, r + i + 2 - RIM)[: g.w]
                    for k, term in enumerate((v, v * v, dn, dn * v)):
                        sums[k] = sums[k] + sum_rows(term)
    to_all(st_ref, [jnp.sum(v, 0, keepdims=True) for v in sums])


def own_transposed(g, source, first, lane, s, dt_ref):
    span = g.h * g.wp
    block = source[first : first + span, lane : lane + g.c]
    inside = lax.broadcasted_iota(jnp.int32, (span, 1), 0) % g.wp < g.w
    dt_ref[:, s * span : (s + 1) * span] = jnp.where(inside, block, jnp.zeros_like(block)).T


def kernel_gradient(g, core, field, rows_field, first_row, dt_ref, keep, send):
    chans, half = g.c, g.c // 2
    span = g.h * g.wp
    mine = pl.ds(pl.multiple_of(core * half, half), half)
    other = pl.ds(pl.multiple_of((1 - core) * half, half), half)
    lhs = jnp.concatenate([dt_ref[mine, :], dt_ref[other, :]], axis=0)
    for a in range(3):
        starts = [(s * rows_field + first_row + a) * g.wp for s in range(g.s)]
        acc = dot(lhs, jnp.concatenate([field[at : at + span, :] for at in starts], axis=0))
        for b in range(3):
            keep[a * 3 + b] = acc[0:half, b * chans : (b + 1) * chans]
            send[a * 3 + b] = acc[half:, b * chans : (b + 1) * chans]


def second_gradient_kernel(
    g, count, z2, st, params, ext, cot, ra, rb, rb_edge, h, out_ref, d_ref, keep, send, dt_ref
):
    place = Place()
    rows = g.cot_tall
    total = total_of(st)
    mean, rstd = stats_of(total, count)
    sum_dn = total[2:3]
    sum_dx = rstd * (total[3:4] - mean * sum_dn)
    k0 = params[2:3] * rstd
    k1 = k0 * (sum_dn / count)
    k2 = k0 * rstd * (sum_dx / count)
    shift = params[3:4]
    edge = edge_mask(place, g)

    def cotangent(s, i):
        if g.near <= i < g.near + g.h:
            return wide(cot, s, i - g.near)
        k = i if i < g.near else i - g.near - g.h
        k += RIM
        return jnp.where(
            place.odd_row == (i < g.near), wide(ra, s, k), far_row(rb, rb_edge, s, k)
        )

    for s in range(g.s):
        for i in range(rows):
            r = i + RIM - g.near
            start = (s * rows + i) * g.wp
            centred = z2[start : start + g.wp, :] - mean
            d = k0 * cotangent(s, i) - k1 - centred * k2
            store_shifted(d_ref, start, in_grid(d, r, g, place, edge))
            if RIM <= r < RIM + g.h:
                masked = wide(ext, s, r - RIM)[: g.w]
                out_ref[s, r - RIM] = (masked + (centred[: g.w] * k0 + shift)).astype(BF16)
        own_transposed(g, d_ref, (s * rows + g.near) * g.wp, g.c, s, dt_ref)
    kernel_gradient(g, place.core, h, g.tall - 2, RIM - 2, dt_ref, keep, send)


def transposed_conv(g, d_ref, w, s, rows_in, r, chunk):
    acc = None
    size = chunk * g.wp
    for a in range(3):
        start = (s * rows_in + r + a) * g.wp
        for b in range(3):
            tap = (2 - a) * 3 + (2 - b)
            term = dot_nt(
                d_ref[start : start + size, b * g.c : (b + 1) * g.c],
                w[tap * g.c : (tap + 1) * g.c, :],
            )
            acc = term if acc is None else acc + term
    return acc


def hidden_gradient_kernel(g, chunk, count, d, w, z1, st, params, dn_ref, st_ref):
    rows_in, rows_out, z_rows = g.tall - 4, g.tall - 6, g.tall - 2
    mean, rstd = stats_of(total_of(st), count)
    scale = params[0:1] * rstd
    shift = params[1:2] - mean * scale
    s0 = jnp.zeros((8, g.c), F32)
    s1 = jnp.zeros((8, g.c), F32)
    for s in range(g.s):
        for r in range(0, rows_out, chunk):
            acc = transposed_conv(g, d, w, s, rows_in, r, chunk)
            at = (s * z_rows + r + 2) * g.wp
            z = z1[at : at + chunk * g.wp, :]
            dn = jnp.where(z * scale + shift > 0, acc, 0.0)
            dn_ref[(s * rows_out + r) * g.wp : (s * rows_out + r + chunk) * g.wp, :] = dn
            for i in range(chunk):
                if RIM <= r + i + 3 < RIM + g.h:
                    v = dn[i * g.wp : i * g.wp + g.w]
                    s0 = s0 + sum_rows(v)
                    s1 = s1 + sum_rows(v * (z[i * g.wp : i * g.wp + g.w] - mean))
    to_all(st_ref, [jnp.sum(s0, 0, keepdims=True), jnp.sum(s1, 0, keepdims=True) * rstd])


def first_gradient_kernel(
    g, count, dn, z, st, st3, params, ext, ra, rb, rb_edge, e_ref, keep, send, x_ref, dt_ref
):
    place = Place()
    rows = g.tall - 6
    mean, rstd = stats_of(total_of(st), count)
    total = total_of(st3)
    k0 = params[0:1] * rstd
    k1 = k0 * (total[0:1] / count)
    k2 = k0 * rstd * (total[1:2] / count)
    edge = edge_mask(place, g)
    for s in range(g.s):
        for i in range(rows):
            at = (s * rows + i) * g.wp
            z_at = (s * (g.tall - 2) + i + 2) * g.wp
            d = k0 * dn[at : at + g.wp, :] - k1 - (z[z_at : z_at + g.wp, :] - mean) * k2
            e_ref[at : at + g.wp, :] = in_grid(d, i + 3, g, place, edge).astype(BF16)
        own_transposed(g, e_ref, (s * rows + 1) * g.wp, 0, s, dt_ref)
        above = jnp.where(place.odd_row, wide(ra, s, RIM - 1), far_row(rb, rb_edge, s, RIM - 1))
        below = jnp.where(place.odd_row, far_row(rb, rb_edge, s, 0), wide(ra, s, 0))
        for i in range(rows):
            row = above if i == 0 else below if i == rows - 1 else wide(ext, s, i - 1)
            place_shifted(x_ref, s * rows + i, row)
    kernel_gradient(g, place.core, x_ref, rows, 0, dt_ref, keep, send)


def input_gradient_kernel(g, chunk, e, w, cot, occ, master, out_ref, share_ref, e_ref, sem):
    rows_in = g.tall - 6
    start = pl.multiple_of(Place().index * share_ref.shape[0], 8)
    copy = pltpu.make_async_copy(master.at[pl.ds(start, share_ref.shape[0])], share_ref, sem)
    copy.start()
    for s in range(g.s):
        for i in range(rows_in):
            at = (s * rows_in + i) * g.wp
            store_shifted(e_ref, at, wide(e, slice(at, at + g.wp)))
        mask = pixel_mask(occ, s)
        for r in range(0, g.h, chunk):
            acc = transposed_conv(g, e_ref, w, s, rows_in, r, chunk)
            for i in range(chunk):
                v = acc[i * g.wp : i * g.wp + g.w]
                out_ref[s, r + i] = (wide(cot, s, r + i) + v) * mask[:, r + i : r + i + 1]
    copy.wait()


def pair_sum_kernel(keep, got, out_ref):
    taps, half, chans = keep.shape
    for t in range(taps):
        out_ref[t * chans : (t + 1) * chans, :] = (keep[t] + got[t]).astype(BF16).T


def message_kernel(keep, got, second, out_far, out_ref, sems):
    taps, half, chans = keep.shape
    copies = []
    for t in range(taps):
        rows = pl.ds(t * chans, chans)
        total = (keep[t] + got[t]).astype(BF16).T
        out_ref[rows, :] = jnp.concatenate([total, second[rows, :]], axis=1)
        copies.append(pltpu.make_async_copy(out_ref.at[rows], out_far.at[rows], sems.at[t]))
        copies[-1].start()
    for copy in copies:
        copy.wait()


def adamw(weight, grad, first, second, rate):
    first_new = 0.9 * first + 0.1 * grad
    second_new = 0.999 * second + 0.001 * grad * grad
    first_hat = first_new / (1.0 - 0.9**STEP)
    second_hat = second_new / (1.0 - 0.999**STEP)
    weight_new = weight - rate * (first_hat / (jnp.sqrt(second_hat) + 1e-08) + 0.01 * weight)
    return (weight_new, first_new, second_new)


def update_kernel(
    count, parts, w, first, second, st2, st3, params, n_first, n_second,
    grad_out, w_out, first_out, second_out, n_grad, n_out, n_first_out, n_second_out
):
    devices, rows, lanes = parts.shape
    lanes //= 2
    ncols = lax.axis_size("cols")
    total2, total3 = total_of(st2), total_of(st3)
    mean, rstd = stats_of(total2, count)
    sum_dn = total2[2:3]
    grads = jnp.concatenate(
        [total3[1:2], total3[0:1], rstd * (total2[3:4] - mean * sum_dn), sum_dn], axis=0
    )
    n_grad[...] = grads
    n_out[...], n_first_out[...], n_second_out[...] = adamw(
        params[...], grads, n_first[...], n_second[...], 0.75
    )
    grads = []
    for k in range(2):
        for half in range(2):
            grad = None
            for source in range(devices):
                if (source // ncols) % 2 == half:
                    term = wide(parts, source, slice(None), slice(k * lanes, (k + 1) * lanes))
                    grad = term if grad is None else grad + term
            grads.append((pl.ds(2 * half + k, rows, stride=4), grad))
    for at, grad in grads:
        new = adamw(w[at, :], grad, first[at, :], second[at, :], 0.02)
        grad_out[at, :] = grad
        w_out[at, :], first_out[at, :], second_out[at, :] = new


def swapped(block, axis, first):
    count = lax.axis_size(axis)
    pairs = []
    for i in range(first, count - 1, 2):
        pairs += [(i, i + 1), (i + 1, i)]
    return lax.ppermute(block, axis, pairs)


def to_chunks(flat):
    return flat.reshape(2, -1, 128).transpose(1, 0, 2).reshape(-1, 128)


def from_chunks(rows):
    return rows.reshape(-1, 2, 128).transpose(1, 0, 2).reshape(2, -1)


def exchange(parts):
    return lax.all_to_all(parts, BOTH, 0, 0, tiled=True)


def body(
    features,
    occupancy,
    cotangent,
    conv_weights,
    conv_first,
    conv_second,
    norm_scale_bias,
    norm_first,
    norm_second,
):
    scenes, height, width, chans = features.shape
    g = Geometry(scenes, height, width, chans)
    wp = g.wp
    devices = lax.axis_size("rows") * lax.axis_size("cols")
    count = float(scenes * height * width * devices)
    taps = 9 * chans
    n0, n1, n2, n3 = (scenes * wp * (g.tall - 2 * i) for i in range(4))
    own_pixels = scenes * height * wp
    dma = pltpu.SemaphoreType.DMA

    def conv_flops(n):
        return 2 * n * taps * chans

    side = shape_of((scenes, g.side, chans), BF16)
    own, c, d, b = kernel_call(
        functools.partial(pack_kernel, g),
        [
            shape_of(features.shape, BF16),
            side,
            side,
            shape_of((scenes, RIM + g.near, width, chans), BF16),
        ],
        1e8,
        far=(0, 1, 2),
        scratch=[
            pltpu.VMEM(features.shape, BF16),
            pltpu.VMEM(features.shape, BF16),
            pltpu.VMEM(occupancy.shape, jnp.int32),
            dma((3, scenes)),
        ],
    )(features, occupancy, cotangent)
    rb = swapped(b, "rows", 1)
    rc, rd = swapped(c, "cols", 0), swapped(d, "cols", 1)
    chunked = to_chunks(conv_weights)
    share = conv_first.shape[1]
    chunk_shape = shape_of((share // 64, 128), F32)
    weights = (taps, chans)
    w1, w2 = kernel_call(
        prepare_kernel,
        [held(weights, BF16)] * 2,
        0,
        size=1024,
        far=(0,),
        scratch=[pltpu.VMEM((9, chunked.shape[0] // 9, 128), F32), dma((9,))],
    )(chunked)
    rc, w1, w2 = lax.optimization_barrier((rc, w1, w2))

    def wide_rows(rows):
        return shape_of((scenes, rows, wp, chans), BF16)

    ext, cot_ext, a, b_edge = kernel_call(
        functools.partial(assemble_kernel, g),
        [wide_rows(n) for n in (height, height, RIM + g.near)]
        + [shape_of((scenes, RIM + g.near, 2 * RIM, chans), BF16)],
        0,
        size=1024,
    )(own, cotangent, rc, rd)
    z1, st = kernel_call(
        functools.partial(own_conv_kernel, g),
        [held((n1, chans), F32), held((16, chans), F32)],
        0,
        size=1024,
        scratch=[pltpu.VMEM((scenes * height * wp, 3 * chans), BF16)],
    )(ext, w1)
    b_edge, st = lax.optimization_barrier((b_edge, st))
    rb_edge = swapped(b_edge, "rows", 1)
    a, rb, rb_edge = lax.optimization_barrier((a, rb, rb_edge))
    ra = swapped(a, "rows", 0)
    z1, st = kernel_call(
        functools.partial(rim_conv_kernel, g),
        [held((n1, chans), F32), shape_of((devices, 2, chans), F32)],
        0,
        size=1024,
        scratch=[pltpu.VMEM((scenes * 2 * (RIM + 2) * wp, 3 * chans), BF16)],
        alias={6: 0},
    )(ext, ra, rb, rb_edge, w1, st, z1)
    st1 = exchange(st)
    h, z2, st = kernel_call(
        functools.partial(second_conv_kernel, g, 6, count),
        [
            held((n1, 3 * chans), BF16),
            held((n2, chans), F32),
            shape_of((devices, 4, chans), F32),
        ],
        conv_flops(n2),
    )(z1, st1, norm_scale_bias, w2, cot_ext)
    st2 = exchange(st)
    grad_shape = held((9, chans // 2, chans), F32)
    block_out, d, keep2, send2 = kernel_call(
        functools.partial(second_gradient_kernel, g, count),
        [
            shape_of(features.shape, BF16),
            held((n2, 3 * chans), BF16),
            grad_shape,
            grad_shape,
        ],
        conv_flops(own_pixels),
        scratch=[pltpu.VMEM((chans, own_pixels), BF16)],
    )(z2, st2, norm_scale_bias, ext, cot_ext, ra, rb, rb_edge, h)
    got2 = swapped(send2, "rows", 0)
    dn1, st = kernel_call(
        functools.partial(hidden_gradient_kernel, g, 5, count),
        [held((n3, chans), F32), shape_of((devices, 2, chans), F32)],
        conv_flops(n3),
    )(d, w2, z1, st1, norm_scale_bias)
    st, got2 = lax.optimization_barrier((st, got2))
    st3 = exchange(st)
    e, keep1, send1 = kernel_call(
        functools.partial(first_gradient_kernel, g, count),
        [held((n3, chans), BF16), grad_shape, grad_shape],
        conv_flops(own_pixels),
        scratch=[pltpu.VMEM((n3, 3 * chans), BF16), pltpu.VMEM((chans, own_pixels), BF16)],
    )(dn1, z1, st1, st3, norm_scale_bias, ext, ra, rb, rb_edge)
    got1 = swapped(send1, "rows", 0)
    keep2, got2, keep1 = lax.optimization_barrier((keep2, got2, keep1))
    (second,) = kernel_call(pair_sum_kernel, [held((taps, chans // 2), BF16)], 1e9)(keep2, got2)
    (parts,) = kernel_call(
        message_kernel,
        [stored((taps, chans), BF16)],
        1e9,
        far_out=(0,),
        scratch=[pltpu.VMEM((taps, chans), BF16), dma((9,))],
    )(keep1, got1, second)
    parts = exchange(parts.reshape(devices, taps // devices, chans))
    grad_input, own_weights = kernel_call(
        functools.partial(input_gradient_kernel, g, 8),
        [shape_of(features.shape, F32), chunk_shape],
        conv_flops(own_pixels),
        far=(4,),
        scratch=[pltpu.VMEM((n3, 3 * chans), BF16), dma],
    )(e, w1, cotangent, occupancy, chunked)

    norm_shape = shape_of(norm_first.shape, F32)
    updated = kernel_call(
        functools.partial(update_kernel, count),
        [chunk_shape] * 4 + [norm_shape] * 4,
        1e8,
    )(
        parts, own_weights, to_chunks(conv_first), to_chunks(conv_second), st2, st3,
        norm_scale_bias, norm_first, norm_second,
    )
    return (block_out, grad_input, *map(from_chunks, updated[:4]), *updated[4:])


def solution(mesh):
    tile = P(None, "rows", "cols", None)
    share = P(None, ("rows", "cols"))
    return jax.shard_map(
        body,
        mesh=mesh,
        in_specs=(tile, P(None, "rows", "cols"), tile, P(), share, share, P(), P(), P()),
        out_specs=(tile, tile, share, share, share, share, P(), P(), P(), P()),
        check_vma=False,
    )
```

time: 155 us -> 109 us (0.70)
  starting transfers between devices: 45.3 us -> 14.1 us
  local copies, waits for them, and re-layouts: 32.5 us -> 2.79 us
  blocking collectives: 8.29 us -> 32.1 us
  Pallas kernels: 33.3 us -> 26.4 us
  other arithmetic: 4.65 us -> 0 us
  waiting for transfers between devices: 28.1 us -> 32.2 us
    unnamed x84 -> x22, local copies, waits for them, and re-layouts: 27 us -> 2.79 us
    all_to_all x1 -> x3, blocking collectives: 8.29 us -> 32.1 us  [exchange(): return lax.all_to_all(parts, BOTH, 0, 0, tiled=True)]
    all_to_all x4 -> x1, starting transfers between devices: 19.8 us -> 2.65 us  [exchange(): return lax.all_to_all(parts, BOTH, 0, 0, tiled=True)]
    ppermute x10 -> x7, starting transfers between devices: 25.5 us -> 11.5 us  [swapped(): return lax.ppermute(block, axis, pairs)]
    ppermute x10 -> x7, waiting for transfers between devices: 0.58 us -> 8.7 us  [swapped(): return lax.ppermute(block, axis, pairs)]
    pallas_call x10 -> x13, Pallas kernels: 33.3 us -> 26.4 us  [call(): pl.pallas_call(body, out_shape=out_shape, in_specs=specs, out_specs=[pl.B...]
    all_to_all x4 -> x1, waiting for transfers between devices: 27.6 us -> 23.5 us  [exchange(): return lax.all_to_all(parts, BOTH, 0, 0, tiled=True)]
    slice x4 -> x0, local copies, waits for them, and re-layouts: 3.5 us -> none  [the longest x1 1.74 us: body(): cot_down = shifted(cotangent[:, :rim], 'rows', -1)]
  transfers between devices with their start and end apart: 14 -> 8, of which waited for: 4 -> 4; matrix products, arithmetic and copies ran while one was open for 6% -> 0% of each run, Pallas kernels for 13% -> 10%
where the time goes in v1:
time: 109 us
  waiting for transfers between devices  32.2 us (30%)
  blocking collectives  32.1 us (29%)
  Pallas kernels  26.4 us (24%)
  starting transfers between devices  14.1 us (13%)
  local copies, waits for them, and re-layouts  2.79 us (3%)
    all_to_all x3, blocking collectives, exchange(): return lax.all_to_all(parts, BOTH, 0, 0, tiled=True)  32.1 us
    pallas_call x13, Pallas kernels, call(): pl.pallas_call(body, out_shape=out_shape, in_specs=specs, out_specs=[pl.B...  26.4 us
    all_to_all x1, waiting for transfers between devices, exchange(): return lax.all_to_all(parts, BOTH, 0, 0, tiled=True)  23.5 us
    ppermute x7, starting transfers between devices, swapped(): return lax.ppermute(block, axis, pairs)  11.5 us
    ppermute x7, waiting for transfers between devices, swapped(): return lax.ppermute(block, axis, pairs)  8.7 us
    unnamed x22, local copies, waits for them, and re-layouts  2.79 us
    all_to_all x1, starting transfers between devices, exchange(): return lax.all_to_all(parts, BOTH, 0, 0, tiled=True)  2.65 us
  transfers between devices with their start and end apart: 8, of which 4 were waited for; matrix products, arithmetic and copies ran while one was open for 0% of the time, Pallas kernels for 10%

profile of v1, /device:TPU:1, one launch (start us, length us, event | category | flops | bytes accessed | tf_op | source)
XLA Modules:
  0.0 108.5 jit_solution(12241712935898304188)
XLA Ops:
  0.6 1.7 %shard_map.168 = (bf16[4,8,40,256]{3,2,1,0:T(8,128)(2,1)S(1)}, bf16[4,48,256]{2,1,0:T(8,128)(2,1)S(1)}, bf16[4,48,256]{2,1,0:T(8,128)(2,1)S(1)}, bf16[4,6,40,256]{3,2,1,0:T(8,128)(2,1)S(1)}) custom-call(bf16[4,8,40,256]{3,2,1,0:T(8,128)(2,1)} %features.1, s32[4,8,40]{2,1,0:T(8,128)} %occ.1, bf16[4,8,40,256]{3,2,1,0:T(8,128)(2,1)} %cot.5), custom_call_target="tpu_custom_call" | custom-call | flops 100000000 | bytes 4194304 | tf_op jit(solution)/shard_map/pallas_call | solution.py:39
  2.3 4.5 %collective-permute-start.2 = (bf16[4,6,40,256]{3,2,1,0:T(8,128)(2,1)S(1)}, bf16[4,6,40,256]{3,2,1,0:T(8,128)(2,1)S(1)}, u32[]{:S(2)}, u32[]{:S(2)}) collective-permute-start(bf16[4,6,40,256]{3,2,1,0:T(8,128)(2,1)S(1)} %get-tuple-element.67), channel_id=1, source_target_pairs={{4,8},{8,4},{12,16},{16,12},{20,24},{24,20},{5,9},{9,5},{13,17},{1... | collective-permute-start | bytes 1474568 | tf_op jit(solution)/shard_map/ppermute | solution.py:532
  6.8 1.4 %collective-permute-start = (bf16[4,48,256]{2,1,0:T(8,128)(2,1)S(1)}, bf16[4,48,256]{2,1,0:T(8,128)(2,1)S(1)}, u32[]{:S(2)}, u32[]{:S(2)}) collective-permute-start(bf16[4,48,256]{2,1,0:T(8,128)(2,1)S(1)} %get-tuple-element.60), channel_id=1, source_target_pairs={{0,1},{1,0},{2,3},{3,2},{4,5},{5,4},{6,7},{7,6},{8,9},{9,8},{10,11... | collective-permute-start | bytes 294920 | tf_op jit(solution)/shard_map/ppermute | solution.py:532
  8.2 0.7 collective-permute-start.1
  8.9 0.0 copy-start
  8.9 2.5 %shard_map.169 = (bf16[2304,256]{1,0:T(8,128)(2,1)S(1)}, bf16[2304,256]{1,0:T(8,128)(2,1)S(1)}) custom-call(f32[9216,128]{1,0:T(8,128)} %bitcast.38), custom_call_target="tpu_custom_call" | custom-call | bytes 1024 | tf_op jit(solution)/shard_map/pallas_call | solution.py:39
  11.4 0.0 collective-permute-done.rc
  11.4 0.0 collective-permute-done.1.rd
  11.4 0.0 copy-done
  11.4 0.3 shard_map.170
  11.7 1.6 %shard_map.171 = (f32[2688,256]{1,0:T(8,128)S(1)}, f32[16,256]{1,0:T(8,128)S(1)}) custom-call(bf16[4,8,48,256]{3,2,1,0:T(8,128)(2,1)S(1)} %get-tuple-element.65.ext, bf16[2304,256]{1,0:T(8,128)(2,1)S(1)} %get-tuple-element.69.w), custom_call_target="tpu_custom_call" | custom-call | bytes 1024 | tf_op jit(solution)/shard_map/pallas_call | solution.py:39
  13.2 2.5 %collective-permute-start.3 = (bf16[4,6,8,256]{3,2,1,0:T(8,128)(2,1)S(1)}, bf16[4,6,8,256]{3,2,1,0:T(8,128)(2,1)S(1)}, u32[]{:S(2)}, u32[]{:S(2)}) collective-permute-start(bf16[4,6,8,256]{3,2,1,0:T(8,128)(2,1)S(1)} %get-tuple-element.71), channel_id=1, source_target_pairs={{4,8},{8,4},{12,16},{16,12},{20,24},{24,20},{5,9},{9,5},{13,17},{1... | collective-permute-start | bytes 294920 | tf_op jit(solution)/shard_map/ppermute | solution.py:532
  15.8 4.4 %collective-permute-done.3.rb_edge = bf16[4,6,8,256]{3,2,1,0:T(8,128)(2,1)S(1)} collective-permute-done((bf16[4,6,8,256]{3,2,1,0:T(8,128)(2,1)S(1)}, bf16[4,6,8,256]{3,2,1,0:T(8,128)(2,1)S(1)}, u32[]{:S(2)}, u32[]{:S(2)}) %collective-permute-start.3) | collective-permute-done | bytes 98336 | tf_op jit(solution)/shard_map/ppermute | solution.py:532
  20.2 0.0 collective-permute-done.2.rb
  20.2 0.0 collective-permute-start.4
  20.2 2.0 %collective-permute-done.4.ra = bf16[4,6,48,256]{3,2,1,0:T(8,128)(2,1)S(1)} collective-permute-done((bf16[4,6,48,256]{3,2,1,0:T(8,128)(2,1)S(1)}, bf16[4,6,48,256]{3,2,1,0:T(8,128)(2,1)S(1)}, u32[]{:S(2)}, u32[]{:S(2)}) %collective-permute-start.4) | collective-permute-done | bytes 589856 | tf_op jit(solution)/shard_map/ppermute | solution.py:532
  22.2 2.1 %shard_map.172 = (f32[2688,256]{1,0:T(8,128)S(1)}, f32[32,2,256]{2,1,0:T(2,128)S(1)}) custom-call(bf16[4,8,48,256]{3,2,1,0:T(8,128)(2,1)S(1)} %get-tuple-element.65.ext, bf16[4,6,48,256]{3,2,1,0:T(8,128)(2,1)S(1)} %collective-permute-done.4.ra, bf16[4,6,40,256]{3,2,1,0:T(8,128)(2,1)S(1)} %collective-permute-done.2.rb, ...), custom_call_target="tpu_custom_call", output_to_operand_aliasing={{0}: (6, {})} | custom-call | bytes 1024 | tf_op jit(solution)/shard_map/pallas_call | solution.py:39
  24.3 14.1 %all_to_all.20.st = f32[32,2,256]{2,1,0:T(2,128)S(1)} all-to-all(f32[32,2,256]{2,1,0:T(2,128)S(1)} %get-tuple-element.78), channel_id=1, replica_groups=mesh['rows'=8,'cols'=4] {'rows','cols'}, dimensions={0} | all-to-all | bytes 131072 | tf_op jit(solution)/shard_map/all_to_all | solution.py:544
  38.3 0.0 copy-done.8
  38.3 3.2 %shard_map.173 = (bf16[2688,768]{1,0:T(8,128)(2,1)S(1)}, f32[2304,256]{1,0:T(8,128)S(1)}, f32[32,4,256]{2,1,0:T(4,128)S(1)}) custom-call(f32[2688,256]{1,0:T(8,128)S(1)} %get-tuple-element.77.z1.z, f32[32,2,256]{2,1,0:T(2,128)S(1)} %all_to_all.20.st, f32[4,256]{1,0:T(4,128)S(1)} %copy-done.8, bf16[2304,256]{1,0:T(8,128)(2,1)S(1)} %get-tuple-element.79.w, ...), custom_call_target="tpu_custom_call" | custom-call | flops 2717908992 | bytes 4194304 | tf_op jit(solution)/shard_map/pallas_call | solution.py:39
  41.6 9.7 %all_to_all.21.st.st2 = f32[32,4,256]{2,1,0:T(4,128)S(1)} all-to-all(f32[32,4,256]{2,1,0:T(4,128)S(1)} %get-tuple-element.82), channel_id=1, replica_groups=mesh['rows'=8,'cols'=4] {'rows','cols'}, dimensions={0} | all-to-all | bytes 262144 | tf_op jit(solution)/shard_map/all_to_all | solution.py:544
  51.3 3.4 %shard_map.174 = (bf16[4,8,40,256]{3,2,1,0:T(8,128)(2,1)}, bf16[2304,768]{1,0:T(8,128)(2,1)S(1)}, f32[9,128,256]{2,1,0:T(8,128)S(1)}, f32[9,128,256]{2,1,0:T(8,128)S(1)}) custom-call(f32[2304,256]{1,0:T(8,128)S(1)} %get-tuple-element.81.z2, f32[32,4,256]{2,1,0:T(4,128)S(1)} %all_to_all.21.st.st2, f32[4,256]{1,0:T(4,128)S(1)} %copy-done.8, ...), custom_call_target="tpu_custom_call" | custom-call | flops 1811939328 | bytes 4194304 | tf_op jit(solution)/shard_map/pallas_call | solution.py:39
  54.7 1.4 %collective-permute-start.5 = (f32[9,128,256]{2,1,0:T(8,128)S(1)}, f32[9,128,256]{2,1,0:T(8,128)S(1)}, u32[]{:S(2)}, u32[]{:S(2)}) collective-permute-start(f32[9,128,256]{2,1,0:T(8,128)S(1)} %get-tuple-element.88), channel_id=1, source_target_pairs={{0,4},{4,0},{8,12},{12,8},{16,20},{20,16},{24,28},{28,24},{1,5},{5... | collective-permute-start | bytes 3538952 | tf_op jit(solution)/shard_map/ppermute | solution.py:532
  56.1 2.7 %shard_map.175 = (f32[1920,256]{1,0:T(8,128)S(1)}, f32[32,2,256]{2,1,0:T(2,128)S(1)}) custom-call(bf16[2304,768]{1,0:T(8,128)(2,1)S(1)} %get-tuple-element.85.d, bf16[2304,256]{1,0:T(8,128)(2,1)S(1)} %get-tuple-element.79.w, f32[2688,256]{1,0:T(8,128)S(1)} %get-tuple-element.77.z1.z, f32[32,2,256]{2,1,0:T(2,128)S(1)} %all_to_all.20.st, f32[4,256]{1,0:T(4,128)S(1)} %copy-done.8), custom_call_target="tpu_custom_call" | custom-call | flops 2264924160 | bytes 4194304 | tf_op jit(solution)/shard_map/pallas_call | solution.py:39
  58.8 0.0 collective-permute-done.5.got
  58.9 8.4 %all_to_all.22.st3 = f32[32,2,256]{2,1,0:T(2,128)S(1)} all-to-all(f32[32,2,256]{2,1,0:T(2,128)S(1)} %get-tuple-element.89), channel_id=1, replica_groups=mesh['rows'=8,'cols'=4] {'rows','cols'}, dimensions={0} | all-to-all | bytes 131072 | tf_op jit(solution)/shard_map/all_to_all | solution.py:544
  67.2 2.7 %shard_map.176 = (bf16[1920,256]{1,0:T(8,128)(2,1)S(1)}, f32[9,128,256]{2,1,0:T(8,128)S(1)}, f32[9,128,256]{2,1,0:T(8,128)S(1)}) custom-call(f32[1920,256]{1,0:T(8,128)S(1)} %get-tuple-element.86.dn, f32[2688,256]{1,0:T(8,128)S(1)} %get-tuple-element.77.z1.z, f32[32,2,256]{2,1,0:T(2,128)S(1)} %all_to_all.20.st, f32[32,2,256]{2,1,0:T(2,128)S(1)} %all_to_all.22.st3, ...), custom_call_target="tpu_custom_call" | custom-call | flops 1811939328 | bytes 4194304 | tf_op jit(solution)/shard_map/pallas_call | solution.py:39
  69.9 0.0 copy-start.1
  69.9 1.0 collective-permute-start.6
  70.9 0.2 shard_map.178.second
  71.1 0.0 copy-done.1
  71.1 2.3 %collective-permute-done.6.got = f32[9,128,256]{2,1,0:T(8,128)S(1)} collective-permute-done((f32[9,128,256]{2,1,0:T(8,128)S(1)}, f32[9,128,256]{2,1,0:T(8,128)S(1)}, u32[]{:S(2)}, u32[]{:S(2)}) %collective-permute-start.6) | collective-permute-done | bytes 1179680 | tf_op jit(solution)/shard_map/ppermute | solution.py:532
  73.4 1.2 %shard_map.179 = bf16[2304,256]{1,0:T(8,128)(2,1)} custom-call(f32[9,128,256]{2,1,0:T(8,128)S(1)} %get-tuple-element.95.keep, f32[9,128,256]{2,1,0:T(8,128)S(1)} %collective-permute-done.6.got, bf16[2304,128]{1,0:T(8,128)(2,1)S(1)} %shard_map.178.second), custom_call_target="tpu_custom_call" | custom-call | flops 1000000000 | bytes 4194304 | tf_op jit(solution)/shard_map/pallas_call | solution.py:39
  74.6 0.0 copy-start.7
  74.6 2.6 %all-to-all-start.3 = ((bf16[32,72,256]{2,1,0:T(8,128)(2,1)}), bf16[32,72,256]{2,1,0:T(8,128)(2,1)S(1)}, u32[]{:S(2)}, u32[]{:S(2)}) async-start(bf16[32,72,256]{2,1,0:T(8,128)(2,1)} %bitcast.40), calls=%async_computation.3 | async-start | bytes 2359296 | tf_op jit(solution)/shard_map/all_to_all | solution.py:544
  77.3 0.0 copy-done.7
  77.3 0.0 copy-start.2
  77.3 1.2 %copy-done.2 = bf16[1920,256]{1,0:T(8,128)(2,1)S(1)} copy-done((bf16[1920,256]{1,0:T(8,128)(2,1)S(1)}, bf16[1920,256]{1,0:T(8,128)(2,1)}, u32[]{:S(2)}) %copy-start.2) | copy-done | bytes 983064
  78.5 3.8 %shard_map.177 = (f32[4,8,40,256]{3,2,1,0:T(8,128)}, f32[288,128]{1,0:T(8,128)S(1)}) custom-call(bf16[1920,256]{1,0:T(8,128)(2,1)S(1)} %copy-done.2, bf16[2304,256]{1,0:T(8,128)(2,1)S(1)} %get-tuple-element.69.w, bf16[4,8,40,256]{3,2,1,0:T(8,128)(2,1)S(1)} %copy-done, s32[4,8,40]{2,1,0:T(8,128)S(1)} %copy-done.7, f32[9216,128]{1,0:T(8,128)} %bitcast.39), custom_call_target="tpu_custom_call" | custom-call | flops 1811939328 | bytes 4194304 | tf_op jit(solution)/shard_map/pallas_call | solution.py:39
  82.3 0.0 copy-start.5
  82.3 0.7 copy-done.5
  83.0 23.5 %all-to-all-done.3.parts = bf16[32,72,256]{2,1,0:T(8,128)(2,1)S(1)} async-done(((bf16[32,72,256]{2,1,0:T(8,128)(2,1)}), bf16[32,72,256]{2,1,0:T(8,128)(2,1)S(1)}, u32[]{:S(2)}, u32[]{:S(2)}) %all-to-all-start.3) | async-done | bytes 1179680 | tf_op jit(solution)/shard_map/all_to_all | solution.py:544
  106.5 0.0 copy-done.3
  106.5 0.0 copy-done.4
  106.5 0.0 copy-done.9
  106.5 0.0 copy-done.10
  106.5 0.9 copy-done.6
  107.4 1.1 %shard_map.180 = (f32[288,128]{1,0:T(8,128)}, f32[288,128]{1,0:T(8,128)}, f32[288,128]{1,0:T(8,128)}, f32[288,128]{1,0:T(8,128)}, f32[4,256]{1,0:T(4,128)}, /*in...) custom-call(bf16[32,72,256]{2,1,0:T(8,128)(2,1)S(1)} %all-to-all-done.3.parts, f32[288,128]{1,0:T(8,128)S(1)} %copy-done.6, ...), custom_call_target="tpu_custom_call" | custom-call | flops 100000000 | bytes 4194304 | tf_op jit(solution)/shard_map/pallas_call | solution.py:39
  (6 shorter events, 0.0 us)
Async XLA Ops:
  2.3 17.9 %collective-permute-start.2 = (bf16[4,6,40,256]{3,2,1,0:T(8,128)(2,1)S(1)}, bf16[4,6,40,256]{3,2,1,0:T(8,128)(2,1)S(1)}, u32[]{:S(2)}, u32[]{:S(2)}) collective-permute-start(bf16[4,6,40,256]{3,2,1,0:T(8,128)(2,1)S(1)} %get-tuple-element.67), channel_id=1, source_target_pairs={{4,8},{8,4},{12,16},{16,12},{20,24},{24,20},{5,9},{9,5},{13,17},{1... | collective-permute-start | bytes 1474568 | tf_op jit(solution)/shard_map/ppermute | solution.py:532
  6.8 4.5 %collective-permute-start = (bf16[4,48,256]{2,1,0:T(8,128)(2,1)S(1)}, bf16[4,48,256]{2,1,0:T(8,128)(2,1)S(1)}, u32[]{:S(2)}, u32[]{:S(2)}) collective-permute-start(bf16[4,48,256]{2,1,0:T(8,128)(2,1)S(1)} %get-tuple-element.60), channel_id=1, source_target_pairs={{0,1},{1,0},{2,3},{3,2},{4,5},{5,4},{6,7},{7,6},{8,9},{9,8},{10,11... | collective-permute-start | bytes 294920 | tf_op jit(solution)/shard_map/ppermute | solution.py:532
  8.2 3.2 %collective-permute-start.1 = (bf16[4,48,256]{2,1,0:T(8,128)(2,1)S(1)}, bf16[4,48,256]{2,1,0:T(8,128)(2,1)S(1)}, u32[]{:S(2)}, u32[]{:S(2)}) collective-permute-start(bf16[4,48,256]{2,1,0:T(8,128)(2,1)S(1)} %get-tuple-element.64), channel_id=1, source_target_pairs={{1,2},{2,1},{5,6},{6,5},{9,10},{10,9},{13,14},{14,13},{17,18},{18,... | collective-permute-start | bytes 294920 | tf_op jit(solution)/shard_map/ppermute | solution.py:532
  8.9 2.5 %copy-start = (bf16[4,8,40,256]{3,2,1,0:T(8,128)(2,1)S(1)}, bf16[4,8,40,256]{3,2,1,0:T(8,128)(2,1)}, u32[]{:S(2)}) copy-start(bf16[4,8,40,256]{3,2,1,0:T(8,128)(2,1)} %cot.5) | copy-start | bytes 1966084
  13.2 7.0 %collective-permute-start.3 = (bf16[4,6,8,256]{3,2,1,0:T(8,128)(2,1)S(1)}, bf16[4,6,8,256]{3,2,1,0:T(8,128)(2,1)S(1)}, u32[]{:S(2)}, u32[]{:S(2)}) collective-permute-start(bf16[4,6,8,256]{3,2,1,0:T(8,128)(2,1)S(1)} %get-tuple-element.71), channel_id=1, source_target_pairs={{4,8},{8,4},{12,16},{16,12},{20,24},{24,20},{5,9},{9,5},{13,17},{1... | collective-permute-start | bytes 294920 | tf_op jit(solution)/shard_map/ppermute | solution.py:532
  20.2 2.0 %collective-permute-start.4 = (bf16[4,6,48,256]{3,2,1,0:T(8,128)(2,1)S(1)}, bf16[4,6,48,256]{3,2,1,0:T(8,128)(2,1)S(1)}, u32[]{:S(2)}, u32[]{:S(2)}) collective-permute-start(bf16[4,6,48,256]{3,2,1,0:T(8,128)(2,1)S(1)} %get-tuple-element.72), channel_id=1, source_target_pairs={{0,4},{4,0},{8,12},{12,8},{16,20},{20,16},{24,28},{28,24},{1,5},{5... | collective-permute-start | bytes 1769480 | tf_op jit(solution)/shard_map/ppermute | solution.py:532
  22.2 16.1 %copy-start.8 = (f32[4,256]{1,0:T(4,128)S(1)}, f32[4,256]{1,0:T(4,128)}, u32[]{:S(2)}) copy-start(f32[4,256]{1,0:T(4,128)} %params.9) | copy-start | bytes 12292
  54.7 4.2 %collective-permute-start.5 = (f32[9,128,256]{2,1,0:T(8,128)S(1)}, f32[9,128,256]{2,1,0:T(8,128)S(1)}, u32[]{:S(2)}, u32[]{:S(2)}) collective-permute-start(f32[9,128,256]{2,1,0:T(8,128)S(1)} %get-tuple-element.88), channel_id=1, source_target_pairs={{0,4},{4,0},{8,12},{12,8},{16,20},{20,16},{24,28},{28,24},{1,5},{5... | collective-permute-start | bytes 3538952 | tf_op jit(solution)/shard_map/ppermute | solution.py:532
  69.9 1.2 %copy-start.1 = (bf16[1920,256]{1,0:T(8,128)(2,1)}, bf16[1920,256]{1,0:T(8,128)(2,1)S(1)}, u32[]{:S(2)}) copy-start(bf16[1920,256]{1,0:T(8,128)(2,1)S(1)} %get-tuple-element.90.e) | copy-start | bytes 2949124
  69.9 3.5 %collective-permute-start.6 = (f32[9,128,256]{2,1,0:T(8,128)S(1)}, f32[9,128,256]{2,1,0:T(8,128)S(1)}, u32[]{:S(2)}, u32[]{:S(2)}) collective-permute-start(f32[9,128,256]{2,1,0:T(8,128)S(1)} %get-tuple-element.96), channel_id=1, source_target_pairs={{0,4},{4,0},{8,12},{12,8},{16,20},{20,16},{24,28},{28,24},{1,5},{5... | collective-permute-start | bytes 3538952 | tf_op jit(solution)/shard_map/ppermute | solution.py:532
  74.6 2.7 %copy-start.7 = (s32[4,8,40]{2,1,0:T(8,128)S(1)}, s32[4,8,40]{2,1,0:T(8,128)}, u32[]{:S(2)}) copy-start(s32[4,8,40]{2,1,0:T(8,128)} %occ.1) | copy-start | bytes 15364
  74.6 31.9 %all-to-all-start.3 = ((bf16[32,72,256]{2,1,0:T(8,128)(2,1)}), bf16[32,72,256]{2,1,0:T(8,128)(2,1)S(1)}, u32[]{:S(2)}, u32[]{:S(2)}) async-start(bf16[32,72,256]{2,1,0:T(8,128)(2,1)} %bitcast.40), calls=%async_computation.3 | async-start | bytes 2359296 | tf_op jit(solution)/shard_map/all_to_all | solution.py:544
  77.3 1.2 %copy-start.2 = (bf16[1920,256]{1,0:T(8,128)(2,1)S(1)}, bf16[1920,256]{1,0:T(8,128)(2,1)}, u32[]{:S(2)}) copy-start(bf16[1920,256]{1,0:T(8,128)(2,1)} %copy-done.1) | copy-start | bytes 2949124
  78.5 28.0 %copy-start.3 = (f32[2,18432]{1,0:T(2,128)S(1)}, f32[2,18432]{1,0:T(2,128)}, u32[]{:S(2)}) copy-start(f32[2,18432]{1,0:T(2,128)} %param.13) | copy-start | bytes 442372
  78.5 28.0 %copy-start.4 = (f32[2,18432]{1,0:T(2,128)S(1)}, f32[2,18432]{1,0:T(2,128)}, u32[]{:S(2)}) copy-start(f32[2,18432]{1,0:T(2,128)} %param.14) | copy-start | bytes 442372
  78.5 28.0 %copy-start.9 = (f32[4,256]{1,0:T(4,128)S(1)}, f32[4,256]{1,0:T(4,128)}, u32[]{:S(2)}) copy-start(f32[4,256]{1,0:T(4,128)} %n_first.1) | copy-start | bytes 12292
  78.5 28.0 %copy-start.10 = (f32[4,256]{1,0:T(4,128)S(1)}, f32[4,256]{1,0:T(4,128)}, u32[]{:S(2)}) copy-start(f32[4,256]{1,0:T(4,128)} %n_second.1) | copy-start | bytes 12292
  82.3 0.7 copy-start.5
  106.5 0.9 copy-start.6

commit v2 on v1

--- a/solution.py
+++ b/solution.py
@@ -10,7 +10,9 @@
 
 STEP = 5
 BOTH = ("rows", "cols")
-RIM = 4
+RIM = 3
+COLS = 4
+SIDE = 2 * COLS
 F32, BF16 = jnp.float32, jnp.bfloat16
 
 
@@ -77,22 +79,23 @@
         ref[i] = value
 
 
-def store_shifted(ref, start, row):
+def store_shifted(ref, start, row, offsets=(0, 1, 2)):
     width, chans = row.shape
-    at = pl.ds(start if isinstance(start, int) else pl.multiple_of(start, 16), width)
-    ref[at, 0:chans] = pltpu.roll(row, 1, 0).astype(BF16)
-    ref[at, chans : 2 * chans] = row.astype(BF16)
-    ref[at, 2 * chans : 3 * chans] = pltpu.roll(row, width - 1, 0).astype(BF16)
+    for b in offsets:
+        moved = row if b == 1 else pltpu.roll(row, 1 if b == 0 else width - 1, 0)
+        ref[start : start + width, b * chans : (b + 1) * chans] = moved.astype(BF16)
 
 
 class Geometry:
     def __init__(self, scenes, height, width, chans):
         self.s, self.h, self.w, self.c = scenes, height, width, chans
-        self.wp = width + 2 * RIM
+        self.wp = width + SIDE
         self.tall = height + 2 * RIM
-        self.near = RIM // 2
+        self.near = RIM - 2
+        self.near_cols = COLS - 2
         self.cot_tall = height + 2 * self.near
-        self.side = (RIM + self.near) * height
+        self.side = (COLS + self.near_cols) * height
+        self.corner = -(-(COLS * RIM + self.near_cols * self.near) // 16) * 16
 
 
 class Place:
@@ -113,8 +116,16 @@
     return ref[index].astype(F32)
 
 
-def far_row(rb, rb_edge, s, k):
-    return jnp.concatenate([wide(rb, s, k), wide(rb_edge, s, k)], axis=0)
+def far_rows(g, place, rb, rb_c, rb_d, s):
+    right, left = sides(g, place, rb_c, rb_d, s)
+    rows = []
+    for k in range(RIM + g.near):
+        width = COLS if k < RIM else g.near_cols
+        at = COLS * min(k, RIM) + g.near_cols * max(k - RIM, 0)
+        rows.append(
+            jnp.concatenate([wide(rb, s, k), side_columns(g, right, left, at, width)], axis=0)
+        )
+    return rows
 
 
 def pixel_mask(occ, s):
@@ -131,8 +142,8 @@
 
 
 def edge_mask(place, g):
-    where = lax.broadcasted_iota(jnp.int32, (2 * RIM, g.c), 0)
-    return jnp.where(where < RIM, place.right, place.left)
+    where = lax.broadcasted_iota(jnp.int32, (SIDE, g.c), 0)
+    return jnp.where(where < SIDE // 2, place.right, place.left)
 
 
 def sum_rows(value):
@@ -140,7 +151,9 @@
     return jnp.sum(value.reshape(rows // 8, 8, chans), axis=0)
 
 
-def pack_kernel(g, features, occ_far, cot, own, c_ref, d_ref, b_ref, given, seen, occ, sems):
+def pack_kernel(
+    g, features, occ_far, cot, own, c_ref, d_ref, b_ref, bc_ref, bd_ref, given, seen, occ, sems
+):
     copies = []
     flags = pltpu.make_async_copy(occ_far, occ, sems.at[2, 0])
     flags.start()
@@ -156,11 +169,6 @@
     odd, odd_row = Place().odd_col, Place().odd_row
     flags.wait()
 
-    def put(s, at, rights, lefts):
-        right, left = jnp.concatenate(rights, axis=0), jnp.concatenate(lefts, axis=0)
-        c_ref[s, at : at + 16] = jnp.where(odd, left, right).astype(BF16)
-        d_ref[s, at : at + 16] = jnp.where(odd, right, left).astype(BF16)
-
     for s in range(g.s):
         mask = pixel_mask(occ, s)
         for copy in copies[s]:
@@ -171,48 +179,54 @@
             rows.append(row)
             own[s, r] = row.astype(BF16)
         cots = [wide(seen, s, r) for r in range(g.h)]
-        for k in range(RIM):
-            b_ref[s, k] = jnp.where(odd_row, rows[g.h - RIM + k], rows[k]).astype(BF16)
-        for k in range(g.near):
-            b_ref[s, RIM + k] = jnp.where(odd_row, cots[g.h - g.near + k], cots[k]).astype(BF16)
-        for width, at, field in ((RIM, 0, rows), (g.near, RIM * g.h, cots)):
-            for k in range(0, g.h, 16 // width):
-                group = field[k : k + 16 // width]
-                put(s, at + width * k, [v[g.w - width :] for v in group], [v[:width] for v in group])
-
-
-def assemble_kernel(g, own, cot, rc, rd, ext, cot_ext, a_ref, b_edge):
+        ends = []
+        for field, count in ((rows, RIM), (cots, g.near)):
+            for k in range(count):
+                ends.append(jnp.where(odd_row, field[g.h - count + k], field[k]))
+                b_ref[s, len(ends) - 1] = ends[-1].astype(BF16)
+        spare = jnp.zeros((g.corner - COLS * RIM - g.near_cols * g.near, g.c), F32)
+        widths = [COLS] * RIM + [g.near_cols] * g.near
+        right = [v[g.w - width :] for v, width in zip(ends, widths, strict=True)]
+        left = [v[:width] for v, width in zip(ends, widths, strict=True)]
+        right, left = (jnp.concatenate(v + [spare], axis=0) for v in (right, left))
+        bc_ref[s] = jnp.where(odd, left, right).astype(BF16)
+        bd_ref[s] = jnp.where(odd, right, left).astype(BF16)
+        right = jnp.concatenate(
+            [v[g.w - COLS :] for v in rows] + [v[g.w - g.near_cols :] for v in cots], axis=0
+        )
+        left = jnp.concatenate([v[:COLS] for v in rows] + [v[: g.near_cols] for v in cots], axis=0)
+        c_ref[s] = jnp.where(odd, left, right).astype(BF16)
+        d_ref[s] = jnp.where(odd, right, left).astype(BF16)
+
+
+def sides(g, place, rc, rd, s):
+    c, d = wide(rc, s), wide(rd, s)
+    return jnp.where(place.odd_col, d, c), jnp.where(place.odd_col, c, d)
+
+
+def side_columns(g, right, left, at, width):
+    parts = [right[at : at + width], jnp.zeros((SIDE - 2 * width, g.c), F32), left[at : at + width]]
+    return jnp.concatenate([part for part in parts if part.shape[0]], axis=0)
+
+
+def assemble_kernel(g, own, cot, rc, rd, ext, cot_ext, a_ref):
     place = Place()
 
-    def rows_of(source, s, at, width):
-        gap = jnp.zeros((2 * RIM - 2 * width, g.c), F32)
-        rows = []
-        for first in range(0, g.h, 16 // width):
-            k = at + width * first
-            c, d = wide(rc, s, slice(k, k + 16)), wide(rd, s, slice(k, k + 16))
-            right, left = jnp.where(place.odd_col, d, c), jnp.where(place.odd_col, c, d)
-            for r in range(first, min(g.h, first + 16 // width)):
-                at_row = slice(width * (r - first), width * (r - first + 1))
-                parts = [wide(source, s, r), right[at_row], gap, left[at_row]]
-                rows.append(jnp.concatenate([p for p in parts if p.shape[0]], axis=0))
-        return rows
-
     odd = place.odd_row
     for s in range(g.s):
-        rows = rows_of(own, s, 0, RIM)
-        top, bottom = rows[:RIM], rows[g.h - RIM :]
-        for r in range(g.h):
-            ext[s, r] = rows[r].astype(BF16)
-        for k in range(RIM):
-            a_ref[s, k] = jnp.where(odd, top[k], bottom[k]).astype(BF16)
-            b_edge[s, k] = jnp.where(odd, bottom[k], top[k])[g.w :].astype(BF16)
-        rows = rows_of(cot, s, RIM * g.h, g.near)
-        for r in range(g.h):
-            cot_ext[s, r] = rows[r].astype(BF16)
-        for k in range(g.near):
-            top, bottom = rows[k], rows[g.h - g.near + k]
-            a_ref[s, RIM + k] = jnp.where(odd, top, bottom).astype(BF16)
-            b_edge[s, RIM + k] = jnp.where(odd, bottom, top)[g.w :].astype(BF16)
+        right, left = sides(g, place, rc, rd, s)
+        for source, full, at, width, count, first in (
+            (own, ext, 0, COLS, RIM, 0),
+            (cot, cot_ext, COLS * g.h, g.near_cols, g.near, RIM),
+        ):
+            rows = []
+            for r in range(g.h):
+                beyond = side_columns(g, right, left, at + width * r, width)
+                rows.append(jnp.concatenate([wide(source, s, r), beyond], axis=0))
+                full[s, r] = rows[r].astype(BF16)
+            for k in range(count):
+                top, bottom = rows[k], rows[g.h - count + k]
+                a_ref[s, first + k] = jnp.where(odd, top, bottom).astype(BF16)
 
 
 def prepare_kernel(w_ref, one_ref, two_ref, buffer, sems):
@@ -249,10 +263,10 @@
     s2 = jnp.zeros((8, g.c), F32)
     for s in range(g.s):
         for r in range(g.h):
-            place_shifted(x_ref, s * g.h + r, wide(ext, s, r))
+            place_shifted(x_ref, s * (g.h + 2) + 1 + r, wide(ext, s, r))
         half = count // 2
         for first in range(0, count, half):
-            acc = dot(window_rows(g, x_ref, s * g.h + first, half), w[...])
+            acc = dot(window_rows(g, x_ref, s * (g.h + 2) + 1 + first, half), w[...])
             at = (s * (g.tall - 2) + RIM + first) * g.wp
             z_ref[at : at + half * g.wp, :] = acc
             for i in range(half):
@@ -263,21 +277,31 @@
     st_ref[8:16] = s2
 
 
-def rim_conv_kernel(g, ext, ra, rb, rb_edge, w, st_in, z_in, z_ref, st_ref, x_ref):
-    del z_in
-    odd = Place().odd_row
+def rim_conv_kernel(
+    g, ext, ra, rb, rb_c, rb_d, w, st_in, z_in, x_in, z_ref, st_ref, x_own, cot_ref, x_ref
+):
+    del z_in, x_in
+    place = Place()
+    odd = place.odd_row
     s1, s2 = st_in[0:8], st_in[8:16]
     span = RIM + 2
     for s in range(g.s):
+        far = far_rows(g, place, rb, rb_c, rb_d, s)
+        near = [wide(ra, s, k) for k in range(RIM + g.near)]
         for side in range(2):
             base = span * (2 * s + side)
+            beyond = [
+                jnp.where(odd, b, a) if side else jnp.where(odd, a, b)
+                for a, b in zip(near, far, strict=True)
+            ]
             for k in range(RIM):
-                near, far = wide(ra, s, k), far_row(rb, rb_edge, s, k)
-                row = jnp.where(odd, near, far) if side == 0 else jnp.where(odd, far, near)
-                place_shifted(x_ref, base + 2 * side + k, row)
-            for j in range(2):
-                own = wide(ext, s, (g.h - 2) * side + j)
-                place_shifted(x_ref, base + RIM * (1 - side) + j, own)
+                place_shifted(x_ref, base + 2 * side + k, beyond[k])
+            next_row = beyond[0 if side else RIM - 1]
+            place_shifted(x_own, s * (g.h + 2) + (g.h + 1) * side, next_row)
+            cot_ref[s, side] = beyond[RIM].astype(BF16)
+            source = (s * (g.h + 2) + 1 + (g.h - 2) * side) * g.wp
+            target = (base + RIM * (1 - side)) * g.wp
+            x_ref[target : target + 2 * g.wp, :] = x_own[source : source + 2 * g.wp, :]
             acc = dot(window_rows(g, x_ref, base, RIM), w[...])
             at = (s * (g.tall - 2) + (g.h + RIM - 2) * side) * g.wp
             z_ref[at : at + RIM * g.wp, :] = acc
@@ -324,9 +348,9 @@
     to_all(st_ref, [jnp.sum(v, 0, keepdims=True) for v in sums])
 
 
-def own_transposed(g, source, first, lane, s, dt_ref):
+def own_transposed(g, source, first, s, dt_ref):
     span = g.h * g.wp
-    block = source[first : first + span, lane : lane + g.c]
+    block = source[first : first + span, :]
     inside = lax.broadcasted_iota(jnp.int32, (span, 1), 0) % g.wp < g.w
     dt_ref[:, s * span : (s + 1) * span] = jnp.where(inside, block, jnp.zeros_like(block)).T
 
@@ -346,7 +370,7 @@
 
 
 def second_gradient_kernel(
-    g, count, z2, st, params, ext, cot, ra, rb, rb_edge, h, out_ref, d_ref, keep, send, dt_ref
+    g, count, z2, st, params, cot, cot_next, h, d_ref, keep, send, dt_ref
 ):
     place = Place()
     rows = g.cot_tall
@@ -357,29 +381,16 @@
     k0 = params[2:3] * rstd
     k1 = k0 * (sum_dn / count)
     k2 = k0 * rstd * (sum_dx / count)
-    shift = params[3:4]
     edge = edge_mask(place, g)
-
-    def cotangent(s, i):
-        if g.near <= i < g.near + g.h:
-            return wide(cot, s, i - g.near)
-        k = i if i < g.near else i - g.near - g.h
-        k += RIM
-        return jnp.where(
-            place.odd_row == (i < g.near), wide(ra, s, k), far_row(rb, rb_edge, s, k)
-        )
-
     for s in range(g.s):
         for i in range(rows):
-            r = i + RIM - g.near
+            rim = not g.near <= i < g.near + g.h
+            dn = wide(cot_next, s, 0 if i < g.near else 1) if rim else wide(cot, s, i - g.near)
             start = (s * rows + i) * g.wp
-            centred = z2[start : start + g.wp, :] - mean
-            d = k0 * cotangent(s, i) - k1 - centred * k2
-            store_shifted(d_ref, start, in_grid(d, r, g, place, edge))
-            if RIM <= r < RIM + g.h:
-                masked = wide(ext, s, r - RIM)[: g.w]
-                out_ref[s, r - RIM] = (masked + (centred[: g.w] * k0 + shift)).astype(BF16)
-        own_transposed(g, d_ref, (s * rows + g.near) * g.wp, g.c, s, dt_ref)
+            d = k0 * dn - k1 - (z2[start : start + g.wp, :] - mean) * k2
+            d = in_grid(d, i + RIM - g.near, g, place, edge)
+            d_ref[start : start + g.wp, :] = d.astype(BF16)
+        own_transposed(g, d_ref, (s * rows + g.near) * g.wp, s, dt_ref)
     kernel_gradient(g, place.core, h, g.tall - 2, RIM - 2, dt_ref, keep, send)
 
 
@@ -398,7 +409,12 @@
     return acc
 
 
-def hidden_gradient_kernel(g, chunk, count, d, w, z1, st, params, dn_ref, st_ref):
+def hidden_gradient_kernel(
+    g, chunk, count, d, w, z1, z2, st, st2, params, ext, dn_ref, st_ref, out_ref, d_ref
+):
+    mean2, rstd2 = stats_of(total_of(st2), count)
+    scale2 = params[2:3] * rstd2
+    shift2 = params[3:4] - mean2 * scale2
     rows_in, rows_out, z_rows = g.tall - 4, g.tall - 6, g.tall - 2
     mean, rstd = stats_of(total_of(st), count)
     scale = params[0:1] * rstd
@@ -406,8 +422,15 @@
     s0 = jnp.zeros((8, g.c), F32)
     s1 = jnp.zeros((8, g.c), F32)
     for s in range(g.s):
+        for i in range(rows_in):
+            at = (s * rows_in + i) * g.wp
+            store_shifted(d_ref, at, wide(d, slice(at, at + g.wp)))
+        for r in range(g.h):
+            at = (s * rows_in + r + g.near) * g.wp
+            normed = z2[at : at + g.w, :] * scale2 + shift2
+            out_ref[s, r] = (wide(ext, s, r)[: g.w] + normed).astype(BF16)
         for r in range(0, rows_out, chunk):
-            acc = transposed_conv(g, d, w, s, rows_in, r, chunk)
+            acc = transposed_conv(g, d_ref, w, s, rows_in, r, chunk)
             at = (s * z_rows + r + 2) * g.wp
             z = z1[at : at + chunk * g.wp, :]
             dn = jnp.where(z * scale + shift > 0, acc, 0.0)
@@ -421,10 +444,9 @@
 
 
 def first_gradient_kernel(
-    g, count, dn, z, st, st3, params, ext, ra, rb, rb_edge, e_ref, keep, send, x_ref, dt_ref
+    g, count, dn, z, st, st3, params, x, e_ref, a_ref, b_ref, keep, send, dt_ref
 ):
     place = Place()
-    rows = g.tall - 6
     mean, rstd = stats_of(total_of(st), count)
     total = total_of(st3)
     k0 = params[0:1] * rstd
@@ -432,52 +454,60 @@
     k2 = k0 * rstd * (total[1:2] / count)
     edge = edge_mask(place, g)
     for s in range(g.s):
-        for i in range(rows):
-            at = (s * rows + i) * g.wp
-            z_at = (s * (g.tall - 2) + i + 2) * g.wp
+        for i in range(g.h):
+            at = (s * g.h + i) * g.wp
+            z_at = (s * (g.tall - 2) + i + RIM - 1) * g.wp
             d = k0 * dn[at : at + g.wp, :] - k1 - (z[z_at : z_at + g.wp, :] - mean) * k2
-            e_ref[at : at + g.wp, :] = in_grid(d, i + 3, g, place, edge).astype(BF16)
-        own_transposed(g, e_ref, (s * rows + 1) * g.wp, 0, s, dt_ref)
-        above = jnp.where(place.odd_row, wide(ra, s, RIM - 1), far_row(rb, rb_edge, s, RIM - 1))
-        below = jnp.where(place.odd_row, far_row(rb, rb_edge, s, 0), wide(ra, s, 0))
-        for i in range(rows):
-            row = above if i == 0 else below if i == rows - 1 else wide(ext, s, i - 1)
-            place_shifted(x_ref, s * rows + i, row)
-    kernel_gradient(g, place.core, x_ref, rows, 0, dt_ref, keep, send)
-
-
-def input_gradient_kernel(g, chunk, e, w, cot, occ, master, out_ref, share_ref, e_ref, sem):
-    rows_in = g.tall - 6
-    start = pl.multiple_of(Place().index * share_ref.shape[0], 8)
-    copy = pltpu.make_async_copy(master.at[pl.ds(start, share_ref.shape[0])], share_ref, sem)
-    copy.start()
-    for s in range(g.s):
+            d = in_grid(d, i + RIM, g, place, edge)
+            e_ref[at : at + g.wp, :] = d.astype(BF16)
+            if i == 0:
+                top = d
+        a_ref[s, 0] = jnp.where(place.odd_row, top, d).astype(BF16)
+        b_ref[s, 0] = jnp.where(place.odd_row, d, top).astype(BF16)
+        own_transposed(g, e_ref, s * g.h * g.wp, s, dt_ref)
+    kernel_gradient(g, place.core, x, g.h + 2, 0, dt_ref, keep, send)
+
+
+def input_gradient_kernel(
+    g, chunk, e, ra, rb, w_far, cot_far, occ, out_ref, w, cot, e_ref, sems
+):
+    rows_in = g.h + 2
+    place = Place()
+    copies = [
+        pltpu.make_async_copy(w_far, w, sems.at[0]),
+        pltpu.make_async_copy(cot_far, cot, sems.at[1]),
+    ]
+    for copy in copies:
+        copy.start()
+    for copy in copies:
+        copy.wait()
+    for s in range(g.s):
+        a, b = wide(ra, s, 0), wide(rb, s, 0)
+        rows = [jnp.where(place.odd_row, a, b)]
+        for r in range(g.h):
+            at = (s * g.h + r) * g.wp
+            rows.append(wide(e, slice(at, at + g.wp)))
+        rows.append(jnp.where(place.odd_row, b, a))
         for i in range(rows_in):
-            at = (s * rows_in + i) * g.wp
-            store_shifted(e_ref, at, wide(e, slice(at, at + g.wp)))
+            place_shifted(e_ref, s * rows_in + i, rows[i])
         mask = pixel_mask(occ, s)
         for r in range(0, g.h, chunk):
             acc = transposed_conv(g, e_ref, w, s, rows_in, r, chunk)
             for i in range(chunk):
                 v = acc[i * g.wp : i * g.wp + g.w]
                 out_ref[s, r + i] = (wide(cot, s, r + i) + v) * mask[:, r + i : r + i + 1]
-    copy.wait()
-
-
-def pair_sum_kernel(keep, got, out_ref):
-    taps, half, chans = keep.shape
-    for t in range(taps):
-        out_ref[t * chans : (t + 1) * chans, :] = (keep[t] + got[t]).astype(BF16).T
-
-
-def message_kernel(keep, got, second, out_far, out_ref, sems):
+
+
+def pair_sum_kernel(lane, keep, got, *refs):
+    *_, out_far, buffer, sems = refs
     taps, half, chans = keep.shape
     copies = []
     for t in range(taps):
         rows = pl.ds(t * chans, chans)
-        total = (keep[t] + got[t]).astype(BF16).T
-        out_ref[rows, :] = jnp.concatenate([total, second[rows, :]], axis=1)
-        copies.append(pltpu.make_async_copy(out_ref.at[rows], out_far.at[rows], sems.at[t]))
+        buffer[rows, :] = (keep[t] + got[t]).astype(BF16).T
+        copies.append(
+            pltpu.make_async_copy(buffer.at[rows], out_far.at[rows, pl.ds(lane, half)], sems.at[t])
+        )
         copies[-1].start()
     for copy in copies:
         copy.wait()
@@ -532,6 +562,22 @@
     return lax.ppermute(block, axis, pairs)
 
 
+def swapped_both(block, first_row, first_col):
+    nrows, ncols = lax.axis_size("rows"), lax.axis_size("cols")
+
+    def partner(i, first, count):
+        j = i + 1 if (i - first) % 2 == 0 else i - 1
+        return j if min(i, j) >= first and max(i, j) < count else None
+
+    pairs = []
+    for i in range(nrows):
+        for j in range(ncols):
+            to = partner(i, first_row, nrows), partner(j, first_col, ncols)
+            if None not in to:
+                pairs.append((i * ncols + j, to[0] * ncols + to[1]))
+    return lax.ppermute(block, BOTH, pairs)
+
+
 def to_chunks(flat):
     return flat.reshape(2, -1, 128).transpose(1, 0, 2).reshape(-1, 128)
 
@@ -569,13 +615,16 @@
         return 2 * n * taps * chans
 
     side = shape_of((scenes, g.side, chans), BF16)
-    own, c, d, b = kernel_call(
+    corner = shape_of((scenes, g.corner, chans), BF16)
+    own, c, d, b, bc, bd = kernel_call(
         functools.partial(pack_kernel, g),
         [
             shape_of(features.shape, BF16),
             side,
             side,
             shape_of((scenes, RIM + g.near, width, chans), BF16),
+            corner,
+            corner,
         ],
         1e8,
         far=(0, 1, 2),
@@ -588,6 +637,7 @@
     )(features, occupancy, cotangent)
     rb = swapped(b, "rows", 1)
     rc, rd = swapped(c, "cols", 0), swapped(d, "cols", 1)
+    rb_c, rb_d = swapped_both(bc, 1, 0), swapped_both(bd, 1, 1)
     chunked = to_chunks(conv_weights)
     share = conv_first.shape[1]
     chunk_shape = shape_of((share // 64, 128), F32)
@@ -600,40 +650,37 @@
         far=(0,),
         scratch=[pltpu.VMEM((9, chunked.shape[0] // 9, 128), F32), dma((9,))],
     )(chunked)
-    rc, w1, w2 = lax.optimization_barrier((rc, w1, w2))
 
     def wide_rows(rows):
         return shape_of((scenes, rows, wp, chans), BF16)
 
-    ext, cot_ext, a, b_edge = kernel_call(
+    ext, cot_ext, a = kernel_call(
         functools.partial(assemble_kernel, g),
-        [wide_rows(n) for n in (height, height, RIM + g.near)]
-        + [shape_of((scenes, RIM + g.near, 2 * RIM, chans), BF16)],
+        [wide_rows(n) for n in (height, height, RIM + g.near)],
         0,
         size=1024,
     )(own, cotangent, rc, rd)
-    z1, st = kernel_call(
+    rows_x = scenes * (height + 2) * wp
+    x_shape = held((rows_x, 3 * chans), BF16)
+    z1, st, x = kernel_call(
         functools.partial(own_conv_kernel, g),
-        [held((n1, chans), F32), held((16, chans), F32)],
+        [held((n1, chans), F32), held((16, chans), F32), x_shape],
         0,
         size=1024,
-        scratch=[pltpu.VMEM((scenes * height * wp, 3 * chans), BF16)],
     )(ext, w1)
-    b_edge, st = lax.optimization_barrier((b_edge, st))
-    rb_edge = swapped(b_edge, "rows", 1)
-    a, rb, rb_edge = lax.optimization_barrier((a, rb, rb_edge))
+    a, rb, rb_c, rb_d, w1 = lax.optimization_barrier((a, rb, rb_c, rb_d, w1))
     ra = swapped(a, "rows", 0)
-    z1, st = kernel_call(
+    z1, st, x, cot_next = kernel_call(
         functools.partial(rim_conv_kernel, g),
-        [held((n1, chans), F32), shape_of((devices, 2, chans), F32)],
+        [held((n1, chans), F32), shape_of((devices, 2, chans), F32), x_shape, wide_rows(2)],
         0,
         size=1024,
         scratch=[pltpu.VMEM((scenes * 2 * (RIM + 2) * wp, 3 * chans), BF16)],
-        alias={6: 0},
-    )(ext, ra, rb, rb_edge, w1, st, z1)
+        alias={7: 0, 8: 2},
+    )(ext, ra, rb, rb_c, rb_d, w1, st, z1, x)
     st1 = exchange(st)
     h, z2, st = kernel_call(
-        functools.partial(second_conv_kernel, g, 6, count),
+        functools.partial(second_conv_kernel, g, 5, count),
         [
             held((n1, 3 * chans), BF16),
             held((n2, chans), F32),
@@ -643,49 +690,64 @@
     )(z1, st1, norm_scale_bias, w2, cot_ext)
     st2 = exchange(st)
     grad_shape = held((9, chans // 2, chans), F32)
-    block_out, d, keep2, send2 = kernel_call(
+    d, keep2, send2 = kernel_call(
         functools.partial(second_gradient_kernel, g, count),
-        [
-            shape_of(features.shape, BF16),
-            held((n2, 3 * chans), BF16),
-            grad_shape,
-            grad_shape,
-        ],
+        [held((n2, chans), BF16), grad_shape, grad_shape],
         conv_flops(own_pixels),
         scratch=[pltpu.VMEM((chans, own_pixels), BF16)],
-    )(z2, st2, norm_scale_bias, ext, cot_ext, ra, rb, rb_edge, h)
+    )(z2, st2, norm_scale_bias, cot_ext, cot_next, h)
     got2 = swapped(send2, "rows", 0)
-    dn1, st = kernel_call(
-        functools.partial(hidden_gradient_kernel, g, 5, count),
-        [held((n3, chans), F32), shape_of((devices, 2, chans), F32)],
+    dn1, st, block_out = kernel_call(
+        functools.partial(hidden_gradient_kernel, g, 8, count),
+        [
+            held((n3, chans), F32),
+            shape_of((devices, 2, chans), F32),
+            shape_of(features.shape, BF16),
+        ],
         conv_flops(n3),
-    )(d, w2, z1, st1, norm_scale_bias)
+        scratch=[pltpu.VMEM((n2, 3 * chans), BF16)],
+    )(d, w2, z1, z2, st1, st2, norm_scale_bias, ext)
     st, got2 = lax.optimization_barrier((st, got2))
     st3 = exchange(st)
-    e, keep1, send1 = kernel_call(
+    e, a, b, keep1, send1 = kernel_call(
         functools.partial(first_gradient_kernel, g, count),
-        [held((n3, chans), BF16), grad_shape, grad_shape],
+        [held((n3, chans), BF16), wide_rows(1), wide_rows(1), grad_shape, grad_shape],
         conv_flops(own_pixels),
-        scratch=[pltpu.VMEM((n3, 3 * chans), BF16), pltpu.VMEM((chans, own_pixels), BF16)],
-    )(dn1, z1, st1, st3, norm_scale_bias, ext, ra, rb, rb_edge)
+        scratch=[pltpu.VMEM((chans, own_pixels), BF16)],
+    )(dn1, z1, st1, st3, norm_scale_bias, x)
     got1 = swapped(send1, "rows", 0)
     keep2, got2, keep1 = lax.optimization_barrier((keep2, got2, keep1))
-    (second,) = kernel_call(pair_sum_kernel, [held((taps, chans // 2), BF16)], 1e9)(keep2, got2)
-    (parts,) = kernel_call(
-        message_kernel,
-        [stored((taps, chans), BF16)],
-        1e9,
-        far_out=(0,),
-        scratch=[pltpu.VMEM((taps, chans), BF16), dma((9,))],
-    )(keep1, got1, second)
+
+    def add_pair(lane, *operands, **options):
+        return kernel_call(
+            functools.partial(pair_sum_kernel, lane),
+            [stored((taps, chans), BF16)],
+            1e9,
+            far_out=(0,),
+            scratch=[pltpu.VMEM((taps, chans // 2), BF16), dma((9,))],
+            **options,
+        )(*operands)
+
+    (parts,) = add_pair(chans // 2, keep2, got2)
+    (parts,) = add_pair(0, keep1, got1, parts, far=(2,), alias={2: 0})
+    parts, chunked = lax.optimization_barrier((parts, chunked))
     parts = exchange(parts.reshape(devices, taps // devices, chans))
-    grad_input, own_weights = kernel_call(
+    ra, rb = swapped(a, "rows", 0), swapped(b, "rows", 1)
+    (grad_input,) = kernel_call(
         functools.partial(input_gradient_kernel, g, 8),
-        [shape_of(features.shape, F32), chunk_shape],
+        [shape_of(features.shape, F32)],
         conv_flops(own_pixels),
-        far=(4,),
-        scratch=[pltpu.VMEM((n3, 3 * chans), BF16), dma],
-    )(e, w1, cotangent, occupancy, chunked)
+        far=(3, 4),
+        scratch=[
+            pltpu.VMEM(weights, BF16),
+            pltpu.VMEM(features.shape, BF16),
+            pltpu.VMEM((rows_x, 3 * chans), BF16),
+            dma((2,)),
+        ],
+    )(e, ra, rb, w1, cotangent, occupancy)
+    own_rows = share // 64
+    first_row = (lax.axis_index("rows") * lax.axis_size("cols") + lax.axis_index("cols")) * own_rows
+    own_weights = lax.dynamic_slice_in_dim(chunked, first_row, own_rows, 0)
 
     norm_shape = shape_of(norm_first.shape, F32)
     updated = kernel_call(

time: 109 us -> 102 us (0.936)
  waiting for transfers between devices: 32.2 us -> 21.4 us
  starting transfers between devices: 14.1 us -> 22.1 us
  blocking collectives: 32.1 us -> 29.6 us
  local copies, waits for them, and re-layouts: 2.79 us -> 0.96 us
    all_to_all x1, waiting for transfers between devices: 23.5 us -> 11.3 us  [exchange(): return lax.all_to_all(parts, BOTH, 0, 0, tiled=True)]
    ppermute x0 -> x2, starting transfers between devices: none -> 6.69 us  [swapped_both(): return lax.ppermute(block, BOTH, pairs)]
    unnamed x22 -> x16, local copies, waits for them, and re-layouts: 2.79 us -> 0.04 us
    all_to_all x3, blocking collectives: 32.1 us -> 29.6 us  [exchange(): return lax.all_to_all(parts, BOTH, 0, 0, tiled=True)]
    ppermute x7 -> x8, waiting for transfers between devices: 8.7 us -> 10.1 us  [swapped(): return lax.ppermute(block, axis, pairs)]
    ppermute x7 -> x8, starting transfers between devices: 11.5 us -> 12.7 us  [swapped(): return lax.ppermute(block, axis, pairs)]
  transfers between devices with their start and end apart: 8 -> 11, of which waited for: 4 -> 4; matrix products, arithmetic and copies ran while one was open for 0% -> 1% of each run, Pallas kernels for 10% -> 13%
where the time goes in v2:
time: 102 us
  blocking collectives  29.6 us (29%)
  Pallas kernels  26.7 us (26%)
  starting transfers between devices  22.1 us (22%)
  waiting for transfers between devices  21.4 us (21%)
    all_to_all x3, blocking collectives, exchange(): return lax.all_to_all(parts, BOTH, 0, 0, tiled=True)  29.6 us
    pallas_call x13, Pallas kernels, call(): pl.pallas_call(body, out_shape=out_shape, in_specs=specs, out_specs=[pl.B...  26.7 us
    ppermute x8, starting transfers between devices, swapped(): return lax.ppermute(block, axis, pairs)  12.7 us
    all_to_all x1, waiting for transfers between devices, exchange(): return lax.all_to_all(parts, BOTH, 0, 0, tiled=True)  11.3 us
    ppermute x8, waiting for transfers between devices, swapped(): return lax.ppermute(block, axis, pairs)  10.1 us
    ppermute x2, starting transfers between devices, swapped_both(): return lax.ppermute(block, BOTH, pairs)  6.69 us
    all_to_all x1, starting transfers between devices, exchange(): return lax.all_to_all(parts, BOTH, 0, 0, tiled=True)  2.65 us
  transfers between devices with their start and end apart: 11, of which 4 were waited for; matrix products, arithmetic and copies ran while one was open for 1% of the time, Pallas kernels for 13%

profile of v2, /device:TPU:1, one launch (start us, length us, event | category | flops | bytes accessed | tf_op | source)
XLA Modules:
  0.0 101.7 jit_solution(11469680495096713051)
XLA Ops:
  0.6 1.7 %shard_map.168 = (bf16[4,8,40,256]{3,2,1,0:T(8,128)(2,1)S(1)}, bf16[4,48,256]{2,1,0:T(8,128)(2,1)S(1)}, bf16[4,48,256]{2,1,0:T(8,128)(2,1)S(1)}, bf16[4,4,40,256...) custom-call(bf16[4,8,40,256]{3,2,1,0:T(8,128)(2,1)} %features.1, ...), custom_call_target="tpu_custom_call" | custom-call | flops 100000000 | bytes 4194304 | tf_op jit(solution)/shard_map/pallas_call | solution.py:41
  2.4 4.5 %collective-permute-start.2 = (bf16[4,4,40,256]{3,2,1,0:T(8,128)(2,1)S(1)}, bf16[4,4,40,256]{3,2,1,0:T(8,128)(2,1)S(1)}, u32[]{:S(2)}, u32[]{:S(2)}) collective-permute-start(bf16[4,4,40,256]{3,2,1,0:T(8,128)(2,1)S(1)} %get-tuple-element.67), channel_id=1, source_target_pairs={{4,8},{8,4},{12,16},{16,12},{20,24},{24,20},{5,9},{9,5},{13,17},{1... | collective-permute-start | bytes 983048 | tf_op jit(solution)/shard_map/ppermute | solution.py:562
  6.9 1.4 %collective-permute-start = (bf16[4,48,256]{2,1,0:T(8,128)(2,1)S(1)}, bf16[4,48,256]{2,1,0:T(8,128)(2,1)S(1)}, u32[]{:S(2)}, u32[]{:S(2)}) collective-permute-start(bf16[4,48,256]{2,1,0:T(8,128)(2,1)S(1)} %get-tuple-element.63), channel_id=1, source_target_pairs={{0,1},{1,0},{2,3},{3,2},{4,5},{5,4},{6,7},{7,6},{8,9},{9,8},{10,11... | collective-permute-start | bytes 294920 | tf_op jit(solution)/shard_map/ppermute | solution.py:562
  8.2 0.7 collective-permute-start.1
  8.9 6.0 %collective-permute-start.3 = (bf16[4,16,256]{2,1,0:T(8,128)(2,1)S(1)}, bf16[4,16,256]{2,1,0:T(8,128)(2,1)S(1)}, u32[]{:S(2)}, u32[]{:S(2)}) collective-permute-start(bf16[4,16,256]{2,1,0:T(8,128)(2,1)S(1)} %get-tuple-element.68), channel_id=1, source_target_pairs={{4,9},{5,8},{6,11},{7,10},{8,5},{9,4},{10,7},{11,6},{12,17},{13,16... | collective-permute-start | bytes 98312 | tf_op jit(solution)/shard_map/ppermute | solution.py:578
  14.9 0.7 collective-permute-start.4
  15.6 0.0 copy-start.1
  15.6 2.5 %shard_map.170 = (bf16[2304,256]{1,0:T(8,128)(2,1)S(1)}, bf16[2304,256]{1,0:T(8,128)(2,1)S(1)}) custom-call(f32[9216,128]{1,0:T(8,128)} %bitcast.38), custom_call_target="tpu_custom_call" | custom-call | bytes 1024 | tf_op jit(solution)/shard_map/pallas_call | solution.py:41
  18.1 0.0 copy-start
  18.1 0.0 collective-permute-done.rc
  18.1 0.0 collective-permute-done.1.rd
  18.1 0.0 copy-done.1
  18.2 0.2 shard_map.169
  18.4 0.0 collective-permute-done.3.rb_c
  18.4 0.0 collective-permute-done.4.rb_d
  18.4 0.0 collective-permute-done.2.rb
  18.4 0.1 collective-permute-start.5
  18.5 1.6 %shard_map.171 = (f32[2304,256]{1,0:T(8,128)S(1)}, f32[16,256]{1,0:T(8,128)S(1)}, bf16[1920,768]{1,0:T(8,128)(2,1)S(1)}) custom-call(bf16[4,8,48,256]{3,2,1,0:T(8,128)(2,1)S(1)} %get-tuple-element.65.ext, bf16[2304,256]{1,0:T(8,128)(2,1)S(1)} %get-tuple-element.75.w.w_far), custom_call_target="tpu_custom_call" | custom-call | bytes 1024 | tf_op jit(solution)/shard_map/pallas_call | solution.py:41
  20.1 0.1 collective-permute-done.5.ra
  20.2 0.0 copy-done
  20.2 1.6 %shard_map.172 = (f32[2304,256]{1,0:T(8,128)S(1)}, f32[32,2,256]{2,1,0:T(2,128)S(1)}, bf16[1920,768]{1,0:T(8,128)(2,1)S(1)}, bf16[4,2,48,256]{3,2,1,0:T(8,128)(2,1)S(1)}) custom-call(bf16[4,8,48,256]{3,2,1,0:T(8,128)(2,1)S(1)} %get-tuple-element.65.ext, ...), custom_call_target="tpu_custom_call", output_to_operand_aliasing={{0}: (7, {}), {2}: (8, {})} | custom-call | bytes 1024 | tf_op jit(solution)/shard_map/pallas_call | solution.py:41
  21.8 11.7 %all_to_all.20.st = f32[32,2,256]{2,1,0:T(2,128)S(1)} all-to-all(f32[32,2,256]{2,1,0:T(2,128)S(1)} %get-tuple-element.80), channel_id=1, replica_groups=mesh['rows'=8,'cols'=4] {'rows','cols'}, dimensions={0} | all-to-all | bytes 131072 | tf_op jit(solution)/shard_map/all_to_all | solution.py:590
  33.5 0.0 copy-done.4
  33.5 2.8 %shard_map.173 = (bf16[2304,768]{1,0:T(8,128)(2,1)S(1)}, f32[1920,256]{1,0:T(8,128)S(1)}, f32[32,4,256]{2,1,0:T(4,128)S(1)}) custom-call(f32[2304,256]{1,0:T(8,128)S(1)} %get-tuple-element.79.z1.z, f32[32,2,256]{2,1,0:T(2,128)S(1)} %all_to_all.20.st, f32[4,256]{1,0:T(4,128)S(1)} %copy-done.4, bf16[2304,256]{1,0:T(8,128)(2,1)S(1)} %get-tuple-element.81.w, ...), custom_call_target="tpu_custom_call" | custom-call | flops 2264924160 | bytes 4194304 | tf_op jit(solution)/shard_map/pallas_call | solution.py:41
  36.3 9.7 %all_to_all.21.st.st2 = f32[32,4,256]{2,1,0:T(4,128)S(1)} all-to-all(f32[32,4,256]{2,1,0:T(4,128)S(1)} %get-tuple-element.84), channel_id=1, replica_groups=mesh['rows'=8,'cols'=4] {'rows','cols'}, dimensions={0} | all-to-all | bytes 262144 | tf_op jit(solution)/shard_map/all_to_all | solution.py:590
  46.0 2.6 %shard_map.174 = (bf16[1920,256]{1,0:T(8,128)(2,1)S(1)}, f32[9,128,256]{2,1,0:T(8,128)S(1)}, f32[9,128,256]{2,1,0:T(8,128)S(1)}) custom-call(f32[1920,256]{1,0:T(8,128)S(1)} %get-tuple-element.83.z2, f32[32,4,256]{2,1,0:T(4,128)S(1)} %all_to_all.21.st.st2, f32[4,256]{1,0:T(4,128)S(1)} %copy-done.4, bf16[4,8,48,256]{3,2,1,0:T(8,128)(2,1)S(1)} %get-tuple-element.82.cot, ...), custom_call_target="tpu_custom_call" | custom-call | flops 1811939328 | bytes 4194304 | tf_op jit(solution)/shard_map/pallas_call | solution.py:41
  48.6 1.4 %collective-permute-start.6 = (f32[9,128,256]{2,1,0:T(8,128)S(1)}, f32[9,128,256]{2,1,0:T(8,128)S(1)}, u32[]{:S(2)}, u32[]{:S(2)}) collective-permute-start(f32[9,128,256]{2,1,0:T(8,128)S(1)} %get-tuple-element.91), channel_id=1, source_target_pairs={{0,4},{4,0},{8,12},{12,8},{16,20},{20,16},{24,28},{28,24},{1,5},{5... | collective-permute-start | bytes 3538952 | tf_op jit(solution)/shard_map/ppermute | solution.py:562
  50.0 3.3 %shard_map.175 = (f32[1536,256]{1,0:T(8,128)S(1)}, f32[32,2,256]{2,1,0:T(2,128)S(1)}, bf16[4,8,40,256]{3,2,1,0:T(8,128)(2,1)}) custom-call(bf16[1920,256]{1,0:T(8,128)(2,1)S(1)} %get-tuple-element.87.d, bf16[2304,256]{1,0:T(8,128)(2,1)S(1)} %get-tuple-element.81.w, f32[2304,256]{1,0:T(8,128)S(1)} %get-tuple-element.79.z1.z, ...), custom_call_target="tpu_custom_call" | custom-call | flops 1811939328 | bytes 4194304 | tf_op jit(solution)/shard_map/pallas_call | solution.py:41
  53.3 0.0 collective-permute-done.6.got
  53.3 8.3 %all_to_all.22.st3 = f32[32,2,256]{2,1,0:T(2,128)S(1)} all-to-all(f32[32,2,256]{2,1,0:T(2,128)S(1)} %get-tuple-element.92), channel_id=1, replica_groups=mesh['rows'=8,'cols'=4] {'rows','cols'}, dimensions={0} | all-to-all | bytes 131072 | tf_op jit(solution)/shard_map/all_to_all | solution.py:590
  61.6 2.5 %shard_map.176 = (bf16[1536,256]{1,0:T(8,128)(2,1)S(1)}, bf16[4,1,48,256]{3,2,1,0:T(8,128)(2,1)S(1)}, bf16[4,1,48,256]{3,2,1,0:T(8,128)(2,1)S(1)}, f32[9,128,256]{2,1,0:T(8,128)S(1)}, f32[9,128,256]{2,1,0:T(8,128)S(1)}) custom-call(f32[1536,256]{1,0:T(8,128)S(1)} %get-tuple-element.89.dn, f32[2304,256]{1,0:T(8,128)S(1)} %get-tuple-element.79.z1.z, ...), custom_call_target="tpu_custom_call" | custom-call | flops 1811939328 | bytes 4194304 | tf_op jit(solution)/shard_map/pallas_call | solution.py:41
  64.2 1.0 collective-permute-start.9
  65.1 1.0 %shard_map.178.refs_0_ = bf16[2304,256]{1,0:T(8,128)(2,1)} custom-call(f32[9,128,256]{2,1,0:T(8,128)S(1)} %get-tuple-element.102.keep, f32[9,128,256]{2,1,0:T(8,128)S(1)} %collective-permute-done.6.got), custom_call_target="tpu_custom_call" | custom-call | flops 1000000000 | bytes 4194304 | tf_op jit(solution)/shard_map/pallas_call | solution.py:41
  66.2 1.4 %collective-permute-done.9.got = f32[9,128,256]{2,1,0:T(8,128)S(1)} collective-permute-done((f32[9,128,256]{2,1,0:T(8,128)S(1)}, f32[9,128,256]{2,1,0:T(8,128)S(1)}, u32[]{:S(2)}, u32[]{:S(2)}) %collective-permute-start.9) | collective-permute-done | bytes 1179680 | tf_op jit(solution)/shard_map/ppermute | solution.py:562
  67.6 1.0 %shard_map.179 = bf16[2304,256]{1,0:T(8,128)(2,1)} custom-call(f32[9,128,256]{2,1,0:T(8,128)S(1)} %get-tuple-element.100.keep, f32[9,128,256]{2,1,0:T(8,128)S(1)} %collective-permute-done.9.got, bf16[2304,256]{1,0:T(8,128)(2,1)} %shard_map.178.refs_0_), custom_call_target="tpu_custom_call", output_to_operand_aliasing={{}: (2, {})} | custom-call | flops 1000000000 | bytes 4194304 | tf_op jit(solution)/shard_map/pallas_call | solution.py:41
  68.6 0.0 copy-start.5
  68.6 2.6 %all-to-all-start.3 = ((bf16[32,72,256]{2,1,0:T(8,128)(2,1)}), bf16[32,72,256]{2,1,0:T(8,128)(2,1)S(1)}, u32[]{:S(2)}, u32[]{:S(2)}) async-start(bf16[32,72,256]{2,1,0:T(8,128)(2,1)} %bitcast.40), calls=%async_computation.3 | async-start | bytes 2359296 | tf_op jit(solution)/shard_map/all_to_all | solution.py:590
  71.3 0.5 collective-permute-start.7
  71.8 3.3 %collective-permute-start.8 = (bf16[4,1,48,256]{3,2,1,0:T(8,128)(2,1)S(1)}, bf16[4,1,48,256]{3,2,1,0:T(8,128)(2,1)S(1)}, u32[]{:S(2)}, u32[]{:S(2)}) collective-permute-start(bf16[4,1,48,256]{3,2,1,0:T(8,128)(2,1)S(1)} %get-tuple-element.96), channel_id=1, source_target_pairs={{4,8},{8,4},{12,16},{16,12},{20,24},{24,20},{5,9},{9,5},{13,17},{1... | collective-permute-start | bytes 294920 | tf_op jit(solution)/shard_map/ppermute | solution.py:562
  75.1 0.0 collective-permute-done.7.ra
  75.1 8.6 %collective-permute-done.8.rb = bf16[4,1,48,256]{3,2,1,0:T(8,128)(2,1)S(1)} collective-permute-done((bf16[4,1,48,256]{3,2,1,0:T(8,128)(2,1)S(1)}, bf16[4,1,48,256]{3,2,1,0:T(8,128)(2,1)S(1)}, u32[]{:S(2)}, u32[]{:S(2)}) %collective-permute-start.8) | collective-permute-done | bytes 98336 | tf_op jit(solution)/shard_map/ppermute | solution.py:562
  83.6 0.0 copy-done.5
  83.7 0.0 copy-start.7
  83.7 4.7 %shard_map.177 = f32[4,8,40,256]{3,2,1,0:T(8,128)} custom-call(bf16[1536,256]{1,0:T(8,128)(2,1)S(1)} %get-tuple-element.94.e, bf16[4,1,48,256]{3,2,1,0:T(8,128)(2,1)S(1)} %collective-permute-done.7.ra, bf16[4,1,48,256]{3,2,1,0:T(8,128)(2,1)S(1)} %collective-permute-done.8.rb, bf16[2304,256]{1,0:T(8,128)(2,1)} %copy-done, bf16[4,8,40,256]{3,2,1,0:T(8,128)(2,1)} %cot_far.1, ...), custom_call_target="tpu_custom_call" | custom-call | flops 1811939328 | bytes 4194304 | tf_op jit(solution)/shard_map/pallas_call | solution.py:41
  88.3 0.9 constant_dynamic-slice_fusion.w
  89.3 11.3 %all-to-all-done.3.parts = bf16[32,72,256]{2,1,0:T(8,128)(2,1)S(1)} async-done(((bf16[32,72,256]{2,1,0:T(8,128)(2,1)}), bf16[32,72,256]{2,1,0:T(8,128)(2,1)S(1)}, u32[]{:S(2)}, u32[]{:S(2)}) %all-to-all-start.3) | async-done | bytes 1179680 | tf_op jit(solution)/shard_map/all_to_all | solution.py:590
  100.6 0.0 copy-done.7
  100.6 1.1 %shard_map.180 = (f32[288,128]{1,0:T(8,128)}, f32[288,128]{1,0:T(8,128)}, f32[288,128]{1,0:T(8,128)}, f32[288,128]{1,0:T(8,128)}, f32[4,256]{1,0:T(4,128)}, /*in...) custom-call(bf16[32,72,256]{2,1,0:T(8,128)(2,1)S(1)} %all-to-all-done.3.parts, ...), custom_call_target="tpu_custom_call" | custom-call | flops 100000000 | bytes 4194304 | tf_op jit(solution)/shard_map/pallas_call | solution.py:41
  (7 shorter events, 0.0 us)
Async XLA Ops:
  2.4 16.0 %collective-permute-start.2 = (bf16[4,4,40,256]{3,2,1,0:T(8,128)(2,1)S(1)}, bf16[4,4,40,256]{3,2,1,0:T(8,128)(2,1)S(1)}, u32[]{:S(2)}, u32[]{:S(2)}) collective-permute-start(bf16[4,4,40,256]{3,2,1,0:T(8,128)(2,1)S(1)} %get-tuple-element.67), channel_id=1, source_target_pairs={{4,8},{8,4},{12,16},{16,12},{20,24},{24,20},{5,9},{9,5},{13,17},{1... | collective-permute-start | bytes 983048 | tf_op jit(solution)/shard_map/ppermute | solution.py:562
  6.9 11.3 %collective-permute-start = (bf16[4,48,256]{2,1,0:T(8,128)(2,1)S(1)}, bf16[4,48,256]{2,1,0:T(8,128)(2,1)S(1)}, u32[]{:S(2)}, u32[]{:S(2)}) collective-permute-start(bf16[4,48,256]{2,1,0:T(8,128)(2,1)S(1)} %get-tuple-element.63), channel_id=1, source_target_pairs={{0,1},{1,0},{2,3},{3,2},{4,5},{5,4},{6,7},{7,6},{8,9},{9,8},{10,11... | collective-permute-start | bytes 294920 | tf_op jit(solution)/shard_map/ppermute | solution.py:562
  8.2 9.9 %collective-permute-start.1 = (bf16[4,48,256]{2,1,0:T(8,128)(2,1)S(1)}, bf16[4,48,256]{2,1,0:T(8,128)(2,1)S(1)}, u32[]{:S(2)}, u32[]{:S(2)}) collective-permute-start(bf16[4,48,256]{2,1,0:T(8,128)(2,1)S(1)} %get-tuple-element.64), channel_id=1, source_target_pairs={{1,2},{2,1},{5,6},{6,5},{9,10},{10,9},{13,14},{14,13},{17,18},{18,... | collective-permute-start | bytes 294920 | tf_op jit(solution)/shard_map/ppermute | solution.py:562
  8.9 9.5 %collective-permute-start.3 = (bf16[4,16,256]{2,1,0:T(8,128)(2,1)S(1)}, bf16[4,16,256]{2,1,0:T(8,128)(2,1)S(1)}, u32[]{:S(2)}, u32[]{:S(2)}) collective-permute-start(bf16[4,16,256]{2,1,0:T(8,128)(2,1)S(1)} %get-tuple-element.68), channel_id=1, source_target_pairs={{4,9},{5,8},{6,11},{7,10},{8,5},{9,4},{10,7},{11,6},{12,17},{13,16... | collective-permute-start | bytes 98312 | tf_op jit(solution)/shard_map/ppermute | solution.py:578
  14.9 3.4 %collective-permute-start.4 = (bf16[4,16,256]{2,1,0:T(8,128)(2,1)S(1)}, bf16[4,16,256]{2,1,0:T(8,128)(2,1)S(1)}, u32[]{:S(2)}, u32[]{:S(2)}) collective-permute-start(bf16[4,16,256]{2,1,0:T(8,128)(2,1)S(1)} %get-tuple-element.69), channel_id=1, source_target_pairs={{5,10},{6,9},{9,6},{10,5},{13,18},{14,17},{17,14},{18,13},{21,26},... | collective-permute-start | bytes 98312 | tf_op jit(solution)/shard_map/ppermute | solution.py:578
  15.6 2.5 %copy-start.1 = (bf16[4,8,40,256]{3,2,1,0:T(8,128)(2,1)S(1)}, bf16[4,8,40,256]{3,2,1,0:T(8,128)(2,1)}, u32[]{:S(2)}) copy-start(bf16[4,8,40,256]{3,2,1,0:T(8,128)(2,1)} %cot_far.1) | copy-start | bytes 1966084
  18.1 2.1 %copy-start = (bf16[2304,256]{1,0:T(8,128)(2,1)}, bf16[2304,256]{1,0:T(8,128)(2,1)S(1)}, u32[]{:S(2)}) copy-start(bf16[2304,256]{1,0:T(8,128)(2,1)S(1)} %get-tuple-element.75.w.w_far) | copy-start | bytes 3538948
  18.4 1.8 %collective-permute-start.5 = (bf16[4,4,48,256]{3,2,1,0:T(8,128)(2,1)S(1)}, bf16[4,4,48,256]{3,2,1,0:T(8,128)(2,1)S(1)}, u32[]{:S(2)}, u32[]{:S(2)}) collective-permute-start(bf16[4,4,48,256]{3,2,1,0:T(8,128)(2,1)S(1)} %get-tuple-element.71), channel_id=1, source_target_pairs={{0,4},{4,0},{8,12},{12,8},{16,20},{20,16},{24,28},{28,24},{1,5},{5... | collective-permute-start | bytes 1179656 | tf_op jit(solution)/shard_map/ppermute | solution.py:562
  20.2 13.3 %copy-start.4 = (f32[4,256]{1,0:T(4,128)S(1)}, f32[4,256]{1,0:T(4,128)}, u32[]{:S(2)}) copy-start(f32[4,256]{1,0:T(4,128)} %params.9) | copy-start | bytes 12292
  48.6 4.7 %collective-permute-start.6 = (f32[9,128,256]{2,1,0:T(8,128)S(1)}, f32[9,128,256]{2,1,0:T(8,128)S(1)}, u32[]{:S(2)}, u32[]{:S(2)}) collective-permute-start(f32[9,128,256]{2,1,0:T(8,128)S(1)} %get-tuple-element.91), channel_id=1, source_target_pairs={{0,4},{4,0},{8,12},{12,8},{16,20},{20,16},{24,28},{28,24},{1,5},{5... | collective-permute-start | bytes 3538952 | tf_op jit(solution)/shard_map/ppermute | solution.py:562
  64.2 3.5 %collective-permute-start.9 = (f32[9,128,256]{2,1,0:T(8,128)S(1)}, f32[9,128,256]{2,1,0:T(8,128)S(1)}, u32[]{:S(2)}, u32[]{:S(2)}) collective-permute-start(f32[9,128,256]{2,1,0:T(8,128)S(1)} %get-tuple-element.101), channel_id=1, source_target_pairs={{0,4},{4,0},{8,12},{12,8},{16,20},{20,16},{24,28},{28,24},{1,5},{5... | collective-permute-start | bytes 3538952 | tf_op jit(solution)/shard_map/ppermute | solution.py:562
  68.6 15.0 %copy-start.5 = (s32[4,8,40]{2,1,0:T(8,128)S(1)}, s32[4,8,40]{2,1,0:T(8,128)}, u32[]{:S(2)}) copy-start(s32[4,8,40]{2,1,0:T(8,128)} %occ.1) | copy-start | bytes 15364
  68.6 31.9 %all-to-all-start.3 = ((bf16[32,72,256]{2,1,0:T(8,128)(2,1)}), bf16[32,72,256]{2,1,0:T(8,128)(2,1)S(1)}, u32[]{:S(2)}, u32[]{:S(2)}) async-start(bf16[32,72,256]{2,1,0:T(8,128)(2,1)} %bitcast.40), calls=%async_computation.3 | async-start | bytes 2359296 | tf_op jit(solution)/shard_map/all_to_all | solution.py:590
  71.3 3.8 %collective-permute-start.7 = (bf16[4,1,48,256]{3,2,1,0:T(8,128)(2,1)S(1)}, bf16[4,1,48,256]{3,2,1,0:T(8,128)(2,1)S(1)}, u32[]{:S(2)}, u32[]{:S(2)}) collective-permute-start(bf16[4,1,48,256]{3,2,1,0:T(8,128)(2,1)S(1)} %get-tuple-element.95), channel_id=1, source_target_pairs={{0,4},{4,0},{8,12},{12,8},{16,20},{20,16},{24,28},{28,24},{1,5},{5... | collective-permute-start | bytes 294920 | tf_op jit(solution)/shard_map/ppermute | solution.py:562
  71.8 11.9 %collective-permute-start.8 = (bf16[4,1,48,256]{3,2,1,0:T(8,128)(2,1)S(1)}, bf16[4,1,48,256]{3,2,1,0:T(8,128)(2,1)S(1)}, u32[]{:S(2)}, u32[]{:S(2)}) collective-permute-start(bf16[4,1,48,256]{3,2,1,0:T(8,128)(2,1)S(1)} %get-tuple-element.96), channel_id=1, source_target_pairs={{4,8},{8,4},{12,16},{16,12},{20,24},{24,20},{5,9},{9,5},{13,17},{1... | collective-permute-start | bytes 294920 | tf_op jit(solution)/shard_map/ppermute | solution.py:562
  83.6 16.9 %copy-start.2 = (f32[2,18432]{1,0:T(2,128)S(1)}, f32[2,18432]{1,0:T(2,128)}, u32[]{:S(2)}) copy-start(f32[2,18432]{1,0:T(2,128)} %param.13) | copy-start | bytes 442372
  83.6 16.9 %copy-start.3 = (f32[2,18432]{1,0:T(2,128)S(1)}, f32[2,18432]{1,0:T(2,128)}, u32[]{:S(2)}) copy-start(f32[2,18432]{1,0:T(2,128)} %param.14) | copy-start | bytes 442372
  83.6 16.9 %copy-start.6 = (f32[4,256]{1,0:T(4,128)S(1)}, f32[4,256]{1,0:T(4,128)}, u32[]{:S(2)}) copy-start(f32[4,256]{1,0:T(4,128)} %n_first.1) | copy-start | bytes 12292
  83.7 16.9 %copy-start.7 = (f32[4,256]{1,0:T(4,128)S(1)}, f32[4,256]{1,0:T(4,128)}, u32[]{:S(2)}) copy-start(f32[4,256]{1,0:T(4,128)} %n_second.1) | copy-start | bytes 12292

commit v3 on v2

--- a/solution.py
+++ b/solution.py
@@ -107,6 +107,7 @@
         self.right = (col < ncols - 1).astype(F32)
         self.left = (col > 0).astype(F32)
         self.core = row % 2
+        self.second = row // 2 % 2
         self.odd_row = row % 2 == 1
         self.odd_col = col % 2 == 1
         self.index = row * ncols + col
@@ -366,7 +367,11 @@
         acc = dot(lhs, jnp.concatenate([field[at : at + span, :] for at in starts], axis=0))
         for b in range(3):
             keep[a * 3 + b] = acc[0:half, b * chans : (b + 1) * chans]
-            send[a * 3 + b] = acc[half:, b * chans : (b + 1) * chans]
+            other_half = acc[half:, b * chans : (b + 1) * chans]
+            if isinstance(send, tuple):
+                send[a][b] = other_half.astype(BF16)
+            else:
+                send[a * 3 + b] = other_half
 
 
 def second_gradient_kernel(
@@ -444,7 +449,7 @@
 
 
 def first_gradient_kernel(
-    g, count, dn, z, st, st3, params, x, e_ref, a_ref, b_ref, keep, send, dt_ref
+    g, count, dn, z, st, st3, params, x, e_ref, a_ref, b_ref, keep, send0, send1, send2, dt_ref
 ):
     place = Place()
     mean, rstd = stats_of(total_of(st), count)
@@ -465,7 +470,7 @@
         a_ref[s, 0] = jnp.where(place.odd_row, top, d).astype(BF16)
         b_ref[s, 0] = jnp.where(place.odd_row, d, top).astype(BF16)
         own_transposed(g, e_ref, s * g.h * g.wp, s, dt_ref)
-    kernel_gradient(g, place.core, x, g.h + 2, 0, dt_ref, keep, send)
+    kernel_gradient(g, place.core, x, g.h + 2, 0, dt_ref, keep, (send0, send1, send2))
 
 
 def input_gradient_kernel(
@@ -498,16 +503,59 @@
                 out_ref[s, r + i] = (wide(cot, s, r + i) + v) * mask[:, r + i : r + i + 1]
 
 
-def pair_sum_kernel(lane, keep, got, *refs):
-    *_, out_far, buffer, sems = refs
+def pair_total(keep, got, t):
+    other = got[t] if len(got) > 3 else got[t // 3][t % 3].astype(F32)
+    return keep[t] + other
+
+
+def pair_sum_kernel(lane, keep, *refs):
+    *got, out_far, buffer, sems = refs
+    got = got[0] if len(got) == 1 else got[:3]
     taps, half, chans = keep.shape
     copies = []
     for t in range(taps):
         rows = pl.ds(t * chans, chans)
-        buffer[rows, :] = (keep[t] + got[t]).astype(BF16).T
+        buffer[rows, :] = pair_total(keep, got, t).astype(BF16).T
         copies.append(
             pltpu.make_async_copy(buffer.at[rows], out_far.at[rows, pl.ds(lane, half)], sems.at[t])
         )
+        copies[-1].start()
+    for copy in copies:
+        copy.wait()
+
+
+def half_rows(share):
+    return -(-(share // 2) // 8) * 8
+
+
+def split_kernel(keep, got, kept_ref, sent_ref, buffer):
+    taps, half, chans = keep.shape
+    devices, rows, _ = kept_ref.shape
+    share = taps * chans // devices
+    for t in range(taps):
+        buffer[t * chans : (t + 1) * chans, :] = pair_total(keep, got, t).T
+    second = Place().second
+    for i in range(devices):
+        mine = pl.multiple_of(i * share + (share - rows) * second, 8)
+        other = pl.multiple_of(i * share + (share - rows) * (1 - second), 8)
+        kept_ref[i] = buffer[pl.ds(mine, rows), :]
+        sent_ref[i] = buffer[pl.ds(other, rows), :].astype(BF16)
+
+
+def message_kernel(keep, got0, got1, got2, kept, came, out_far, buffer, out_ref, sems):
+    taps, half, chans = keep.shape
+    devices, rows, _ = kept.shape
+    share = taps * chans // devices
+    for t in range(taps):
+        buffer[t * chans : (t + 1) * chans, :] = pair_total(keep, (got0, got1, got2), t).T
+    copies = []
+    count = sems.shape[0]
+    for part in range(count):
+        mine = pl.ds(part * devices // count, devices // count)
+        for i in range(part * devices // count, (part + 1) * devices // count):
+            first = buffer[i * share : (i + 1) * share, :]
+            out_ref[i] = jnp.concatenate([first, kept[i] + wide(came, i)], axis=0).astype(BF16)
+        copies.append(pltpu.make_async_copy(out_ref.at[mine], out_far.at[mine], sems.at[part]))
         copies[-1].start()
     for copy in copies:
         copy.wait()
@@ -523,12 +571,11 @@
 
 
 def update_kernel(
-    count, parts, w, first, second, st2, st3, params, n_first, n_second,
+    count, parts, w, first_m, second_m, st2, st3, params, n_first, n_second,
     grad_out, w_out, first_out, second_out, n_grad, n_out, n_first_out, n_second_out
 ):
-    devices, rows, lanes = parts.shape
-    lanes //= 2
-    ncols = lax.axis_size("cols")
+    devices, ncols = parts.shape[0], lax.axis_size("cols")
+    share = w.shape[0] // 4
     total2, total3 = total_of(st2), total_of(st3)
     mean, rstd = stats_of(total2, count)
     sum_dn = total2[2:3]
@@ -539,17 +586,30 @@
     n_out[...], n_first_out[...], n_second_out[...] = adamw(
         params[...], grads, n_first[...], n_second[...], 0.75
     )
+    def over(chosen, rows, lanes):
+        total = None
+        for source in range(devices):
+            if chosen(source // ncols):
+                term = wide(parts, source)[rows, lanes]
+                total = term if total is None else total + term
+        return total
+
     grads = []
-    for k in range(2):
-        for half in range(2):
-            grad = None
-            for source in range(devices):
-                if (source // ncols) % 2 == half:
-                    term = wide(parts, source, slice(None), slice(k * lanes, (k + 1) * lanes))
-                    grad = term if grad is None else grad + term
-            grads.append((pl.ds(2 * half + k, rows, stride=4), grad))
-    for at, grad in grads:
-        new = adamw(w[at, :], grad, first[at, :], second[at, :], 0.02)
+    every = slice(None)
+    for half in range(2):
+        if parts.shape[2] == 256:
+            for k in range(2):
+                lanes = slice(k * 128, (k + 1) * 128)
+                grads.append((k, half, over(lambda row: row % 2 == half, every, lanes)))
+        else:
+            rows = half_rows(share)
+            first = over(lambda row: row % 2 == half, slice(0, share), every)
+            upper = over(lambda row: row % 4 == half, slice(share, None), every)
+            lower = over(lambda row: row % 4 == half + 2, slice(2 * rows, None), every)
+            grads += [(0, half, first), (1, half, jnp.concatenate([upper, lower], axis=0))]
+    for k, half, grad in grads:
+        at = pl.ds(2 * half + k, share, stride=4)
+        new = adamw(w[at, :], grad, first_m[at, :], second_m[at, :], 0.02)
         grad_out[at, :] = grad
         w_out[at, :], first_out[at, :], second_out[at, :] = new
 
@@ -702,36 +762,65 @@
         [
             held((n3, chans), F32),
             shape_of((devices, 2, chans), F32),
-            shape_of(features.shape, BF16),
+            held(features.shape, BF16),
         ],
         conv_flops(n3),
         scratch=[pltpu.VMEM((n2, 3 * chans), BF16)],
     )(d, w2, z1, z2, st1, st2, norm_scale_bias, ext)
-    st, got2 = lax.optimization_barrier((st, got2))
-    st3 = exchange(st)
-    e, a, b, keep1, send1 = kernel_call(
+    nrows = lax.axis_size("rows")
+    cut_again = nrows % 4 == 0 and taps // devices % 8 == 0
+    if cut_again:
+        got2, st = lax.optimization_barrier((got2, st))
+        kept_shape = (devices, half_rows(taps // devices), chans // 2)
+        kept, sent = kernel_call(
+            split_kernel,
+            [held(kept_shape, F32), held(kept_shape, BF16)],
+            1e8,
+            scratch=[pltpu.VMEM((taps, chans // 2), F32)],
+        )(keep2, got2)
+        st, kept = lax.optimization_barrier((st, kept))
+        st3 = exchange(st)
+    else:
+        st, got2 = lax.optimization_barrier((st, got2))
+        st3 = exchange(st)
+    cut = held((3, chans // 2, chans), BF16)
+    e, a, b, keep1, *send1 = kernel_call(
         functools.partial(first_gradient_kernel, g, count),
-        [held((n3, chans), BF16), wide_rows(1), wide_rows(1), grad_shape, grad_shape],
-        conv_flops(own_pixels),
+        [held((n3, chans), BF16), wide_rows(1), wide_rows(1), grad_shape, cut, cut, cut],
+        0,
+        size=1024,
         scratch=[pltpu.VMEM((chans, own_pixels), BF16)],
     )(dn1, z1, st1, st3, norm_scale_bias, x)
-    got1 = swapped(send1, "rows", 0)
-    keep2, got2, keep1 = lax.optimization_barrier((keep2, got2, keep1))
-
-    def add_pair(lane, *operands, **options):
-        return kernel_call(
-            functools.partial(pair_sum_kernel, lane),
-            [stored((taps, chans), BF16)],
+    got1 = [swapped(part, "rows", 0) for part in send1]
+    share_rows = taps // devices
+    buffer = pltpu.VMEM((taps, chans // 2), F32)
+    if cut_again:
+        came = lax.ppermute(sent, "rows", [(i, i ^ 2) for i in range(nrows)])
+        rows = share_rows + kept.shape[1]
+        (parts,) = kernel_call(
+            message_kernel,
+            [stored((devices, rows, chans // 2), BF16)],
             1e9,
             far_out=(0,),
-            scratch=[pltpu.VMEM((taps, chans // 2), BF16), dma((9,))],
-            **options,
-        )(*operands)
-
-    (parts,) = add_pair(chans // 2, keep2, got2)
-    (parts,) = add_pair(0, keep1, got1, parts, far=(2,), alias={2: 0})
+            scratch=[buffer, pltpu.VMEM((devices, rows, chans // 2), BF16), dma((4,))],
+        )(keep1, *got1, kept, came)
+    else:
+
+        def add_pair(lane, *operands, **options):
+            return kernel_call(
+                functools.partial(pair_sum_kernel, lane),
+                [stored((taps, chans), BF16)],
+                1e9,
+                far_out=(0,),
+                scratch=[pltpu.VMEM((taps, chans // 2), BF16), dma((9,))],
+                **options,
+            )(*operands)
+
+        (parts,) = add_pair(chans // 2, keep2, got2)
+        (parts,) = add_pair(0, keep1, *got1, parts, far=(4,), alias={4: 0})
+        parts = parts.reshape(devices, share_rows, chans)
     parts, chunked = lax.optimization_barrier((parts, chunked))
-    parts = exchange(parts.reshape(devices, taps // devices, chans))
+    parts = exchange(parts)
     ra, rb = swapped(a, "rows", 0), swapped(b, "rows", 1)
     (grad_input,) = kernel_call(
         functools.partial(input_gradient_kernel, g, 8),

time: 102 us -> 97.3 us (0.954)
  waiting for transfers between devices: 21.4 us -> 14.9 us
  blocking collectives: 29.6 us -> 31.3 us
  Pallas kernels: 26.7 us -> 25.3 us
    all_to_all x1, waiting for transfers between devices: 11.3 us -> 7.91 us  [exchange(): return lax.all_to_all(parts, BOTH, 0, 0, tiled=True)]
    ppermute x8 -> x10, waiting for transfers between devices: 10.1 us -> 6.94 us  [swapped(): return lax.ppermute(block, axis, pairs)]
    all_to_all x3, blocking collectives: 29.6 us -> 31.3 us  [exchange(): return lax.all_to_all(parts, BOTH, 0, 0, tiled=True)]
    pallas_call x13, Pallas kernels: 26.7 us -> 25.3 us  [call(): pl.pallas_call(body, out_shape=out_shape, in_specs=specs, out_specs=[pl.B...]
    ppermute x8 -> x10, starting transfers between devices: 12.7 us -> 13 us  [swapped(): return lax.ppermute(block, axis, pairs)]
  transfers between devices with their start and end apart: 11 -> 14, of which waited for: 4 -> 6; matrix products, arithmetic and copies ran while one was open for 1% -> 2% of each run, Pallas kernels for 13% -> 14%
where the time goes in v3:
time: 97.3 us; the launch traced here: 96.9 us
  blocking collectives  31.3 us (32%)
  Pallas kernels  25.3 us (26%)
  starting transfers between devices  22.8 us (23%)
  waiting for transfers between devices  14.9 us (15%)
  local copies, waits for them, and re-layouts  1.8 us (2%)
    all_to_all x3, blocking collectives, exchange(): return lax.all_to_all(parts, BOTH, 0, 0, tiled=True)  31.3 us
    pallas_call x13, Pallas kernels, call(): pl.pallas_call(body, out_shape=out_shape, in_specs=specs, out_specs=[pl.B...  25.3 us
    ppermute x10, starting transfers between devices, swapped(): return lax.ppermute(block, axis, pairs)  13 us
    all_to_all x1, waiting for transfers between devices, exchange(): return lax.all_to_all(parts, BOTH, 0, 0, tiled=True)  7.91 us
    ppermute x10, waiting for transfers between devices, swapped(): return lax.ppermute(block, axis, pairs)  6.94 us
    ppermute x2, starting transfers between devices, swapped_both(): return lax.ppermute(block, BOTH, pairs)  6.69 us
    all_to_all x1, starting transfers between devices, exchange(): return lax.all_to_all(parts, BOTH, 0, 0, tiled=True)  2.54 us
  transfers between devices with their start and end apart: 14, of which 6 were waited for; matrix products, arithmetic and copies ran while one was open for 2% of the time, Pallas kernels for 14%

profile of v3, /device:TPU:1, one launch (start us, length us, event | category | flops | bytes accessed | tf_op | source)
XLA Modules:
  0.0 96.9 jit_solution(15061235207624450410)
XLA Ops:
  0.6 1.7 %shard_map.168 = (bf16[4,8,40,256]{3,2,1,0:T(8,128)(2,1)S(1)}, bf16[4,48,256]{2,1,0:T(8,128)(2,1)S(1)}, bf16[4,48,256]{2,1,0:T(8,128)(2,1)S(1)}, bf16[4,4,40,256...) custom-call(bf16[4,8,40,256]{3,2,1,0:T(8,128)(2,1)} %features.1, ...), custom_call_target="tpu_custom_call" | custom-call | flops 100000000 | bytes 4194304 | tf_op jit(solution)/shard_map/pallas_call | solution.py:41
  2.4 4.5 %collective-permute-start.2 = (bf16[4,4,40,256]{3,2,1,0:T(8,128)(2,1)S(1)}, bf16[4,4,40,256]{3,2,1,0:T(8,128)(2,1)S(1)}, u32[]{:S(2)}, u32[]{:S(2)}) collective-permute-start(bf16[4,4,40,256]{3,2,1,0:T(8,128)(2,1)S(1)} %get-tuple-element.70), channel_id=1, source_target_pairs={{4,8},{8,4},{12,16},{16,12},{20,24},{24,20},{5,9},{9,5},{13,17},{1... | collective-permute-start | bytes 983048 | tf_op jit(solution)/shard_map/ppermute | solution.py:622
  6.9 1.4 %collective-permute-start = (bf16[4,48,256]{2,1,0:T(8,128)(2,1)S(1)}, bf16[4,48,256]{2,1,0:T(8,128)(2,1)S(1)}, u32[]{:S(2)}, u32[]{:S(2)}) collective-permute-start(bf16[4,48,256]{2,1,0:T(8,128)(2,1)S(1)} %get-tuple-element.66), channel_id=1, source_target_pairs={{0,1},{1,0},{2,3},{3,2},{4,5},{5,4},{6,7},{7,6},{8,9},{9,8},{10,11... | collective-permute-start | bytes 294920 | tf_op jit(solution)/shard_map/ppermute | solution.py:622
  8.2 0.7 collective-permute-start.1
  8.9 6.0 %collective-permute-start.3 = (bf16[4,16,256]{2,1,0:T(8,128)(2,1)S(1)}, bf16[4,16,256]{2,1,0:T(8,128)(2,1)S(1)}, u32[]{:S(2)}, u32[]{:S(2)}) collective-permute-start(bf16[4,16,256]{2,1,0:T(8,128)(2,1)S(1)} %get-tuple-element.71), channel_id=1, source_target_pairs={{4,9},{5,8},{6,11},{7,10},{8,5},{9,4},{10,7},{11,6},{12,17},{13,16... | collective-permute-start | bytes 98312 | tf_op jit(solution)/shard_map/ppermute | solution.py:638
  14.9 0.7 collective-permute-start.4
  15.6 0.0 copy-start.1
  15.6 2.5 %shard_map.170 = (bf16[2304,256]{1,0:T(8,128)(2,1)S(1)}, bf16[2304,256]{1,0:T(8,128)(2,1)S(1)}) custom-call(f32[9216,128]{1,0:T(8,128)} %bitcast.37), custom_call_target="tpu_custom_call" | custom-call | bytes 1024 | tf_op jit(solution)/shard_map/pallas_call | solution.py:41
  18.1 0.0 collective-permute-done.rc
  18.1 0.0 collective-permute-done.1.rd
  18.2 0.2 shard_map.169
  18.4 0.0 collective-permute-done.3.rb_c
  18.4 0.0 collective-permute-done.4.rb_d
  18.4 0.0 collective-permute-done.2.rb
  18.4 0.1 collective-permute-start.5
  18.5 1.6 %shard_map.171 = (f32[2304,256]{1,0:T(8,128)S(1)}, f32[16,256]{1,0:T(8,128)S(1)}, bf16[1920,768]{1,0:T(8,128)(2,1)S(1)}) custom-call(bf16[4,8,48,256]{3,2,1,0:T(8,128)(2,1)S(1)} %get-tuple-element.68.ext, bf16[2304,256]{1,0:T(8,128)(2,1)S(1)} %get-tuple-element.78.w.w_far), custom_call_target="tpu_custom_call" | custom-call | bytes 1024 | tf_op jit(solution)/shard_map/pallas_call | solution.py:41
  20.1 0.1 collective-permute-done.5.ra
  20.2 1.6 %shard_map.172 = (f32[2304,256]{1,0:T(8,128)S(1)}, f32[32,2,256]{2,1,0:T(2,128)S(1)}, bf16[1920,768]{1,0:T(8,128)(2,1)S(1)}, bf16[4,2,48,256]{3,2,1,0:T(8,128)(2,1)S(1)}) custom-call(bf16[4,8,48,256]{3,2,1,0:T(8,128)(2,1)S(1)} %get-tuple-element.68.ext, ...), custom_call_target="tpu_custom_call", output_to_operand_aliasing={{0}: (7, {}), {2}: (8, {})} | custom-call | bytes 1024 | tf_op jit(solution)/shard_map/pallas_call | solution.py:41
  21.8 11.7 %all_to_all.20.st = f32[32,2,256]{2,1,0:T(2,128)S(1)} all-to-all(f32[32,2,256]{2,1,0:T(2,128)S(1)} %get-tuple-element.83), channel_id=1, replica_groups=mesh['rows'=8,'cols'=4] {'rows','cols'}, dimensions={0} | all-to-all | bytes 131072 | tf_op jit(solution)/shard_map/all_to_all | solution.py:650
  33.5 2.7 %shard_map.173 = (bf16[2304,768]{1,0:T(8,128)(2,1)S(1)}, f32[1920,256]{1,0:T(8,128)S(1)}, f32[32,4,256]{2,1,0:T(4,128)S(1)}) custom-call(f32[2304,256]{1,0:T(8,128)S(1)} %get-tuple-element.82.z1.z, f32[32,2,256]{2,1,0:T(2,128)S(1)} %all_to_all.20.st, f32[4,256]{1,0:T(4,128)S(1)} %copy-done.4, bf16[2304,256]{1,0:T(8,128)(2,1)S(1)} %get-tuple-element.84.w, ...), custom_call_target="tpu_custom_call" | custom-call | flops 2264924160 | bytes 4194304 | tf_op jit(solution)/shard_map/pallas_call | solution.py:41
  36.2 9.7 %all_to_all.21.st.st2 = f32[32,4,256]{2,1,0:T(4,128)S(1)} all-to-all(f32[32,4,256]{2,1,0:T(4,128)S(1)} %get-tuple-element.87), channel_id=1, replica_groups=mesh['rows'=8,'cols'=4] {'rows','cols'}, dimensions={0} | all-to-all | bytes 262144 | tf_op jit(solution)/shard_map/all_to_all | solution.py:650
  45.8 2.6 %shard_map.174 = (bf16[1920,256]{1,0:T(8,128)(2,1)S(1)}, f32[9,128,256]{2,1,0:T(8,128)S(1)}, f32[9,128,256]{2,1,0:T(8,128)S(1)}) custom-call(f32[1920,256]{1,0:T(8,128)S(1)} %get-tuple-element.86.z2, f32[32,4,256]{2,1,0:T(4,128)S(1)} %all_to_all.21.st.st2, f32[4,256]{1,0:T(4,128)S(1)} %copy-done.4, bf16[4,8,48,256]{3,2,1,0:T(8,128)(2,1)S(1)} %get-tuple-element.85.cot, ...), custom_call_target="tpu_custom_call" | custom-call | flops 1811939328 | bytes 4194304 | tf_op jit(solution)/shard_map/pallas_call | solution.py:41
  48.5 1.4 %collective-permute-start.6 = (f32[9,128,256]{2,1,0:T(8,128)S(1)}, f32[9,128,256]{2,1,0:T(8,128)S(1)}, u32[]{:S(2)}, u32[]{:S(2)}) collective-permute-start(f32[9,128,256]{2,1,0:T(8,128)S(1)} %get-tuple-element.93), channel_id=1, source_target_pairs={{0,4},{4,0},{8,12},{12,8},{16,20},{20,16},{24,28},{28,24},{1,5},{5... | collective-permute-start | bytes 3538952 | tf_op jit(solution)/shard_map/ppermute | solution.py:622
  49.9 2.5 %shard_map.175 = (f32[1536,256]{1,0:T(8,128)S(1)}, f32[32,2,256]{2,1,0:T(2,128)S(1)}, bf16[4,8,40,256]{3,2,1,0:T(8,128)(2,1)S(1)}) custom-call(bf16[1920,256]{1,0:T(8,128)(2,1)S(1)} %get-tuple-element.90.d, bf16[2304,256]{1,0:T(8,128)(2,1)S(1)} %get-tuple-element.84.w, f32[2304,256]{1,0:T(8,128)S(1)} %get-tuple-element.82.z1.z, ...), custom_call_target="tpu_custom_call" | custom-call | flops 1811939328 | bytes 4194304 | tf_op jit(solution)/shard_map/pallas_call | solution.py:41
  52.3 0.0 collective-permute-done.6.got
  52.4 0.6 shard_map.176
  53.0 0.6 collective-permute-start.12
  53.5 9.9 %all_to_all.22.st3 = f32[32,2,256]{2,1,0:T(2,128)S(1)} all-to-all(f32[32,2,256]{2,1,0:T(2,128)S(1)} %get-tuple-element.99), channel_id=1, replica_groups=mesh['rows'=8,'cols'=4] {'rows','cols'}, dimensions={0} | all-to-all | bytes 131072 | tf_op jit(solution)/shard_map/all_to_all | solution.py:650
  63.5 2.5 %shard_map.177 = (bf16[1536,256]{1,0:T(8,128)(2,1)S(1)}, bf16[4,1,48,256]{3,2,1,0:T(8,128)(2,1)S(1)}, bf16[4,1,48,256]{3,2,1,0:T(8,128)(2,1)S(1)}, f32[9,128,256...) custom-call(f32[1536,256]{1,0:T(8,128)S(1)} %get-tuple-element.92.dn, ...), custom_call_target="tpu_custom_call" | custom-call | bytes 1024 | tf_op jit(solution)/shard_map/pallas_call | solution.py:41
  66.0 0.7 collective-permute-start.10
  66.7 0.1 collective-permute-start.11
  66.8 0.4 collective-permute-start.9
  67.2 0.6 collective-permute-done.10.got1
  67.7 0.4 collective-permute-done.11.got2
  68.1 0.3 collective-permute-done.9.got0
  68.4 0.0 collective-permute-done.12.came
  68.4 1.1 %shard_map.179 = bf16[32,112,128]{2,1,0:T(8,128)(2,1)} custom-call(f32[9,128,256]{2,1,0:T(8,128)S(1)} %get-tuple-element.104.keep, bf16[3,128,256]{2,1,0:T(8,128)(2,1)S(1)} %collective-permute-done.9.got0, bf16[3,128,256]{2,1,0:T(8,128)(2,1)S(1)} %collective-permute-done.10.got1, bf16[3,128,256]{2,1,0:T(8,128)(2,1)S(1)} %collective-permute-done.11.got2, ...), custom_call_target="tpu_custom_call" | custom-call | flops 1000000000 | bytes 4194304 | tf_op jit(solution)/shard_map/pallas_call | solution.py:41
  69.5 0.0 copy-start.5
  69.5 2.5 %all-to-all-start.3 = ((bf16[32,112,128]{2,1,0:T(8,128)(2,1)}), bf16[32,112,128]{2,1,0:T(8,128)(2,1)S(1)}, u32[]{:S(2)}, u32[]{:S(2)}) async-start(bf16[32,112,128]{2,1,0:T(8,128)(2,1)} %shard_map.179), calls=%async_computation.3 | async-start | bytes 1835008 | tf_op jit(solution)/shard_map/all_to_all | solution.py:650
  72.0 0.5 collective-permute-start.7
  72.5 3.3 %collective-permute-start.8 = (bf16[4,1,48,256]{3,2,1,0:T(8,128)(2,1)S(1)}, bf16[4,1,48,256]{3,2,1,0:T(8,128)(2,1)S(1)}, u32[]{:S(2)}, u32[]{:S(2)}) collective-permute-start(bf16[4,1,48,256]{3,2,1,0:T(8,128)(2,1)S(1)} %get-tuple-element.103), channel_id=1, source_target_pairs={{4,8},{8,4},{12,16},{16,12},{20,24},{24,20},{5,9},{9,5},{13,17},{1... | collective-permute-start | bytes 294920 | tf_op jit(solution)/shard_map/ppermute | solution.py:622
  75.8 0.8 copy.30
  76.7 5.6 %collective-permute-done.8.rb = bf16[4,1,48,256]{3,2,1,0:T(8,128)(2,1)S(1)} collective-permute-done((bf16[4,1,48,256]{3,2,1,0:T(8,128)(2,1)S(1)}, bf16[4,1,48,256]{3,2,1,0:T(8,128)(2,1)S(1)}, u32[]{:S(2)}, u32[]{:S(2)}) %collective-permute-start.8) | collective-permute-done | bytes 98336 | tf_op jit(solution)/shard_map/ppermute | solution.py:622
  82.3 0.0 copy-start.7
  82.3 4.7 %shard_map.178 = f32[4,8,40,256]{3,2,1,0:T(8,128)} custom-call(bf16[1536,256]{1,0:T(8,128)(2,1)S(1)} %get-tuple-element.101.e, bf16[4,1,48,256]{3,2,1,0:T(8,128)(2,1)S(1)} %collective-permute-done.7.ra, bf16[4,1,48,256]{3,2,1,0:T(8,128)(2,1)S(1)} %collective-permute-done.8.rb, bf16[2304,256]{1,0:T(8,128)(2,1)} %copy-done, bf16[4,8,40,256]{3,2,1,0:T(8,128)(2,1)} %cot_far.1, ...), custom_call_target="tpu_custom_call" | custom-call | flops 1811939328 | bytes 4194304 | tf_op jit(solution)/shard_map/pallas_call | solution.py:41
  86.9 0.9 constant_dynamic-slice_fusion.w
  87.9 7.9 %all-to-all-done.3.parts = bf16[32,112,128]{2,1,0:T(8,128)(2,1)S(1)} async-done(((bf16[32,112,128]{2,1,0:T(8,128)(2,1)}), bf16[32,112,128]{2,1,0:T(8,128)(2,1)S(1)}, u32[]{:S(2)}, u32[]{:S(2)}) %all-to-all-start.3) | async-done | bytes 917536 | tf_op jit(solution)/shard_map/all_to_all | solution.py:650
  95.8 1.1 %shard_map.180 = (f32[288,128]{1,0:T(8,128)}, f32[288,128]{1,0:T(8,128)}, f32[288,128]{1,0:T(8,128)}, f32[288,128]{1,0:T(8,128)}, f32[4,256]{1,0:T(4,128)}, /*in...) custom-call(bf16[32,112,128]{2,1,0:T(8,128)(2,1)S(1)} %all-to-all-done.3.parts, ...), custom_call_target="tpu_custom_call" | custom-call | flops 100000000 | bytes 4194304 | tf_op jit(solution)/shard_map/pallas_call | solution.py:41
  (14 shorter events, 0.0 us)
Async XLA Ops:
  2.4 16.0 %collective-permute-start.2 = (bf16[4,4,40,256]{3,2,1,0:T(8,128)(2,1)S(1)}, bf16[4,4,40,256]{3,2,1,0:T(8,128)(2,1)S(1)}, u32[]{:S(2)}, u32[]{:S(2)}) collective-permute-start(bf16[4,4,40,256]{3,2,1,0:T(8,128)(2,1)S(1)} %get-tuple-element.70), channel_id=1, source_target_pairs={{4,8},{8,4},{12,16},{16,12},{20,24},{24,20},{5,9},{9,5},{13,17},{1... | collective-permute-start | bytes 983048 | tf_op jit(solution)/shard_map/ppermute | solution.py:622
  6.9 11.3 %collective-permute-start = (bf16[4,48,256]{2,1,0:T(8,128)(2,1)S(1)}, bf16[4,48,256]{2,1,0:T(8,128)(2,1)S(1)}, u32[]{:S(2)}, u32[]{:S(2)}) collective-permute-start(bf16[4,48,256]{2,1,0:T(8,128)(2,1)S(1)} %get-tuple-element.66), channel_id=1, source_target_pairs={{0,1},{1,0},{2,3},{3,2},{4,5},{5,4},{6,7},{7,6},{8,9},{9,8},{10,11... | collective-permute-start | bytes 294920 | tf_op jit(solution)/shard_map/ppermute | solution.py:622
  8.2 9.9 %collective-permute-start.1 = (bf16[4,48,256]{2,1,0:T(8,128)(2,1)S(1)}, bf16[4,48,256]{2,1,0:T(8,128)(2,1)S(1)}, u32[]{:S(2)}, u32[]{:S(2)}) collective-permute-start(bf16[4,48,256]{2,1,0:T(8,128)(2,1)S(1)} %get-tuple-element.67), channel_id=1, source_target_pairs={{1,2},{2,1},{5,6},{6,5},{9,10},{10,9},{13,14},{14,13},{17,18},{18,... | collective-permute-start | bytes 294920 | tf_op jit(solution)/shard_map/ppermute | solution.py:622
  8.9 9.5 %collective-permute-start.3 = (bf16[4,16,256]{2,1,0:T(8,128)(2,1)S(1)}, bf16[4,16,256]{2,1,0:T(8,128)(2,1)S(1)}, u32[]{:S(2)}, u32[]{:S(2)}) collective-permute-start(bf16[4,16,256]{2,1,0:T(8,128)(2,1)S(1)} %get-tuple-element.71), channel_id=1, source_target_pairs={{4,9},{5,8},{6,11},{7,10},{8,5},{9,4},{10,7},{11,6},{12,17},{13,16... | collective-permute-start | bytes 98312 | tf_op jit(solution)/shard_map/ppermute | solution.py:638
  14.9 3.4 %collective-permute-start.4 = (bf16[4,16,256]{2,1,0:T(8,128)(2,1)S(1)}, bf16[4,16,256]{2,1,0:T(8,128)(2,1)S(1)}, u32[]{:S(2)}, u32[]{:S(2)}) collective-permute-start(bf16[4,16,256]{2,1,0:T(8,128)(2,1)S(1)} %get-tuple-element.72), channel_id=1, source_target_pairs={{5,10},{6,9},{9,6},{10,5},{13,18},{14,17},{17,14},{18,13},{21,26},... | collective-permute-start | bytes 98312 | tf_op jit(solution)/shard_map/ppermute | solution.py:638
  15.6 2.5 %copy-start.1 = (bf16[4,8,40,256]{3,2,1,0:T(8,128)(2,1)S(1)}, bf16[4,8,40,256]{3,2,1,0:T(8,128)(2,1)}, u32[]{:S(2)}) copy-start(bf16[4,8,40,256]{3,2,1,0:T(8,128)(2,1)} %cot_far.1) | copy-start | bytes 1966084
  18.1 3.7 %copy-start = (bf16[2304,256]{1,0:T(8,128)(2,1)}, bf16[2304,256]{1,0:T(8,128)(2,1)S(1)}, u32[]{:S(2)}) copy-start(bf16[2304,256]{1,0:T(8,128)(2,1)S(1)} %get-tuple-element.78.w.w_far) | copy-start | bytes 3538948
  18.4 1.8 %collective-permute-start.5 = (bf16[4,4,48,256]{3,2,1,0:T(8,128)(2,1)S(1)}, bf16[4,4,48,256]{3,2,1,0:T(8,128)(2,1)S(1)}, u32[]{:S(2)}, u32[]{:S(2)}) collective-permute-start(bf16[4,4,48,256]{3,2,1,0:T(8,128)(2,1)S(1)} %get-tuple-element.74), channel_id=1, source_target_pairs={{0,4},{4,0},{8,12},{12,8},{16,20},{20,16},{24,28},{28,24},{1,5},{5... | collective-permute-start | bytes 1179656 | tf_op jit(solution)/shard_map/ppermute | solution.py:622
  20.2 13.3 %copy-start.4 = (f32[4,256]{1,0:T(4,128)S(1)}, f32[4,256]{1,0:T(4,128)}, u32[]{:S(2)}) copy-start(f32[4,256]{1,0:T(4,128)} %params.9) | copy-start | bytes 12292
  48.5 3.9 %collective-permute-start.6 = (f32[9,128,256]{2,1,0:T(8,128)S(1)}, f32[9,128,256]{2,1,0:T(8,128)S(1)}, u32[]{:S(2)}, u32[]{:S(2)}) collective-permute-start(f32[9,128,256]{2,1,0:T(8,128)S(1)} %get-tuple-element.93), channel_id=1, source_target_pairs={{0,4},{4,0},{8,12},{12,8},{16,20},{20,16},{24,28},{28,24},{1,5},{5... | collective-permute-start | bytes 3538952 | tf_op jit(solution)/shard_map/ppermute | solution.py:622
  53.0 15.4 %collective-permute-start.12 = (bf16[32,40,128]{2,1,0:T(8,128)(2,1)S(1)}, bf16[32,40,128]{2,1,0:T(8,128)(2,1)S(1)}, u32[]{:S(2)}, u32[]{:S(2)}) collective-permute-start(bf16[32,40,128]{2,1,0:T(8,128)(2,1)S(1)} %get-tuple-element.109), channel_id=1, source_target_pairs={{0,8},{4,12},{8,0},{12,4},{16,24},{20,28},{24,16},{28,20},{1,9},{5... | collective-permute-start | bytes 983048 | tf_op jit(solution)/shard_map/ppermute | solution.py:798
  66.0 1.8 %collective-permute-start.10 = (bf16[3,128,256]{2,1,0:T(8,128)(2,1)S(1)}, bf16[3,128,256]{2,1,0:T(8,128)(2,1)S(1)}, u32[]{:S(2)}, u32[]{:S(2)}) collective-permute-start(bf16[3,128,256]{2,1,0:T(8,128)(2,1)S(1)} %get-tuple-element.106), channel_id=1, source_target_pairs={{0,4},{4,0},{8,12},{12,8},{16,20},{20,16},{24,28},{28,24},{1,5},{5... | collective-permute-start | bytes 589832 | tf_op jit(solution)/shard_map/ppermute | solution.py:622
  66.7 1.4 %collective-permute-start.11 = (bf16[3,128,256]{2,1,0:T(8,128)(2,1)S(1)}, bf16[3,128,256]{2,1,0:T(8,128)(2,1)S(1)}, u32[]{:S(2)}, u32[]{:S(2)}) collective-permute-start(bf16[3,128,256]{2,1,0:T(8,128)(2,1)S(1)} %get-tuple-element.107), channel_id=1, source_target_pairs={{0,4},{4,0},{8,12},{12,8},{16,20},{20,16},{24,28},{28,24},{1,5},{5... | collective-permute-start | bytes 589832 | tf_op jit(solution)/shard_map/ppermute | solution.py:622
  66.8 1.6 %collective-permute-start.9 = (bf16[3,128,256]{2,1,0:T(8,128)(2,1)S(1)}, bf16[3,128,256]{2,1,0:T(8,128)(2,1)S(1)}, u32[]{:S(2)}, u32[]{:S(2)}) collective-permute-start(bf16[3,128,256]{2,1,0:T(8,128)(2,1)S(1)} %get-tuple-element.105), channel_id=1, source_target_pairs={{0,4},{4,0},{8,12},{12,8},{16,20},{20,16},{24,28},{28,24},{1,5},{5... | collective-permute-start | bytes 589832 | tf_op jit(solution)/shard_map/ppermute | solution.py:622
  69.5 12.7 %copy-start.5 = (s32[4,8,40]{2,1,0:T(8,128)S(1)}, s32[4,8,40]{2,1,0:T(8,128)}, u32[]{:S(2)}) copy-start(s32[4,8,40]{2,1,0:T(8,128)} %occ.1) | copy-start | bytes 15364
  69.5 26.3 %all-to-all-start.3 = ((bf16[32,112,128]{2,1,0:T(8,128)(2,1)}), bf16[32,112,128]{2,1,0:T(8,128)(2,1)S(1)}, u32[]{:S(2)}, u32[]{:S(2)}) async-start(bf16[32,112,128]{2,1,0:T(8,128)(2,1)} %shard_map.179), calls=%async_computation.3 | async-start | bytes 1835008 | tf_op jit(solution)/shard_map/all_to_all | solution.py:650
  72.0 4.6 %collective-permute-start.7 = (bf16[4,1,48,256]{3,2,1,0:T(8,128)(2,1)S(1)}, bf16[4,1,48,256]{3,2,1,0:T(8,128)(2,1)S(1)}, u32[]{:S(2)}, u32[]{:S(2)}) collective-permute-start(bf16[4,1,48,256]{3,2,1,0:T(8,128)(2,1)S(1)} %get-tuple-element.102), channel_id=1, source_target_pairs={{0,4},{4,0},{8,12},{12,8},{16,20},{20,16},{24,28},{28,24},{1,5},{5... | collective-permute-start | bytes 294920 | tf_op jit(solution)/shard_map/ppermute | solution.py:622
  72.5 9.7 %collective-permute-start.8 = (bf16[4,1,48,256]{3,2,1,0:T(8,128)(2,1)S(1)}, bf16[4,1,48,256]{3,2,1,0:T(8,128)(2,1)S(1)}, u32[]{:S(2)}, u32[]{:S(2)}) collective-permute-start(bf16[4,1,48,256]{3,2,1,0:T(8,128)(2,1)S(1)} %get-tuple-element.103), channel_id=1, source_target_pairs={{4,8},{8,4},{12,16},{16,12},{20,24},{24,20},{5,9},{9,5},{13,17},{1... | collective-permute-start | bytes 294920 | tf_op jit(solution)/shard_map/ppermute | solution.py:622
  82.2 13.5 %copy-start.2 = (f32[2,18432]{1,0:T(2,128)S(1)}, f32[2,18432]{1,0:T(2,128)}, u32[]{:S(2)}) copy-start(f32[2,18432]{1,0:T(2,128)} %param.13) | copy-start | bytes 442372
  82.2 13.5 %copy-start.3 = (f32[2,18432]{1,0:T(2,128)S(1)}, f32[2,18432]{1,0:T(2,128)}, u32[]{:S(2)}) copy-start(f32[2,18432]{1,0:T(2,128)} %param.14) | copy-start | bytes 442372
  82.2 13.5 %copy-start.6 = (f32[4,256]{1,0:T(4,128)S(1)}, f32[4,256]{1,0:T(4,128)}, u32[]{:S(2)}) copy-start(f32[4,256]{1,0:T(4,128)} %n_first.1) | copy-start | bytes 12292
  82.3 13.5 %copy-start.7 = (f32[4,256]{1,0:T(4,128)S(1)}, f32[4,256]{1,0:T(4,128)}, u32[]{:S(2)}) copy-start(f32[4,256]{1,0:T(4,128)} %n_second.1) | copy-start | bytes 12292

commit v4 on v3

--- a/solution.py
+++ b/solution.py
@@ -356,22 +356,36 @@
     dt_ref[:, s * span : (s + 1) * span] = jnp.where(inside, block, jnp.zeros_like(block)).T
 
 
-def kernel_gradient(g, core, field, rows_field, first_row, dt_ref, keep, send):
+def kernel_gradient(g, core, field, rows_field, first_row, dt_ref, keep, send, first, prepare):
     chans, half = g.c, g.c // 2
     span = g.h * g.wp
     mine = pl.ds(pl.multiple_of(core * half, half), half)
     other = pl.ds(pl.multiple_of((1 - core) * half, half), half)
-    lhs = jnp.concatenate([dt_ref[mine, :], dt_ref[other, :]], axis=0)
-    for a in range(3):
-        starts = [(s * rows_field + first_row + a) * g.wp for s in range(g.s)]
-        acc = dot(lhs, jnp.concatenate([field[at : at + span, :] for at in starts], axis=0))
-        for b in range(3):
-            keep[a * 3 + b] = acc[0:half, b * chans : (b + 1) * chans]
-            other_half = acc[half:, b * chans : (b + 1) * chans]
-            if isinstance(send, tuple):
-                send[a][b] = other_half.astype(BF16)
-            else:
-                send[a * 3 + b] = other_half
+    totals = [None] * 3
+    cut = g.s // 2
+    groups = (range(cut), range(cut, g.s))
+    for s in groups[0]:
+        prepare(s)
+    for group in groups:
+        lanes = slice(group[0] * span, (group[-1] + 1) * span)
+        lhs = jnp.concatenate([dt_ref[mine, lanes], dt_ref[other, lanes]], axis=0)
+        for a in range(3):
+            starts = [(s * rows_field + first_row + a) * g.wp for s in group]
+            acc = dot(lhs, jnp.concatenate([field[at : at + span, :] for at in starts], axis=0))
+            if group[0] == 0 and a < len(groups[1]):
+                prepare(groups[1][a])
+            if group[0] == 0:
+                for b in range(3):
+                    keep[a * 3 + b] = acc[0:half, b * chans : (b + 1) * chans]
+                    first[a * 3 + b] = acc[half:, b * chans : (b + 1) * chans]
+                continue
+            for b in range(3):
+                keep[a * 3 + b] += acc[0:half, b * chans : (b + 1) * chans]
+                other_half = first[a * 3 + b] + acc[half:, b * chans : (b + 1) * chans]
+                if isinstance(send, tuple):
+                    send[a][b] = other_half.astype(BF16)
+                else:
+                    send[a * 3 + b] = other_half
 
 
 def second_gradient_kernel(
@@ -387,7 +401,7 @@
     k1 = k0 * (sum_dn / count)
     k2 = k0 * rstd * (sum_dx / count)
     edge = edge_mask(place, g)
-    for s in range(g.s):
+    def prepare(s):
         for i in range(rows):
             rim = not g.near <= i < g.near + g.h
             dn = wide(cot_next, s, 0 if i < g.near else 1) if rim else wide(cot, s, i - g.near)
@@ -396,7 +410,7 @@
             d = in_grid(d, i + RIM - g.near, g, place, edge)
             d_ref[start : start + g.wp, :] = d.astype(BF16)
         own_transposed(g, d_ref, (s * rows + g.near) * g.wp, s, dt_ref)
-    kernel_gradient(g, place.core, h, g.tall - 2, RIM - 2, dt_ref, keep, send)
+    kernel_gradient(g, place.core, h, g.tall - 2, RIM - 2, dt_ref, keep, send, send, prepare)
 
 
 def transposed_conv(g, d_ref, w, s, rows_in, r, chunk):
@@ -449,7 +463,7 @@
 
 
 def first_gradient_kernel(
-    g, count, dn, z, st, st3, params, x, e_ref, a_ref, b_ref, keep, send0, send1, send2, dt_ref
+    g, count, dn, z, st, st3, params, x, e_ref, a_ref, b_ref, keep, send0, send1, send2, dt_ref, first
 ):
     place = Place()
     mean, rstd = stats_of(total_of(st), count)
@@ -458,7 +472,8 @@
     k1 = k0 * (total[0:1] / count)
     k2 = k0 * rstd * (total[1:2] / count)
     edge = edge_mask(place, g)
-    for s in range(g.s):
+
+    def prepare(s):
         for i in range(g.h):
             at = (s * g.h + i) * g.wp
             z_at = (s * (g.tall - 2) + i + RIM - 1) * g.wp
@@ -470,7 +485,8 @@
         a_ref[s, 0] = jnp.where(place.odd_row, top, d).astype(BF16)
         b_ref[s, 0] = jnp.where(place.odd_row, d, top).astype(BF16)
         own_transposed(g, e_ref, s * g.h * g.wp, s, dt_ref)
-    kernel_gradient(g, place.core, x, g.h + 2, 0, dt_ref, keep, (send0, send1, send2))
+    send = (send0, send1, send2)
+    kernel_gradient(g, place.core, x, g.h + 2, 0, dt_ref, keep, send, first, prepare)
 
 
 def input_gradient_kernel(
@@ -789,7 +805,7 @@
         [held((n3, chans), BF16), wide_rows(1), wide_rows(1), grad_shape, cut, cut, cut],
         0,
         size=1024,
-        scratch=[pltpu.VMEM((chans, own_pixels), BF16)],
+        scratch=[pltpu.VMEM((chans, own_pixels), BF16), pltpu.VMEM(grad_shape.shape, F32)],
     )(dn1, z1, st1, st3, norm_scale_bias, x)
     got1 = [swapped(part, "rows", 0) for part in send1]
     share_rows = taps // devices

time: 97.3 us -> 96.9 us (level)
  no operation moved by 1% of the time
where the time goes in v4:
time: 96.9 us; the launch traced here: 96.5 us
  blocking collectives  31.3 us (32%)
  Pallas kernels  24.9 us (26%)
  starting transfers between devices  22.7 us (23%)
  waiting for transfers between devices  14.9 us (15%)
  local copies, waits for them, and re-layouts  1.8 us (2%)
    all_to_all x3, blocking collectives, exchange(): return lax.all_to_all(parts, BOTH, 0, 0, tiled=True)  31.3 us
    pallas_call x13, Pallas kernels, call(): pl.pallas_call(body, out_shape=out_shape, in_specs=specs, out_specs=[pl.B...  24.9 us
    ppermute x10, starting transfers between devices, swapped(): return lax.ppermute(block, axis, pairs)  13 us
    all_to_all x1, waiting for transfers between devices, exchange(): return lax.all_to_all(parts, BOTH, 0, 0, tiled=True)  7.9 us
    ppermute x10, waiting for transfers between devices, swapped(): return lax.ppermute(block, axis, pairs)  6.96 us
    ppermute x2, starting transfers between devices, swapped_both(): return lax.ppermute(block, BOTH, pairs)  6.69 us
    all_to_all x1, starting transfers between devices, exchange(): return lax.all_to_all(parts, BOTH, 0, 0, tiled=True)  2.54 us
  transfers between devices with their start and end apart: 14, of which 6 were waited for; matrix products, arithmetic and copies ran while one was open for 2% of the time, Pallas kernels for 14%

profile of v4, /device:TPU:1, one launch (start us, length us, event | category | flops | bytes accessed | tf_op | source)
XLA Modules:
  0.0 96.5 jit_solution(6892149753717572279)
XLA Ops:
  0.6 1.7 %shard_map.168 = (bf16[4,8,40,256]{3,2,1,0:T(8,128)(2,1)S(1)}, bf16[4,48,256]{2,1,0:T(8,128)(2,1)S(1)}, bf16[4,48,256]{2,1,0:T(8,128)(2,1)S(1)}, bf16[4,4,40,256...) custom-call(bf16[4,8,40,256]{3,2,1,0:T(8,128)(2,1)} %features.1, ...), custom_call_target="tpu_custom_call" | custom-call | flops 100000000 | bytes 4194304 | tf_op jit(solution)/shard_map/pallas_call | solution.py:41
  2.4 4.5 %collective-permute-start.2 = (bf16[4,4,40,256]{3,2,1,0:T(8,128)(2,1)S(1)}, bf16[4,4,40,256]{3,2,1,0:T(8,128)(2,1)S(1)}, u32[]{:S(2)}, u32[]{:S(2)}) collective-permute-start(bf16[4,4,40,256]{3,2,1,0:T(8,128)(2,1)S(1)} %get-tuple-element.70), channel_id=1, source_target_pairs={{4,8},{8,4},{12,16},{16,12},{20,24},{24,20},{5,9},{9,5},{13,17},{1... | collective-permute-start | bytes 983048 | tf_op jit(solution)/shard_map/ppermute | solution.py:638
  6.9 1.4 %collective-permute-start = (bf16[4,48,256]{2,1,0:T(8,128)(2,1)S(1)}, bf16[4,48,256]{2,1,0:T(8,128)(2,1)S(1)}, u32[]{:S(2)}, u32[]{:S(2)}) collective-permute-start(bf16[4,48,256]{2,1,0:T(8,128)(2,1)S(1)} %get-tuple-element.66), channel_id=1, source_target_pairs={{0,1},{1,0},{2,3},{3,2},{4,5},{5,4},{6,7},{7,6},{8,9},{9,8},{10,11... | collective-permute-start | bytes 294920 | tf_op jit(solution)/shard_map/ppermute | solution.py:638
  8.2 0.7 collective-permute-start.1
  8.9 6.0 %collective-permute-start.3 = (bf16[4,16,256]{2,1,0:T(8,128)(2,1)S(1)}, bf16[4,16,256]{2,1,0:T(8,128)(2,1)S(1)}, u32[]{:S(2)}, u32[]{:S(2)}) collective-permute-start(bf16[4,16,256]{2,1,0:T(8,128)(2,1)S(1)} %get-tuple-element.71), channel_id=1, source_target_pairs={{4,9},{5,8},{6,11},{7,10},{8,5},{9,4},{10,7},{11,6},{12,17},{13,16... | collective-permute-start | bytes 98312 | tf_op jit(solution)/shard_map/ppermute | solution.py:654
  14.9 0.7 collective-permute-start.4
  15.6 0.0 copy-start.1
  15.6 2.5 %shard_map.170 = (bf16[2304,256]{1,0:T(8,128)(2,1)S(1)}, bf16[2304,256]{1,0:T(8,128)(2,1)S(1)}) custom-call(f32[9216,128]{1,0:T(8,128)} %bitcast.37), custom_call_target="tpu_custom_call" | custom-call | bytes 1024 | tf_op jit(solution)/shard_map/pallas_call | solution.py:41
  18.1 0.0 collective-permute-done.rc
  18.1 0.0 collective-permute-done.1.rd
  18.2 0.2 shard_map.169
  18.4 0.0 collective-permute-done.3.rb_c
  18.4 0.0 collective-permute-done.4.rb_d
  18.4 0.0 collective-permute-done.2.rb
  18.4 0.1 collective-permute-start.5
  18.5 1.6 %shard_map.171 = (f32[2304,256]{1,0:T(8,128)S(1)}, f32[16,256]{1,0:T(8,128)S(1)}, bf16[1920,768]{1,0:T(8,128)(2,1)S(1)}) custom-call(bf16[4,8,48,256]{3,2,1,0:T(8,128)(2,1)S(1)} %get-tuple-element.68.ext, bf16[2304,256]{1,0:T(8,128)(2,1)S(1)} %get-tuple-element.78.w.w_far), custom_call_target="tpu_custom_call" | custom-call | bytes 1024 | tf_op jit(solution)/shard_map/pallas_call | solution.py:41
  20.1 0.1 collective-permute-done.5.ra
  20.2 1.6 %shard_map.172 = (f32[2304,256]{1,0:T(8,128)S(1)}, f32[32,2,256]{2,1,0:T(2,128)S(1)}, bf16[1920,768]{1,0:T(8,128)(2,1)S(1)}, bf16[4,2,48,256]{3,2,1,0:T(8,128)(2,1)S(1)}) custom-call(bf16[4,8,48,256]{3,2,1,0:T(8,128)(2,1)S(1)} %get-tuple-element.68.ext, ...), custom_call_target="tpu_custom_call", output_to_operand_aliasing={{0}: (7, {}), {2}: (8, {})} | custom-call | bytes 1024 | tf_op jit(solution)/shard_map/pallas_call | solution.py:41
  21.8 11.7 %all_to_all.20.st = f32[32,2,256]{2,1,0:T(2,128)S(1)} all-to-all(f32[32,2,256]{2,1,0:T(2,128)S(1)} %get-tuple-element.83), channel_id=1, replica_groups=mesh['rows'=8,'cols'=4] {'rows','cols'}, dimensions={0} | all-to-all | bytes 131072 | tf_op jit(solution)/shard_map/all_to_all | solution.py:666
  33.5 2.7 %shard_map.173 = (bf16[2304,768]{1,0:T(8,128)(2,1)S(1)}, f32[1920,256]{1,0:T(8,128)S(1)}, f32[32,4,256]{2,1,0:T(4,128)S(1)}) custom-call(f32[2304,256]{1,0:T(8,128)S(1)} %get-tuple-element.82.z1.z, f32[32,2,256]{2,1,0:T(2,128)S(1)} %all_to_all.20.st, f32[4,256]{1,0:T(4,128)S(1)} %copy-done.4, bf16[2304,256]{1,0:T(8,128)(2,1)S(1)} %get-tuple-element.84.w, ...), custom_call_target="tpu_custom_call" | custom-call | flops 2264924160 | bytes 4194304 | tf_op jit(solution)/shard_map/pallas_call | solution.py:41
  36.2 9.7 %all_to_all.21.st.st2 = f32[32,4,256]{2,1,0:T(4,128)S(1)} all-to-all(f32[32,4,256]{2,1,0:T(4,128)S(1)} %get-tuple-element.87), channel_id=1, replica_groups=mesh['rows'=8,'cols'=4] {'rows','cols'}, dimensions={0} | all-to-all | bytes 262144 | tf_op jit(solution)/shard_map/all_to_all | solution.py:666
  45.8 2.4 %shard_map.174 = (bf16[1920,256]{1,0:T(8,128)(2,1)S(1)}, f32[9,128,256]{2,1,0:T(8,128)S(1)}, f32[9,128,256]{2,1,0:T(8,128)S(1)}) custom-call(f32[1920,256]{1,0:T(8,128)S(1)} %get-tuple-element.86.z2, f32[32,4,256]{2,1,0:T(4,128)S(1)} %all_to_all.21.st.st2, f32[4,256]{1,0:T(4,128)S(1)} %copy-done.4, bf16[4,8,48,256]{3,2,1,0:T(8,128)(2,1)S(1)} %get-tuple-element.85.cot, ...), custom_call_target="tpu_custom_call" | custom-call | flops 1811939328 | bytes 4194304 | tf_op jit(solution)/shard_map/pallas_call | solution.py:41
  48.3 1.4 %collective-permute-start.6 = (f32[9,128,256]{2,1,0:T(8,128)S(1)}, f32[9,128,256]{2,1,0:T(8,128)S(1)}, u32[]{:S(2)}, u32[]{:S(2)}) collective-permute-start(f32[9,128,256]{2,1,0:T(8,128)S(1)} %get-tuple-element.93), channel_id=1, source_target_pairs={{0,4},{4,0},{8,12},{12,8},{16,20},{20,16},{24,28},{28,24},{1,5},{5... | collective-permute-start | bytes 3538952 | tf_op jit(solution)/shard_map/ppermute | solution.py:638
  49.7 2.4 %shard_map.175 = (f32[1536,256]{1,0:T(8,128)S(1)}, f32[32,2,256]{2,1,0:T(2,128)S(1)}, bf16[4,8,40,256]{3,2,1,0:T(8,128)(2,1)S(1)}) custom-call(bf16[1920,256]{1,0:T(8,128)(2,1)S(1)} %get-tuple-element.90.d, bf16[2304,256]{1,0:T(8,128)(2,1)S(1)} %get-tuple-element.84.w, f32[2304,256]{1,0:T(8,128)S(1)} %get-tuple-element.82.z1.z, ...), custom_call_target="tpu_custom_call" | custom-call | flops 1811939328 | bytes 4194304 | tf_op jit(solution)/shard_map/pallas_call | solution.py:41
  52.2 0.0 collective-permute-done.6.got
  52.2 0.6 shard_map.176
  52.8 0.6 collective-permute-start.12
  53.4 9.9 %all_to_all.22.st3 = f32[32,2,256]{2,1,0:T(2,128)S(1)} all-to-all(f32[32,2,256]{2,1,0:T(2,128)S(1)} %get-tuple-element.99), channel_id=1, replica_groups=mesh['rows'=8,'cols'=4] {'rows','cols'}, dimensions={0} | all-to-all | bytes 131072 | tf_op jit(solution)/shard_map/all_to_all | solution.py:666
  63.3 2.3 %shard_map.177 = (bf16[1536,256]{1,0:T(8,128)(2,1)S(1)}, bf16[4,1,48,256]{3,2,1,0:T(8,128)(2,1)S(1)}, bf16[4,1,48,256]{3,2,1,0:T(8,128)(2,1)S(1)}, f32[9,128,256...) custom-call(f32[1536,256]{1,0:T(8,128)S(1)} %get-tuple-element.92.dn, ...), custom_call_target="tpu_custom_call" | custom-call | bytes 1024 | tf_op jit(solution)/shard_map/pallas_call | solution.py:41
  65.6 0.7 collective-permute-start.10
  66.3 0.1 collective-permute-start.11
  66.4 0.4 collective-permute-start.9
  66.8 0.6 collective-permute-done.10.got1
  67.4 0.4 collective-permute-done.11.got2
  67.7 0.3 collective-permute-done.9.got0
  68.0 0.0 collective-permute-done.12.came
  68.0 1.1 %shard_map.179 = bf16[32,112,128]{2,1,0:T(8,128)(2,1)} custom-call(f32[9,128,256]{2,1,0:T(8,128)S(1)} %get-tuple-element.104.keep, bf16[3,128,256]{2,1,0:T(8,128)(2,1)S(1)} %collective-permute-done.9.got0, bf16[3,128,256]{2,1,0:T(8,128)(2,1)S(1)} %collective-permute-done.10.got1, bf16[3,128,256]{2,1,0:T(8,128)(2,1)S(1)} %collective-permute-done.11.got2, ...), custom_call_target="tpu_custom_call" | custom-call | flops 1000000000 | bytes 4194304 | tf_op jit(solution)/shard_map/pallas_call | solution.py:41
  69.1 0.0 copy-start.5
  69.1 2.5 %all-to-all-start.3 = ((bf16[32,112,128]{2,1,0:T(8,128)(2,1)}), bf16[32,112,128]{2,1,0:T(8,128)(2,1)S(1)}, u32[]{:S(2)}, u32[]{:S(2)}) async-start(bf16[32,112,128]{2,1,0:T(8,128)(2,1)} %shard_map.179), calls=%async_computation.3 | async-start | bytes 1835008 | tf_op jit(solution)/shard_map/all_to_all | solution.py:666
  71.7 0.5 collective-permute-start.7
  72.1 3.3 %collective-permute-start.8 = (bf16[4,1,48,256]{3,2,1,0:T(8,128)(2,1)S(1)}, bf16[4,1,48,256]{3,2,1,0:T(8,128)(2,1)S(1)}, u32[]{:S(2)}, u32[]{:S(2)}) collective-permute-start(bf16[4,1,48,256]{3,2,1,0:T(8,128)(2,1)S(1)} %get-tuple-element.103), channel_id=1, source_target_pairs={{4,8},{8,4},{12,16},{16,12},{20,24},{24,20},{5,9},{9,5},{13,17},{1... | collective-permute-start | bytes 294920 | tf_op jit(solution)/shard_map/ppermute | solution.py:638
  75.4 0.8 copy.30
  76.3 5.6 %collective-permute-done.8.rb = bf16[4,1,48,256]{3,2,1,0:T(8,128)(2,1)S(1)} collective-permute-done((bf16[4,1,48,256]{3,2,1,0:T(8,128)(2,1)S(1)}, bf16[4,1,48,256]{3,2,1,0:T(8,128)(2,1)S(1)}, u32[]{:S(2)}, u32[]{:S(2)}) %collective-permute-start.8) | collective-permute-done | bytes 98336 | tf_op jit(solution)/shard_map/ppermute | solution.py:638
  81.9 0.0 copy-start.7
  81.9 4.7 %shard_map.178 = f32[4,8,40,256]{3,2,1,0:T(8,128)} custom-call(bf16[1536,256]{1,0:T(8,128)(2,1)S(1)} %get-tuple-element.101.e, bf16[4,1,48,256]{3,2,1,0:T(8,128)(2,1)S(1)} %collective-permute-done.7.ra, bf16[4,1,48,256]{3,2,1,0:T(8,128)(2,1)S(1)} %collective-permute-done.8.rb, bf16[2304,256]{1,0:T(8,128)(2,1)} %copy-done, bf16[4,8,40,256]{3,2,1,0:T(8,128)(2,1)} %cot_far.1, ...), custom_call_target="tpu_custom_call" | custom-call | flops 1811939328 | bytes 4194304 | tf_op jit(solution)/shard_map/pallas_call | solution.py:41
  86.6 0.9 constant_dynamic-slice_fusion.w
  87.5 7.9 %all-to-all-done.3.parts = bf16[32,112,128]{2,1,0:T(8,128)(2,1)S(1)} async-done(((bf16[32,112,128]{2,1,0:T(8,128)(2,1)}), bf16[32,112,128]{2,1,0:T(8,128)(2,1)S(1)}, u32[]{:S(2)}, u32[]{:S(2)}) %all-to-all-start.3) | async-done | bytes 917536 | tf_op jit(solution)/shard_map/all_to_all | solution.py:666
  95.4 1.1 %shard_map.180 = (f32[288,128]{1,0:T(8,128)}, f32[288,128]{1,0:T(8,128)}, f32[288,128]{1,0:T(8,128)}, f32[288,128]{1,0:T(8,128)}, f32[4,256]{1,0:T(4,128)}, /*in...) custom-call(bf16[32,112,128]{2,1,0:T(8,128)(2,1)S(1)} %all-to-all-done.3.parts, ...), custom_call_target="tpu_custom_call" | custom-call | flops 100000000 | bytes 4194304 | tf_op jit(solution)/shard_map/pallas_call | solution.py:41
  (14 shorter events, 0.0 us)
Async XLA Ops:
  2.4 16.0 %collective-permute-start.2 = (bf16[4,4,40,256]{3,2,1,0:T(8,128)(2,1)S(1)}, bf16[4,4,40,256]{3,2,1,0:T(8,128)(2,1)S(1)}, u32[]{:S(2)}, u32[]{:S(2)}) collective-permute-start(bf16[4,4,40,256]{3,2,1,0:T(8,128)(2,1)S(1)} %get-tuple-element.70), channel_id=1, source_target_pairs={{4,8},{8,4},{12,16},{16,12},{20,24},{24,20},{5,9},{9,5},{13,17},{1... | collective-permute-start | bytes 983048 | tf_op jit(solution)/shard_map/ppermute | solution.py:638
  6.9 11.3 %collective-permute-start = (bf16[4,48,256]{2,1,0:T(8,128)(2,1)S(1)}, bf16[4,48,256]{2,1,0:T(8,128)(2,1)S(1)}, u32[]{:S(2)}, u32[]{:S(2)}) collective-permute-start(bf16[4,48,256]{2,1,0:T(8,128)(2,1)S(1)} %get-tuple-element.66), channel_id=1, source_target_pairs={{0,1},{1,0},{2,3},{3,2},{4,5},{5,4},{6,7},{7,6},{8,9},{9,8},{10,11... | collective-permute-start | bytes 294920 | tf_op jit(solution)/shard_map/ppermute | solution.py:638
  8.2 9.9 %collective-permute-start.1 = (bf16[4,48,256]{2,1,0:T(8,128)(2,1)S(1)}, bf16[4,48,256]{2,1,0:T(8,128)(2,1)S(1)}, u32[]{:S(2)}, u32[]{:S(2)}) collective-permute-start(bf16[4,48,256]{2,1,0:T(8,128)(2,1)S(1)} %get-tuple-element.67), channel_id=1, source_target_pairs={{1,2},{2,1},{5,6},{6,5},{9,10},{10,9},{13,14},{14,13},{17,18},{18,... | collective-permute-start | bytes 294920 | tf_op jit(solution)/shard_map/ppermute | solution.py:638
  8.9 9.5 %collective-permute-start.3 = (bf16[4,16,256]{2,1,0:T(8,128)(2,1)S(1)}, bf16[4,16,256]{2,1,0:T(8,128)(2,1)S(1)}, u32[]{:S(2)}, u32[]{:S(2)}) collective-permute-start(bf16[4,16,256]{2,1,0:T(8,128)(2,1)S(1)} %get-tuple-element.71), channel_id=1, source_target_pairs={{4,9},{5,8},{6,11},{7,10},{8,5},{9,4},{10,7},{11,6},{12,17},{13,16... | collective-permute-start | bytes 98312 | tf_op jit(solution)/shard_map/ppermute | solution.py:654
  14.9 3.4 %collective-permute-start.4 = (bf16[4,16,256]{2,1,0:T(8,128)(2,1)S(1)}, bf16[4,16,256]{2,1,0:T(8,128)(2,1)S(1)}, u32[]{:S(2)}, u32[]{:S(2)}) collective-permute-start(bf16[4,16,256]{2,1,0:T(8,128)(2,1)S(1)} %get-tuple-element.72), channel_id=1, source_target_pairs={{5,10},{6,9},{9,6},{10,5},{13,18},{14,17},{17,14},{18,13},{21,26},... | collective-permute-start | bytes 98312 | tf_op jit(solution)/shard_map/ppermute | solution.py:654
  15.6 2.5 %copy-start.1 = (bf16[4,8,40,256]{3,2,1,0:T(8,128)(2,1)S(1)}, bf16[4,8,40,256]{3,2,1,0:T(8,128)(2,1)}, u32[]{:S(2)}) copy-start(bf16[4,8,40,256]{3,2,1,0:T(8,128)(2,1)} %cot_far.1) | copy-start | bytes 1966084
  18.1 3.7 %copy-start = (bf16[2304,256]{1,0:T(8,128)(2,1)}, bf16[2304,256]{1,0:T(8,128)(2,1)S(1)}, u32[]{:S(2)}) copy-start(bf16[2304,256]{1,0:T(8,128)(2,1)S(1)} %get-tuple-element.78.w.w_far) | copy-start | bytes 3538948
  18.4 1.8 %collective-permute-start.5 = (bf16[4,4,48,256]{3,2,1,0:T(8,128)(2,1)S(1)}, bf16[4,4,48,256]{3,2,1,0:T(8,128)(2,1)S(1)}, u32[]{:S(2)}, u32[]{:S(2)}) collective-permute-start(bf16[4,4,48,256]{3,2,1,0:T(8,128)(2,1)S(1)} %get-tuple-element.74), channel_id=1, source_target_pairs={{0,4},{4,0},{8,12},{12,8},{16,20},{20,16},{24,28},{28,24},{1,5},{5... | collective-permute-start | bytes 1179656 | tf_op jit(solution)/shard_map/ppermute | solution.py:638
  20.2 13.3 %copy-start.4 = (f32[4,256]{1,0:T(4,128)S(1)}, f32[4,256]{1,0:T(4,128)}, u32[]{:S(2)}) copy-start(f32[4,256]{1,0:T(4,128)} %params.9) | copy-start | bytes 12292
  48.3 3.9 %collective-permute-start.6 = (f32[9,128,256]{2,1,0:T(8,128)S(1)}, f32[9,128,256]{2,1,0:T(8,128)S(1)}, u32[]{:S(2)}, u32[]{:S(2)}) collective-permute-start(f32[9,128,256]{2,1,0:T(8,128)S(1)} %get-tuple-element.93), channel_id=1, source_target_pairs={{0,4},{4,0},{8,12},{12,8},{16,20},{20,16},{24,28},{28,24},{1,5},{5... | collective-permute-start | bytes 3538952 | tf_op jit(solution)/shard_map/ppermute | solution.py:638
  52.8 15.2 %collective-permute-start.12 = (bf16[32,40,128]{2,1,0:T(8,128)(2,1)S(1)}, bf16[32,40,128]{2,1,0:T(8,128)(2,1)S(1)}, u32[]{:S(2)}, u32[]{:S(2)}) collective-permute-start(bf16[32,40,128]{2,1,0:T(8,128)(2,1)S(1)} %get-tuple-element.109), channel_id=1, source_target_pairs={{0,8},{4,12},{8,0},{12,4},{16,24},{20,28},{24,16},{28,20},{1,9},{5... | collective-permute-start | bytes 983048 | tf_op jit(solution)/shard_map/ppermute | solution.py:814
  65.6 1.8 %collective-permute-start.10 = (bf16[3,128,256]{2,1,0:T(8,128)(2,1)S(1)}, bf16[3,128,256]{2,1,0:T(8,128)(2,1)S(1)}, u32[]{:S(2)}, u32[]{:S(2)}) collective-permute-start(bf16[3,128,256]{2,1,0:T(8,128)(2,1)S(1)} %get-tuple-element.106), channel_id=1, source_target_pairs={{0,4},{4,0},{8,12},{12,8},{16,20},{20,16},{24,28},{28,24},{1,5},{5... | collective-permute-start | bytes 589832 | tf_op jit(solution)/shard_map/ppermute | solution.py:638
  66.3 1.4 %collective-permute-start.11 = (bf16[3,128,256]{2,1,0:T(8,128)(2,1)S(1)}, bf16[3,128,256]{2,1,0:T(8,128)(2,1)S(1)}, u32[]{:S(2)}, u32[]{:S(2)}) collective-permute-start(bf16[3,128,256]{2,1,0:T(8,128)(2,1)S(1)} %get-tuple-element.107), channel_id=1, source_target_pairs={{0,4},{4,0},{8,12},{12,8},{16,20},{20,16},{24,28},{28,24},{1,5},{5... | collective-permute-start | bytes 589832 | tf_op jit(solution)/shard_map/ppermute | solution.py:638
  66.4 1.6 %collective-permute-start.9 = (bf16[3,128,256]{2,1,0:T(8,128)(2,1)S(1)}, bf16[3,128,256]{2,1,0:T(8,128)(2,1)S(1)}, u32[]{:S(2)}, u32[]{:S(2)}) collective-permute-start(bf16[3,128,256]{2,1,0:T(8,128)(2,1)S(1)} %get-tuple-element.105), channel_id=1, source_target_pairs={{0,4},{4,0},{8,12},{12,8},{16,20},{20,16},{24,28},{28,24},{1,5},{5... | collective-permute-start | bytes 589832 | tf_op jit(solution)/shard_map/ppermute | solution.py:638
  69.1 12.7 %copy-start.5 = (s32[4,8,40]{2,1,0:T(8,128)S(1)}, s32[4,8,40]{2,1,0:T(8,128)}, u32[]{:S(2)}) copy-start(s32[4,8,40]{2,1,0:T(8,128)} %occ.1) | copy-start | bytes 15364
  69.1 26.3 %all-to-all-start.3 = ((bf16[32,112,128]{2,1,0:T(8,128)(2,1)}), bf16[32,112,128]{2,1,0:T(8,128)(2,1)S(1)}, u32[]{:S(2)}, u32[]{:S(2)}) async-start(bf16[32,112,128]{2,1,0:T(8,128)(2,1)} %shard_map.179), calls=%async_computation.3 | async-start | bytes 1835008 | tf_op jit(solution)/shard_map/all_to_all | solution.py:666
  71.7 4.6 %collective-permute-start.7 = (bf16[4,1,48,256]{3,2,1,0:T(8,128)(2,1)S(1)}, bf16[4,1,48,256]{3,2,1,0:T(8,128)(2,1)S(1)}, u32[]{:S(2)}, u32[]{:S(2)}) collective-permute-start(bf16[4,1,48,256]{3,2,1,0:T(8,128)(2,1)S(1)} %get-tuple-element.102), channel_id=1, source_target_pairs={{0,4},{4,0},{8,12},{12,8},{16,20},{20,16},{24,28},{28,24},{1,5},{5... | collective-permute-start | bytes 294920 | tf_op jit(solution)/shard_map/ppermute | solution.py:638
  72.1 9.7 %collective-permute-start.8 = (bf16[4,1,48,256]{3,2,1,0:T(8,128)(2,1)S(1)}, bf16[4,1,48,256]{3,2,1,0:T(8,128)(2,1)S(1)}, u32[]{:S(2)}, u32[]{:S(2)}) collective-permute-start(bf16[4,1,48,256]{3,2,1,0:T(8,128)(2,1)S(1)} %get-tuple-element.103), channel_id=1, source_target_pairs={{4,8},{8,4},{12,16},{16,12},{20,24},{24,20},{5,9},{9,5},{13,17},{1... | collective-permute-start | bytes 294920 | tf_op jit(solution)/shard_map/ppermute | solution.py:638
  81.9 13.5 %copy-start.2 = (f32[2,18432]{1,0:T(2,128)S(1)}, f32[2,18432]{1,0:T(2,128)}, u32[]{:S(2)}) copy-start(f32[2,18432]{1,0:T(2,128)} %param.13) | copy-start | bytes 442372
  81.9 13.5 %copy-start.3 = (f32[2,18432]{1,0:T(2,128)S(1)}, f32[2,18432]{1,0:T(2,128)}, u32[]{:S(2)}) copy-start(f32[2,18432]{1,0:T(2,128)} %param.14) | copy-start | bytes 442372
  81.9 13.5 %copy-start.6 = (f32[4,256]{1,0:T(4,128)S(1)}, f32[4,256]{1,0:T(4,128)}, u32[]{:S(2)}) copy-start(f32[4,256]{1,0:T(4,128)} %n_first.1) | copy-start | bytes 12292
  81.9 13.5 %copy-start.7 = (f32[4,256]{1,0:T(4,128)S(1)}, f32[4,256]{1,0:T(4,128)}, u32[]{:S(2)}) copy-start(f32[4,256]{1,0:T(4,128)} %n_second.1) | copy-start | bytes 12292

commit v5 on v4

--- a/solution.py
+++ b/solution.py
@@ -382,10 +382,7 @@
             for b in range(3):
                 keep[a * 3 + b] += acc[0:half, b * chans : (b + 1) * chans]
                 other_half = first[a * 3 + b] + acc[half:, b * chans : (b + 1) * chans]
-                if isinstance(send, tuple):
-                    send[a][b] = other_half.astype(BF16)
-                else:
-                    send[a * 3 + b] = other_half
+                send[a * 3 + b] = other_half
 
 
 def second_gradient_kernel(
@@ -462,8 +459,33 @@
     to_all(st_ref, [jnp.sum(s0, 0, keepdims=True), jnp.sum(s1, 0, keepdims=True) * rstd])
 
 
+def half_gradient(g, which, field, rows_field, first_row, dt_ref, out_ref, sums, prepare=None):
+    chans, half = g.c, g.c // 2
+    span = g.h * g.wp
+    channels = pl.ds(pl.multiple_of(which * half, half), half)
+    cut = g.s // 2
+    groups = range(cut), range(cut, g.s)
+    if prepare is not None:
+        for s in groups[0]:
+            prepare(s)
+    for group in groups:
+        lhs = dt_ref[channels, group[0] * span : (group[-1] + 1) * span]
+        for a in range(3):
+            starts = [(s * rows_field + first_row + a) * g.wp for s in group]
+            acc = dot(lhs, jnp.concatenate([field[at : at + span, :] for at in starts], axis=0))
+            if group[0] == 0 and prepare is not None and a < len(groups[1]):
+                prepare(groups[1][a])
+            for b in range(3):
+                part = acc[:, b * chans : (b + 1) * chans]
+                if group[0] == 0:
+                    sums[a * 3 + b] = part
+                else:
+                    rows = slice((a * 3 + b) * chans, (a * 3 + b + 1) * chans)
+                    out_ref[rows, :] = (sums[a * 3 + b] + part).T.astype(out_ref.dtype)
+
+
 def first_gradient_kernel(
-    g, count, dn, z, st, st3, params, x, e_ref, a_ref, b_ref, keep, send0, send1, send2, dt_ref, first
+    g, count, dn, z, st, st3, params, x, e_ref, a_ref, b_ref, send, dt_ref, first
 ):
     place = Place()
     mean, rstd = stats_of(total_of(st), count)
@@ -485,8 +507,11 @@
         a_ref[s, 0] = jnp.where(place.odd_row, top, d).astype(BF16)
         b_ref[s, 0] = jnp.where(place.odd_row, d, top).astype(BF16)
         own_transposed(g, e_ref, s * g.h * g.wp, s, dt_ref)
-    send = (send0, send1, send2)
-    kernel_gradient(g, place.core, x, g.h + 2, 0, dt_ref, keep, send, first, prepare)
+    half_gradient(g, 1 - place.core, x, g.h + 2, 0, dt_ref, send, first, prepare)
+
+
+def first_own_kernel(g, x, dt_ref, keep, first):
+    half_gradient(g, Place().core, x, g.h + 2, 0, dt_ref, keep, first)
 
 
 def input_gradient_kernel(
@@ -520,18 +545,22 @@
 
 
 def pair_total(keep, got, t):
-    other = got[t] if len(got) > 3 else got[t // 3][t % 3].astype(F32)
-    return keep[t] + other
-
-
-def pair_sum_kernel(lane, keep, *refs):
-    *got, out_far, buffer, sems = refs
-    got = got[0] if len(got) == 1 else got[:3]
-    taps, half, chans = keep.shape
+    if keep.ndim == 3:
+        return (keep[t] + wide(got, t)).T
+    chans = 2 * keep.shape[1]
+    rows = slice(t * chans, (t + 1) * chans)
+    return keep[rows, :] + wide(got, rows)
+
+
+def pair_sum_kernel(lane, keep, got, *refs):
+    *_, out_far, buffer, sems = refs
+    half = buffer.shape[1]
+    chans = 2 * half
+    taps = buffer.shape[0] // chans
     copies = []
     for t in range(taps):
         rows = pl.ds(t * chans, chans)
-        buffer[rows, :] = pair_total(keep, got, t).astype(BF16).T
+        buffer[rows, :] = pair_total(keep, got, t).astype(BF16)
         copies.append(
             pltpu.make_async_copy(buffer.at[rows], out_far.at[rows, pl.ds(lane, half)], sems.at[t])
         )
@@ -549,7 +578,7 @@
     devices, rows, _ = kept_ref.shape
     share = taps * chans // devices
     for t in range(taps):
-        buffer[t * chans : (t + 1) * chans, :] = pair_total(keep, got, t).T
+        buffer[t * chans : (t + 1) * chans, :] = pair_total(keep, got, t)
     second = Place().second
     for i in range(devices):
         mine = pl.multiple_of(i * share + (share - rows) * second, 8)
@@ -558,19 +587,22 @@
         sent_ref[i] = buffer[pl.ds(other, rows), :].astype(BF16)
 
 
-def message_kernel(keep, got0, got1, got2, kept, came, out_far, buffer, out_ref, sems):
-    taps, half, chans = keep.shape
-    devices, rows, _ = kept.shape
-    share = taps * chans // devices
-    for t in range(taps):
-        buffer[t * chans : (t + 1) * chans, :] = pair_total(keep, (got0, got1, got2), t).T
+def join_kernel(kept, came, out_ref):
+    for i in range(kept.shape[0]):
+        out_ref[i] = kept[i] + wide(came, i)
+
+
+def message_kernel(keep, got, kept, out_far, out_ref, sems):
+    devices = kept.shape[0]
+    share = keep.shape[0] // devices
     copies = []
     count = sems.shape[0]
     for part in range(count):
         mine = pl.ds(part * devices // count, devices // count)
         for i in range(part * devices // count, (part + 1) * devices // count):
-            first = buffer[i * share : (i + 1) * share, :]
-            out_ref[i] = jnp.concatenate([first, kept[i] + wide(came, i)], axis=0).astype(BF16)
+            rows = slice(i * share, (i + 1) * share)
+            first = keep[rows, :] + wide(got, rows)
+            out_ref[i] = jnp.concatenate([first, kept[i]], axis=0).astype(BF16)
         copies.append(pltpu.make_async_copy(out_ref.at[mine], out_far.at[mine], sems.at[part]))
         copies[-1].start()
     for copy in copies:
@@ -795,31 +827,44 @@
             scratch=[pltpu.VMEM((taps, chans // 2), F32)],
         )(keep2, got2)
         st, kept = lax.optimization_barrier((st, kept))
+        came = lax.ppermute(sent, "rows", [(i, i ^ 2) for i in range(nrows)])
         st3 = exchange(st)
     else:
         st, got2 = lax.optimization_barrier((st, got2))
         st3 = exchange(st)
-    cut = held((3, chans // 2, chans), BF16)
-    e, a, b, keep1, *send1 = kernel_call(
+    if cut_again:
+        kept, st3 = lax.optimization_barrier((kept, st3))
+        (kept,) = kernel_call(join_kernel, [held(kept_shape, F32)], 0, size=1024)(kept, came)
+        dn1, kept = lax.optimization_barrier((dn1, kept))
+    sent_shape = held((taps, chans // 2), BF16)
+    part = pltpu.VMEM(grad_shape.shape, F32)
+    e, a, b, send1, dt = kernel_call(
         functools.partial(first_gradient_kernel, g, count),
-        [held((n3, chans), BF16), wide_rows(1), wide_rows(1), grad_shape, cut, cut, cut],
+        [
+            held((n3, chans), BF16),
+            wide_rows(1),
+            wide_rows(1),
+            sent_shape,
+            held((chans, own_pixels), BF16),
+        ],
         0,
         size=1024,
-        scratch=[pltpu.VMEM((chans, own_pixels), BF16), pltpu.VMEM(grad_shape.shape, F32)],
+        scratch=[part],
     )(dn1, z1, st1, st3, norm_scale_bias, x)
-    got1 = [swapped(part, "rows", 0) for part in send1]
+    (keep1,) = kernel_call(
+        functools.partial(first_own_kernel, g), [held((taps, chans // 2), F32)], 0, size=1024, scratch=[part]
+    )(x, dt)
+    got1 = swapped(send1, "rows", 0)
     share_rows = taps // devices
-    buffer = pltpu.VMEM((taps, chans // 2), F32)
     if cut_again:
-        came = lax.ppermute(sent, "rows", [(i, i ^ 2) for i in range(nrows)])
         rows = share_rows + kept.shape[1]
         (parts,) = kernel_call(
             message_kernel,
             [stored((devices, rows, chans // 2), BF16)],
             1e9,
             far_out=(0,),
-            scratch=[buffer, pltpu.VMEM((devices, rows, chans // 2), BF16), dma((4,))],
-        )(keep1, *got1, kept, came)
+            scratch=[pltpu.VMEM((devices, rows, chans // 2), BF16), dma((4,))],
+        )(keep1, got1, kept)
     else:
 
         def add_pair(lane, *operands, **options):
@@ -833,7 +878,7 @@
             )(*operands)
 
         (parts,) = add_pair(chans // 2, keep2, got2)
-        (parts,) = add_pair(0, keep1, *got1, parts, far=(4,), alias={4: 0})
+        (parts,) = add_pair(0, keep1, got1, parts, far=(2,), alias={2: 0})
         parts = parts.reshape(devices, share_rows, chans)
     parts, chunked = lax.optimization_barrier((parts, chunked))
     parts = exchange(parts)

time: 96.9 us -> 96.3 us (level)
    ppermute x10 -> x8, waiting for transfers between devices: 6.96 us -> 6.13 us  [swapped(): return lax.ppermute(block, axis, pairs)]
    pallas_call x13 -> x15, Pallas kernels: 24.9 us -> 25.5 us  [call(): pl.pallas_call(body, out_shape=out_shape, in_specs=specs, out_specs=[pl.B...]
    ppermute x10 -> x8, starting transfers between devices: 13 us -> 12.5 us  [swapped(): return lax.ppermute(block, axis, pairs)]
  transfers between devices with their start and end apart: 14 -> 12, of which waited for: 6 -> 4; matrix products, arithmetic and copies ran while one was open for 2% -> 2% of each run, Pallas kernels for 14% -> 13%
where the time goes in v5:
time: 96.3 us; the launch traced here: 95.9 us
  blocking collectives  31.3 us (33%)
  Pallas kernels  25.5 us (26%)
  starting transfers between devices  22.4 us (23%)
  waiting for transfers between devices  14 us (15%)
  local copies, waits for them, and re-layouts  1.8 us (2%)
    all_to_all x3, blocking collectives, exchange(): return lax.all_to_all(parts, BOTH, 0, 0, tiled=True)  31.3 us
    pallas_call x15, Pallas kernels, call(): pl.pallas_call(body, out_shape=out_shape, in_specs=specs, out_specs=[pl.B...  25.5 us
    ppermute x8, starting transfers between devices, swapped(): return lax.ppermute(block, axis, pairs)  12.5 us
    all_to_all x1, waiting for transfers between devices, exchange(): return lax.all_to_all(parts, BOTH, 0, 0, tiled=True)  7.9 us
    ppermute x2, starting transfers between devices, swapped_both(): return lax.ppermute(block, BOTH, pairs)  6.69 us
    ppermute x8, waiting for transfers between devices, swapped(): return lax.ppermute(block, axis, pairs)  6.13 us
    all_to_all x1, starting transfers between devices, exchange(): return lax.all_to_all(parts, BOTH, 0, 0, tiled=True)  2.63 us
  transfers between devices with their start and end apart: 12, of which 4 were waited for; matrix products, arithmetic and copies ran while one was open for 2% of the time, Pallas kernels for 13%

profile of v5, /device:TPU:1, one launch (start us, length us, event | category | flops | bytes accessed | tf_op | source)
XLA Modules:
  0.0 95.9 jit_solution(8733074788317581372)
XLA Ops:
  0.6 1.7 %shard_map.168 = (bf16[4,8,40,256]{3,2,1,0:T(8,128)(2,1)S(1)}, bf16[4,48,256]{2,1,0:T(8,128)(2,1)S(1)}, bf16[4,48,256]{2,1,0:T(8,128)(2,1)S(1)}, bf16[4,4,40,256...) custom-call(bf16[4,8,40,256]{3,2,1,0:T(8,128)(2,1)} %features.1, ...), custom_call_target="tpu_custom_call" | custom-call | flops 100000000 | bytes 4194304 | tf_op jit(solution)/shard_map/pallas_call | solution.py:41
  2.4 4.5 %collective-permute-start.2 = (bf16[4,4,40,256]{3,2,1,0:T(8,128)(2,1)S(1)}, bf16[4,4,40,256]{3,2,1,0:T(8,128)(2,1)S(1)}, u32[]{:S(2)}, u32[]{:S(2)}) collective-permute-start(bf16[4,4,40,256]{3,2,1,0:T(8,128)(2,1)S(1)} %get-tuple-element.72), channel_id=1, source_target_pairs={{4,8},{8,4},{12,16},{16,12},{20,24},{24,20},{5,9},{9,5},{13,17},{1... | collective-permute-start | bytes 983048 | tf_op jit(solution)/shard_map/ppermute | solution.py:670
  6.9 1.4 %collective-permute-start = (bf16[4,48,256]{2,1,0:T(8,128)(2,1)S(1)}, bf16[4,48,256]{2,1,0:T(8,128)(2,1)S(1)}, u32[]{:S(2)}, u32[]{:S(2)}) collective-permute-start(bf16[4,48,256]{2,1,0:T(8,128)(2,1)S(1)} %get-tuple-element.68), channel_id=1, source_target_pairs={{0,1},{1,0},{2,3},{3,2},{4,5},{5,4},{6,7},{7,6},{8,9},{9,8},{10,11... | collective-permute-start | bytes 294920 | tf_op jit(solution)/shard_map/ppermute | solution.py:670
  8.2 0.7 collective-permute-start.1
  8.9 6.0 %collective-permute-start.3 = (bf16[4,16,256]{2,1,0:T(8,128)(2,1)S(1)}, bf16[4,16,256]{2,1,0:T(8,128)(2,1)S(1)}, u32[]{:S(2)}, u32[]{:S(2)}) collective-permute-start(bf16[4,16,256]{2,1,0:T(8,128)(2,1)S(1)} %get-tuple-element.73), channel_id=1, source_target_pairs={{4,9},{5,8},{6,11},{7,10},{8,5},{9,4},{10,7},{11,6},{12,17},{13,16... | collective-permute-start | bytes 98312 | tf_op jit(solution)/shard_map/ppermute | solution.py:686
  14.9 0.7 collective-permute-start.4
  15.6 0.0 copy-start.1
  15.6 2.5 %shard_map.170 = (bf16[2304,256]{1,0:T(8,128)(2,1)S(1)}, bf16[2304,256]{1,0:T(8,128)(2,1)S(1)}) custom-call(f32[9216,128]{1,0:T(8,128)} %bitcast.37), custom_call_target="tpu_custom_call" | custom-call | bytes 1024 | tf_op jit(solution)/shard_map/pallas_call | solution.py:41
  18.1 0.0 collective-permute-done.rc
  18.1 0.0 collective-permute-done.1.rd
  18.1 0.0 copy-done.1
  18.2 0.2 shard_map.169
  18.4 0.0 collective-permute-done.3.rb_c
  18.4 0.0 collective-permute-done.4.rb_d
  18.4 0.0 collective-permute-done.2.rb
  18.4 0.1 collective-permute-start.5
  18.5 1.6 %shard_map.171 = (f32[2304,256]{1,0:T(8,128)S(1)}, f32[16,256]{1,0:T(8,128)S(1)}, bf16[1920,768]{1,0:T(8,128)(2,1)S(1)}) custom-call(bf16[4,8,48,256]{3,2,1,0:T(8,128)(2,1)S(1)} %get-tuple-element.70.ext, bf16[2304,256]{1,0:T(8,128)(2,1)S(1)} %get-tuple-element.80.w.w_far), custom_call_target="tpu_custom_call" | custom-call | bytes 1024 | tf_op jit(solution)/shard_map/pallas_call | solution.py:41
  20.1 0.1 collective-permute-done.5.ra
  20.2 1.6 %shard_map.172 = (f32[2304,256]{1,0:T(8,128)S(1)}, f32[32,2,256]{2,1,0:T(2,128)S(1)}, bf16[1920,768]{1,0:T(8,128)(2,1)S(1)}, bf16[4,2,48,256]{3,2,1,0:T(8,128)(2,1)S(1)}) custom-call(bf16[4,8,48,256]{3,2,1,0:T(8,128)(2,1)S(1)} %get-tuple-element.70.ext, ...), custom_call_target="tpu_custom_call", output_to_operand_aliasing={{0}: (7, {}), {2}: (8, {})} | custom-call | bytes 1024 | tf_op jit(solution)/shard_map/pallas_call | solution.py:41
  21.9 11.7 %all_to_all.20.st = f32[32,2,256]{2,1,0:T(2,128)S(1)} all-to-all(f32[32,2,256]{2,1,0:T(2,128)S(1)} %get-tuple-element.85), channel_id=1, replica_groups=mesh['rows'=8,'cols'=4] {'rows','cols'}, dimensions={0} | all-to-all | bytes 131072 | tf_op jit(solution)/shard_map/all_to_all | solution.py:698
  33.5 2.8 %shard_map.173 = (bf16[2304,768]{1,0:T(8,128)(2,1)S(1)}, f32[1920,256]{1,0:T(8,128)S(1)}, f32[32,4,256]{2,1,0:T(4,128)S(1)}) custom-call(f32[2304,256]{1,0:T(8,128)S(1)} %get-tuple-element.84.z1.z, f32[32,2,256]{2,1,0:T(2,128)S(1)} %all_to_all.20.st, f32[4,256]{1,0:T(4,128)S(1)} %copy-done.4, bf16[2304,256]{1,0:T(8,128)(2,1)S(1)} %get-tuple-element.86.w, ...), custom_call_target="tpu_custom_call" | custom-call | flops 2264924160 | bytes 4194304 | tf_op jit(solution)/shard_map/pallas_call | solution.py:41
  36.3 9.7 %all_to_all.21.st.st2 = f32[32,4,256]{2,1,0:T(4,128)S(1)} all-to-all(f32[32,4,256]{2,1,0:T(4,128)S(1)} %get-tuple-element.89), channel_id=1, replica_groups=mesh['rows'=8,'cols'=4] {'rows','cols'}, dimensions={0} | all-to-all | bytes 262144 | tf_op jit(solution)/shard_map/all_to_all | solution.py:698
  46.0 2.5 %shard_map.174 = (bf16[1920,256]{1,0:T(8,128)(2,1)S(1)}, f32[9,128,256]{2,1,0:T(8,128)S(1)}, f32[9,128,256]{2,1,0:T(8,128)S(1)}) custom-call(f32[1920,256]{1,0:T(8,128)S(1)} %get-tuple-element.88.z2, f32[32,4,256]{2,1,0:T(4,128)S(1)} %all_to_all.21.st.st2, f32[4,256]{1,0:T(4,128)S(1)} %copy-done.4, bf16[4,8,48,256]{3,2,1,0:T(8,128)(2,1)S(1)} %get-tuple-element.87.cot, ...), custom_call_target="tpu_custom_call" | custom-call | flops 1811939328 | bytes 4194304 | tf_op jit(solution)/shard_map/pallas_call | solution.py:41
  48.4 1.4 %collective-permute-start.6 = (f32[9,128,256]{2,1,0:T(8,128)S(1)}, f32[9,128,256]{2,1,0:T(8,128)S(1)}, u32[]{:S(2)}, u32[]{:S(2)}) collective-permute-start(f32[9,128,256]{2,1,0:T(8,128)S(1)} %get-tuple-element.95), channel_id=1, source_target_pairs={{0,4},{4,0},{8,12},{12,8},{16,20},{20,16},{24,28},{28,24},{1,5},{5... | collective-permute-start | bytes 3538952 | tf_op jit(solution)/shard_map/ppermute | solution.py:670
  49.9 2.5 %shard_map.175 = (f32[1536,256]{1,0:T(8,128)S(1)}, f32[32,2,256]{2,1,0:T(2,128)S(1)}, bf16[4,8,40,256]{3,2,1,0:T(8,128)(2,1)S(1)}) custom-call(bf16[1920,256]{1,0:T(8,128)(2,1)S(1)} %get-tuple-element.92.d, bf16[2304,256]{1,0:T(8,128)(2,1)S(1)} %get-tuple-element.86.w, f32[2304,256]{1,0:T(8,128)S(1)} %get-tuple-element.84.z1.z, ...), custom_call_target="tpu_custom_call" | custom-call | flops 1811939328 | bytes 4194304 | tf_op jit(solution)/shard_map/pallas_call | solution.py:41
  52.4 0.0 collective-permute-done.6.got
  52.4 0.6 shard_map.176
  53.0 0.6 collective-permute-start.7
  53.5 9.9 %all_to_all.22.st3 = f32[32,2,256]{2,1,0:T(2,128)S(1)} all-to-all(f32[32,2,256]{2,1,0:T(2,128)S(1)} %get-tuple-element.102), channel_id=1, replica_groups=mesh['rows'=8,'cols'=4] {'rows','cols'}, dimensions={0} | all-to-all | bytes 131072 | tf_op jit(solution)/shard_map/all_to_all | solution.py:698
  63.5 0.0 collective-permute-done.7.came
  63.5 0.1 shard_map.177.kept
  63.5 1.5 %shard_map.178 = (bf16[1536,256]{1,0:T(8,128)(2,1)S(1)}, bf16[4,1,48,256]{3,2,1,0:T(8,128)(2,1)S(1)}, bf16[4,1,48,256]{3,2,1,0:T(8,128)(2,1)S(1)}, bf16[2304,128]{1,0:T(8,128)(2,1)S(1)}, bf16[256,1536]{1,0:T(8,128)(2,1)S(1)}) custom-call(f32[1536,256]{1,0:T(8,128)S(1)} %get-tuple-element.105.dn, f32[2304,256]{1,0:T(8,128)S(1)} %get-tuple-element.84.z1.z, ...), custom_call_target="tpu_custom_call" | custom-call | bytes 1024 | tf_op jit(solution)/shard_map/pallas_call | solution.py:41
  65.1 0.7 collective-permute-start.10
  65.8 1.2 %shard_map.180.keep = f32[2304,128]{1,0:T(8,128)S(1)} custom-call(bf16[1920,768]{1,0:T(8,128)(2,1)S(1)} %get-tuple-element.107.x, bf16[256,1536]{1,0:T(8,128)(2,1)S(1)} %get-tuple-element.111.dt_ref), custom_call_target="tpu_custom_call" | custom-call | bytes 1024 | tf_op jit(solution)/shard_map/pallas_call | solution.py:41
  67.0 0.4 collective-permute-done.10.got
  67.4 1.0 %shard_map.181 = bf16[32,112,128]{2,1,0:T(8,128)(2,1)} custom-call(f32[2304,128]{1,0:T(8,128)S(1)} %shard_map.180.keep, bf16[2304,128]{1,0:T(8,128)(2,1)S(1)} %collective-permute-done.10.got, f32[32,40,128]{2,1,0:T(8,128)S(1)} %shard_map.177.kept), custom_call_target="tpu_custom_call" | custom-call | flops 1000000000 | bytes 4194304 | tf_op jit(solution)/shard_map/pallas_call | solution.py:41
  68.4 0.0 copy-start.5
  68.4 2.6 %all-to-all-start.3 = ((bf16[32,112,128]{2,1,0:T(8,128)(2,1)}), bf16[32,112,128]{2,1,0:T(8,128)(2,1)S(1)}, u32[]{:S(2)}, u32[]{:S(2)}) async-start(bf16[32,112,128]{2,1,0:T(8,128)(2,1)} %shard_map.181), calls=%async_computation.3 | async-start | bytes 1835008 | tf_op jit(solution)/shard_map/all_to_all | solution.py:698
  71.1 0.5 collective-permute-start.8
  71.5 3.3 %collective-permute-start.9 = (bf16[4,1,48,256]{3,2,1,0:T(8,128)(2,1)S(1)}, bf16[4,1,48,256]{3,2,1,0:T(8,128)(2,1)S(1)}, u32[]{:S(2)}, u32[]{:S(2)}) collective-permute-start(bf16[4,1,48,256]{3,2,1,0:T(8,128)(2,1)S(1)} %get-tuple-element.110), channel_id=1, source_target_pairs={{4,8},{8,4},{12,16},{16,12},{20,24},{24,20},{5,9},{9,5},{13,17},{1... | collective-permute-start | bytes 294920 | tf_op jit(solution)/shard_map/ppermute | solution.py:670
  74.8 0.8 copy.30
  75.7 0.0 collective-permute-done.8.ra
  75.7 5.6 %collective-permute-done.9.rb = bf16[4,1,48,256]{3,2,1,0:T(8,128)(2,1)S(1)} collective-permute-done((bf16[4,1,48,256]{3,2,1,0:T(8,128)(2,1)S(1)}, bf16[4,1,48,256]{3,2,1,0:T(8,128)(2,1)S(1)}, u32[]{:S(2)}, u32[]{:S(2)}) %collective-permute-start.9) | collective-permute-done | bytes 98336 | tf_op jit(solution)/shard_map/ppermute | solution.py:670
  81.3 0.0 copy-start.7
  81.3 4.7 %shard_map.179 = f32[4,8,40,256]{3,2,1,0:T(8,128)} custom-call(bf16[1536,256]{1,0:T(8,128)(2,1)S(1)} %get-tuple-element.108.e, bf16[4,1,48,256]{3,2,1,0:T(8,128)(2,1)S(1)} %collective-permute-done.8.ra, bf16[4,1,48,256]{3,2,1,0:T(8,128)(2,1)S(1)} %collective-permute-done.9.rb, bf16[2304,256]{1,0:T(8,128)(2,1)} %copy-done, bf16[4,8,40,256]{3,2,1,0:T(8,128)(2,1)} %cot_far.1, ...), custom_call_target="tpu_custom_call" | custom-call | flops 1811939328 | bytes 4194304 | tf_op jit(solution)/shard_map/pallas_call | solution.py:41
  86.0 0.9 constant_dynamic-slice_fusion.w
  86.9 7.9 %all-to-all-done.3.parts = bf16[32,112,128]{2,1,0:T(8,128)(2,1)S(1)} async-done(((bf16[32,112,128]{2,1,0:T(8,128)(2,1)}), bf16[32,112,128]{2,1,0:T(8,128)(2,1)S(1)}, u32[]{:S(2)}, u32[]{:S(2)}) %all-to-all-start.3) | async-done | bytes 917536 | tf_op jit(solution)/shard_map/all_to_all | solution.py:698
  94.8 1.1 %shard_map.182 = (f32[288,128]{1,0:T(8,128)}, f32[288,128]{1,0:T(8,128)}, f32[288,128]{1,0:T(8,128)}, f32[288,128]{1,0:T(8,128)}, f32[4,256]{1,0:T(4,128)}, /*in...) custom-call(bf16[32,112,128]{2,1,0:T(8,128)(2,1)S(1)} %all-to-all-done.3.parts, ...), custom_call_target="tpu_custom_call" | custom-call | flops 100000000 | bytes 4194304 | tf_op jit(solution)/shard_map/pallas_call | solution.py:41
  (12 shorter events, 0.0 us)
Async XLA Ops:
  2.4 16.0 %collective-permute-start.2 = (bf16[4,4,40,256]{3,2,1,0:T(8,128)(2,1)S(1)}, bf16[4,4,40,256]{3,2,1,0:T(8,128)(2,1)S(1)}, u32[]{:S(2)}, u32[]{:S(2)}) collective-permute-start(bf16[4,4,40,256]{3,2,1,0:T(8,128)(2,1)S(1)} %get-tuple-element.72), channel_id=1, source_target_pairs={{4,8},{8,4},{12,16},{16,12},{20,24},{24,20},{5,9},{9,5},{13,17},{1... | collective-permute-start | bytes 983048 | tf_op jit(solution)/shard_map/ppermute | solution.py:670
  6.9 11.3 %collective-permute-start = (bf16[4,48,256]{2,1,0:T(8,128)(2,1)S(1)}, bf16[4,48,256]{2,1,0:T(8,128)(2,1)S(1)}, u32[]{:S(2)}, u32[]{:S(2)}) collective-permute-start(bf16[4,48,256]{2,1,0:T(8,128)(2,1)S(1)} %get-tuple-element.68), channel_id=1, source_target_pairs={{0,1},{1,0},{2,3},{3,2},{4,5},{5,4},{6,7},{7,6},{8,9},{9,8},{10,11... | collective-permute-start | bytes 294920 | tf_op jit(solution)/shard_map/ppermute | solution.py:670
  8.2 9.9 %collective-permute-start.1 = (bf16[4,48,256]{2,1,0:T(8,128)(2,1)S(1)}, bf16[4,48,256]{2,1,0:T(8,128)(2,1)S(1)}, u32[]{:S(2)}, u32[]{:S(2)}) collective-permute-start(bf16[4,48,256]{2,1,0:T(8,128)(2,1)S(1)} %get-tuple-element.69), channel_id=1, source_target_pairs={{1,2},{2,1},{5,6},{6,5},{9,10},{10,9},{13,14},{14,13},{17,18},{18,... | collective-permute-start | bytes 294920 | tf_op jit(solution)/shard_map/ppermute | solution.py:670
  8.9 9.5 %collective-permute-start.3 = (bf16[4,16,256]{2,1,0:T(8,128)(2,1)S(1)}, bf16[4,16,256]{2,1,0:T(8,128)(2,1)S(1)}, u32[]{:S(2)}, u32[]{:S(2)}) collective-permute-start(bf16[4,16,256]{2,1,0:T(8,128)(2,1)S(1)} %get-tuple-element.73), channel_id=1, source_target_pairs={{4,9},{5,8},{6,11},{7,10},{8,5},{9,4},{10,7},{11,6},{12,17},{13,16... | collective-permute-start | bytes 98312 | tf_op jit(solution)/shard_map/ppermute | solution.py:686
  14.9 3.4 %collective-permute-start.4 = (bf16[4,16,256]{2,1,0:T(8,128)(2,1)S(1)}, bf16[4,16,256]{2,1,0:T(8,128)(2,1)S(1)}, u32[]{:S(2)}, u32[]{:S(2)}) collective-permute-start(bf16[4,16,256]{2,1,0:T(8,128)(2,1)S(1)} %get-tuple-element.74), channel_id=1, source_target_pairs={{5,10},{6,9},{9,6},{10,5},{13,18},{14,17},{17,14},{18,13},{21,26},... | collective-permute-start | bytes 98312 | tf_op jit(solution)/shard_map/ppermute | solution.py:686
  15.6 2.5 %copy-start.1 = (bf16[4,8,40,256]{3,2,1,0:T(8,128)(2,1)S(1)}, bf16[4,8,40,256]{3,2,1,0:T(8,128)(2,1)}, u32[]{:S(2)}) copy-start(bf16[4,8,40,256]{3,2,1,0:T(8,128)(2,1)} %cot_far.1) | copy-start | bytes 1966084
  18.1 3.7 %copy-start = (bf16[2304,256]{1,0:T(8,128)(2,1)}, bf16[2304,256]{1,0:T(8,128)(2,1)S(1)}, u32[]{:S(2)}) copy-start(bf16[2304,256]{1,0:T(8,128)(2,1)S(1)} %get-tuple-element.80.w.w_far) | copy-start | bytes 3538948
  18.4 1.8 %collective-permute-start.5 = (bf16[4,4,48,256]{3,2,1,0:T(8,128)(2,1)S(1)}, bf16[4,4,48,256]{3,2,1,0:T(8,128)(2,1)S(1)}, u32[]{:S(2)}, u32[]{:S(2)}) collective-permute-start(bf16[4,4,48,256]{3,2,1,0:T(8,128)(2,1)S(1)} %get-tuple-element.76), channel_id=1, source_target_pairs={{0,4},{4,0},{8,12},{12,8},{16,20},{20,16},{24,28},{28,24},{1,5},{5... | collective-permute-start | bytes 1179656 | tf_op jit(solution)/shard_map/ppermute | solution.py:670
  20.2 13.3 %copy-start.4 = (f32[4,256]{1,0:T(4,128)S(1)}, f32[4,256]{1,0:T(4,128)}, u32[]{:S(2)}) copy-start(f32[4,256]{1,0:T(4,128)} %params.9) | copy-start | bytes 12292
  48.4 3.9 %collective-permute-start.6 = (f32[9,128,256]{2,1,0:T(8,128)S(1)}, f32[9,128,256]{2,1,0:T(8,128)S(1)}, u32[]{:S(2)}, u32[]{:S(2)}) collective-permute-start(f32[9,128,256]{2,1,0:T(8,128)S(1)} %get-tuple-element.95), channel_id=1, source_target_pairs={{0,4},{4,0},{8,12},{12,8},{16,20},{20,16},{24,28},{28,24},{1,5},{5... | collective-permute-start | bytes 3538952 | tf_op jit(solution)/shard_map/ppermute | solution.py:670
  53.0 10.5 %collective-permute-start.7 = (bf16[32,40,128]{2,1,0:T(8,128)(2,1)S(1)}, bf16[32,40,128]{2,1,0:T(8,128)(2,1)S(1)}, u32[]{:S(2)}, u32[]{:S(2)}) collective-permute-start(bf16[32,40,128]{2,1,0:T(8,128)(2,1)S(1)} %get-tuple-element.104), channel_id=1, source_target_pairs={{0,8},{4,12},{8,0},{12,4},{16,24},{20,28},{24,16},{28,20},{1,9},{5... | collective-permute-start | bytes 983048 | tf_op jit(solution)/shard_map/ppermute | solution.py:830
  65.1 2.3 %collective-permute-start.10 = (bf16[2304,128]{1,0:T(8,128)(2,1)S(1)}, bf16[2304,128]{1,0:T(8,128)(2,1)S(1)}, u32[]{:S(2)}, u32[]{:S(2)}) collective-permute-start(bf16[2304,128]{1,0:T(8,128)(2,1)S(1)} %get-tuple-element.112), channel_id=1, source_target_pairs={{0,4},{4,0},{8,12},{12,8},{16,20},{20,16},{24,28},{28,24},{1,5},{5... | collective-permute-start | bytes 1769480 | tf_op jit(solution)/shard_map/ppermute | solution.py:670
  68.4 12.8 %copy-start.5 = (s32[4,8,40]{2,1,0:T(8,128)S(1)}, s32[4,8,40]{2,1,0:T(8,128)}, u32[]{:S(2)}) copy-start(s32[4,8,40]{2,1,0:T(8,128)} %occ.1) | copy-start | bytes 15364
  68.4 26.4 %all-to-all-start.3 = ((bf16[32,112,128]{2,1,0:T(8,128)(2,1)}), bf16[32,112,128]{2,1,0:T(8,128)(2,1)S(1)}, u32[]{:S(2)}, u32[]{:S(2)}) async-start(bf16[32,112,128]{2,1,0:T(8,128)(2,1)} %shard_map.181), calls=%async_computation.3 | async-start | bytes 1835008 | tf_op jit(solution)/shard_map/all_to_all | solution.py:698
  71.1 4.6 %collective-permute-start.8 = (bf16[4,1,48,256]{3,2,1,0:T(8,128)(2,1)S(1)}, bf16[4,1,48,256]{3,2,1,0:T(8,128)(2,1)S(1)}, u32[]{:S(2)}, u32[]{:S(2)}) collective-permute-start(bf16[4,1,48,256]{3,2,1,0:T(8,128)(2,1)S(1)} %get-tuple-element.109), channel_id=1, source_target_pairs={{0,4},{4,0},{8,12},{12,8},{16,20},{20,16},{24,28},{28,24},{1,5},{5... | collective-permute-start | bytes 294920 | tf_op jit(solution)/shard_map/ppermute | solution.py:670
  71.5 9.7 %collective-permute-start.9 = (bf16[4,1,48,256]{3,2,1,0:T(8,128)(2,1)S(1)}, bf16[4,1,48,256]{3,2,1,0:T(8,128)(2,1)S(1)}, u32[]{:S(2)}, u32[]{:S(2)}) collective-permute-start(bf16[4,1,48,256]{3,2,1,0:T(8,128)(2,1)S(1)} %get-tuple-element.110), channel_id=1, source_target_pairs={{4,8},{8,4},{12,16},{16,12},{20,24},{24,20},{5,9},{9,5},{13,17},{1... | collective-permute-start | bytes 294920 | tf_op jit(solution)/shard_map/ppermute | solution.py:670
  81.3 13.5 %copy-start.2 = (f32[2,18432]{1,0:T(2,128)S(1)}, f32[2,18432]{1,0:T(2,128)}, u32[]{:S(2)}) copy-start(f32[2,18432]{1,0:T(2,128)} %param.13) | copy-start | bytes 442372
  81.3 13.5 %copy-start.3 = (f32[2,18432]{1,0:T(2,128)S(1)}, f32[2,18432]{1,0:T(2,128)}, u32[]{:S(2)}) copy-start(f32[2,18432]{1,0:T(2,128)} %param.14) | copy-start | bytes 442372
  81.3 13.5 %copy-start.6 = (f32[4,256]{1,0:T(4,128)S(1)}, f32[4,256]{1,0:T(4,128)}, u32[]{:S(2)}) copy-start(f32[4,256]{1,0:T(4,128)} %n_first.1) | copy-start | bytes 12292
  81.3 13.5 %copy-start.7 = (f32[4,256]{1,0:T(4,128)S(1)}, f32[4,256]{1,0:T(4,128)}, u32[]{:S(2)}) copy-start(f32[4,256]{1,0:T(4,128)} %n_second.1) | copy-start | bytes 12292

commit v6 on v5

--- a/solution.py
+++ b/solution.py
@@ -313,6 +313,11 @@
     to_all(st_ref, [jnp.sum(s1, 0, keepdims=True), jnp.sum(s2, 0, keepdims=True)])
 
 
+def typical_hidden(params):
+    scale, shift = params[0:1], params[1:2]
+    return 0.5 * (shift + jnp.sqrt(shift * shift + 0.64 * scale * scale))
+
+
 def stats_of(total, count):
     mean = total[0:1] / count
     var = total[1:2] / count - mean * mean
@@ -356,7 +361,7 @@
     dt_ref[:, s * span : (s + 1) * span] = jnp.where(inside, block, jnp.zeros_like(block)).T
 
 
-def kernel_gradient(g, core, field, rows_field, first_row, dt_ref, keep, send, first, prepare):
+def kernel_gradient(g, core, field, rows_field, first_row, dt_ref, keep, send, first, prepare, adjust=None):
     chans, half = g.c, g.c // 2
     span = g.h * g.wp
     mine = pl.ds(pl.multiple_of(core * half, half), half)
@@ -380,13 +385,17 @@
                     first[a * 3 + b] = acc[half:, b * chans : (b + 1) * chans]
                 continue
             for b in range(3):
-                keep[a * 3 + b] += acc[0:half, b * chans : (b + 1) * chans]
+                own_half = keep[a * 3 + b] + acc[0:half, b * chans : (b + 1) * chans]
                 other_half = first[a * 3 + b] + acc[half:, b * chans : (b + 1) * chans]
+                if adjust is not None:
+                    own_half = own_half - adjust(a * 3 + b, mine)
+                    other_half = other_half - adjust(a * 3 + b, other)
+                keep[a * 3 + b] = own_half
                 send[a * 3 + b] = other_half
 
 
 def second_gradient_kernel(
-    g, count, z2, st, params, cot, cot_next, h, d_ref, keep, send, dt_ref
+    g, count, z2, st, params, cot, cot_next, h, d_ref, keep, send, sums_ref, dt_ref, columns
 ):
     place = Place()
     rows = g.cot_tall
@@ -398,16 +407,53 @@
     k1 = k0 * (sum_dn / count)
     k2 = k0 * rstd * (sum_dx / count)
     edge = edge_mask(place, g)
+    added = [[None] * 3 for _ in range(g.h)]
+
     def prepare(s):
         for i in range(rows):
             rim = not g.near <= i < g.near + g.h
             dn = wide(cot_next, s, 0 if i < g.near else 1) if rim else wide(cot, s, i - g.near)
             start = (s * rows + i) * g.wp
             d = k0 * dn - k1 - (z2[start : start + g.wp, :] - mean) * k2
-            d = in_grid(d, i + RIM - g.near, g, place, edge)
-            d_ref[start : start + g.wp, :] = d.astype(BF16)
+            d = in_grid(d, i + RIM - g.near, g, place, edge).astype(BF16)
+            d_ref[start : start + g.wp, :] = d
+            if not rim:
+                row = d.astype(F32)[: g.w]
+                parts = sum_rows(row), row[:8], row[g.w - 8 :]
+                r = i - g.near
+                added[r] = [v if u is None else u + v for u, v in zip(added[r], parts, strict=True)]
         own_transposed(g, d_ref, (s * rows + g.near) * g.wp, s, dt_ref)
-    kernel_gradient(g, place.core, h, g.tall - 2, RIM - 2, dt_ref, keep, send, send, prepare)
+        if s == g.s - 1:
+            tap_sums()
+
+    def tap_sums():
+        found = [[None] * 3 for _ in range(3)]
+        for b in range(3):
+            line = []
+            for r in range(g.h):
+                value = jnp.sum(added[r][0], axis=0, keepdims=True)
+                if b == 0:
+                    value = value - (1.0 - place.left) * added[r][1][:1]
+                if b == 2:
+                    value = value - (1.0 - place.right) * added[r][2][7:]
+                line.append(value)
+            every = functools.reduce(lambda u, v: u + v, line)
+            found[0][b] = every - (1.0 - place.above) * line[0]
+            found[1][b] = every
+            found[2][b] = every - (1.0 - place.below) * line[-1]
+        table = jnp.concatenate(sum(found, []) + [jnp.zeros((7, g.c), F32)], axis=0)
+        sums_ref[...] = table
+        spare = jnp.zeros((columns.shape[1] - 16, g.c), F32)
+        columns[...] = jnp.concatenate([table, spare], axis=0).T
+
+    typical = typical_hidden(params)
+
+    def adjust(tap, rows):
+        return columns[rows, tap : tap + 1] * typical
+
+    kernel_gradient(
+        g, place.core, h, g.tall - 2, RIM - 2, dt_ref, keep, send, send, prepare, adjust
+    )
 
 
 def transposed_conv(g, d_ref, w, s, rows_in, r, chunk):
@@ -426,7 +472,7 @@
 
 
 def hidden_gradient_kernel(
-    g, chunk, count, d, w, z1, z2, st, st2, params, ext, dn_ref, st_ref, out_ref, d_ref
+    g, chunk, count, d, w, z1, z2, st, st2, params, ext, sums, dn_ref, st_ref, out_ref, d_ref
 ):
     mean2, rstd2 = stats_of(total_of(st2), count)
     scale2 = params[2:3] * rstd2
@@ -456,7 +502,15 @@
                     v = dn[i * g.wp : i * g.wp + g.w]
                     s0 = s0 + sum_rows(v)
                     s1 = s1 + sum_rows(v * (z[i * g.wp : i * g.wp + g.w] - mean))
-    to_all(st_ref, [jnp.sum(s0, 0, keepdims=True), jnp.sum(s1, 0, keepdims=True) * rstd])
+    own = [jnp.sum(s0, 0, keepdims=True), jnp.sum(s1, 0, keepdims=True) * rstd]
+    devices, count, _ = st_ref.shape
+    if count == 2:
+        to_all(st_ref, own)
+    else:
+        share = 9 * g.c // devices
+        for i in range(devices):
+            taps = i * share // g.c, (i * share + share - 1) // g.c
+            st_ref[i] = jnp.concatenate(own + [sums[t : t + 1] for t in taps], axis=0)
 
 
 def half_gradient(g, which, field, rows_field, first_row, dt_ref, out_ref, sums, prepare=None):
@@ -620,7 +674,7 @@
 
 def update_kernel(
     count, parts, w, first_m, second_m, st2, st3, params, n_first, n_second,
-    grad_out, w_out, first_out, second_out, n_grad, n_out, n_first_out, n_second_out
+    grad_out, w_out, first_out, second_out, n_grad, n_out, n_first_out, n_second_out, typical_rows
 ):
     devices, ncols = parts.shape[0], lax.axis_size("cols")
     share = w.shape[0] // 4
@@ -644,17 +698,28 @@
 
     grads = []
     every = slice(None)
+    if parts.shape[2] != 256:
+        chans = params.shape[1]
+        column = jnp.broadcast_to(typical_hidden(params), (128, chans)).T
+        typical_rows[0:chans] = column
+        typical_rows[chans:] = column
+        first_typical = pl.multiple_of(Place().index * share % chans, 8)
+        wrap = chans - first_typical
+        place_rows = lax.broadcasted_iota(jnp.int32, (share, 128), 0)
     for half in range(2):
         if parts.shape[2] == 256:
             for k in range(2):
                 lanes = slice(k * 128, (k + 1) * 128)
                 grads.append((k, half, over(lambda row: row % 2 == half, every, lanes)))
         else:
-            rows = half_rows(share)
-            first = over(lambda row: row % 2 == half, slice(0, share), every)
+            grads.append((0, half, over(lambda row: row % 2 == half, slice(0, share), every)))
+            size = half_rows(share)
             upper = over(lambda row: row % 4 == half, slice(share, None), every)
-            lower = over(lambda row: row % 4 == half + 2, slice(2 * rows, None), every)
-            grads += [(0, half, first), (1, half, jnp.concatenate([upper, lower], axis=0))]
+            lower = over(lambda row: row % 4 == half + 2, slice(2 * size, None), every)
+            lanes = slice(half * 128, (half + 1) * 128)
+            sums = jnp.where(place_rows < wrap, total3[2:3, lanes], total3[3:4, lanes])
+            back = typical_rows[pl.ds(first_typical, share), :] * sums
+            grads.append((1, half, jnp.concatenate([upper, lower], axis=0) + back))
     for k, half, grad in grads:
         at = pl.ds(2 * half + k, share, stride=4)
         new = adamw(w[at, :], grad, first_m[at, :], second_m[at, :], 0.02)
@@ -798,25 +863,25 @@
     )(z1, st1, norm_scale_bias, w2, cot_ext)
     st2 = exchange(st)
     grad_shape = held((9, chans // 2, chans), F32)
-    d, keep2, send2 = kernel_call(
+    nrows = lax.axis_size("rows")
+    cut_again = nrows % 4 == 0 and taps // devices % 8 == 0
+    d, keep2, send2, sums = kernel_call(
         functools.partial(second_gradient_kernel, g, count),
-        [held((n2, chans), BF16), grad_shape, grad_shape],
+        [held((n2, chans), BF16), grad_shape, grad_shape, held((16, chans), F32)],
         conv_flops(own_pixels),
-        scratch=[pltpu.VMEM((chans, own_pixels), BF16)],
+        scratch=[pltpu.VMEM((chans, own_pixels), BF16), pltpu.VMEM((chans, 128), F32)],
     )(z2, st2, norm_scale_bias, cot_ext, cot_next, h)
     got2 = swapped(send2, "rows", 0)
     dn1, st, block_out = kernel_call(
         functools.partial(hidden_gradient_kernel, g, 8, count),
         [
             held((n3, chans), F32),
-            shape_of((devices, 2, chans), F32),
+            shape_of((devices, 4 if cut_again else 2, chans), F32),
             held(features.shape, BF16),
         ],
         conv_flops(n3),
         scratch=[pltpu.VMEM((n2, 3 * chans), BF16)],
-    )(d, w2, z1, z2, st1, st2, norm_scale_bias, ext)
-    nrows = lax.axis_size("rows")
-    cut_again = nrows % 4 == 0 and taps // devices % 8 == 0
+    )(d, w2, z1, z2, st1, st2, norm_scale_bias, ext, sums)
     if cut_again:
         got2, st = lax.optimization_barrier((got2, st))
         kept_shape = (devices, half_rows(taps // devices), chans // 2)
@@ -904,6 +969,7 @@
         functools.partial(update_kernel, count),
         [chunk_shape] * 4 + [norm_shape] * 4,
         1e8,
+        scratch=[pltpu.VMEM((2 * chans, 128), F32)],
     )(
         parts, own_weights, to_chunks(conv_first), to_chunks(conv_second), st2, st3,
         norm_scale_bias, norm_first, norm_second,

time: 96.3 us -> 97.3 us (1.010)
  no operation moved by 1% of the time
where the time goes in v6:
time: 97.3 us; the launch traced here: 96.8 us
  blocking collectives  32 us (33%)
  Pallas kernels  25.8 us (27%)
  starting transfers between devices  22.3 us (23%)
  waiting for transfers between devices  14 us (14%)
  local copies, waits for them, and re-layouts  1.8 us (2%)
    all_to_all x3, blocking collectives, exchange(): return lax.all_to_all(parts, BOTH, 0, 0, tiled=True)  32 us
    pallas_call x15, Pallas kernels, call(): pl.pallas_call(body, out_shape=out_shape, in_specs=specs, out_specs=[pl.B...  25.8 us
    ppermute x8, starting transfers between devices, swapped(): return lax.ppermute(block, axis, pairs)  12.4 us
    all_to_all x1, waiting for transfers between devices, exchange(): return lax.all_to_all(parts, BOTH, 0, 0, tiled=True)  7.91 us
    ppermute x2, starting transfers between devices, swapped_both(): return lax.ppermute(block, BOTH, pairs)  6.69 us
    ppermute x8, waiting for transfers between devices, swapped(): return lax.ppermute(block, axis, pairs)  6.13 us
    all_to_all x1, starting transfers between devices, exchange(): return lax.all_to_all(parts, BOTH, 0, 0, tiled=True)  2.63 us
  transfers between devices with their start and end apart: 12, of which 4 were waited for; matrix products, arithmetic and copies ran while one was open for 2% of the time, Pallas kernels for 13%

profile of v6, /device:TPU:1, one launch (start us, length us, event | category | flops | bytes accessed | tf_op | source)
XLA Modules:
  0.0 96.8 jit_solution(15719889872954340091)
XLA Ops:
  0.6 1.7 %shard_map.168 = (bf16[4,8,40,256]{3,2,1,0:T(8,128)(2,1)S(1)}, bf16[4,48,256]{2,1,0:T(8,128)(2,1)S(1)}, bf16[4,48,256]{2,1,0:T(8,128)(2,1)S(1)}, bf16[4,4,40,256...) custom-call(bf16[4,8,40,256]{3,2,1,0:T(8,128)(2,1)} %features.1, ...), custom_call_target="tpu_custom_call" | custom-call | flops 100000000 | bytes 4194304 | tf_op jit(solution)/shard_map/pallas_call | solution.py:41
  2.4 4.5 %collective-permute-start.2 = (bf16[4,4,40,256]{3,2,1,0:T(8,128)(2,1)S(1)}, bf16[4,4,40,256]{3,2,1,0:T(8,128)(2,1)S(1)}, u32[]{:S(2)}, u32[]{:S(2)}) collective-permute-start(bf16[4,4,40,256]{3,2,1,0:T(8,128)(2,1)S(1)} %get-tuple-element.73), channel_id=1, source_target_pairs={{4,8},{8,4},{12,16},{16,12},{20,24},{24,20},{5,9},{9,5},{13,17},{1... | collective-permute-start | bytes 983048 | tf_op jit(solution)/shard_map/ppermute | solution.py:735
  6.9 1.4 %collective-permute-start = (bf16[4,48,256]{2,1,0:T(8,128)(2,1)S(1)}, bf16[4,48,256]{2,1,0:T(8,128)(2,1)S(1)}, u32[]{:S(2)}, u32[]{:S(2)}) collective-permute-start(bf16[4,48,256]{2,1,0:T(8,128)(2,1)S(1)} %get-tuple-element.69), channel_id=1, source_target_pairs={{0,1},{1,0},{2,3},{3,2},{4,5},{5,4},{6,7},{7,6},{8,9},{9,8},{10,11... | collective-permute-start | bytes 294920 | tf_op jit(solution)/shard_map/ppermute | solution.py:735
  8.2 0.7 collective-permute-start.1
  8.9 6.0 %collective-permute-start.3 = (bf16[4,16,256]{2,1,0:T(8,128)(2,1)S(1)}, bf16[4,16,256]{2,1,0:T(8,128)(2,1)S(1)}, u32[]{:S(2)}, u32[]{:S(2)}) collective-permute-start(bf16[4,16,256]{2,1,0:T(8,128)(2,1)S(1)} %get-tuple-element.74), channel_id=1, source_target_pairs={{4,9},{5,8},{6,11},{7,10},{8,5},{9,4},{10,7},{11,6},{12,17},{13,16... | collective-permute-start | bytes 98312 | tf_op jit(solution)/shard_map/ppermute | solution.py:751
  14.9 0.7 collective-permute-start.4
  15.6 0.0 copy-start.1
  15.6 2.5 %shard_map.170 = (bf16[2304,256]{1,0:T(8,128)(2,1)S(1)}, bf16[2304,256]{1,0:T(8,128)(2,1)S(1)}) custom-call(f32[9216,128]{1,0:T(8,128)} %bitcast.37), custom_call_target="tpu_custom_call" | custom-call | bytes 1024 | tf_op jit(solution)/shard_map/pallas_call | solution.py:41
  18.1 0.0 collective-permute-done.rc
  18.1 0.0 collective-permute-done.1.rd
  18.2 0.2 shard_map.169
  18.4 0.0 collective-permute-done.3.rb_c
  18.4 0.0 collective-permute-done.4.rb_d
  18.4 0.0 collective-permute-done.2.rb
  18.4 0.1 collective-permute-start.5
  18.5 1.6 %shard_map.171 = (f32[2304,256]{1,0:T(8,128)S(1)}, f32[16,256]{1,0:T(8,128)S(1)}, bf16[1920,768]{1,0:T(8,128)(2,1)S(1)}) custom-call(bf16[4,8,48,256]{3,2,1,0:T(8,128)(2,1)S(1)} %get-tuple-element.71.ext, bf16[2304,256]{1,0:T(8,128)(2,1)S(1)} %get-tuple-element.81.w.w_far), custom_call_target="tpu_custom_call" | custom-call | bytes 1024 | tf_op jit(solution)/shard_map/pallas_call | solution.py:41
  20.1 0.1 collective-permute-done.5.ra
  20.2 1.6 %shard_map.172 = (f32[2304,256]{1,0:T(8,128)S(1)}, f32[32,2,256]{2,1,0:T(2,128)S(1)}, bf16[1920,768]{1,0:T(8,128)(2,1)S(1)}, bf16[4,2,48,256]{3,2,1,0:T(8,128)(2,1)S(1)}) custom-call(bf16[4,8,48,256]{3,2,1,0:T(8,128)(2,1)S(1)} %get-tuple-element.71.ext, ...), custom_call_target="tpu_custom_call", output_to_operand_aliasing={{0}: (7, {}), {2}: (8, {})} | custom-call | bytes 1024 | tf_op jit(solution)/shard_map/pallas_call | solution.py:41
  21.9 11.7 %all_to_all.20.st = f32[32,2,256]{2,1,0:T(2,128)S(1)} all-to-all(f32[32,2,256]{2,1,0:T(2,128)S(1)} %get-tuple-element.86), channel_id=1, replica_groups=mesh['rows'=8,'cols'=4] {'rows','cols'}, dimensions={0} | all-to-all | bytes 131072 | tf_op jit(solution)/shard_map/all_to_all | solution.py:763
  33.5 2.8 %shard_map.173 = (bf16[2304,768]{1,0:T(8,128)(2,1)S(1)}, f32[1920,256]{1,0:T(8,128)S(1)}, f32[32,4,256]{2,1,0:T(4,128)S(1)}) custom-call(f32[2304,256]{1,0:T(8,128)S(1)} %get-tuple-element.85.z1.z, f32[32,2,256]{2,1,0:T(2,128)S(1)} %all_to_all.20.st, f32[4,256]{1,0:T(4,128)S(1)} %copy-done.4, bf16[2304,256]{1,0:T(8,128)(2,1)S(1)} %get-tuple-element.87.w, ...), custom_call_target="tpu_custom_call" | custom-call | flops 2264924160 | bytes 4194304 | tf_op jit(solution)/shard_map/pallas_call | solution.py:41
  36.3 9.7 %all_to_all.21.st.st2 = f32[32,4,256]{2,1,0:T(4,128)S(1)} all-to-all(f32[32,4,256]{2,1,0:T(4,128)S(1)} %get-tuple-element.90), channel_id=1, replica_groups=mesh['rows'=8,'cols'=4] {'rows','cols'}, dimensions={0} | all-to-all | bytes 262144 | tf_op jit(solution)/shard_map/all_to_all | solution.py:763
  46.0 2.6 %shard_map.174 = (bf16[1920,256]{1,0:T(8,128)(2,1)S(1)}, f32[9,128,256]{2,1,0:T(8,128)S(1)}, f32[9,128,256]{2,1,0:T(8,128)S(1)}, f32[16,256]{1,0:T(8,128)S(1)}) custom-call(f32[1920,256]{1,0:T(8,128)S(1)} %get-tuple-element.89.z2, f32[32,4,256]{2,1,0:T(4,128)S(1)} %all_to_all.21.st.st2, f32[4,256]{1,0:T(4,128)S(1)} %copy-done.4, ...), custom_call_target="tpu_custom_call" | custom-call | flops 1811939328 | bytes 4194304 | tf_op jit(solution)/shard_map/pallas_call | solution.py:41
  48.6 1.4 %collective-permute-start.6 = (f32[9,128,256]{2,1,0:T(8,128)S(1)}, f32[9,128,256]{2,1,0:T(8,128)S(1)}, u32[]{:S(2)}, u32[]{:S(2)}) collective-permute-start(f32[9,128,256]{2,1,0:T(8,128)S(1)} %get-tuple-element.97), channel_id=1, source_target_pairs={{0,4},{4,0},{8,12},{12,8},{16,20},{20,16},{24,28},{28,24},{1,5},{5... | collective-permute-start | bytes 3538952 | tf_op jit(solution)/shard_map/ppermute | solution.py:735
  50.1 2.5 %shard_map.175 = (f32[1536,256]{1,0:T(8,128)S(1)}, f32[32,4,256]{2,1,0:T(4,128)S(1)}, bf16[4,8,40,256]{3,2,1,0:T(8,128)(2,1)S(1)}) custom-call(bf16[1920,256]{1,0:T(8,128)(2,1)S(1)} %get-tuple-element.93.d, bf16[2304,256]{1,0:T(8,128)(2,1)S(1)} %get-tuple-element.87.w, f32[2304,256]{1,0:T(8,128)S(1)} %get-tuple-element.85.z1.z, ...), custom_call_target="tpu_custom_call" | custom-call | flops 1811939328 | bytes 4194304 | tf_op jit(solution)/shard_map/pallas_call | solution.py:41
  52.6 0.0 collective-permute-done.6.got
  52.6 0.6 shard_map.176
  53.2 0.6 collective-permute-start.7
  53.8 10.7 %all_to_all.22.st3 = f32[32,4,256]{2,1,0:T(4,128)S(1)} all-to-all(f32[32,4,256]{2,1,0:T(4,128)S(1)} %get-tuple-element.104), channel_id=1, replica_groups=mesh['rows'=8,'cols'=4] {'rows','cols'}, dimensions={0} | all-to-all | bytes 262144 | tf_op jit(solution)/shard_map/all_to_all | solution.py:763
  64.4 0.0 collective-permute-done.7.came
  64.4 0.1 shard_map.177.kept
  64.5 1.6 %shard_map.178 = (bf16[1536,256]{1,0:T(8,128)(2,1)S(1)}, bf16[4,1,48,256]{3,2,1,0:T(8,128)(2,1)S(1)}, bf16[4,1,48,256]{3,2,1,0:T(8,128)(2,1)S(1)}, bf16[2304,128]{1,0:T(8,128)(2,1)S(1)}, bf16[256,1536]{1,0:T(8,128)(2,1)S(1)}) custom-call(f32[1536,256]{1,0:T(8,128)S(1)} %get-tuple-element.107.dn, f32[2304,256]{1,0:T(8,128)S(1)} %get-tuple-element.85.z1.z, ...), custom_call_target="tpu_custom_call" | custom-call | bytes 1024 | tf_op jit(solution)/shard_map/pallas_call | solution.py:41
  66.1 0.6 collective-permute-start.10
  66.7 1.2 %shard_map.180.keep = f32[2304,128]{1,0:T(8,128)S(1)} custom-call(bf16[1920,768]{1,0:T(8,128)(2,1)S(1)} %get-tuple-element.109.x, bf16[256,1536]{1,0:T(8,128)(2,1)S(1)} %get-tuple-element.113.dt_ref), custom_call_target="tpu_custom_call" | custom-call | bytes 1024 | tf_op jit(solution)/shard_map/pallas_call | solution.py:41
  67.9 0.4 collective-permute-done.10.got
  68.3 1.0 %shard_map.181 = bf16[32,112,128]{2,1,0:T(8,128)(2,1)} custom-call(f32[2304,128]{1,0:T(8,128)S(1)} %shard_map.180.keep, bf16[2304,128]{1,0:T(8,128)(2,1)S(1)} %collective-permute-done.10.got, f32[32,40,128]{2,1,0:T(8,128)S(1)} %shard_map.177.kept), custom_call_target="tpu_custom_call" | custom-call | flops 1000000000 | bytes 4194304 | tf_op jit(solution)/shard_map/pallas_call | solution.py:41
  69.3 0.0 copy-start.5
  69.3 2.6 %all-to-all-start.3 = ((bf16[32,112,128]{2,1,0:T(8,128)(2,1)}), bf16[32,112,128]{2,1,0:T(8,128)(2,1)S(1)}, u32[]{:S(2)}, u32[]{:S(2)}) async-start(bf16[32,112,128]{2,1,0:T(8,128)(2,1)} %shard_map.181), calls=%async_computation.3 | async-start | bytes 1835008 | tf_op jit(solution)/shard_map/all_to_all | solution.py:763
  72.0 0.5 collective-permute-start.8
  72.4 3.3 %collective-permute-start.9 = (bf16[4,1,48,256]{3,2,1,0:T(8,128)(2,1)S(1)}, bf16[4,1,48,256]{3,2,1,0:T(8,128)(2,1)S(1)}, u32[]{:S(2)}, u32[]{:S(2)}) collective-permute-start(bf16[4,1,48,256]{3,2,1,0:T(8,128)(2,1)S(1)} %get-tuple-element.112), channel_id=1, source_target_pairs={{4,8},{8,4},{12,16},{16,12},{20,24},{24,20},{5,9},{9,5},{13,17},{1... | collective-permute-start | bytes 294920 | tf_op jit(solution)/shard_map/ppermute | solution.py:735
  75.7 0.8 copy.30
  76.6 0.0 collective-permute-done.8.ra
  76.6 5.6 %collective-permute-done.9.rb = bf16[4,1,48,256]{3,2,1,0:T(8,128)(2,1)S(1)} collective-permute-done((bf16[4,1,48,256]{3,2,1,0:T(8,128)(2,1)S(1)}, bf16[4,1,48,256]{3,2,1,0:T(8,128)(2,1)S(1)}, u32[]{:S(2)}, u32[]{:S(2)}) %collective-permute-start.9) | collective-permute-done | bytes 98336 | tf_op jit(solution)/shard_map/ppermute | solution.py:735
  82.2 0.0 copy-start.7
  82.2 4.7 %shard_map.179 = f32[4,8,40,256]{3,2,1,0:T(8,128)} custom-call(bf16[1536,256]{1,0:T(8,128)(2,1)S(1)} %get-tuple-element.110.e, bf16[4,1,48,256]{3,2,1,0:T(8,128)(2,1)S(1)} %collective-permute-done.8.ra, bf16[4,1,48,256]{3,2,1,0:T(8,128)(2,1)S(1)} %collective-permute-done.9.rb, bf16[2304,256]{1,0:T(8,128)(2,1)} %copy-done, bf16[4,8,40,256]{3,2,1,0:T(8,128)(2,1)} %cot_far.1, ...), custom_call_target="tpu_custom_call" | custom-call | flops 1811939328 | bytes 4194304 | tf_op jit(solution)/shard_map/pallas_call | solution.py:41
  86.8 0.9 constant_dynamic-slice_fusion.w
  87.8 7.9 %all-to-all-done.3.parts = bf16[32,112,128]{2,1,0:T(8,128)(2,1)S(1)} async-done(((bf16[32,112,128]{2,1,0:T(8,128)(2,1)}), bf16[32,112,128]{2,1,0:T(8,128)(2,1)S(1)}, u32[]{:S(2)}, u32[]{:S(2)}) %all-to-all-start.3) | async-done | bytes 917536 | tf_op jit(solution)/shard_map/all_to_all | solution.py:763
  95.7 0.0 copy-done.3
  95.7 1.1 %shard_map.182 = (f32[288,128]{1,0:T(8,128)}, f32[288,128]{1,0:T(8,128)}, f32[288,128]{1,0:T(8,128)}, f32[288,128]{1,0:T(8,128)}, f32[4,256]{1,0:T(4,128)}, /*in...) custom-call(bf16[32,112,128]{2,1,0:T(8,128)(2,1)S(1)} %all-to-all-done.3.parts, ...), custom_call_target="tpu_custom_call" | custom-call | flops 100000000 | bytes 4194304 | tf_op jit(solution)/shard_map/pallas_call | solution.py:41
  (12 shorter events, 0.0 us)
Async XLA Ops:
  2.4 16.0 %collective-permute-start.2 = (bf16[4,4,40,256]{3,2,1,0:T(8,128)(2,1)S(1)}, bf16[4,4,40,256]{3,2,1,0:T(8,128)(2,1)S(1)}, u32[]{:S(2)}, u32[]{:S(2)}) collective-permute-start(bf16[4,4,40,256]{3,2,1,0:T(8,128)(2,1)S(1)} %get-tuple-element.73), channel_id=1, source_target_pairs={{4,8},{8,4},{12,16},{16,12},{20,24},{24,20},{5,9},{9,5},{13,17},{1... | collective-permute-start | bytes 983048 | tf_op jit(solution)/shard_map/ppermute | solution.py:735
  6.9 11.3 %collective-permute-start = (bf16[4,48,256]{2,1,0:T(8,128)(2,1)S(1)}, bf16[4,48,256]{2,1,0:T(8,128)(2,1)S(1)}, u32[]{:S(2)}, u32[]{:S(2)}) collective-permute-start(bf16[4,48,256]{2,1,0:T(8,128)(2,1)S(1)} %get-tuple-element.69), channel_id=1, source_target_pairs={{0,1},{1,0},{2,3},{3,2},{4,5},{5,4},{6,7},{7,6},{8,9},{9,8},{10,11... | collective-permute-start | bytes 294920 | tf_op jit(solution)/shard_map/ppermute | solution.py:735
  8.2 9.9 %collective-permute-start.1 = (bf16[4,48,256]{2,1,0:T(8,128)(2,1)S(1)}, bf16[4,48,256]{2,1,0:T(8,128)(2,1)S(1)}, u32[]{:S(2)}, u32[]{:S(2)}) collective-permute-start(bf16[4,48,256]{2,1,0:T(8,128)(2,1)S(1)} %get-tuple-element.70), channel_id=1, source_target_pairs={{1,2},{2,1},{5,6},{6,5},{9,10},{10,9},{13,14},{14,13},{17,18},{18,... | collective-permute-start | bytes 294920 | tf_op jit(solution)/shard_map/ppermute | solution.py:735
  8.9 9.5 %collective-permute-start.3 = (bf16[4,16,256]{2,1,0:T(8,128)(2,1)S(1)}, bf16[4,16,256]{2,1,0:T(8,128)(2,1)S(1)}, u32[]{:S(2)}, u32[]{:S(2)}) collective-permute-start(bf16[4,16,256]{2,1,0:T(8,128)(2,1)S(1)} %get-tuple-element.74), channel_id=1, source_target_pairs={{4,9},{5,8},{6,11},{7,10},{8,5},{9,4},{10,7},{11,6},{12,17},{13,16... | collective-permute-start | bytes 98312 | tf_op jit(solution)/shard_map/ppermute | solution.py:751
  14.9 3.4 %collective-permute-start.4 = (bf16[4,16,256]{2,1,0:T(8,128)(2,1)S(1)}, bf16[4,16,256]{2,1,0:T(8,128)(2,1)S(1)}, u32[]{:S(2)}, u32[]{:S(2)}) collective-permute-start(bf16[4,16,256]{2,1,0:T(8,128)(2,1)S(1)} %get-tuple-element.75), channel_id=1, source_target_pairs={{5,10},{6,9},{9,6},{10,5},{13,18},{14,17},{17,14},{18,13},{21,26},... | collective-permute-start | bytes 98312 | tf_op jit(solution)/shard_map/ppermute | solution.py:751
  15.6 2.5 %copy-start.1 = (bf16[4,8,40,256]{3,2,1,0:T(8,128)(2,1)S(1)}, bf16[4,8,40,256]{3,2,1,0:T(8,128)(2,1)}, u32[]{:S(2)}) copy-start(bf16[4,8,40,256]{3,2,1,0:T(8,128)(2,1)} %cot_far.1) | copy-start | bytes 1966084
  18.1 3.7 %copy-start = (bf16[2304,256]{1,0:T(8,128)(2,1)}, bf16[2304,256]{1,0:T(8,128)(2,1)S(1)}, u32[]{:S(2)}) copy-start(bf16[2304,256]{1,0:T(8,128)(2,1)S(1)} %get-tuple-element.81.w.w_far) | copy-start | bytes 3538948
  18.4 1.8 %collective-permute-start.5 = (bf16[4,4,48,256]{3,2,1,0:T(8,128)(2,1)S(1)}, bf16[4,4,48,256]{3,2,1,0:T(8,128)(2,1)S(1)}, u32[]{:S(2)}, u32[]{:S(2)}) collective-permute-start(bf16[4,4,48,256]{3,2,1,0:T(8,128)(2,1)S(1)} %get-tuple-element.77), channel_id=1, source_target_pairs={{0,4},{4,0},{8,12},{12,8},{16,20},{20,16},{24,28},{28,24},{1,5},{5... | collective-permute-start | bytes 1179656 | tf_op jit(solution)/shard_map/ppermute | solution.py:735
  20.2 13.3 %copy-start.4 = (f32[4,256]{1,0:T(4,128)S(1)}, f32[4,256]{1,0:T(4,128)}, u32[]{:S(2)}) copy-start(f32[4,256]{1,0:T(4,128)} %params.9) | copy-start | bytes 12292
  48.6 3.9 %collective-permute-start.6 = (f32[9,128,256]{2,1,0:T(8,128)S(1)}, f32[9,128,256]{2,1,0:T(8,128)S(1)}, u32[]{:S(2)}, u32[]{:S(2)}) collective-permute-start(f32[9,128,256]{2,1,0:T(8,128)S(1)} %get-tuple-element.97), channel_id=1, source_target_pairs={{0,4},{4,0},{8,12},{12,8},{16,20},{20,16},{24,28},{28,24},{1,5},{5... | collective-permute-start | bytes 3538952 | tf_op jit(solution)/shard_map/ppermute | solution.py:735
  53.2 11.2 %collective-permute-start.7 = (bf16[32,40,128]{2,1,0:T(8,128)(2,1)S(1)}, bf16[32,40,128]{2,1,0:T(8,128)(2,1)S(1)}, u32[]{:S(2)}, u32[]{:S(2)}) collective-permute-start(bf16[32,40,128]{2,1,0:T(8,128)(2,1)S(1)} %get-tuple-element.106), channel_id=1, source_target_pairs={{0,8},{4,12},{8,0},{12,4},{16,24},{20,28},{24,16},{28,20},{1,9},{5... | collective-permute-start | bytes 983048 | tf_op jit(solution)/shard_map/ppermute | solution.py:895
  66.1 2.2 %collective-permute-start.10 = (bf16[2304,128]{1,0:T(8,128)(2,1)S(1)}, bf16[2304,128]{1,0:T(8,128)(2,1)S(1)}, u32[]{:S(2)}, u32[]{:S(2)}) collective-permute-start(bf16[2304,128]{1,0:T(8,128)(2,1)S(1)} %get-tuple-element.114), channel_id=1, source_target_pairs={{0,4},{4,0},{8,12},{12,8},{16,20},{20,16},{24,28},{28,24},{1,5},{5... | collective-permute-start | bytes 1769480 | tf_op jit(solution)/shard_map/ppermute | solution.py:735
  69.3 12.8 %copy-start.5 = (s32[4,8,40]{2,1,0:T(8,128)S(1)}, s32[4,8,40]{2,1,0:T(8,128)}, u32[]{:S(2)}) copy-start(s32[4,8,40]{2,1,0:T(8,128)} %occ.1) | copy-start | bytes 15364
  69.3 26.4 %all-to-all-start.3 = ((bf16[32,112,128]{2,1,0:T(8,128)(2,1)}), bf16[32,112,128]{2,1,0:T(8,128)(2,1)S(1)}, u32[]{:S(2)}, u32[]{:S(2)}) async-start(bf16[32,112,128]{2,1,0:T(8,128)(2,1)} %shard_map.181), calls=%async_computation.3 | async-start | bytes 1835008 | tf_op jit(solution)/shard_map/all_to_all | solution.py:763
  72.0 4.6 %collective-permute-start.8 = (bf16[4,1,48,256]{3,2,1,0:T(8,128)(2,1)S(1)}, bf16[4,1,48,256]{3,2,1,0:T(8,128)(2,1)S(1)}, u32[]{:S(2)}, u32[]{:S(2)}) collective-permute-start(bf16[4,1,48,256]{3,2,1,0:T(8,128)(2,1)S(1)} %get-tuple-element.111), channel_id=1, source_target_pairs={{0,4},{4,0},{8,12},{12,8},{16,20},{20,16},{24,28},{28,24},{1,5},{5... | collective-permute-start | bytes 294920 | tf_op jit(solution)/shard_map/ppermute | solution.py:735
  72.4 9.7 %collective-permute-start.9 = (bf16[4,1,48,256]{3,2,1,0:T(8,128)(2,1)S(1)}, bf16[4,1,48,256]{3,2,1,0:T(8,128)(2,1)S(1)}, u32[]{:S(2)}, u32[]{:S(2)}) collective-permute-start(bf16[4,1,48,256]{3,2,1,0:T(8,128)(2,1)S(1)} %get-tuple-element.112), channel_id=1, source_target_pairs={{4,8},{8,4},{12,16},{16,12},{20,24},{24,20},{5,9},{9,5},{13,17},{1... | collective-permute-start | bytes 294920 | tf_op jit(solution)/shard_map/ppermute | solution.py:735
  82.2 13.5 %copy-start.2 = (f32[2,18432]{1,0:T(2,128)S(1)}, f32[2,18432]{1,0:T(2,128)}, u32[]{:S(2)}) copy-start(f32[2,18432]{1,0:T(2,128)} %param.13) | copy-start | bytes 442372
  82.2 13.5 %copy-start.3 = (f32[2,18432]{1,0:T(2,128)S(1)}, f32[2,18432]{1,0:T(2,128)}, u32[]{:S(2)}) copy-start(f32[2,18432]{1,0:T(2,128)} %param.14) | copy-start | bytes 442372
  82.2 13.5 %copy-start.6 = (f32[4,256]{1,0:T(4,128)S(1)}, f32[4,256]{1,0:T(4,128)}, u32[]{:S(2)}) copy-start(f32[4,256]{1,0:T(4,128)} %n_first.1) | copy-start | bytes 12292
  82.2 13.5 %copy-start.7 = (f32[4,256]{1,0:T(4,128)S(1)}, f32[4,256]{1,0:T(4,128)}, u32[]{:S(2)}) copy-start(f32[4,256]{1,0:T(4,128)} %n_second.1) | copy-start | bytes 12292

commit v7 on v5

--- a/solution.py
+++ b/solution.py
@@ -313,13 +313,18 @@
     to_all(st_ref, [jnp.sum(s1, 0, keepdims=True), jnp.sum(s2, 0, keepdims=True)])
 
 
+def typical_hidden(params):
+    scale, shift = params[0:1], params[1:2]
+    return 0.5 * (shift + jnp.sqrt(shift * shift + 0.64 * scale * scale))
+
+
 def stats_of(total, count):
     mean = total[0:1] / count
     var = total[1:2] / count - mean * mean
     return mean, lax.rsqrt(var + 1e-05)
 
 
-def second_conv_kernel(g, chunk, count, z1, st, params, w, cot, h_ref, z_ref, st_ref):
+def second_conv_kernel(g, chunk, count, z1, st, params, w, cot, h_ref, z_ref, st_ref, own_ref):
     rows_in, rows_out = g.tall - 2, g.tall - 4
     place = Place()
     mean, rstd = stats_of(total_of(st), count)
@@ -346,7 +351,9 @@
                     dn = wide(cot, s, r + i + 2 - RIM)[: g.w]
                     for k, term in enumerate((v, v * v, dn, dn * v)):
                         sums[k] = sums[k] + sum_rows(term)
-    to_all(st_ref, [jnp.sum(v, 0, keepdims=True) for v in sums])
+    own = [jnp.sum(v, 0, keepdims=True) for v in sums]
+    own_ref[0:4] = jnp.concatenate(own, axis=0)
+    to_all(st_ref, own)
 
 
 def own_transposed(g, source, first, s, dt_ref):
@@ -356,7 +363,7 @@
     dt_ref[:, s * span : (s + 1) * span] = jnp.where(inside, block, jnp.zeros_like(block)).T
 
 
-def kernel_gradient(g, core, field, rows_field, first_row, dt_ref, keep, send, first, prepare):
+def kernel_gradient(g, core, field, rows_field, first_row, dt_ref, keep, send, first, prepare, less):
     chans, half = g.c, g.c // 2
     span = g.h * g.wp
     mine = pl.ds(pl.multiple_of(core * half, half), half)
@@ -380,13 +387,13 @@
                     first[a * 3 + b] = acc[half:, b * chans : (b + 1) * chans]
                 continue
             for b in range(3):
-                keep[a * 3 + b] += acc[0:half, b * chans : (b + 1) * chans]
-                other_half = first[a * 3 + b] + acc[half:, b * chans : (b + 1) * chans]
-                send[a * 3 + b] = other_half
+                keep[a * 3 + b] += acc[0:half, b * chans : (b + 1) * chans] - less(mine)
+                other_half = first[a * 3 + b] + acc[half:, b * chans : (b + 1) * chans] - less(other)
+                send[a * 3 + b] = other_half.astype(BF16)
 
 
 def second_gradient_kernel(
-    g, count, z2, st, params, cot, cot_next, h, d_ref, keep, send, dt_ref
+    g, count, z2, st, own, params, cot, cot_next, h, d_ref, keep, send, dt_ref, sums, first
 ):
     place = Place()
     rows = g.cot_tall
@@ -407,7 +414,16 @@
             d = in_grid(d, i + RIM - g.near, g, place, edge)
             d_ref[start : start + g.wp, :] = d.astype(BF16)
         own_transposed(g, d_ref, (s * rows + g.near) * g.wp, s, dt_ref)
-    kernel_gradient(g, place.core, h, g.tall - 2, RIM - 2, dt_ref, keep, send, send, prepare)
+    pixels = float(g.s * g.h * g.w)
+    tile_sum = k0 * own[2:3] - pixels * k1 - k2 * (own[0:1] - pixels * mean)
+    sums[...] = jnp.broadcast_to(tile_sum, (sums.shape[1], g.c)).T
+    typical = typical_hidden(params)
+
+    def less(channels):
+        column = sums[channels, :]
+        return jnp.concatenate([column] * (g.c // column.shape[1]), axis=1) * typical
+
+    kernel_gradient(g, place.core, h, g.tall - 2, RIM - 2, dt_ref, keep, send, first, prepare, less)
 
 
 def transposed_conv(g, d_ref, w, s, rows_in, r, chunk):
@@ -426,8 +442,9 @@
 
 
 def hidden_gradient_kernel(
-    g, chunk, count, d, w, z1, z2, st, st2, params, ext, dn_ref, st_ref, out_ref, d_ref
+    g, chunk, count, scenes, d, w, z1, z2, st, st2, params, ext, *refs
 ):
+    *before, dn_ref, st_ref, out_ref, d_ref = refs
     mean2, rstd2 = stats_of(total_of(st2), count)
     scale2 = params[2:3] * rstd2
     shift2 = params[3:4] - mean2 * scale2
@@ -435,9 +452,9 @@
     mean, rstd = stats_of(total_of(st), count)
     scale = params[0:1] * rstd
     shift = params[1:2] - mean * scale
-    s0 = jnp.zeros((8, g.c), F32)
-    s1 = jnp.zeros((8, g.c), F32)
-    for s in range(g.s):
+    s0 = before[1][0:8] if before else jnp.zeros((8, g.c), F32)
+    s1 = before[1][8:16] if before else jnp.zeros((8, g.c), F32)
+    for s in scenes:
         for i in range(rows_in):
             at = (s * rows_in + i) * g.wp
             store_shifted(d_ref, at, wide(d, slice(at, at + g.wp)))
@@ -456,7 +473,11 @@
                     v = dn[i * g.wp : i * g.wp + g.w]
                     s0 = s0 + sum_rows(v)
                     s1 = s1 + sum_rows(v * (z[i * g.wp : i * g.wp + g.w] - mean))
-    to_all(st_ref, [jnp.sum(s0, 0, keepdims=True), jnp.sum(s1, 0, keepdims=True) * rstd])
+    if not before:
+        st_ref[0:8] = s0
+        st_ref[8:16] = s1
+    else:
+        to_all(st_ref, [jnp.sum(s0, 0, keepdims=True), jnp.sum(s1, 0, keepdims=True) * rstd])
 
 
 def half_gradient(g, which, field, rows_field, first_row, dt_ref, out_ref, sums, prepare=None):
@@ -787,12 +808,13 @@
         alias={7: 0, 8: 2},
     )(ext, ra, rb, rb_c, rb_d, w1, st, z1, x)
     st1 = exchange(st)
-    h, z2, st = kernel_call(
+    h, z2, st, own_sums = kernel_call(
         functools.partial(second_conv_kernel, g, 5, count),
         [
             held((n1, 3 * chans), BF16),
             held((n2, chans), F32),
             shape_of((devices, 4, chans), F32),
+            held((8, chans), F32),
         ],
         conv_flops(n2),
     )(z1, st1, norm_scale_bias, w2, cot_ext)
@@ -800,38 +822,52 @@
     grad_shape = held((9, chans // 2, chans), F32)
     d, keep2, send2 = kernel_call(
         functools.partial(second_gradient_kernel, g, count),
-        [held((n2, chans), BF16), grad_shape, grad_shape],
+        [held((n2, chans), BF16), grad_shape, held(grad_shape.shape, BF16)],
         conv_flops(own_pixels),
-        scratch=[pltpu.VMEM((chans, own_pixels), BF16)],
-    )(z2, st2, norm_scale_bias, cot_ext, cot_next, h)
+        scratch=[
+            pltpu.VMEM((chans, own_pixels), BF16),
+            pltpu.VMEM((chans, 128), F32),
+            pltpu.VMEM(grad_shape.shape, F32),
+        ],
+    )(z2, st2, own_sums, norm_scale_bias, cot_ext, cot_next, h)
     got2 = swapped(send2, "rows", 0)
-    dn1, st, block_out = kernel_call(
-        functools.partial(hidden_gradient_kernel, g, 8, count),
-        [
-            held((n3, chans), F32),
-            shape_of((devices, 2, chans), F32),
-            held(features.shape, BF16),
-        ],
-        conv_flops(n3),
-        scratch=[pltpu.VMEM((n2, 3 * chans), BF16)],
-    )(d, w2, z1, z2, st1, st2, norm_scale_bias, ext)
     nrows = lax.axis_size("rows")
     cut_again = nrows % 4 == 0 and taps // devices % 8 == 0
+    hidden_shape, output_shape = held((n3, chans), F32), held(features.shape, BF16)
+
+    def hidden_gradient(scenes, part_shape, *before, **options):
+        return kernel_call(
+            functools.partial(hidden_gradient_kernel, g, 8, count, scenes),
+            [hidden_shape, part_shape, output_shape],
+            0,
+            size=1024,
+            scratch=[pltpu.VMEM((n2, 3 * chans), BF16)],
+            **options,
+        )(d, w2, z1, z2, st1, st2, norm_scale_bias, ext, *before)
+
+    early = range(3)
+    dn1, part, block_out = hidden_gradient(early, held((16, chans), F32))
+    got2, part = lax.optimization_barrier((got2, part))
     if cut_again:
-        got2, st = lax.optimization_barrier((got2, st))
         kept_shape = (devices, half_rows(taps // devices), chans // 2)
         kept, sent = kernel_call(
             split_kernel,
             [held(kept_shape, F32), held(kept_shape, BF16)],
-            1e8,
+            0,
+            size=1024,
             scratch=[pltpu.VMEM((taps, chans // 2), F32)],
         )(keep2, got2)
-        st, kept = lax.optimization_barrier((st, kept))
         came = lax.ppermute(sent, "rows", [(i, i ^ 2) for i in range(nrows)])
-        st3 = exchange(st)
-    else:
-        st, got2 = lax.optimization_barrier((st, got2))
-        st3 = exchange(st)
+        kept, part = lax.optimization_barrier((kept, part))
+    dn1, st, block_out = hidden_gradient(
+        range(len(early), scenes),
+        shape_of((devices, 2, chans), F32),
+        dn1,
+        part,
+        block_out,
+        alias={8: 0, 10: 2},
+    )
+    st3 = exchange(st)
     if cut_again:
         kept, st3 = lax.optimization_barrier((kept, st3))
         (kept,) = kernel_call(join_kernel, [held(kept_shape, F32)], 0, size=1024)(kept, came)

time: 96.3 us -> 95.8 us (level)
    pallas_call x15 -> x16, Pallas kernels: 25.5 us -> 25.4 us  [call(): pl.pallas_call(body, out_shape=out_shape, in_specs=specs, out_specs=[pl.B...]
where the time goes in v7:
time: 95.8 us; the launch traced here: 95.4 us
  blocking collectives  30.6 us (32%)
  Pallas kernels  25.4 us (27%)
  starting transfers between devices  22.5 us (23%)
  waiting for transfers between devices  14.1 us (15%)
  local copies, waits for them, and re-layouts  1.8 us (2%)
    all_to_all x3, blocking collectives, exchange(): return lax.all_to_all(parts, BOTH, 0, 0, tiled=True)  30.6 us
    pallas_call x16, Pallas kernels, call(): pl.pallas_call(body, out_shape=out_shape, in_specs=specs, out_specs=[pl.B...  25.4 us
    ppermute x8, starting transfers between devices, swapped(): return lax.ppermute(block, axis, pairs)  12.6 us
    all_to_all x1, waiting for transfers between devices, exchange(): return lax.all_to_all(parts, BOTH, 0, 0, tiled=True)  7.9 us
    ppermute x2, starting transfers between devices, swapped_both(): return lax.ppermute(block, BOTH, pairs)  6.69 us
    ppermute x8, waiting for transfers between devices, swapped(): return lax.ppermute(block, axis, pairs)  6.16 us
    all_to_all x1, starting transfers between devices, exchange(): return lax.all_to_all(parts, BOTH, 0, 0, tiled=True)  2.63 us
  transfers between devices with their start and end apart: 12, of which 4 were waited for; matrix products, arithmetic and copies ran while one was open for 2% of the time, Pallas kernels for 13%

profile of v7, /device:TPU:1, one launch (start us, length us, event | category | flops | bytes accessed | tf_op | source)
XLA Modules:
  0.0 95.4 jit_solution(15498754849870686822)
XLA Ops:
  0.6 1.7 %shard_map.168 = (bf16[4,8,40,256]{3,2,1,0:T(8,128)(2,1)S(1)}, bf16[4,48,256]{2,1,0:T(8,128)(2,1)S(1)}, bf16[4,48,256]{2,1,0:T(8,128)(2,1)S(1)}, bf16[4,4,40,256...) custom-call(bf16[4,8,40,256]{3,2,1,0:T(8,128)(2,1)} %features.1, ...), custom_call_target="tpu_custom_call" | custom-call | flops 100000000 | bytes 4194304 | tf_op jit(solution)/shard_map/pallas_call | solution.py:41
  2.4 4.5 %collective-permute-start.2 = (bf16[4,4,40,256]{3,2,1,0:T(8,128)(2,1)S(1)}, bf16[4,4,40,256]{3,2,1,0:T(8,128)(2,1)S(1)}, u32[]{:S(2)}, u32[]{:S(2)}) collective-permute-start(bf16[4,4,40,256]{3,2,1,0:T(8,128)(2,1)S(1)} %get-tuple-element.76), channel_id=1, source_target_pairs={{4,8},{8,4},{12,16},{16,12},{20,24},{24,20},{5,9},{9,5},{13,17},{1... | collective-permute-start | bytes 983048 | tf_op jit(solution)/shard_map/ppermute | solution.py:691
  6.9 1.4 %collective-permute-start = (bf16[4,48,256]{2,1,0:T(8,128)(2,1)S(1)}, bf16[4,48,256]{2,1,0:T(8,128)(2,1)S(1)}, u32[]{:S(2)}, u32[]{:S(2)}) collective-permute-start(bf16[4,48,256]{2,1,0:T(8,128)(2,1)S(1)} %get-tuple-element.72), channel_id=1, source_target_pairs={{0,1},{1,0},{2,3},{3,2},{4,5},{5,4},{6,7},{7,6},{8,9},{9,8},{10,11... | collective-permute-start | bytes 294920 | tf_op jit(solution)/shard_map/ppermute | solution.py:691
  8.2 0.7 collective-permute-start.1
  8.9 6.0 %collective-permute-start.3 = (bf16[4,16,256]{2,1,0:T(8,128)(2,1)S(1)}, bf16[4,16,256]{2,1,0:T(8,128)(2,1)S(1)}, u32[]{:S(2)}, u32[]{:S(2)}) collective-permute-start(bf16[4,16,256]{2,1,0:T(8,128)(2,1)S(1)} %get-tuple-element.77), channel_id=1, source_target_pairs={{4,9},{5,8},{6,11},{7,10},{8,5},{9,4},{10,7},{11,6},{12,17},{13,16... | collective-permute-start | bytes 98312 | tf_op jit(solution)/shard_map/ppermute | solution.py:707
  14.9 0.7 collective-permute-start.4
  15.6 0.0 copy-start.1
  15.6 2.5 %shard_map.170 = (bf16[2304,256]{1,0:T(8,128)(2,1)S(1)}, bf16[2304,256]{1,0:T(8,128)(2,1)S(1)}) custom-call(f32[9216,128]{1,0:T(8,128)} %bitcast.37), custom_call_target="tpu_custom_call" | custom-call | bytes 1024 | tf_op jit(solution)/shard_map/pallas_call | solution.py:41
  18.1 0.0 collective-permute-done.rc
  18.1 0.0 collective-permute-done.1.rd
  18.2 0.2 shard_map.169
  18.4 0.0 collective-permute-done.3.rb_c
  18.4 0.0 collective-permute-done.4.rb_d
  18.4 0.0 collective-permute-done.2.rb
  18.4 0.1 collective-permute-start.5
  18.5 1.6 %shard_map.171 = (f32[2304,256]{1,0:T(8,128)S(1)}, f32[16,256]{1,0:T(8,128)S(1)}, bf16[1920,768]{1,0:T(8,128)(2,1)S(1)}) custom-call(bf16[4,8,48,256]{3,2,1,0:T(8,128)(2,1)S(1)} %get-tuple-element.74.ext, bf16[2304,256]{1,0:T(8,128)(2,1)S(1)} %get-tuple-element.84.w.w_far), custom_call_target="tpu_custom_call" | custom-call | bytes 1024 | tf_op jit(solution)/shard_map/pallas_call | solution.py:41
  20.1 0.1 collective-permute-done.5.ra
  20.2 1.6 %shard_map.172 = (f32[2304,256]{1,0:T(8,128)S(1)}, f32[32,2,256]{2,1,0:T(2,128)S(1)}, bf16[1920,768]{1,0:T(8,128)(2,1)S(1)}, bf16[4,2,48,256]{3,2,1,0:T(8,128)(2,1)S(1)}) custom-call(bf16[4,8,48,256]{3,2,1,0:T(8,128)(2,1)S(1)} %get-tuple-element.74.ext, ...), custom_call_target="tpu_custom_call", output_to_operand_aliasing={{0}: (7, {}), {2}: (8, {})} | custom-call | bytes 1024 | tf_op jit(solution)/shard_map/pallas_call | solution.py:41
  21.8 11.7 %all_to_all.20.st = f32[32,2,256]{2,1,0:T(2,128)S(1)} all-to-all(f32[32,2,256]{2,1,0:T(2,128)S(1)} %get-tuple-element.89), channel_id=1, replica_groups=mesh['rows'=8,'cols'=4] {'rows','cols'}, dimensions={0} | all-to-all | bytes 131072 | tf_op jit(solution)/shard_map/all_to_all | solution.py:719
  33.5 2.7 %shard_map.173 = (bf16[2304,768]{1,0:T(8,128)(2,1)S(1)}, f32[1920,256]{1,0:T(8,128)S(1)}, f32[32,4,256]{2,1,0:T(4,128)S(1)}, f32[8,256]{1,0:T(8,128)S(1)}) custom-call(f32[2304,256]{1,0:T(8,128)S(1)} %get-tuple-element.88.z1.z, f32[32,2,256]{2,1,0:T(2,128)S(1)} %all_to_all.20.st, f32[4,256]{1,0:T(4,128)S(1)} %copy-done.4, ...), custom_call_target="tpu_custom_call" | custom-call | flops 2264924160 | bytes 4194304 | tf_op jit(solution)/shard_map/pallas_call | solution.py:41
  36.2 9.7 %all_to_all.21.st.st2 = f32[32,4,256]{2,1,0:T(4,128)S(1)} all-to-all(f32[32,4,256]{2,1,0:T(4,128)S(1)} %get-tuple-element.93), channel_id=1, replica_groups=mesh['rows'=8,'cols'=4] {'rows','cols'}, dimensions={0} | all-to-all | bytes 262144 | tf_op jit(solution)/shard_map/all_to_all | solution.py:719
  45.8 2.5 %shard_map.174 = (bf16[1920,256]{1,0:T(8,128)(2,1)S(1)}, f32[9,128,256]{2,1,0:T(8,128)S(1)}, bf16[9,128,256]{2,1,0:T(8,128)(2,1)S(1)}) custom-call(f32[1920,256]{1,0:T(8,128)S(1)} %get-tuple-element.92.z2, f32[32,4,256]{2,1,0:T(4,128)S(1)} %all_to_all.21.st.st2, f32[8,256]{1,0:T(8,128)S(1)} %get-tuple-element.94.own, f32[4,256]{1,0:T(4,128)S(1)} %copy-done.4, ...), custom_call_target="tpu_custom_call" | custom-call | flops 1811939328 | bytes 4194304 | tf_op jit(solution)/shard_map/pallas_call | solution.py:41
  48.3 1.4 %collective-permute-start.6 = (bf16[9,128,256]{2,1,0:T(8,128)(2,1)S(1)}, bf16[9,128,256]{2,1,0:T(8,128)(2,1)S(1)}, u32[]{:S(2)}, u32[]{:S(2)}) collective-permute-start(bf16[9,128,256]{2,1,0:T(8,128)(2,1)S(1)} %get-tuple-element.100), channel_id=1, source_target_pairs={{0,4},{4,0},{8,12},{12,8},{16,20},{20,16},{24,28},{28,24},{1,5},{5... | collective-permute-start | bytes 1769480 | tf_op jit(solution)/shard_map/ppermute | solution.py:691
  49.7 1.9 %shard_map.175 = (f32[1536,256]{1,0:T(8,128)S(1)}, f32[16,256]{1,0:T(8,128)S(1)}, bf16[4,8,40,256]{3,2,1,0:T(8,128)(2,1)S(1)}) custom-call(bf16[1920,256]{1,0:T(8,128)(2,1)S(1)} %get-tuple-element.97.d, bf16[2304,256]{1,0:T(8,128)(2,1)S(1)} %get-tuple-element.90.w, f32[2304,256]{1,0:T(8,128)S(1)} %get-tuple-element.88.z1.z, ...), custom_call_target="tpu_custom_call" | custom-call | bytes 1024 | tf_op jit(solution)/shard_map/pallas_call | solution.py:41
  51.6 0.0 collective-permute-done.6.got
  51.6 0.6 shard_map.176
  52.2 0.6 collective-permute-start.7
  52.7 0.8 shard_map.177
  53.5 9.3 %all_to_all.22.st3 = f32[32,2,256]{2,1,0:T(2,128)S(1)} all-to-all(f32[32,2,256]{2,1,0:T(2,128)S(1)} %get-tuple-element.110), channel_id=1, replica_groups=mesh['rows'=8,'cols'=4] {'rows','cols'}, dimensions={0} | all-to-all | bytes 131072 | tf_op jit(solution)/shard_map/all_to_all | solution.py:719
  62.8 0.0 collective-permute-done.7.came
  62.8 0.1 shard_map.178.kept
  62.9 1.5 %shard_map.179 = (bf16[1536,256]{1,0:T(8,128)(2,1)S(1)}, bf16[4,1,48,256]{3,2,1,0:T(8,128)(2,1)S(1)}, bf16[4,1,48,256]{3,2,1,0:T(8,128)(2,1)S(1)}, bf16[2304,128]{1,0:T(8,128)(2,1)S(1)}, bf16[256,1536]{1,0:T(8,128)(2,1)S(1)}) custom-call(f32[1536,256]{1,0:T(8,128)S(1)} %get-tuple-element.113.dn, f32[2304,256]{1,0:T(8,128)S(1)} %get-tuple-element.88.z1.z, ...), custom_call_target="tpu_custom_call" | custom-call | bytes 1024 | tf_op jit(solution)/shard_map/pallas_call | solution.py:41
  64.4 0.9 collective-permute-start.10
  65.3 1.2 %shard_map.181.keep = f32[2304,128]{1,0:T(8,128)S(1)} custom-call(bf16[1920,768]{1,0:T(8,128)(2,1)S(1)} %get-tuple-element.115.x, bf16[256,1536]{1,0:T(8,128)(2,1)S(1)} %get-tuple-element.119.dt_ref), custom_call_target="tpu_custom_call" | custom-call | bytes 1024 | tf_op jit(solution)/shard_map/pallas_call | solution.py:41
  66.5 0.4 collective-permute-done.10.got
  66.9 1.0 %shard_map.182 = bf16[32,112,128]{2,1,0:T(8,128)(2,1)} custom-call(f32[2304,128]{1,0:T(8,128)S(1)} %shard_map.181.keep, bf16[2304,128]{1,0:T(8,128)(2,1)S(1)} %collective-permute-done.10.got, f32[32,40,128]{2,1,0:T(8,128)S(1)} %shard_map.178.kept), custom_call_target="tpu_custom_call" | custom-call | flops 1000000000 | bytes 4194304 | tf_op jit(solution)/shard_map/pallas_call | solution.py:41
  67.9 0.0 copy-start.5
  67.9 2.6 %all-to-all-start.3 = ((bf16[32,112,128]{2,1,0:T(8,128)(2,1)}), bf16[32,112,128]{2,1,0:T(8,128)(2,1)S(1)}, u32[]{:S(2)}, u32[]{:S(2)}) async-start(bf16[32,112,128]{2,1,0:T(8,128)(2,1)} %shard_map.182), calls=%async_computation.3 | async-start | bytes 1835008 | tf_op jit(solution)/shard_map/all_to_all | solution.py:719
  70.6 0.5 collective-permute-start.8
  71.0 3.3 %collective-permute-start.9 = (bf16[4,1,48,256]{3,2,1,0:T(8,128)(2,1)S(1)}, bf16[4,1,48,256]{3,2,1,0:T(8,128)(2,1)S(1)}, u32[]{:S(2)}, u32[]{:S(2)}) collective-permute-start(bf16[4,1,48,256]{3,2,1,0:T(8,128)(2,1)S(1)} %get-tuple-element.118), channel_id=1, source_target_pairs={{4,8},{8,4},{12,16},{16,12},{20,24},{24,20},{5,9},{9,5},{13,17},{1... | collective-permute-start | bytes 294920 | tf_op jit(solution)/shard_map/ppermute | solution.py:691
  74.3 0.8 copy.34
  75.2 0.0 collective-permute-done.8.ra
  75.2 5.6 %collective-permute-done.9.rb = bf16[4,1,48,256]{3,2,1,0:T(8,128)(2,1)S(1)} collective-permute-done((bf16[4,1,48,256]{3,2,1,0:T(8,128)(2,1)S(1)}, bf16[4,1,48,256]{3,2,1,0:T(8,128)(2,1)S(1)}, u32[]{:S(2)}, u32[]{:S(2)}) %collective-permute-start.9) | collective-permute-done | bytes 98336 | tf_op jit(solution)/shard_map/ppermute | solution.py:691
  80.8 0.0 copy-start.7
  80.8 4.7 %shard_map.180 = f32[4,8,40,256]{3,2,1,0:T(8,128)} custom-call(bf16[1536,256]{1,0:T(8,128)(2,1)S(1)} %get-tuple-element.116.e, bf16[4,1,48,256]{3,2,1,0:T(8,128)(2,1)S(1)} %collective-permute-done.8.ra, bf16[4,1,48,256]{3,2,1,0:T(8,128)(2,1)S(1)} %collective-permute-done.9.rb, bf16[2304,256]{1,0:T(8,128)(2,1)} %copy-done, bf16[4,8,40,256]{3,2,1,0:T(8,128)(2,1)} %cot_far.1, ...), custom_call_target="tpu_custom_call" | custom-call | flops 1811939328 | bytes 4194304 | tf_op jit(solution)/shard_map/pallas_call | solution.py:41
  85.5 0.9 constant_dynamic-slice_fusion.w
  86.4 7.9 %all-to-all-done.3.parts = bf16[32,112,128]{2,1,0:T(8,128)(2,1)S(1)} async-done(((bf16[32,112,128]{2,1,0:T(8,128)(2,1)}), bf16[32,112,128]{2,1,0:T(8,128)(2,1)S(1)}, u32[]{:S(2)}, u32[]{:S(2)}) %all-to-all-start.3) | async-done | bytes 917536 | tf_op jit(solution)/shard_map/all_to_all | solution.py:719
  94.3 1.1 %shard_map.183 = (f32[288,128]{1,0:T(8,128)}, f32[288,128]{1,0:T(8,128)}, f32[288,128]{1,0:T(8,128)}, f32[288,128]{1,0:T(8,128)}, f32[4,256]{1,0:T(4,128)}, /*in...) custom-call(bf16[32,112,128]{2,1,0:T(8,128)(2,1)S(1)} %all-to-all-done.3.parts, ...), custom_call_target="tpu_custom_call" | custom-call | flops 100000000 | bytes 4194304 | tf_op jit(solution)/shard_map/pallas_call | solution.py:41
  (13 shorter events, 0.0 us)
Async XLA Ops:
  2.4 16.0 %collective-permute-start.2 = (bf16[4,4,40,256]{3,2,1,0:T(8,128)(2,1)S(1)}, bf16[4,4,40,256]{3,2,1,0:T(8,128)(2,1)S(1)}, u32[]{:S(2)}, u32[]{:S(2)}) collective-permute-start(bf16[4,4,40,256]{3,2,1,0:T(8,128)(2,1)S(1)} %get-tuple-element.76), channel_id=1, source_target_pairs={{4,8},{8,4},{12,16},{16,12},{20,24},{24,20},{5,9},{9,5},{13,17},{1... | collective-permute-start | bytes 983048 | tf_op jit(solution)/shard_map/ppermute | solution.py:691
  6.9 11.3 %collective-permute-start = (bf16[4,48,256]{2,1,0:T(8,128)(2,1)S(1)}, bf16[4,48,256]{2,1,0:T(8,128)(2,1)S(1)}, u32[]{:S(2)}, u32[]{:S(2)}) collective-permute-start(bf16[4,48,256]{2,1,0:T(8,128)(2,1)S(1)} %get-tuple-element.72), channel_id=1, source_target_pairs={{0,1},{1,0},{2,3},{3,2},{4,5},{5,4},{6,7},{7,6},{8,9},{9,8},{10,11... | collective-permute-start | bytes 294920 | tf_op jit(solution)/shard_map/ppermute | solution.py:691
  8.2 9.9 %collective-permute-start.1 = (bf16[4,48,256]{2,1,0:T(8,128)(2,1)S(1)}, bf16[4,48,256]{2,1,0:T(8,128)(2,1)S(1)}, u32[]{:S(2)}, u32[]{:S(2)}) collective-permute-start(bf16[4,48,256]{2,1,0:T(8,128)(2,1)S(1)} %get-tuple-element.73), channel_id=1, source_target_pairs={{1,2},{2,1},{5,6},{6,5},{9,10},{10,9},{13,14},{14,13},{17,18},{18,... | collective-permute-start | bytes 294920 | tf_op jit(solution)/shard_map/ppermute | solution.py:691
  8.9 9.5 %collective-permute-start.3 = (bf16[4,16,256]{2,1,0:T(8,128)(2,1)S(1)}, bf16[4,16,256]{2,1,0:T(8,128)(2,1)S(1)}, u32[]{:S(2)}, u32[]{:S(2)}) collective-permute-start(bf16[4,16,256]{2,1,0:T(8,128)(2,1)S(1)} %get-tuple-element.77), channel_id=1, source_target_pairs={{4,9},{5,8},{6,11},{7,10},{8,5},{9,4},{10,7},{11,6},{12,17},{13,16... | collective-permute-start | bytes 98312 | tf_op jit(solution)/shard_map/ppermute | solution.py:707
  14.9 3.4 %collective-permute-start.4 = (bf16[4,16,256]{2,1,0:T(8,128)(2,1)S(1)}, bf16[4,16,256]{2,1,0:T(8,128)(2,1)S(1)}, u32[]{:S(2)}, u32[]{:S(2)}) collective-permute-start(bf16[4,16,256]{2,1,0:T(8,128)(2,1)S(1)} %get-tuple-element.78), channel_id=1, source_target_pairs={{5,10},{6,9},{9,6},{10,5},{13,18},{14,17},{17,14},{18,13},{21,26},... | collective-permute-start | bytes 98312 | tf_op jit(solution)/shard_map/ppermute | solution.py:707
  15.6 2.5 %copy-start.1 = (bf16[4,8,40,256]{3,2,1,0:T(8,128)(2,1)S(1)}, bf16[4,8,40,256]{3,2,1,0:T(8,128)(2,1)}, u32[]{:S(2)}) copy-start(bf16[4,8,40,256]{3,2,1,0:T(8,128)(2,1)} %cot_far.1) | copy-start | bytes 1966084
  18.1 3.7 %copy-start = (bf16[2304,256]{1,0:T(8,128)(2,1)}, bf16[2304,256]{1,0:T(8,128)(2,1)S(1)}, u32[]{:S(2)}) copy-start(bf16[2304,256]{1,0:T(8,128)(2,1)S(1)} %get-tuple-element.84.w.w_far) | copy-start | bytes 3538948
  18.4 1.8 %collective-permute-start.5 = (bf16[4,4,48,256]{3,2,1,0:T(8,128)(2,1)S(1)}, bf16[4,4,48,256]{3,2,1,0:T(8,128)(2,1)S(1)}, u32[]{:S(2)}, u32[]{:S(2)}) collective-permute-start(bf16[4,4,48,256]{3,2,1,0:T(8,128)(2,1)S(1)} %get-tuple-element.80), channel_id=1, source_target_pairs={{0,4},{4,0},{8,12},{12,8},{16,20},{20,16},{24,28},{28,24},{1,5},{5... | collective-permute-start | bytes 1179656 | tf_op jit(solution)/shard_map/ppermute | solution.py:691
  20.2 13.3 %copy-start.4 = (f32[4,256]{1,0:T(4,128)S(1)}, f32[4,256]{1,0:T(4,128)}, u32[]{:S(2)}) copy-start(f32[4,256]{1,0:T(4,128)} %params.11) | copy-start | bytes 12292
  48.3 3.3 %collective-permute-start.6 = (bf16[9,128,256]{2,1,0:T(8,128)(2,1)S(1)}, bf16[9,128,256]{2,1,0:T(8,128)(2,1)S(1)}, u32[]{:S(2)}, u32[]{:S(2)}) collective-permute-start(bf16[9,128,256]{2,1,0:T(8,128)(2,1)S(1)} %get-tuple-element.100), channel_id=1, source_target_pairs={{0,4},{4,0},{8,12},{12,8},{16,20},{20,16},{24,28},{28,24},{1,5},{5... | collective-permute-start | bytes 1769480 | tf_op jit(solution)/shard_map/ppermute | solution.py:691
  52.2 10.6 %collective-permute-start.7 = (bf16[32,40,128]{2,1,0:T(8,128)(2,1)S(1)}, bf16[32,40,128]{2,1,0:T(8,128)(2,1)S(1)}, u32[]{:S(2)}, u32[]{:S(2)}) collective-permute-start(bf16[32,40,128]{2,1,0:T(8,128)(2,1)S(1)} %get-tuple-element.112), channel_id=1, source_target_pairs={{0,8},{4,12},{8,0},{12,4},{16,24},{20,28},{24,16},{28,20},{1,9},{5... | collective-permute-start | bytes 983048 | tf_op jit(solution)/shard_map/ppermute | solution.py:860
  64.4 2.5 %collective-permute-start.10 = (bf16[2304,128]{1,0:T(8,128)(2,1)S(1)}, bf16[2304,128]{1,0:T(8,128)(2,1)S(1)}, u32[]{:S(2)}, u32[]{:S(2)}) collective-permute-start(bf16[2304,128]{1,0:T(8,128)(2,1)S(1)} %get-tuple-element.120), channel_id=1, source_target_pairs={{0,4},{4,0},{8,12},{12,8},{16,20},{20,16},{24,28},{28,24},{1,5},{5... | collective-permute-start | bytes 1769480 | tf_op jit(solution)/shard_map/ppermute | solution.py:691
  67.9 12.8 %copy-start.5 = (s32[4,8,40]{2,1,0:T(8,128)S(1)}, s32[4,8,40]{2,1,0:T(8,128)}, u32[]{:S(2)}) copy-start(s32[4,8,40]{2,1,0:T(8,128)} %occ.1) | copy-start | bytes 15364
  67.9 26.4 %all-to-all-start.3 = ((bf16[32,112,128]{2,1,0:T(8,128)(2,1)}), bf16[32,112,128]{2,1,0:T(8,128)(2,1)S(1)}, u32[]{:S(2)}, u32[]{:S(2)}) async-start(bf16[32,112,128]{2,1,0:T(8,128)(2,1)} %shard_map.182), calls=%async_computation.3 | async-start | bytes 1835008 | tf_op jit(solution)/shard_map/all_to_all | solution.py:719
  70.6 4.6 %collective-permute-start.8 = (bf16[4,1,48,256]{3,2,1,0:T(8,128)(2,1)S(1)}, bf16[4,1,48,256]{3,2,1,0:T(8,128)(2,1)S(1)}, u32[]{:S(2)}, u32[]{:S(2)}) collective-permute-start(bf16[4,1,48,256]{3,2,1,0:T(8,128)(2,1)S(1)} %get-tuple-element.117), channel_id=1, source_target_pairs={{0,4},{4,0},{8,12},{12,8},{16,20},{20,16},{24,28},{28,24},{1,5},{5... | collective-permute-start | bytes 294920 | tf_op jit(solution)/shard_map/ppermute | solution.py:691
  71.0 9.7 %collective-permute-start.9 = (bf16[4,1,48,256]{3,2,1,0:T(8,128)(2,1)S(1)}, bf16[4,1,48,256]{3,2,1,0:T(8,128)(2,1)S(1)}, u32[]{:S(2)}, u32[]{:S(2)}) collective-permute-start(bf16[4,1,48,256]{3,2,1,0:T(8,128)(2,1)S(1)} %get-tuple-element.118), channel_id=1, source_target_pairs={{4,8},{8,4},{12,16},{16,12},{20,24},{24,20},{5,9},{9,5},{13,17},{1... | collective-permute-start | bytes 294920 | tf_op jit(solution)/shard_map/ppermute | solution.py:691
  80.8 13.5 %copy-start.2 = (f32[2,18432]{1,0:T(2,128)S(1)}, f32[2,18432]{1,0:T(2,128)}, u32[]{:S(2)}) copy-start(f32[2,18432]{1,0:T(2,128)} %param.13) | copy-start | bytes 442372
  80.8 13.5 %copy-start.3 = (f32[2,18432]{1,0:T(2,128)S(1)}, f32[2,18432]{1,0:T(2,128)}, u32[]{:S(2)}) copy-start(f32[2,18432]{1,0:T(2,128)} %param.14) | copy-start | bytes 442372
  80.8 13.5 %copy-start.6 = (f32[4,256]{1,0:T(4,128)S(1)}, f32[4,256]{1,0:T(4,128)}, u32[]{:S(2)}) copy-start(f32[4,256]{1,0:T(4,128)} %n_first.1) | copy-start | bytes 12292
  80.8 13.5 %copy-start.7 = (f32[4,256]{1,0:T(4,128)S(1)}, f32[4,256]{1,0:T(4,128)}, u32[]{:S(2)}) copy-start(f32[4,256]{1,0:T(4,128)} %n_second.1) | copy-start | bytes 12292

commit v8 on v7

--- a/solution.py
+++ b/solution.py
@@ -383,13 +383,13 @@
                 prepare(groups[1][a])
             if group[0] == 0:
                 for b in range(3):
-                    keep[a * 3 + b] = acc[0:half, b * chans : (b + 1) * chans]
-                    first[a * 3 + b] = acc[half:, b * chans : (b + 1) * chans]
+                    first[a * 3 + b] = acc[:, b * chans : (b + 1) * chans]
                 continue
             for b in range(3):
-                keep[a * 3 + b] += acc[0:half, b * chans : (b + 1) * chans] - less(mine)
-                other_half = first[a * 3 + b] + acc[half:, b * chans : (b + 1) * chans] - less(other)
-                send[a * 3 + b] = other_half.astype(BF16)
+                rows = slice((a * 3 + b) * chans, (a * 3 + b + 1) * chans)
+                part = acc[:, b * chans : (b + 1) * chans] + first[a * 3 + b]
+                keep[rows, :] = (part[0:half] - less(mine)).T
+                send[rows, :] = (part[half:] - less(other)).T.astype(BF16)
 
 
 def second_gradient_kernel(
@@ -566,8 +566,6 @@
 
 
 def pair_total(keep, got, t):
-    if keep.ndim == 3:
-        return (keep[t] + wide(got, t)).T
     chans = 2 * keep.shape[1]
     rows = slice(t * chans, (t + 1) * chans)
     return keep[rows, :] + wide(got, rows)
@@ -595,7 +593,9 @@
 
 
 def split_kernel(keep, got, kept_ref, sent_ref, buffer):
-    taps, half, chans = keep.shape
+    half = keep.shape[1]
+    chans = 2 * half
+    taps = keep.shape[0] // chans
     devices, rows, _ = kept_ref.shape
     share = taps * chans // devices
     for t in range(taps):
@@ -819,7 +819,7 @@
         conv_flops(n2),
     )(z1, st1, norm_scale_bias, w2, cot_ext)
     st2 = exchange(st)
-    grad_shape = held((9, chans // 2, chans), F32)
+    grad_shape = held((taps, chans // 2), F32)
     d, keep2, send2 = kernel_call(
         functools.partial(second_gradient_kernel, g, count),
         [held((n2, chans), BF16), grad_shape, held(grad_shape.shape, BF16)],
@@ -827,7 +827,7 @@
         scratch=[
             pltpu.VMEM((chans, own_pixels), BF16),
             pltpu.VMEM((chans, 128), F32),
-            pltpu.VMEM(grad_shape.shape, F32),
+            pltpu.VMEM((9, chans, chans), F32),
         ],
     )(z2, st2, own_sums, norm_scale_bias, cot_ext, cot_next, h)
     got2 = swapped(send2, "rows", 0)
@@ -873,7 +873,7 @@
         (kept,) = kernel_call(join_kernel, [held(kept_shape, F32)], 0, size=1024)(kept, came)
         dn1, kept = lax.optimization_barrier((dn1, kept))
     sent_shape = held((taps, chans // 2), BF16)
-    part = pltpu.VMEM(grad_shape.shape, F32)
+    part = pltpu.VMEM((9, chans // 2, chans), F32)
     e, a, b, send1, dt = kernel_call(
         functools.partial(first_gradient_kernel, g, count),
         [

time: 95.8 us -> 95.6 us (level)
  no operation moved by 1% of the time
where the time goes in v8:
time: 95.6 us; the launch traced here: 95.1 us
  blocking collectives  30.6 us (32%)
  Pallas kernels  25.1 us (26%)
  starting transfers between devices  22.6 us (24%)
  waiting for transfers between devices  14.1 us (15%)
  local copies, waits for them, and re-layouts  1.8 us (2%)
    all_to_all x3, blocking collectives, exchange(): return lax.all_to_all(parts, BOTH, 0, 0, tiled=True)  30.6 us
    pallas_call x16, Pallas kernels, call(): pl.pallas_call(body, out_shape=out_shape, in_specs=specs, out_specs=[pl.B...  25.1 us
    ppermute x8, starting transfers between devices, swapped(): return lax.ppermute(block, axis, pairs)  12.7 us
    all_to_all x1, waiting for transfers between devices, exchange(): return lax.all_to_all(parts, BOTH, 0, 0, tiled=True)  7.9 us
    ppermute x2, starting transfers between devices, swapped_both(): return lax.ppermute(block, BOTH, pairs)  6.69 us
    ppermute x8, waiting for transfers between devices, swapped(): return lax.ppermute(block, axis, pairs)  6.16 us
    all_to_all x1, starting transfers between devices, exchange(): return lax.all_to_all(parts, BOTH, 0, 0, tiled=True)  2.63 us
  transfers between devices with their start and end apart: 12, of which 4 were waited for; matrix products, arithmetic and copies ran while one was open for 2% of the time, Pallas kernels for 13%

profile of v8, /device:TPU:1, one launch (start us, length us, event | category | flops | bytes accessed | tf_op | source)
XLA Modules:
  0.0 95.1 jit_solution(13773739045195157391)
XLA Ops:
  0.6 1.7 %shard_map.168 = (bf16[4,8,40,256]{3,2,1,0:T(8,128)(2,1)S(1)}, bf16[4,48,256]{2,1,0:T(8,128)(2,1)S(1)}, bf16[4,48,256]{2,1,0:T(8,128)(2,1)S(1)}, bf16[4,4,40,256...) custom-call(bf16[4,8,40,256]{3,2,1,0:T(8,128)(2,1)} %features.1, ...), custom_call_target="tpu_custom_call" | custom-call | flops 100000000 | bytes 4194304 | tf_op jit(solution)/shard_map/pallas_call | solution.py:41
  2.4 4.5 %collective-permute-start.2 = (bf16[4,4,40,256]{3,2,1,0:T(8,128)(2,1)S(1)}, bf16[4,4,40,256]{3,2,1,0:T(8,128)(2,1)S(1)}, u32[]{:S(2)}, u32[]{:S(2)}) collective-permute-start(bf16[4,4,40,256]{3,2,1,0:T(8,128)(2,1)S(1)} %get-tuple-element.76), channel_id=1, source_target_pairs={{4,8},{8,4},{12,16},{16,12},{20,24},{24,20},{5,9},{9,5},{13,17},{1... | collective-permute-start | bytes 983048 | tf_op jit(solution)/shard_map/ppermute | solution.py:691
  6.9 1.4 %collective-permute-start = (bf16[4,48,256]{2,1,0:T(8,128)(2,1)S(1)}, bf16[4,48,256]{2,1,0:T(8,128)(2,1)S(1)}, u32[]{:S(2)}, u32[]{:S(2)}) collective-permute-start(bf16[4,48,256]{2,1,0:T(8,128)(2,1)S(1)} %get-tuple-element.72), channel_id=1, source_target_pairs={{0,1},{1,0},{2,3},{3,2},{4,5},{5,4},{6,7},{7,6},{8,9},{9,8},{10,11... | collective-permute-start | bytes 294920 | tf_op jit(solution)/shard_map/ppermute | solution.py:691
  8.2 0.7 collective-permute-start.1
  8.9 6.0 %collective-permute-start.3 = (bf16[4,16,256]{2,1,0:T(8,128)(2,1)S(1)}, bf16[4,16,256]{2,1,0:T(8,128)(2,1)S(1)}, u32[]{:S(2)}, u32[]{:S(2)}) collective-permute-start(bf16[4,16,256]{2,1,0:T(8,128)(2,1)S(1)} %get-tuple-element.77), channel_id=1, source_target_pairs={{4,9},{5,8},{6,11},{7,10},{8,5},{9,4},{10,7},{11,6},{12,17},{13,16... | collective-permute-start | bytes 98312 | tf_op jit(solution)/shard_map/ppermute | solution.py:707
  14.9 0.7 collective-permute-start.4
  15.6 0.0 copy-start.1
  15.6 2.5 %shard_map.170 = (bf16[2304,256]{1,0:T(8,128)(2,1)S(1)}, bf16[2304,256]{1,0:T(8,128)(2,1)S(1)}) custom-call(f32[9216,128]{1,0:T(8,128)} %bitcast.37), custom_call_target="tpu_custom_call" | custom-call | bytes 1024 | tf_op jit(solution)/shard_map/pallas_call | solution.py:41
  18.1 0.0 collective-permute-done.rc
  18.1 0.0 collective-permute-done.1.rd
  18.2 0.2 shard_map.169
  18.4 0.0 collective-permute-done.3.rb_c
  18.4 0.0 collective-permute-done.4.rb_d
  18.4 0.0 collective-permute-done.2.rb
  18.4 0.1 collective-permute-start.5
  18.5 1.6 %shard_map.171 = (f32[2304,256]{1,0:T(8,128)S(1)}, f32[16,256]{1,0:T(8,128)S(1)}, bf16[1920,768]{1,0:T(8,128)(2,1)S(1)}) custom-call(bf16[4,8,48,256]{3,2,1,0:T(8,128)(2,1)S(1)} %get-tuple-element.74.ext, bf16[2304,256]{1,0:T(8,128)(2,1)S(1)} %get-tuple-element.84.w.w_far), custom_call_target="tpu_custom_call" | custom-call | bytes 1024 | tf_op jit(solution)/shard_map/pallas_call | solution.py:41
  20.1 0.1 collective-permute-done.5.ra
  20.2 1.6 %shard_map.172 = (f32[2304,256]{1,0:T(8,128)S(1)}, f32[32,2,256]{2,1,0:T(2,128)S(1)}, bf16[1920,768]{1,0:T(8,128)(2,1)S(1)}, bf16[4,2,48,256]{3,2,1,0:T(8,128)(2,1)S(1)}) custom-call(bf16[4,8,48,256]{3,2,1,0:T(8,128)(2,1)S(1)} %get-tuple-element.74.ext, ...), custom_call_target="tpu_custom_call", output_to_operand_aliasing={{0}: (7, {}), {2}: (8, {})} | custom-call | bytes 1024 | tf_op jit(solution)/shard_map/pallas_call | solution.py:41
  21.8 11.7 %all_to_all.20.st = f32[32,2,256]{2,1,0:T(2,128)S(1)} all-to-all(f32[32,2,256]{2,1,0:T(2,128)S(1)} %get-tuple-element.89), channel_id=1, replica_groups=mesh['rows'=8,'cols'=4] {'rows','cols'}, dimensions={0} | all-to-all | bytes 131072 | tf_op jit(solution)/shard_map/all_to_all | solution.py:719
  33.5 2.7 %shard_map.173 = (bf16[2304,768]{1,0:T(8,128)(2,1)S(1)}, f32[1920,256]{1,0:T(8,128)S(1)}, f32[32,4,256]{2,1,0:T(4,128)S(1)}, f32[8,256]{1,0:T(8,128)S(1)}) custom-call(f32[2304,256]{1,0:T(8,128)S(1)} %get-tuple-element.88.z1.z, f32[32,2,256]{2,1,0:T(2,128)S(1)} %all_to_all.20.st, f32[4,256]{1,0:T(4,128)S(1)} %copy-done.4, ...), custom_call_target="tpu_custom_call" | custom-call | flops 2264924160 | bytes 4194304 | tf_op jit(solution)/shard_map/pallas_call | solution.py:41
  36.2 9.7 %all_to_all.21.st.st2 = f32[32,4,256]{2,1,0:T(4,128)S(1)} all-to-all(f32[32,4,256]{2,1,0:T(4,128)S(1)} %get-tuple-element.93), channel_id=1, replica_groups=mesh['rows'=8,'cols'=4] {'rows','cols'}, dimensions={0} | all-to-all | bytes 262144 | tf_op jit(solution)/shard_map/all_to_all | solution.py:719
  45.8 2.5 %shard_map.174 = (bf16[1920,256]{1,0:T(8,128)(2,1)S(1)}, f32[2304,128]{1,0:T(8,128)S(1)}, bf16[2304,128]{1,0:T(8,128)(2,1)S(1)}) custom-call(f32[1920,256]{1,0:T(8,128)S(1)} %get-tuple-element.92.z2, f32[32,4,256]{2,1,0:T(4,128)S(1)} %all_to_all.21.st.st2, f32[8,256]{1,0:T(8,128)S(1)} %get-tuple-element.94.own, f32[4,256]{1,0:T(4,128)S(1)} %copy-done.4, ...), custom_call_target="tpu_custom_call" | custom-call | flops 1811939328 | bytes 4194304 | tf_op jit(solution)/shard_map/pallas_call | solution.py:41
  48.4 1.4 %collective-permute-start.6 = (bf16[2304,128]{1,0:T(8,128)(2,1)S(1)}, bf16[2304,128]{1,0:T(8,128)(2,1)S(1)}, u32[]{:S(2)}, u32[]{:S(2)}) collective-permute-start(bf16[2304,128]{1,0:T(8,128)(2,1)S(1)} %get-tuple-element.100), channel_id=1, source_target_pairs={{0,4},{4,0},{8,12},{12,8},{16,20},{20,16},{24,28},{28,24},{1,5},{5... | collective-permute-start | bytes 1769480 | tf_op jit(solution)/shard_map/ppermute | solution.py:691
  49.8 1.9 %shard_map.175 = (f32[1536,256]{1,0:T(8,128)S(1)}, f32[16,256]{1,0:T(8,128)S(1)}, bf16[4,8,40,256]{3,2,1,0:T(8,128)(2,1)S(1)}) custom-call(bf16[1920,256]{1,0:T(8,128)(2,1)S(1)} %get-tuple-element.97.d, bf16[2304,256]{1,0:T(8,128)(2,1)S(1)} %get-tuple-element.90.w, f32[2304,256]{1,0:T(8,128)S(1)} %get-tuple-element.88.z1.z, ...), custom_call_target="tpu_custom_call" | custom-call | bytes 1024 | tf_op jit(solution)/shard_map/pallas_call | solution.py:41
  51.7 0.0 collective-permute-done.6.got
  51.7 0.2 shard_map.176
  51.9 0.6 collective-permute-start.7
  52.5 0.8 shard_map.177
  53.2 9.3 %all_to_all.22.st3 = f32[32,2,256]{2,1,0:T(2,128)S(1)} all-to-all(f32[32,2,256]{2,1,0:T(2,128)S(1)} %get-tuple-element.110), channel_id=1, replica_groups=mesh['rows'=8,'cols'=4] {'rows','cols'}, dimensions={0} | all-to-all | bytes 131072 | tf_op jit(solution)/shard_map/all_to_all | solution.py:719
  62.5 0.0 collective-permute-done.7.came
  62.5 0.1 shard_map.178.kept
  62.6 1.5 %shard_map.179 = (bf16[1536,256]{1,0:T(8,128)(2,1)S(1)}, bf16[4,1,48,256]{3,2,1,0:T(8,128)(2,1)S(1)}, bf16[4,1,48,256]{3,2,1,0:T(8,128)(2,1)S(1)}, bf16[2304,128]{1,0:T(8,128)(2,1)S(1)}, bf16[256,1536]{1,0:T(8,128)(2,1)S(1)}) custom-call(f32[1536,256]{1,0:T(8,128)S(1)} %get-tuple-element.113.dn, f32[2304,256]{1,0:T(8,128)S(1)} %get-tuple-element.88.z1.z, ...), custom_call_target="tpu_custom_call" | custom-call | bytes 1024 | tf_op jit(solution)/shard_map/pallas_call | solution.py:41
  64.1 0.9 collective-permute-start.10
  65.0 1.2 %shard_map.181.keep = f32[2304,128]{1,0:T(8,128)S(1)} custom-call(bf16[1920,768]{1,0:T(8,128)(2,1)S(1)} %get-tuple-element.115.x, bf16[256,1536]{1,0:T(8,128)(2,1)S(1)} %get-tuple-element.119.dt_ref), custom_call_target="tpu_custom_call" | custom-call | bytes 1024 | tf_op jit(solution)/shard_map/pallas_call | solution.py:41
  66.2 0.4 collective-permute-done.10.got
  66.6 1.0 %shard_map.182 = bf16[32,112,128]{2,1,0:T(8,128)(2,1)} custom-call(f32[2304,128]{1,0:T(8,128)S(1)} %shard_map.181.keep, bf16[2304,128]{1,0:T(8,128)(2,1)S(1)} %collective-permute-done.10.got, f32[32,40,128]{2,1,0:T(8,128)S(1)} %shard_map.178.kept), custom_call_target="tpu_custom_call" | custom-call | flops 1000000000 | bytes 4194304 | tf_op jit(solution)/shard_map/pallas_call | solution.py:41
  67.6 0.0 copy-start.5
  67.7 2.6 %all-to-all-start.3 = ((bf16[32,112,128]{2,1,0:T(8,128)(2,1)}), bf16[32,112,128]{2,1,0:T(8,128)(2,1)S(1)}, u32[]{:S(2)}, u32[]{:S(2)}) async-start(bf16[32,112,128]{2,1,0:T(8,128)(2,1)} %shard_map.182), calls=%async_computation.3 | async-start | bytes 1835008 | tf_op jit(solution)/shard_map/all_to_all | solution.py:719
  70.3 0.5 collective-permute-start.8
  70.8 3.3 %collective-permute-start.9 = (bf16[4,1,48,256]{3,2,1,0:T(8,128)(2,1)S(1)}, bf16[4,1,48,256]{3,2,1,0:T(8,128)(2,1)S(1)}, u32[]{:S(2)}, u32[]{:S(2)}) collective-permute-start(bf16[4,1,48,256]{3,2,1,0:T(8,128)(2,1)S(1)} %get-tuple-element.118), channel_id=1, source_target_pairs={{4,8},{8,4},{12,16},{16,12},{20,24},{24,20},{5,9},{9,5},{13,17},{1... | collective-permute-start | bytes 294920 | tf_op jit(solution)/shard_map/ppermute | solution.py:691
  74.1 0.8 copy.34
  74.9 0.0 collective-permute-done.8.ra
  74.9 5.6 %collective-permute-done.9.rb = bf16[4,1,48,256]{3,2,1,0:T(8,128)(2,1)S(1)} collective-permute-done((bf16[4,1,48,256]{3,2,1,0:T(8,128)(2,1)S(1)}, bf16[4,1,48,256]{3,2,1,0:T(8,128)(2,1)S(1)}, u32[]{:S(2)}, u32[]{:S(2)}) %collective-permute-start.9) | collective-permute-done | bytes 98336 | tf_op jit(solution)/shard_map/ppermute | solution.py:691
  80.5 0.0 copy-start.7
  80.5 4.7 %shard_map.180 = f32[4,8,40,256]{3,2,1,0:T(8,128)} custom-call(bf16[1536,256]{1,0:T(8,128)(2,1)S(1)} %get-tuple-element.116.e, bf16[4,1,48,256]{3,2,1,0:T(8,128)(2,1)S(1)} %collective-permute-done.8.ra, bf16[4,1,48,256]{3,2,1,0:T(8,128)(2,1)S(1)} %collective-permute-done.9.rb, bf16[2304,256]{1,0:T(8,128)(2,1)} %copy-done, bf16[4,8,40,256]{3,2,1,0:T(8,128)(2,1)} %cot_far.1, ...), custom_call_target="tpu_custom_call" | custom-call | flops 1811939328 | bytes 4194304 | tf_op jit(solution)/shard_map/pallas_call | solution.py:41
  85.2 0.9 constant_dynamic-slice_fusion.w
  86.1 7.9 %all-to-all-done.3.parts = bf16[32,112,128]{2,1,0:T(8,128)(2,1)S(1)} async-done(((bf16[32,112,128]{2,1,0:T(8,128)(2,1)}), bf16[32,112,128]{2,1,0:T(8,128)(2,1)S(1)}, u32[]{:S(2)}, u32[]{:S(2)}) %all-to-all-start.3) | async-done | bytes 917536 | tf_op jit(solution)/shard_map/all_to_all | solution.py:719
  94.0 1.1 %shard_map.183 = (f32[288,128]{1,0:T(8,128)}, f32[288,128]{1,0:T(8,128)}, f32[288,128]{1,0:T(8,128)}, f32[288,128]{1,0:T(8,128)}, f32[4,256]{1,0:T(4,128)}, /*in...) custom-call(bf16[32,112,128]{2,1,0:T(8,128)(2,1)S(1)} %all-to-all-done.3.parts, ...), custom_call_target="tpu_custom_call" | custom-call | flops 100000000 | bytes 4194304 | tf_op jit(solution)/shard_map/pallas_call | solution.py:41
  (13 shorter events, 0.0 us)
Async XLA Ops:
  2.4 16.0 %collective-permute-start.2 = (bf16[4,4,40,256]{3,2,1,0:T(8,128)(2,1)S(1)}, bf16[4,4,40,256]{3,2,1,0:T(8,128)(2,1)S(1)}, u32[]{:S(2)}, u32[]{:S(2)}) collective-permute-start(bf16[4,4,40,256]{3,2,1,0:T(8,128)(2,1)S(1)} %get-tuple-element.76), channel_id=1, source_target_pairs={{4,8},{8,4},{12,16},{16,12},{20,24},{24,20},{5,9},{9,5},{13,17},{1... | collective-permute-start | bytes 983048 | tf_op jit(solution)/shard_map/ppermute | solution.py:691
  6.9 11.3 %collective-permute-start = (bf16[4,48,256]{2,1,0:T(8,128)(2,1)S(1)}, bf16[4,48,256]{2,1,0:T(8,128)(2,1)S(1)}, u32[]{:S(2)}, u32[]{:S(2)}) collective-permute-start(bf16[4,48,256]{2,1,0:T(8,128)(2,1)S(1)} %get-tuple-element.72), channel_id=1, source_target_pairs={{0,1},{1,0},{2,3},{3,2},{4,5},{5,4},{6,7},{7,6},{8,9},{9,8},{10,11... | collective-permute-start | bytes 294920 | tf_op jit(solution)/shard_map/ppermute | solution.py:691
  8.2 9.9 %collective-permute-start.1 = (bf16[4,48,256]{2,1,0:T(8,128)(2,1)S(1)}, bf16[4,48,256]{2,1,0:T(8,128)(2,1)S(1)}, u32[]{:S(2)}, u32[]{:S(2)}) collective-permute-start(bf16[4,48,256]{2,1,0:T(8,128)(2,1)S(1)} %get-tuple-element.73), channel_id=1, source_target_pairs={{1,2},{2,1},{5,6},{6,5},{9,10},{10,9},{13,14},{14,13},{17,18},{18,... | collective-permute-start | bytes 294920 | tf_op jit(solution)/shard_map/ppermute | solution.py:691
  8.9 9.5 %collective-permute-start.3 = (bf16[4,16,256]{2,1,0:T(8,128)(2,1)S(1)}, bf16[4,16,256]{2,1,0:T(8,128)(2,1)S(1)}, u32[]{:S(2)}, u32[]{:S(2)}) collective-permute-start(bf16[4,16,256]{2,1,0:T(8,128)(2,1)S(1)} %get-tuple-element.77), channel_id=1, source_target_pairs={{4,9},{5,8},{6,11},{7,10},{8,5},{9,4},{10,7},{11,6},{12,17},{13,16... | collective-permute-start | bytes 98312 | tf_op jit(solution)/shard_map/ppermute | solution.py:707
  14.9 3.4 %collective-permute-start.4 = (bf16[4,16,256]{2,1,0:T(8,128)(2,1)S(1)}, bf16[4,16,256]{2,1,0:T(8,128)(2,1)S(1)}, u32[]{:S(2)}, u32[]{:S(2)}) collective-permute-start(bf16[4,16,256]{2,1,0:T(8,128)(2,1)S(1)} %get-tuple-element.78), channel_id=1, source_target_pairs={{5,10},{6,9},{9,6},{10,5},{13,18},{14,17},{17,14},{18,13},{21,26},... | collective-permute-start | bytes 98312 | tf_op jit(solution)/shard_map/ppermute | solution.py:707
  15.6 2.5 %copy-start.1 = (bf16[4,8,40,256]{3,2,1,0:T(8,128)(2,1)S(1)}, bf16[4,8,40,256]{3,2,1,0:T(8,128)(2,1)}, u32[]{:S(2)}) copy-start(bf16[4,8,40,256]{3,2,1,0:T(8,128)(2,1)} %cot_far.1) | copy-start | bytes 1966084
  18.1 3.7 %copy-start = (bf16[2304,256]{1,0:T(8,128)(2,1)}, bf16[2304,256]{1,0:T(8,128)(2,1)S(1)}, u32[]{:S(2)}) copy-start(bf16[2304,256]{1,0:T(8,128)(2,1)S(1)} %get-tuple-element.84.w.w_far) | copy-start | bytes 3538948
  18.4 1.8 %collective-permute-start.5 = (bf16[4,4,48,256]{3,2,1,0:T(8,128)(2,1)S(1)}, bf16[4,4,48,256]{3,2,1,0:T(8,128)(2,1)S(1)}, u32[]{:S(2)}, u32[]{:S(2)}) collective-permute-start(bf16[4,4,48,256]{3,2,1,0:T(8,128)(2,1)S(1)} %get-tuple-element.80), channel_id=1, source_target_pairs={{0,4},{4,0},{8,12},{12,8},{16,20},{20,16},{24,28},{28,24},{1,5},{5... | collective-permute-start | bytes 1179656 | tf_op jit(solution)/shard_map/ppermute | solution.py:691
  20.2 13.3 %copy-start.4 = (f32[4,256]{1,0:T(4,128)S(1)}, f32[4,256]{1,0:T(4,128)}, u32[]{:S(2)}) copy-start(f32[4,256]{1,0:T(4,128)} %params.11) | copy-start | bytes 12292
  48.4 3.3 %collective-permute-start.6 = (bf16[2304,128]{1,0:T(8,128)(2,1)S(1)}, bf16[2304,128]{1,0:T(8,128)(2,1)S(1)}, u32[]{:S(2)}, u32[]{:S(2)}) collective-permute-start(bf16[2304,128]{1,0:T(8,128)(2,1)S(1)} %get-tuple-element.100), channel_id=1, source_target_pairs={{0,4},{4,0},{8,12},{12,8},{16,20},{20,16},{24,28},{28,24},{1,5},{5... | collective-permute-start | bytes 1769480 | tf_op jit(solution)/shard_map/ppermute | solution.py:691
  51.9 10.6 %collective-permute-start.7 = (bf16[32,40,128]{2,1,0:T(8,128)(2,1)S(1)}, bf16[32,40,128]{2,1,0:T(8,128)(2,1)S(1)}, u32[]{:S(2)}, u32[]{:S(2)}) collective-permute-start(bf16[32,40,128]{2,1,0:T(8,128)(2,1)S(1)} %get-tuple-element.112), channel_id=1, source_target_pairs={{0,8},{4,12},{8,0},{12,4},{16,24},{20,28},{24,16},{28,20},{1,9},{5... | collective-permute-start | bytes 983048 | tf_op jit(solution)/shard_map/ppermute | solution.py:860
  64.1 2.5 %collective-permute-start.10 = (bf16[2304,128]{1,0:T(8,128)(2,1)S(1)}, bf16[2304,128]{1,0:T(8,128)(2,1)S(1)}, u32[]{:S(2)}, u32[]{:S(2)}) collective-permute-start(bf16[2304,128]{1,0:T(8,128)(2,1)S(1)} %get-tuple-element.120), channel_id=1, source_target_pairs={{0,4},{4,0},{8,12},{12,8},{16,20},{20,16},{24,28},{28,24},{1,5},{5... | collective-permute-start | bytes 1769480 | tf_op jit(solution)/shard_map/ppermute | solution.py:691
  67.6 12.8 %copy-start.5 = (s32[4,8,40]{2,1,0:T(8,128)S(1)}, s32[4,8,40]{2,1,0:T(8,128)}, u32[]{:S(2)}) copy-start(s32[4,8,40]{2,1,0:T(8,128)} %occ.1) | copy-start | bytes 15364
  67.7 26.4 %all-to-all-start.3 = ((bf16[32,112,128]{2,1,0:T(8,128)(2,1)}), bf16[32,112,128]{2,1,0:T(8,128)(2,1)S(1)}, u32[]{:S(2)}, u32[]{:S(2)}) async-start(bf16[32,112,128]{2,1,0:T(8,128)(2,1)} %shard_map.182), calls=%async_computation.3 | async-start | bytes 1835008 | tf_op jit(solution)/shard_map/all_to_all | solution.py:719
  70.3 4.6 %collective-permute-start.8 = (bf16[4,1,48,256]{3,2,1,0:T(8,128)(2,1)S(1)}, bf16[4,1,48,256]{3,2,1,0:T(8,128)(2,1)S(1)}, u32[]{:S(2)}, u32[]{:S(2)}) collective-permute-start(bf16[4,1,48,256]{3,2,1,0:T(8,128)(2,1)S(1)} %get-tuple-element.117), channel_id=1, source_target_pairs={{0,4},{4,0},{8,12},{12,8},{16,20},{20,16},{24,28},{28,24},{1,5},{5... | collective-permute-start | bytes 294920 | tf_op jit(solution)/shard_map/ppermute | solution.py:691
  70.8 9.7 %collective-permute-start.9 = (bf16[4,1,48,256]{3,2,1,0:T(8,128)(2,1)S(1)}, bf16[4,1,48,256]{3,2,1,0:T(8,128)(2,1)S(1)}, u32[]{:S(2)}, u32[]{:S(2)}) collective-permute-start(bf16[4,1,48,256]{3,2,1,0:T(8,128)(2,1)S(1)} %get-tuple-element.118), channel_id=1, source_target_pairs={{4,8},{8,4},{12,16},{16,12},{20,24},{24,20},{5,9},{9,5},{13,17},{1... | collective-permute-start | bytes 294920 | tf_op jit(solution)/shard_map/ppermute | solution.py:691
  80.5 13.5 %copy-start.2 = (f32[2,18432]{1,0:T(2,128)S(1)}, f32[2,18432]{1,0:T(2,128)}, u32[]{:S(2)}) copy-start(f32[2,18432]{1,0:T(2,128)} %param.13) | copy-start | bytes 442372
  80.5 13.5 %copy-start.3 = (f32[2,18432]{1,0:T(2,128)S(1)}, f32[2,18432]{1,0:T(2,128)}, u32[]{:S(2)}) copy-start(f32[2,18432]{1,0:T(2,128)} %param.14) | copy-start | bytes 442372
  80.5 13.5 %copy-start.6 = (f32[4,256]{1,0:T(4,128)S(1)}, f32[4,256]{1,0:T(4,128)}, u32[]{:S(2)}) copy-start(f32[4,256]{1,0:T(4,128)} %n_first.1) | copy-start | bytes 12292
  80.5 13.5 %copy-start.7 = (f32[4,256]{1,0:T(4,128)S(1)}, f32[4,256]{1,0:T(4,128)}, u32[]{:S(2)}) copy-start(f32[4,256]{1,0:T(4,128)} %n_second.1) | copy-start | bytes 12292

commit v9 on v8

--- a/solution.py
+++ b/solution.py
@@ -107,7 +107,7 @@
         self.right = (col < ncols - 1).astype(F32)
         self.left = (col > 0).astype(F32)
         self.core = row % 2
-        self.second = row // 2 % 2
+        self.second = row // 4 % 2
         self.odd_row = row % 2 == 1
         self.odd_col = col % 2 == 1
         self.index = row * ncols + col
@@ -673,8 +673,8 @@
         else:
             rows = half_rows(share)
             first = over(lambda row: row % 2 == half, slice(0, share), every)
-            upper = over(lambda row: row % 4 == half, slice(share, None), every)
-            lower = over(lambda row: row % 4 == half + 2, slice(2 * rows, None), every)
+            upper = over(lambda row: row % 2 == half and row // 4 % 2 == 0, slice(share, None), every)
+            lower = over(lambda row: row % 2 == half and row // 4 % 2 == 1, slice(2 * rows, None), every)
             grads += [(0, half, first), (1, half, jnp.concatenate([upper, lower], axis=0))]
     for k, half, grad in grads:
         at = pl.ds(2 * half + k, share, stride=4)
@@ -832,7 +832,7 @@
     )(z2, st2, own_sums, norm_scale_bias, cot_ext, cot_next, h)
     got2 = swapped(send2, "rows", 0)
     nrows = lax.axis_size("rows")
-    cut_again = nrows % 4 == 0 and taps // devices % 8 == 0
+    cut_again = nrows % 8 == 0 and taps // devices % 8 == 0
     hidden_shape, output_shape = held((n3, chans), F32), held(features.shape, BF16)
 
     def hidden_gradient(scenes, part_shape, *before, **options):
@@ -857,7 +857,7 @@
             size=1024,
             scratch=[pltpu.VMEM((taps, chans // 2), F32)],
         )(keep2, got2)
-        came = lax.ppermute(sent, "rows", [(i, i ^ 2) for i in range(nrows)])
+        came = lax.ppermute(sent, "rows", [(i, i ^ 4) for i in range(nrows)])
         kept, part = lax.optimization_barrier((kept, part))
     dn1, st, block_out = hidden_gradient(
         range(len(early), scenes),

time: 95.6 us -> 95.5 us (level)
  no operation moved by 1% of the time
where the time goes in v9:
time: 95.5 us; the launch traced here: 95.1 us
  blocking collectives  30.5 us (32%)
  Pallas kernels  25.1 us (26%)
  starting transfers between devices  22.7 us (24%)
  waiting for transfers between devices  14.1 us (15%)
  local copies, waits for them, and re-layouts  1.8 us (2%)
    all_to_all x3, blocking collectives, exchange(): return lax.all_to_all(parts, BOTH, 0, 0, tiled=True)  30.5 us
    pallas_call x16, Pallas kernels, call(): pl.pallas_call(body, out_shape=out_shape, in_specs=specs, out_specs=[pl.B...  25.1 us
    ppermute x8, starting transfers between devices, swapped(): return lax.ppermute(block, axis, pairs)  12.8 us
    all_to_all x1, waiting for transfers between devices, exchange(): return lax.all_to_all(parts, BOTH, 0, 0, tiled=True)  7.9 us
    ppermute x2, starting transfers between devices, swapped_both(): return lax.ppermute(block, BOTH, pairs)  6.69 us
    ppermute x8, waiting for transfers between devices, swapped(): return lax.ppermute(block, axis, pairs)  6.16 us
    all_to_all x1, starting transfers between devices, exchange(): return lax.all_to_all(parts, BOTH, 0, 0, tiled=True)  2.63 us
  transfers between devices with their start and end apart: 12, of which 4 were waited for; matrix products, arithmetic and copies ran while one was open for 2% of the time, Pallas kernels for 13%

profile of v9, /device:TPU:1, one launch (start us, length us, event | category | flops | bytes accessed | tf_op | source)
XLA Modules:
  0.0 95.1 jit_solution(12813050755845541414)
XLA Ops:
  0.6 1.7 %shard_map.168 = (bf16[4,8,40,256]{3,2,1,0:T(8,128)(2,1)S(1)}, bf16[4,48,256]{2,1,0:T(8,128)(2,1)S(1)}, bf16[4,48,256]{2,1,0:T(8,128)(2,1)S(1)}, bf16[4,4,40,256...) custom-call(bf16[4,8,40,256]{3,2,1,0:T(8,128)(2,1)} %features.1, ...), custom_call_target="tpu_custom_call" | custom-call | flops 100000000 | bytes 4194304 | tf_op jit(solution)/shard_map/pallas_call | solution.py:41
  2.4 4.5 %collective-permute-start.2 = (bf16[4,4,40,256]{3,2,1,0:T(8,128)(2,1)S(1)}, bf16[4,4,40,256]{3,2,1,0:T(8,128)(2,1)S(1)}, u32[]{:S(2)}, u32[]{:S(2)}) collective-permute-start(bf16[4,4,40,256]{3,2,1,0:T(8,128)(2,1)S(1)} %get-tuple-element.76), channel_id=1, source_target_pairs={{4,8},{8,4},{12,16},{16,12},{20,24},{24,20},{5,9},{9,5},{13,17},{1... | collective-permute-start | bytes 983048 | tf_op jit(solution)/shard_map/ppermute | solution.py:691
  6.9 1.4 %collective-permute-start = (bf16[4,48,256]{2,1,0:T(8,128)(2,1)S(1)}, bf16[4,48,256]{2,1,0:T(8,128)(2,1)S(1)}, u32[]{:S(2)}, u32[]{:S(2)}) collective-permute-start(bf16[4,48,256]{2,1,0:T(8,128)(2,1)S(1)} %get-tuple-element.72), channel_id=1, source_target_pairs={{0,1},{1,0},{2,3},{3,2},{4,5},{5,4},{6,7},{7,6},{8,9},{9,8},{10,11... | collective-permute-start | bytes 294920 | tf_op jit(solution)/shard_map/ppermute | solution.py:691
  8.2 0.7 collective-permute-start.1
  8.9 6.0 %collective-permute-start.3 = (bf16[4,16,256]{2,1,0:T(8,128)(2,1)S(1)}, bf16[4,16,256]{2,1,0:T(8,128)(2,1)S(1)}, u32[]{:S(2)}, u32[]{:S(2)}) collective-permute-start(bf16[4,16,256]{2,1,0:T(8,128)(2,1)S(1)} %get-tuple-element.77), channel_id=1, source_target_pairs={{4,9},{5,8},{6,11},{7,10},{8,5},{9,4},{10,7},{11,6},{12,17},{13,16... | collective-permute-start | bytes 98312 | tf_op jit(solution)/shard_map/ppermute | solution.py:707
  14.9 0.7 collective-permute-start.4
  15.6 0.0 copy-start.1
  15.6 2.5 %shard_map.170 = (bf16[2304,256]{1,0:T(8,128)(2,1)S(1)}, bf16[2304,256]{1,0:T(8,128)(2,1)S(1)}) custom-call(f32[9216,128]{1,0:T(8,128)} %bitcast.37), custom_call_target="tpu_custom_call" | custom-call | bytes 1024 | tf_op jit(solution)/shard_map/pallas_call | solution.py:41
  18.1 0.0 collective-permute-done.rc
  18.1 0.0 collective-permute-done.1.rd
  18.2 0.2 shard_map.169
  18.4 0.0 collective-permute-done.3.rb_c
  18.4 0.0 collective-permute-done.4.rb_d
  18.4 0.0 collective-permute-done.2.rb
  18.4 0.1 collective-permute-start.5
  18.5 1.6 %shard_map.171 = (f32[2304,256]{1,0:T(8,128)S(1)}, f32[16,256]{1,0:T(8,128)S(1)}, bf16[1920,768]{1,0:T(8,128)(2,1)S(1)}) custom-call(bf16[4,8,48,256]{3,2,1,0:T(8,128)(2,1)S(1)} %get-tuple-element.74.ext, bf16[2304,256]{1,0:T(8,128)(2,1)S(1)} %get-tuple-element.84.w.w_far), custom_call_target="tpu_custom_call" | custom-call | bytes 1024 | tf_op jit(solution)/shard_map/pallas_call | solution.py:41
  20.1 0.1 collective-permute-done.5.ra
  20.2 1.6 %shard_map.172 = (f32[2304,256]{1,0:T(8,128)S(1)}, f32[32,2,256]{2,1,0:T(2,128)S(1)}, bf16[1920,768]{1,0:T(8,128)(2,1)S(1)}, bf16[4,2,48,256]{3,2,1,0:T(8,128)(2,1)S(1)}) custom-call(bf16[4,8,48,256]{3,2,1,0:T(8,128)(2,1)S(1)} %get-tuple-element.74.ext, ...), custom_call_target="tpu_custom_call", output_to_operand_aliasing={{0}: (7, {}), {2}: (8, {})} | custom-call | bytes 1024 | tf_op jit(solution)/shard_map/pallas_call | solution.py:41
  21.8 11.7 %all_to_all.20.st = f32[32,2,256]{2,1,0:T(2,128)S(1)} all-to-all(f32[32,2,256]{2,1,0:T(2,128)S(1)} %get-tuple-element.89), channel_id=1, replica_groups=mesh['rows'=8,'cols'=4] {'rows','cols'}, dimensions={0} | all-to-all | bytes 131072 | tf_op jit(solution)/shard_map/all_to_all | solution.py:719
  33.5 2.7 %shard_map.173 = (bf16[2304,768]{1,0:T(8,128)(2,1)S(1)}, f32[1920,256]{1,0:T(8,128)S(1)}, f32[32,4,256]{2,1,0:T(4,128)S(1)}, f32[8,256]{1,0:T(8,128)S(1)}) custom-call(f32[2304,256]{1,0:T(8,128)S(1)} %get-tuple-element.88.z1.z, f32[32,2,256]{2,1,0:T(2,128)S(1)} %all_to_all.20.st, f32[4,256]{1,0:T(4,128)S(1)} %copy-done.4, ...), custom_call_target="tpu_custom_call" | custom-call | flops 2264924160 | bytes 4194304 | tf_op jit(solution)/shard_map/pallas_call | solution.py:41
  36.2 9.7 %all_to_all.21.st.st2 = f32[32,4,256]{2,1,0:T(4,128)S(1)} all-to-all(f32[32,4,256]{2,1,0:T(4,128)S(1)} %get-tuple-element.93), channel_id=1, replica_groups=mesh['rows'=8,'cols'=4] {'rows','cols'}, dimensions={0} | all-to-all | bytes 262144 | tf_op jit(solution)/shard_map/all_to_all | solution.py:719
  45.8 2.5 %shard_map.174 = (bf16[1920,256]{1,0:T(8,128)(2,1)S(1)}, f32[2304,128]{1,0:T(8,128)S(1)}, bf16[2304,128]{1,0:T(8,128)(2,1)S(1)}) custom-call(f32[1920,256]{1,0:T(8,128)S(1)} %get-tuple-element.92.z2, f32[32,4,256]{2,1,0:T(4,128)S(1)} %all_to_all.21.st.st2, f32[8,256]{1,0:T(8,128)S(1)} %get-tuple-element.94.own, f32[4,256]{1,0:T(4,128)S(1)} %copy-done.4, ...), custom_call_target="tpu_custom_call" | custom-call | flops 1811939328 | bytes 4194304 | tf_op jit(solution)/shard_map/pallas_call | solution.py:41
  48.4 1.4 %collective-permute-start.6 = (bf16[2304,128]{1,0:T(8,128)(2,1)S(1)}, bf16[2304,128]{1,0:T(8,128)(2,1)S(1)}, u32[]{:S(2)}, u32[]{:S(2)}) collective-permute-start(bf16[2304,128]{1,0:T(8,128)(2,1)S(1)} %get-tuple-element.100), channel_id=1, source_target_pairs={{0,4},{4,0},{8,12},{12,8},{16,20},{20,16},{24,28},{28,24},{1,5},{5... | collective-permute-start | bytes 1769480 | tf_op jit(solution)/shard_map/ppermute | solution.py:691
  49.8 1.9 %shard_map.175 = (f32[1536,256]{1,0:T(8,128)S(1)}, f32[16,256]{1,0:T(8,128)S(1)}, bf16[4,8,40,256]{3,2,1,0:T(8,128)(2,1)S(1)}) custom-call(bf16[1920,256]{1,0:T(8,128)(2,1)S(1)} %get-tuple-element.97.d, bf16[2304,256]{1,0:T(8,128)(2,1)S(1)} %get-tuple-element.90.w, f32[2304,256]{1,0:T(8,128)S(1)} %get-tuple-element.88.z1.z, ...), custom_call_target="tpu_custom_call" | custom-call | bytes 1024 | tf_op jit(solution)/shard_map/pallas_call | solution.py:41
  51.7 0.0 collective-permute-done.6.got
  51.7 0.2 shard_map.176
  51.9 0.6 collective-permute-start.7
  52.5 0.8 shard_map.177
  53.3 9.1 %all_to_all.22.st3 = f32[32,2,256]{2,1,0:T(2,128)S(1)} all-to-all(f32[32,2,256]{2,1,0:T(2,128)S(1)} %get-tuple-element.110), channel_id=1, replica_groups=mesh['rows'=8,'cols'=4] {'rows','cols'}, dimensions={0} | all-to-all | bytes 131072 | tf_op jit(solution)/shard_map/all_to_all | solution.py:719
  62.4 0.0 collective-permute-done.7.came
  62.4 0.1 shard_map.178.kept
  62.5 1.5 %shard_map.179 = (bf16[1536,256]{1,0:T(8,128)(2,1)S(1)}, bf16[4,1,48,256]{3,2,1,0:T(8,128)(2,1)S(1)}, bf16[4,1,48,256]{3,2,1,0:T(8,128)(2,1)S(1)}, bf16[2304,128]{1,0:T(8,128)(2,1)S(1)}, bf16[256,1536]{1,0:T(8,128)(2,1)S(1)}) custom-call(f32[1536,256]{1,0:T(8,128)S(1)} %get-tuple-element.113.dn, f32[2304,256]{1,0:T(8,128)S(1)} %get-tuple-element.88.z1.z, ...), custom_call_target="tpu_custom_call" | custom-call | bytes 1024 | tf_op jit(solution)/shard_map/pallas_call | solution.py:41
  64.0 1.0 %collective-permute-start.10 = (bf16[2304,128]{1,0:T(8,128)(2,1)S(1)}, bf16[2304,128]{1,0:T(8,128)(2,1)S(1)}, u32[]{:S(2)}, u32[]{:S(2)}) collective-permute-start(bf16[2304,128]{1,0:T(8,128)(2,1)S(1)} %get-tuple-element.120), channel_id=1, source_target_pairs={{0,4},{4,0},{8,12},{12,8},{16,20},{20,16},{24,28},{28,24},{1,5},{5... | collective-permute-start | bytes 1769480 | tf_op jit(solution)/shard_map/ppermute | solution.py:691
  65.0 1.2 %shard_map.181.keep = f32[2304,128]{1,0:T(8,128)S(1)} custom-call(bf16[1920,768]{1,0:T(8,128)(2,1)S(1)} %get-tuple-element.115.x, bf16[256,1536]{1,0:T(8,128)(2,1)S(1)} %get-tuple-element.119.dt_ref), custom_call_target="tpu_custom_call" | custom-call | bytes 1024 | tf_op jit(solution)/shard_map/pallas_call | solution.py:41
  66.2 0.4 collective-permute-done.10.got
  66.6 1.0 %shard_map.182 = bf16[32,112,128]{2,1,0:T(8,128)(2,1)} custom-call(f32[2304,128]{1,0:T(8,128)S(1)} %shard_map.181.keep, bf16[2304,128]{1,0:T(8,128)(2,1)S(1)} %collective-permute-done.10.got, f32[32,40,128]{2,1,0:T(8,128)S(1)} %shard_map.178.kept), custom_call_target="tpu_custom_call" | custom-call | flops 1000000000 | bytes 4194304 | tf_op jit(solution)/shard_map/pallas_call | solution.py:41
  67.6 0.0 copy-start.5
  67.6 2.6 %all-to-all-start.3 = ((bf16[32,112,128]{2,1,0:T(8,128)(2,1)}), bf16[32,112,128]{2,1,0:T(8,128)(2,1)S(1)}, u32[]{:S(2)}, u32[]{:S(2)}) async-start(bf16[32,112,128]{2,1,0:T(8,128)(2,1)} %shard_map.182), calls=%async_computation.3 | async-start | bytes 1835008 | tf_op jit(solution)/shard_map/all_to_all | solution.py:719
  70.3 0.5 collective-permute-start.8
  70.7 3.3 %collective-permute-start.9 = (bf16[4,1,48,256]{3,2,1,0:T(8,128)(2,1)S(1)}, bf16[4,1,48,256]{3,2,1,0:T(8,128)(2,1)S(1)}, u32[]{:S(2)}, u32[]{:S(2)}) collective-permute-start(bf16[4,1,48,256]{3,2,1,0:T(8,128)(2,1)S(1)} %get-tuple-element.118), channel_id=1, source_target_pairs={{4,8},{8,4},{12,16},{16,12},{20,24},{24,20},{5,9},{9,5},{13,17},{1... | collective-permute-start | bytes 294920 | tf_op jit(solution)/shard_map/ppermute | solution.py:691
  74.0 0.8 copy.34
  74.9 0.0 collective-permute-done.8.ra
  74.9 5.6 %collective-permute-done.9.rb = bf16[4,1,48,256]{3,2,1,0:T(8,128)(2,1)S(1)} collective-permute-done((bf16[4,1,48,256]{3,2,1,0:T(8,128)(2,1)S(1)}, bf16[4,1,48,256]{3,2,1,0:T(8,128)(2,1)S(1)}, u32[]{:S(2)}, u32[]{:S(2)}) %collective-permute-start.9) | collective-permute-done | bytes 98336 | tf_op jit(solution)/shard_map/ppermute | solution.py:691
  80.5 0.0 copy-start.7
  80.5 4.7 %shard_map.180 = f32[4,8,40,256]{3,2,1,0:T(8,128)} custom-call(bf16[1536,256]{1,0:T(8,128)(2,1)S(1)} %get-tuple-element.116.e, bf16[4,1,48,256]{3,2,1,0:T(8,128)(2,1)S(1)} %collective-permute-done.8.ra, bf16[4,1,48,256]{3,2,1,0:T(8,128)(2,1)S(1)} %collective-permute-done.9.rb, bf16[2304,256]{1,0:T(8,128)(2,1)} %copy-done, bf16[4,8,40,256]{3,2,1,0:T(8,128)(2,1)} %cot_far.1, ...), custom_call_target="tpu_custom_call" | custom-call | flops 1811939328 | bytes 4194304 | tf_op jit(solution)/shard_map/pallas_call | solution.py:41
  85.2 0.9 constant_dynamic-slice_fusion.w
  86.1 7.9 %all-to-all-done.3.parts = bf16[32,112,128]{2,1,0:T(8,128)(2,1)S(1)} async-done(((bf16[32,112,128]{2,1,0:T(8,128)(2,1)}), bf16[32,112,128]{2,1,0:T(8,128)(2,1)S(1)}, u32[]{:S(2)}, u32[]{:S(2)}) %all-to-all-start.3) | async-done | bytes 917536 | tf_op jit(solution)/shard_map/all_to_all | solution.py:719
  94.0 1.1 %shard_map.183 = (f32[288,128]{1,0:T(8,128)}, f32[288,128]{1,0:T(8,128)}, f32[288,128]{1,0:T(8,128)}, f32[288,128]{1,0:T(8,128)}, f32[4,256]{1,0:T(4,128)}, /*in...) custom-call(bf16[32,112,128]{2,1,0:T(8,128)(2,1)S(1)} %all-to-all-done.3.parts, ...), custom_call_target="tpu_custom_call" | custom-call | flops 100000000 | bytes 4194304 | tf_op jit(solution)/shard_map/pallas_call | solution.py:41
  (13 shorter events, 0.0 us)
Async XLA Ops:
  2.4 16.0 %collective-permute-start.2 = (bf16[4,4,40,256]{3,2,1,0:T(8,128)(2,1)S(1)}, bf16[4,4,40,256]{3,2,1,0:T(8,128)(2,1)S(1)}, u32[]{:S(2)}, u32[]{:S(2)}) collective-permute-start(bf16[4,4,40,256]{3,2,1,0:T(8,128)(2,1)S(1)} %get-tuple-element.76), channel_id=1, source_target_pairs={{4,8},{8,4},{12,16},{16,12},{20,24},{24,20},{5,9},{9,5},{13,17},{1... | collective-permute-start | bytes 983048 | tf_op jit(solution)/shard_map/ppermute | solution.py:691
  6.9 11.3 %collective-permute-start = (bf16[4,48,256]{2,1,0:T(8,128)(2,1)S(1)}, bf16[4,48,256]{2,1,0:T(8,128)(2,1)S(1)}, u32[]{:S(2)}, u32[]{:S(2)}) collective-permute-start(bf16[4,48,256]{2,1,0:T(8,128)(2,1)S(1)} %get-tuple-element.72), channel_id=1, source_target_pairs={{0,1},{1,0},{2,3},{3,2},{4,5},{5,4},{6,7},{7,6},{8,9},{9,8},{10,11... | collective-permute-start | bytes 294920 | tf_op jit(solution)/shard_map/ppermute | solution.py:691
  8.2 9.9 %collective-permute-start.1 = (bf16[4,48,256]{2,1,0:T(8,128)(2,1)S(1)}, bf16[4,48,256]{2,1,0:T(8,128)(2,1)S(1)}, u32[]{:S(2)}, u32[]{:S(2)}) collective-permute-start(bf16[4,48,256]{2,1,0:T(8,128)(2,1)S(1)} %get-tuple-element.73), channel_id=1, source_target_pairs={{1,2},{2,1},{5,6},{6,5},{9,10},{10,9},{13,14},{14,13},{17,18},{18,... | collective-permute-start | bytes 294920 | tf_op jit(solution)/shard_map/ppermute | solution.py:691
  8.9 9.5 %collective-permute-start.3 = (bf16[4,16,256]{2,1,0:T(8,128)(2,1)S(1)}, bf16[4,16,256]{2,1,0:T(8,128)(2,1)S(1)}, u32[]{:S(2)}, u32[]{:S(2)}) collective-permute-start(bf16[4,16,256]{2,1,0:T(8,128)(2,1)S(1)} %get-tuple-element.77), channel_id=1, source_target_pairs={{4,9},{5,8},{6,11},{7,10},{8,5},{9,4},{10,7},{11,6},{12,17},{13,16... | collective-permute-start | bytes 98312 | tf_op jit(solution)/shard_map/ppermute | solution.py:707
  14.9 3.4 %collective-permute-start.4 = (bf16[4,16,256]{2,1,0:T(8,128)(2,1)S(1)}, bf16[4,16,256]{2,1,0:T(8,128)(2,1)S(1)}, u32[]{:S(2)}, u32[]{:S(2)}) collective-permute-start(bf16[4,16,256]{2,1,0:T(8,128)(2,1)S(1)} %get-tuple-element.78), channel_id=1, source_target_pairs={{5,10},{6,9},{9,6},{10,5},{13,18},{14,17},{17,14},{18,13},{21,26},... | collective-permute-start | bytes 98312 | tf_op jit(solution)/shard_map/ppermute | solution.py:707
  15.6 2.5 %copy-start.1 = (bf16[4,8,40,256]{3,2,1,0:T(8,128)(2,1)S(1)}, bf16[4,8,40,256]{3,2,1,0:T(8,128)(2,1)}, u32[]{:S(2)}) copy-start(bf16[4,8,40,256]{3,2,1,0:T(8,128)(2,1)} %cot_far.1) | copy-start | bytes 1966084
  18.1 3.7 %copy-start = (bf16[2304,256]{1,0:T(8,128)(2,1)}, bf16[2304,256]{1,0:T(8,128)(2,1)S(1)}, u32[]{:S(2)}) copy-start(bf16[2304,256]{1,0:T(8,128)(2,1)S(1)} %get-tuple-element.84.w.w_far) | copy-start | bytes 3538948
  18.4 1.8 %collective-permute-start.5 = (bf16[4,4,48,256]{3,2,1,0:T(8,128)(2,1)S(1)}, bf16[4,4,48,256]{3,2,1,0:T(8,128)(2,1)S(1)}, u32[]{:S(2)}, u32[]{:S(2)}) collective-permute-start(bf16[4,4,48,256]{3,2,1,0:T(8,128)(2,1)S(1)} %get-tuple-element.80), channel_id=1, source_target_pairs={{0,4},{4,0},{8,12},{12,8},{16,20},{20,16},{24,28},{28,24},{1,5},{5... | collective-permute-start | bytes 1179656 | tf_op jit(solution)/shard_map/ppermute | solution.py:691
  20.2 13.3 %copy-start.4 = (f32[4,256]{1,0:T(4,128)S(1)}, f32[4,256]{1,0:T(4,128)}, u32[]{:S(2)}) copy-start(f32[4,256]{1,0:T(4,128)} %params.11) | copy-start | bytes 12292
  48.4 3.3 %collective-permute-start.6 = (bf16[2304,128]{1,0:T(8,128)(2,1)S(1)}, bf16[2304,128]{1,0:T(8,128)(2,1)S(1)}, u32[]{:S(2)}, u32[]{:S(2)}) collective-permute-start(bf16[2304,128]{1,0:T(8,128)(2,1)S(1)} %get-tuple-element.100), channel_id=1, source_target_pairs={{0,4},{4,0},{8,12},{12,8},{16,20},{20,16},{24,28},{28,24},{1,5},{5... | collective-permute-start | bytes 1769480 | tf_op jit(solution)/shard_map/ppermute | solution.py:691
  51.9 10.5 %collective-permute-start.7 = (bf16[32,40,128]{2,1,0:T(8,128)(2,1)S(1)}, bf16[32,40,128]{2,1,0:T(8,128)(2,1)S(1)}, u32[]{:S(2)}, u32[]{:S(2)}) collective-permute-start(bf16[32,40,128]{2,1,0:T(8,128)(2,1)S(1)} %get-tuple-element.112), channel_id=1, source_target_pairs={{0,16},{4,20},{8,24},{12,28},{16,0},{20,4},{24,8},{28,12},{1,17},{... | collective-permute-start | bytes 983048 | tf_op jit(solution)/shard_map/ppermute | solution.py:860
  64.0 2.6 %collective-permute-start.10 = (bf16[2304,128]{1,0:T(8,128)(2,1)S(1)}, bf16[2304,128]{1,0:T(8,128)(2,1)S(1)}, u32[]{:S(2)}, u32[]{:S(2)}) collective-permute-start(bf16[2304,128]{1,0:T(8,128)(2,1)S(1)} %get-tuple-element.120), channel_id=1, source_target_pairs={{0,4},{4,0},{8,12},{12,8},{16,20},{20,16},{24,28},{28,24},{1,5},{5... | collective-permute-start | bytes 1769480 | tf_op jit(solution)/shard_map/ppermute | solution.py:691
  67.6 12.8 %copy-start.5 = (s32[4,8,40]{2,1,0:T(8,128)S(1)}, s32[4,8,40]{2,1,0:T(8,128)}, u32[]{:S(2)}) copy-start(s32[4,8,40]{2,1,0:T(8,128)} %occ.1) | copy-start | bytes 15364
  67.6 26.4 %all-to-all-start.3 = ((bf16[32,112,128]{2,1,0:T(8,128)(2,1)}), bf16[32,112,128]{2,1,0:T(8,128)(2,1)S(1)}, u32[]{:S(2)}, u32[]{:S(2)}) async-start(bf16[32,112,128]{2,1,0:T(8,128)(2,1)} %shard_map.182), calls=%async_computation.3 | async-start | bytes 1835008 | tf_op jit(solution)/shard_map/all_to_all | solution.py:719
  70.3 4.6 %collective-permute-start.8 = (bf16[4,1,48,256]{3,2,1,0:T(8,128)(2,1)S(1)}, bf16[4,1,48,256]{3,2,1,0:T(8,128)(2,1)S(1)}, u32[]{:S(2)}, u32[]{:S(2)}) collective-permute-start(bf16[4,1,48,256]{3,2,1,0:T(8,128)(2,1)S(1)} %get-tuple-element.117), channel_id=1, source_target_pairs={{0,4},{4,0},{8,12},{12,8},{16,20},{20,16},{24,28},{28,24},{1,5},{5... | collective-permute-start | bytes 294920 | tf_op jit(solution)/shard_map/ppermute | solution.py:691
  70.7 9.7 %collective-permute-start.9 = (bf16[4,1,48,256]{3,2,1,0:T(8,128)(2,1)S(1)}, bf16[4,1,48,256]{3,2,1,0:T(8,128)(2,1)S(1)}, u32[]{:S(2)}, u32[]{:S(2)}) collective-permute-start(bf16[4,1,48,256]{3,2,1,0:T(8,128)(2,1)S(1)} %get-tuple-element.118), channel_id=1, source_target_pairs={{4,8},{8,4},{12,16},{16,12},{20,24},{24,20},{5,9},{9,5},{13,17},{1... | collective-permute-start | bytes 294920 | tf_op jit(solution)/shard_map/ppermute | solution.py:691
  80.5 13.5 %copy-start.2 = (f32[2,18432]{1,0:T(2,128)S(1)}, f32[2,18432]{1,0:T(2,128)}, u32[]{:S(2)}) copy-start(f32[2,18432]{1,0:T(2,128)} %param.13) | copy-start | bytes 442372
  80.5 13.5 %copy-start.3 = (f32[2,18432]{1,0:T(2,128)S(1)}, f32[2,18432]{1,0:T(2,128)}, u32[]{:S(2)}) copy-start(f32[2,18432]{1,0:T(2,128)} %param.14) | copy-start | bytes 442372
  80.5 13.5 %copy-start.6 = (f32[4,256]{1,0:T(4,128)S(1)}, f32[4,256]{1,0:T(4,128)}, u32[]{:S(2)}) copy-start(f32[4,256]{1,0:T(4,128)} %n_first.1) | copy-start | bytes 12292
  80.5 13.5 %copy-start.7 = (f32[4,256]{1,0:T(4,128)S(1)}, f32[4,256]{1,0:T(4,128)}, u32[]{:S(2)}) copy-start(f32[4,256]{1,0:T(4,128)} %n_second.1) | copy-start | bytes 12292

commit v10 on v9

--- a/solution.py
+++ b/solution.py
@@ -107,7 +107,7 @@
         self.right = (col < ncols - 1).astype(F32)
         self.left = (col > 0).astype(F32)
         self.core = row % 2
-        self.second = row // 4 % 2
+        self.second, self.third = row // 4 % 2, row // 2 % 2
         self.odd_row = row % 2 == 1
         self.odd_col = col % 2 == 1
         self.index = row * ncols + col
@@ -480,6 +480,18 @@
         to_all(st_ref, [jnp.sum(s0, 0, keepdims=True), jnp.sum(s1, 0, keepdims=True) * rstd])
 
 
+def put(refs, rows, value):
+    if not isinstance(refs, tuple):
+        refs = (refs,)
+    at = 0
+    for ref in refs:
+        first, last = max(rows.start, at), min(rows.stop, at + ref.shape[0])
+        if first < last:
+            part = value[first - rows.start : last - rows.start]
+            ref[first - at : last - at, :] = part.astype(ref.dtype)
+        at += ref.shape[0]
+
+
 def half_gradient(g, which, field, rows_field, first_row, dt_ref, out_ref, sums, prepare=None):
     chans, half = g.c, g.c // 2
     span = g.h * g.wp
@@ -502,12 +514,13 @@
                     sums[a * 3 + b] = part
                 else:
                     rows = slice((a * 3 + b) * chans, (a * 3 + b + 1) * chans)
-                    out_ref[rows, :] = (sums[a * 3 + b] + part).T.astype(out_ref.dtype)
+                    put(out_ref, rows, (sums[a * 3 + b] + part).T)
 
 
 def first_gradient_kernel(
-    g, count, dn, z, st, st3, params, x, e_ref, a_ref, b_ref, send, dt_ref, first
+    g, count, dn, z, st, st3, params, x, e_ref, a_ref, b_ref, *refs
 ):
+    *send, dt_ref, first = refs
     place = Place()
     mean, rstd = stats_of(total_of(st), count)
     total = total_of(st3)
@@ -528,7 +541,7 @@
         a_ref[s, 0] = jnp.where(place.odd_row, top, d).astype(BF16)
         b_ref[s, 0] = jnp.where(place.odd_row, d, top).astype(BF16)
         own_transposed(g, e_ref, s * g.h * g.wp, s, dt_ref)
-    half_gradient(g, 1 - place.core, x, g.h + 2, 0, dt_ref, send, first, prepare)
+    half_gradient(g, 1 - place.core, x, g.h + 2, 0, dt_ref, tuple(send), first, prepare)
 
 
 def first_own_kernel(g, x, dt_ref, keep, first):
@@ -608,22 +621,41 @@
         sent_ref[i] = buffer[pl.ds(other, rows), :].astype(BF16)
 
 
-def join_kernel(kept, came, out_ref):
-    for i in range(kept.shape[0]):
-        out_ref[i] = kept[i] + wide(came, i)
-
-
-def message_kernel(keep, got, kept, out_far, out_ref, sems):
+def split_again_kernel(kept, came, kept_ref, sent_ref, buffer):
+    devices, rows, _ = kept_ref.shape
+    spare = kept.shape[1] - rows
+    third = Place().third
+    for i in range(devices):
+        buffer[i] = kept[i] + wide(came, i)
+    for i in range(devices):
+        kept_ref[i] = buffer[i, pl.ds(pl.multiple_of(spare * third, 8), rows)]
+    for j in range(devices // 2):
+        large = buffer[2 * j + 1 - third, pl.ds(pl.multiple_of(spare * (1 - third), 8), rows)]
+        small = buffer[2 * j + third, pl.ds(pl.multiple_of(rows * (1 - third), 8), spare)]
+        sent_ref[j] = jnp.concatenate([large, small], axis=0).astype(BF16)
+
+
+def message_kernel(keep, *refs):
+    *got, kept, came, out_far, out_ref, sems = refs
     devices = kept.shape[0]
     share = keep.shape[0] // devices
     copies = []
     count = sems.shape[0]
+    rows = kept.shape[1]
+    spare = came.shape[1] - rows
+    third = Place().third
+    none = jnp.zeros((rows - spare, kept.shape[2]), F32)
     for part in range(count):
-        mine = pl.ds(part * devices // count, devices // count)
-        for i in range(part * devices // count, (part + 1) * devices // count):
-            rows = slice(i * share, (i + 1) * share)
-            first = keep[rows, :] + wide(got, rows)
-            out_ref[i] = jnp.concatenate([first, kept[i]], axis=0).astype(BF16)
+        per = devices // count
+        mine = pl.ds(part * per, per)
+        for k in range(per):
+            i = part * per + k
+            first = keep[i * share : (i + 1) * share, :]
+            first = first + wide(got[part], slice(k * share, (k + 1) * share))
+            others = wide(came, i // 2)
+            small = [others[rows:], none] if i % 2 else [none, others[rows:]]
+            second = kept[i] + jnp.where(third == i % 2, others[:rows], jnp.concatenate(small, axis=0))
+            out_ref[i] = jnp.concatenate([first, second], axis=0).astype(BF16)
         copies.append(pltpu.make_async_copy(out_ref.at[mine], out_far.at[mine], sems.at[part]))
         copies[-1].start()
     for copy in copies:
@@ -671,11 +703,21 @@
                 lanes = slice(k * 128, (k + 1) * 128)
                 grads.append((k, half, over(lambda row: row % 2 == half, every, lanes)))
         else:
-            rows = half_rows(share)
-            first = over(lambda row: row % 2 == half, slice(0, share), every)
-            upper = over(lambda row: row % 2 == half and row // 4 % 2 == 0, slice(share, None), every)
-            lower = over(lambda row: row % 2 == half and row // 4 % 2 == 1, slice(2 * rows, None), every)
-            grads += [(0, half, first), (1, half, jnp.concatenate([upper, lower], axis=0))]
+            grads.append((0, half, over(lambda row: row % 2 == half, slice(0, share), every)))
+            size = half_rows(share)
+            last = half_rows(size)
+            spare = size - last
+            odd = lax.axis_index("cols") % 2 == 1
+            blocks = []
+            for second in range(2):
+                one, two = (
+                    over(lambda r, row=half + 4 * second + 2 * third: r % 8 == row, slice(share, None), every)
+                    for third in range(2)
+                )
+                middle = jnp.where(odd, two[: last - spare], one[spare:])
+                blocks.append(jnp.concatenate([one[:spare], middle, two[last - spare :]], axis=0))
+            blocks[1] = blocks[1][2 * size - share :]
+            grads.append((1, half, jnp.concatenate(blocks, axis=0)))
     for k, half, grad in grads:
         at = pl.ds(2 * half + k, share, stride=4)
         new = adamw(w[at, :], grad, first_m[at, :], second_m[at, :], 0.02)
@@ -832,7 +874,7 @@
     )(z2, st2, own_sums, norm_scale_bias, cot_ext, cot_next, h)
     got2 = swapped(send2, "rows", 0)
     nrows = lax.axis_size("rows")
-    cut_again = nrows % 8 == 0 and taps // devices % 8 == 0
+    cut_again = nrows % 8 == 0 and lax.axis_size("cols") % 2 == 0 and taps // devices % 8 == 0
     hidden_shape, output_shape = held((n3, chans), F32), held(features.shape, BF16)
 
     def hidden_gradient(scenes, part_shape, *before, **options):
@@ -870,19 +912,24 @@
     st3 = exchange(st)
     if cut_again:
         kept, st3 = lax.optimization_barrier((kept, st3))
-        (kept,) = kernel_call(join_kernel, [held(kept_shape, F32)], 0, size=1024)(kept, came)
+        again_shape = (devices, half_rows(kept_shape[1]), chans // 2)
+        kept, sent = kernel_call(
+            split_again_kernel,
+            [held(again_shape, F32), held((devices // 2, *kept_shape[1:]), BF16)],
+            0,
+            size=1024,
+            scratch=[pltpu.VMEM(kept_shape, F32)],
+        )(kept, came)
+        came = lax.ppermute(sent, "rows", [(i, i ^ 2) for i in range(nrows)])
         dn1, kept = lax.optimization_barrier((dn1, kept))
-    sent_shape = held((taps, chans // 2), BF16)
+    cuts = 4 if cut_again else 1
+    sent_shape = held((taps // cuts, chans // 2), BF16)
     part = pltpu.VMEM((9, chans // 2, chans), F32)
-    e, a, b, send1, dt = kernel_call(
+    e, a, b, *send1, dt = kernel_call(
         functools.partial(first_gradient_kernel, g, count),
-        [
-            held((n3, chans), BF16),
-            wide_rows(1),
-            wide_rows(1),
-            sent_shape,
-            held((chans, own_pixels), BF16),
-        ],
+        [held((n3, chans), BF16), wide_rows(1), wide_rows(1)]
+        + [sent_shape] * cuts
+        + [held((chans, own_pixels), BF16)],
         0,
         size=1024,
         scratch=[part],
@@ -890,7 +937,7 @@
     (keep1,) = kernel_call(
         functools.partial(first_own_kernel, g), [held((taps, chans // 2), F32)], 0, size=1024, scratch=[part]
     )(x, dt)
-    got1 = swapped(send1, "rows", 0)
+    got1 = [swapped(part, "rows", 0) for part in send1]
     share_rows = taps // devices
     if cut_again:
         rows = share_rows + kept.shape[1]
@@ -900,7 +947,7 @@
             1e9,
             far_out=(0,),
             scratch=[pltpu.VMEM((devices, rows, chans // 2), BF16), dma((4,))],
-        )(keep1, got1, kept)
+        )(keep1, *got1, kept, came)
     else:
 
         def add_pair(lane, *operands, **options):
@@ -914,7 +961,7 @@
             )(*operands)
 
         (parts,) = add_pair(chans // 2, keep2, got2)
-        (parts,) = add_pair(0, keep1, got1, parts, far=(2,), alias={2: 0})
+        (parts,) = add_pair(0, keep1, *got1, parts, far=(2,), alias={2: 0})
         parts = parts.reshape(devices, share_rows, chans)
     parts, chunked = lax.optimization_barrier((parts, chunked))
     parts = exchange(parts)

time: 95.5 us -> 94.9 us (level)
  waiting for transfers between devices: 14.1 us -> 11 us
  starting transfers between devices: 22.7 us -> 25.1 us
    all_to_all x1, waiting for transfers between devices: 7.9 us -> 5.62 us  [exchange(): return lax.all_to_all(parts, BOTH, 0, 0, tiled=True)]
    all_to_all x1, starting transfers between devices: 2.63 us -> 3.82 us  [exchange(): return lax.all_to_all(parts, BOTH, 0, 0, tiled=True)]
    ppermute x8 -> x11, waiting for transfers between devices: 6.16 us -> 5.32 us  [swapped(): return lax.ppermute(block, axis, pairs)]
    ppermute x8 -> x11, starting transfers between devices: 12.8 us -> 13.3 us  [swapped(): return lax.ppermute(block, axis, pairs)]
  transfers between devices with their start and end apart: 12 -> 16, of which waited for: 4 -> 4; matrix products, arithmetic and copies ran while one was open for 2% -> 2% of each run, Pallas kernels for 13% -> 15%
where the time goes in v10:
time: 94.9 us; the launch traced here: 94.4 us
  blocking collectives  30.5 us (32%)
  Pallas kernels  25.1 us (26%)
  starting transfers between devices  25.1 us (26%)
  waiting for transfers between devices  11 us (12%)
  local copies, waits for them, and re-layouts  1.8 us (2%)
  between operations  0.97 us (1%)
    all_to_all x3, blocking collectives, exchange(): return lax.all_to_all(parts, BOTH, 0, 0, tiled=True)  30.5 us
    pallas_call x16, Pallas kernels, call(): pl.pallas_call(body, out_shape=out_shape, in_specs=specs, out_specs=[pl.B...  25.1 us
    ppermute x11, starting transfers between devices, swapped(): return lax.ppermute(block, axis, pairs)  13.3 us
    ppermute x2, starting transfers between devices, swapped_both(): return lax.ppermute(block, BOTH, pairs)  6.69 us
    all_to_all x1, waiting for transfers between devices, exchange(): return lax.all_to_all(parts, BOTH, 0, 0, tiled=True)  5.62 us
    ppermute x11, waiting for transfers between devices, swapped(): return lax.ppermute(block, axis, pairs)  5.32 us
    all_to_all x1, starting transfers between devices, exchange(): return lax.all_to_all(parts, BOTH, 0, 0, tiled=True)  3.82 us
  transfers between devices with their start and end apart: 16, of which 4 were waited for; matrix products, arithmetic and copies ran while one was open for 2% of the time, Pallas kernels for 15%

profile of v10, /device:TPU:1, one launch (start us, length us, event | category | flops | bytes accessed | tf_op | source)
XLA Modules:
  0.0 94.4 jit_solution(14979561635393220277)
XLA Ops:
  0.6 1.7 %shard_map.168 = (bf16[4,8,40,256]{3,2,1,0:T(8,128)(2,1)S(1)}, bf16[4,48,256]{2,1,0:T(8,128)(2,1)S(1)}, bf16[4,48,256]{2,1,0:T(8,128)(2,1)S(1)}, bf16[4,4,40,256...) custom-call(bf16[4,8,40,256]{3,2,1,0:T(8,128)(2,1)} %features.1, ...), custom_call_target="tpu_custom_call" | custom-call | flops 100000000 | bytes 4194304 | tf_op jit(solution)/shard_map/pallas_call | solution.py:41
  2.4 4.5 %collective-permute-start.2 = (bf16[4,4,40,256]{3,2,1,0:T(8,128)(2,1)S(1)}, bf16[4,4,40,256]{3,2,1,0:T(8,128)(2,1)S(1)}, u32[]{:S(2)}, u32[]{:S(2)}) collective-permute-start(bf16[4,4,40,256]{3,2,1,0:T(8,128)(2,1)S(1)} %get-tuple-element.81), channel_id=1, source_target_pairs={{4,8},{8,4},{12,16},{16,12},{20,24},{24,20},{5,9},{9,5},{13,17},{1... | collective-permute-start | bytes 983048 | tf_op jit(solution)/shard_map/ppermute | solution.py:733
  6.9 1.4 %collective-permute-start = (bf16[4,48,256]{2,1,0:T(8,128)(2,1)S(1)}, bf16[4,48,256]{2,1,0:T(8,128)(2,1)S(1)}, u32[]{:S(2)}, u32[]{:S(2)}) collective-permute-start(bf16[4,48,256]{2,1,0:T(8,128)(2,1)S(1)} %get-tuple-element.77), channel_id=1, source_target_pairs={{0,1},{1,0},{2,3},{3,2},{4,5},{5,4},{6,7},{7,6},{8,9},{9,8},{10,11... | collective-permute-start | bytes 294920 | tf_op jit(solution)/shard_map/ppermute | solution.py:733
  8.2 0.7 collective-permute-start.1
  8.9 6.0 %collective-permute-start.3 = (bf16[4,16,256]{2,1,0:T(8,128)(2,1)S(1)}, bf16[4,16,256]{2,1,0:T(8,128)(2,1)S(1)}, u32[]{:S(2)}, u32[]{:S(2)}) collective-permute-start(bf16[4,16,256]{2,1,0:T(8,128)(2,1)S(1)} %get-tuple-element.82), channel_id=1, source_target_pairs={{4,9},{5,8},{6,11},{7,10},{8,5},{9,4},{10,7},{11,6},{12,17},{13,16... | collective-permute-start | bytes 98312 | tf_op jit(solution)/shard_map/ppermute | solution.py:749
  14.9 0.7 collective-permute-start.4
  15.6 0.0 copy-start.1
  15.6 2.5 %shard_map.170 = (bf16[2304,256]{1,0:T(8,128)(2,1)S(1)}, bf16[2304,256]{1,0:T(8,128)(2,1)S(1)}) custom-call(f32[9216,128]{1,0:T(8,128)} %bitcast.37), custom_call_target="tpu_custom_call" | custom-call | bytes 1024 | tf_op jit(solution)/shard_map/pallas_call | solution.py:41
  18.1 0.0 collective-permute-done.rc
  18.2 0.2 shard_map.169
  18.4 0.0 collective-permute-done.4.rb_d
  18.4 0.0 collective-permute-done.2.rb
  18.4 0.1 collective-permute-start.5
  18.5 1.6 %shard_map.171 = (f32[2304,256]{1,0:T(8,128)S(1)}, f32[16,256]{1,0:T(8,128)S(1)}, bf16[1920,768]{1,0:T(8,128)(2,1)S(1)}) custom-call(bf16[4,8,48,256]{3,2,1,0:T(8,128)(2,1)S(1)} %get-tuple-element.79.ext, bf16[2304,256]{1,0:T(8,128)(2,1)S(1)} %get-tuple-element.89.w.w_far), custom_call_target="tpu_custom_call" | custom-call | bytes 1024 | tf_op jit(solution)/shard_map/pallas_call | solution.py:41
  20.1 0.1 collective-permute-done.5.ra
  20.2 1.6 %shard_map.172 = (f32[2304,256]{1,0:T(8,128)S(1)}, f32[32,2,256]{2,1,0:T(2,128)S(1)}, bf16[1920,768]{1,0:T(8,128)(2,1)S(1)}, bf16[4,2,48,256]{3,2,1,0:T(8,128)(2,1)S(1)}) custom-call(bf16[4,8,48,256]{3,2,1,0:T(8,128)(2,1)S(1)} %get-tuple-element.79.ext, ...), custom_call_target="tpu_custom_call", output_to_operand_aliasing={{0}: (7, {}), {2}: (8, {})} | custom-call | bytes 1024 | tf_op jit(solution)/shard_map/pallas_call | solution.py:41
  21.8 11.7 %all_to_all.20.st = f32[32,2,256]{2,1,0:T(2,128)S(1)} all-to-all(f32[32,2,256]{2,1,0:T(2,128)S(1)} %get-tuple-element.94), channel_id=1, replica_groups=mesh['rows'=8,'cols'=4] {'rows','cols'}, dimensions={0} | all-to-all | bytes 131072 | tf_op jit(solution)/shard_map/all_to_all | solution.py:761
  33.5 2.7 %shard_map.173 = (bf16[2304,768]{1,0:T(8,128)(2,1)S(1)}, f32[1920,256]{1,0:T(8,128)S(1)}, f32[32,4,256]{2,1,0:T(4,128)S(1)}, f32[8,256]{1,0:T(8,128)S(1)}) custom-call(f32[2304,256]{1,0:T(8,128)S(1)} %get-tuple-element.93.z1.z, f32[32,2,256]{2,1,0:T(2,128)S(1)} %all_to_all.20.st, f32[4,256]{1,0:T(4,128)S(1)} %copy-done.4, ...), custom_call_target="tpu_custom_call" | custom-call | flops 2264924160 | bytes 4194304 | tf_op jit(solution)/shard_map/pallas_call | solution.py:41
  36.2 9.7 %all_to_all.21.st.st2 = f32[32,4,256]{2,1,0:T(4,128)S(1)} all-to-all(f32[32,4,256]{2,1,0:T(4,128)S(1)} %get-tuple-element.98), channel_id=1, replica_groups=mesh['rows'=8,'cols'=4] {'rows','cols'}, dimensions={0} | all-to-all | bytes 262144 | tf_op jit(solution)/shard_map/all_to_all | solution.py:761
  45.8 2.5 %shard_map.174 = (bf16[1920,256]{1,0:T(8,128)(2,1)S(1)}, f32[2304,128]{1,0:T(8,128)S(1)}, bf16[2304,128]{1,0:T(8,128)(2,1)S(1)}) custom-call(f32[1920,256]{1,0:T(8,128)S(1)} %get-tuple-element.97.z2, f32[32,4,256]{2,1,0:T(4,128)S(1)} %all_to_all.21.st.st2, f32[8,256]{1,0:T(8,128)S(1)} %get-tuple-element.99.own, f32[4,256]{1,0:T(4,128)S(1)} %copy-done.4, ...), custom_call_target="tpu_custom_call" | custom-call | flops 1811939328 | bytes 4194304 | tf_op jit(solution)/shard_map/pallas_call | solution.py:41
  48.4 1.4 %collective-permute-start.6 = (bf16[2304,128]{1,0:T(8,128)(2,1)S(1)}, bf16[2304,128]{1,0:T(8,128)(2,1)S(1)}, u32[]{:S(2)}, u32[]{:S(2)}) collective-permute-start(bf16[2304,128]{1,0:T(8,128)(2,1)S(1)} %get-tuple-element.105), channel_id=1, source_target_pairs={{0,4},{4,0},{8,12},{12,8},{16,20},{20,16},{24,28},{28,24},{1,5},{5... | collective-permute-start | bytes 1769480 | tf_op jit(solution)/shard_map/ppermute | solution.py:733
  49.8 1.9 %shard_map.175 = (f32[1536,256]{1,0:T(8,128)S(1)}, f32[16,256]{1,0:T(8,128)S(1)}, bf16[4,8,40,256]{3,2,1,0:T(8,128)(2,1)S(1)}) custom-call(bf16[1920,256]{1,0:T(8,128)(2,1)S(1)} %get-tuple-element.102.d, bf16[2304,256]{1,0:T(8,128)(2,1)S(1)} %get-tuple-element.95.w, f32[2304,256]{1,0:T(8,128)S(1)} %get-tuple-element.93.z1.z, ...), custom_call_target="tpu_custom_call" | custom-call | bytes 1024 | tf_op jit(solution)/shard_map/pallas_call | solution.py:41
  51.7 0.0 collective-permute-done.6.got
  51.7 0.2 shard_map.176
  51.9 0.6 collective-permute-start.7
  52.5 0.8 shard_map.177
  53.3 9.1 %all_to_all.22.st3 = f32[32,2,256]{2,1,0:T(2,128)S(1)} all-to-all(f32[32,2,256]{2,1,0:T(2,128)S(1)} %get-tuple-element.115), channel_id=1, replica_groups=mesh['rows'=8,'cols'=4] {'rows','cols'}, dimensions={0} | all-to-all | bytes 131072 | tf_op jit(solution)/shard_map/all_to_all | solution.py:761
  62.4 0.1 shard_map.178
  62.5 0.7 collective-permute-start.14
  63.2 1.5 %shard_map.179 = (bf16[1536,256]{1,0:T(8,128)(2,1)S(1)}, bf16[4,1,48,256]{3,2,1,0:T(8,128)(2,1)S(1)}, bf16[4,1,48,256]{3,2,1,0:T(8,128)(2,1)S(1)}, bf16[576,128]...) custom-call(f32[1536,256]{1,0:T(8,128)S(1)} %get-tuple-element.119.d, ...), custom_call_target="tpu_custom_call" | custom-call | bytes 1024 | tf_op jit(solution)/shard_map/pallas_call | solution.py:41
  64.7 1.0 %collective-permute-start.10 = (bf16[576,128]{1,0:T(8,128)(2,1)S(1)}, bf16[576,128]{1,0:T(8,128)(2,1)S(1)}, u32[]{:S(2)}, u32[]{:S(2)}) collective-permute-start(bf16[576,128]{1,0:T(8,128)(2,1)S(1)} %get-tuple-element.126), channel_id=1, source_target_pairs={{0,4},{4,0},{8,12},{12,8},{16,20},{20,16},{24,28},{28,24},{1,5},{5... | collective-permute-start | bytes 442376 | tf_op jit(solution)/shard_map/ppermute | solution.py:733
  65.7 0.1 collective-permute-start.11
  65.8 0.4 collective-permute-start.12
  66.2 0.1 collective-permute-start.13
  66.3 1.2 %shard_map.181.keep = f32[2304,128]{1,0:T(8,128)S(1)} custom-call(bf16[1920,768]{1,0:T(8,128)(2,1)S(1)} %get-tuple-element.121.x, bf16[256,1536]{1,0:T(8,128)(2,1)S(1)} %get-tuple-element.125.dt_ref), custom_call_target="tpu_custom_call" | custom-call | bytes 1024 | tf_op jit(solution)/shard_map/pallas_call | solution.py:41
  67.5 0.1 collective-permute-done.13.refs_3_
  67.6 0.9 %shard_map.182 = bf16[32,96,128]{2,1,0:T(8,128)(2,1)} custom-call(f32[2304,128]{1,0:T(8,128)S(1)} %shard_map.181.keep, bf16[576,128]{1,0:T(8,128)(2,1)S(1)} %collective-permute-done.10.refs_0_, bf16[576,128]{1,0:T(8,128)(2,1)S(1)} %collective-permute-done.11.refs_1_, bf16[576,128]{1,0:T(8,128)(2,1)S(1)} %collective-permute-done.12.refs_2_, ...), custom_call_target="tpu_custom_call" | custom-call | flops 1000000000 | bytes 4194304 | tf_op jit(solution)/shard_map/pallas_call | solution.py:41
  68.6 0.0 copy-start.5
  68.6 3.8 %all-to-all-start.3 = ((bf16[32,96,128]{2,1,0:T(8,128)(2,1)}), bf16[32,96,128]{2,1,0:T(8,128)(2,1)S(1)}, u32[]{:S(2)}, u32[]{:S(2)}) async-start(bf16[32,96,128]{2,1,0:T(8,128)(2,1)} %shard_map.182), calls=%async_computation.3 | async-start | bytes 1572864 | tf_op jit(solution)/shard_map/all_to_all | solution.py:761
  72.4 0.5 collective-permute-start.8
  72.9 3.3 %collective-permute-start.9 = (bf16[4,1,48,256]{3,2,1,0:T(8,128)(2,1)S(1)}, bf16[4,1,48,256]{3,2,1,0:T(8,128)(2,1)S(1)}, u32[]{:S(2)}, u32[]{:S(2)}) collective-permute-start(bf16[4,1,48,256]{3,2,1,0:T(8,128)(2,1)S(1)} %get-tuple-element.124), channel_id=1, source_target_pairs={{4,8},{8,4},{12,16},{16,12},{20,24},{24,20},{5,9},{9,5},{13,17},{1... | collective-permute-start | bytes 294920 | tf_op jit(solution)/shard_map/ppermute | solution.py:733
  76.2 0.8 copy.34
  77.0 5.1 %collective-permute-done.9.rb = bf16[4,1,48,256]{3,2,1,0:T(8,128)(2,1)S(1)} collective-permute-done((bf16[4,1,48,256]{3,2,1,0:T(8,128)(2,1)S(1)}, bf16[4,1,48,256]{3,2,1,0:T(8,128)(2,1)S(1)}, u32[]{:S(2)}, u32[]{:S(2)}) %collective-permute-start.9) | collective-permute-done | bytes 98336 | tf_op jit(solution)/shard_map/ppermute | solution.py:733
  82.1 0.0 copy-start.7
  82.1 4.7 %shard_map.180 = f32[4,8,40,256]{3,2,1,0:T(8,128)} custom-call(bf16[1536,256]{1,0:T(8,128)(2,1)S(1)} %get-tuple-element.122.e, bf16[4,1,48,256]{3,2,1,0:T(8,128)(2,1)S(1)} %collective-permute-done.8.ra, bf16[4,1,48,256]{3,2,1,0:T(8,128)(2,1)S(1)} %collective-permute-done.9.rb, bf16[2304,256]{1,0:T(8,128)(2,1)} %copy-done, bf16[4,8,40,256]{3,2,1,0:T(8,128)(2,1)} %cot_far.1, ...), custom_call_target="tpu_custom_call" | custom-call | flops 1811939328 | bytes 4194304 | tf_op jit(solution)/shard_map/pallas_call | solution.py:41
  86.8 0.9 constant_dynamic-slice_fusion.w
  87.7 5.6 %all-to-all-done.3.parts = bf16[32,96,128]{2,1,0:T(8,128)(2,1)S(1)} async-done(((bf16[32,96,128]{2,1,0:T(8,128)(2,1)}), bf16[32,96,128]{2,1,0:T(8,128)(2,1)S(1)}, u32[]{:S(2)}, u32[]{:S(2)}) %all-to-all-start.3) | async-done | bytes 786464 | tf_op jit(solution)/shard_map/all_to_all | solution.py:761
  93.4 1.0 %shard_map.183 = (f32[288,128]{1,0:T(8,128)}, f32[288,128]{1,0:T(8,128)}, f32[288,128]{1,0:T(8,128)}, f32[288,128]{1,0:T(8,128)}, f32[4,256]{1,0:T(4,128)}, /*in...) custom-call(bf16[32,96,128]{2,1,0:T(8,128)(2,1)S(1)} %all-to-all-done.3.parts, ...), custom_call_target="tpu_custom_call" | custom-call | flops 100000000 | bytes 4194304 | tf_op jit(solution)/shard_map/pallas_call | solution.py:41
  (21 shorter events, 0.0 us)
Async XLA Ops:
  2.4 16.0 %collective-permute-start.2 = (bf16[4,4,40,256]{3,2,1,0:T(8,128)(2,1)S(1)}, bf16[4,4,40,256]{3,2,1,0:T(8,128)(2,1)S(1)}, u32[]{:S(2)}, u32[]{:S(2)}) collective-permute-start(bf16[4,4,40,256]{3,2,1,0:T(8,128)(2,1)S(1)} %get-tuple-element.81), channel_id=1, source_target_pairs={{4,8},{8,4},{12,16},{16,12},{20,24},{24,20},{5,9},{9,5},{13,17},{1... | collective-permute-start | bytes 983048 | tf_op jit(solution)/shard_map/ppermute | solution.py:733
  6.9 11.3 %collective-permute-start = (bf16[4,48,256]{2,1,0:T(8,128)(2,1)S(1)}, bf16[4,48,256]{2,1,0:T(8,128)(2,1)S(1)}, u32[]{:S(2)}, u32[]{:S(2)}) collective-permute-start(bf16[4,48,256]{2,1,0:T(8,128)(2,1)S(1)} %get-tuple-element.77), channel_id=1, source_target_pairs={{0,1},{1,0},{2,3},{3,2},{4,5},{5,4},{6,7},{7,6},{8,9},{9,8},{10,11... | collective-permute-start | bytes 294920 | tf_op jit(solution)/shard_map/ppermute | solution.py:733
  8.2 9.9 %collective-permute-start.1 = (bf16[4,48,256]{2,1,0:T(8,128)(2,1)S(1)}, bf16[4,48,256]{2,1,0:T(8,128)(2,1)S(1)}, u32[]{:S(2)}, u32[]{:S(2)}) collective-permute-start(bf16[4,48,256]{2,1,0:T(8,128)(2,1)S(1)} %get-tuple-element.78), channel_id=1, source_target_pairs={{1,2},{2,1},{5,6},{6,5},{9,10},{10,9},{13,14},{14,13},{17,18},{18,... | collective-permute-start | bytes 294920 | tf_op jit(solution)/shard_map/ppermute | solution.py:733
  8.9 9.5 %collective-permute-start.3 = (bf16[4,16,256]{2,1,0:T(8,128)(2,1)S(1)}, bf16[4,16,256]{2,1,0:T(8,128)(2,1)S(1)}, u32[]{:S(2)}, u32[]{:S(2)}) collective-permute-start(bf16[4,16,256]{2,1,0:T(8,128)(2,1)S(1)} %get-tuple-element.82), channel_id=1, source_target_pairs={{4,9},{5,8},{6,11},{7,10},{8,5},{9,4},{10,7},{11,6},{12,17},{13,16... | collective-permute-start | bytes 98312 | tf_op jit(solution)/shard_map/ppermute | solution.py:749
  14.9 3.4 %collective-permute-start.4 = (bf16[4,16,256]{2,1,0:T(8,128)(2,1)S(1)}, bf16[4,16,256]{2,1,0:T(8,128)(2,1)S(1)}, u32[]{:S(2)}, u32[]{:S(2)}) collective-permute-start(bf16[4,16,256]{2,1,0:T(8,128)(2,1)S(1)} %get-tuple-element.83), channel_id=1, source_target_pairs={{5,10},{6,9},{9,6},{10,5},{13,18},{14,17},{17,14},{18,13},{21,26},... | collective-permute-start | bytes 98312 | tf_op jit(solution)/shard_map/ppermute | solution.py:749
  15.6 2.5 %copy-start.1 = (bf16[4,8,40,256]{3,2,1,0:T(8,128)(2,1)S(1)}, bf16[4,8,40,256]{3,2,1,0:T(8,128)(2,1)}, u32[]{:S(2)}) copy-start(bf16[4,8,40,256]{3,2,1,0:T(8,128)(2,1)} %cot_far.1) | copy-start | bytes 1966084
  18.1 3.7 %copy-start = (bf16[2304,256]{1,0:T(8,128)(2,1)}, bf16[2304,256]{1,0:T(8,128)(2,1)S(1)}, u32[]{:S(2)}) copy-start(bf16[2304,256]{1,0:T(8,128)(2,1)S(1)} %get-tuple-element.89.w.w_far) | copy-start | bytes 3538948
  18.4 1.8 %collective-permute-start.5 = (bf16[4,4,48,256]{3,2,1,0:T(8,128)(2,1)S(1)}, bf16[4,4,48,256]{3,2,1,0:T(8,128)(2,1)S(1)}, u32[]{:S(2)}, u32[]{:S(2)}) collective-permute-start(bf16[4,4,48,256]{3,2,1,0:T(8,128)(2,1)S(1)} %get-tuple-element.85), channel_id=1, source_target_pairs={{0,4},{4,0},{8,12},{12,8},{16,20},{20,16},{24,28},{28,24},{1,5},{5... | collective-permute-start | bytes 1179656 | tf_op jit(solution)/shard_map/ppermute | solution.py:733
  20.2 13.3 %copy-start.4 = (f32[4,256]{1,0:T(4,128)S(1)}, f32[4,256]{1,0:T(4,128)}, u32[]{:S(2)}) copy-start(f32[4,256]{1,0:T(4,128)} %params.11) | copy-start | bytes 12292
  48.4 3.3 %collective-permute-start.6 = (bf16[2304,128]{1,0:T(8,128)(2,1)S(1)}, bf16[2304,128]{1,0:T(8,128)(2,1)S(1)}, u32[]{:S(2)}, u32[]{:S(2)}) collective-permute-start(bf16[2304,128]{1,0:T(8,128)(2,1)S(1)} %get-tuple-element.105), channel_id=1, source_target_pairs={{0,4},{4,0},{8,12},{12,8},{16,20},{20,16},{24,28},{28,24},{1,5},{5... | collective-permute-start | bytes 1769480 | tf_op jit(solution)/shard_map/ppermute | solution.py:733
  51.9 10.5 %collective-permute-start.7 = (bf16[32,40,128]{2,1,0:T(8,128)(2,1)S(1)}, bf16[32,40,128]{2,1,0:T(8,128)(2,1)S(1)}, u32[]{:S(2)}, u32[]{:S(2)}) collective-permute-start(bf16[32,40,128]{2,1,0:T(8,128)(2,1)S(1)} %get-tuple-element.117), channel_id=1, source_target_pairs={{0,16},{4,20},{8,24},{12,28},{16,0},{20,4},{24,8},{28,12},{1,17},{... | collective-permute-start | bytes 983048 | tf_op jit(solution)/shard_map/ppermute | solution.py:902
  62.5 5.1 %collective-permute-start.14 = (bf16[16,40,128]{2,1,0:T(8,128)(2,1)S(1)}, bf16[16,40,128]{2,1,0:T(8,128)(2,1)S(1)}, u32[]{:S(2)}, u32[]{:S(2)}) collective-permute-start(bf16[16,40,128]{2,1,0:T(8,128)(2,1)S(1)} %get-tuple-element.131), channel_id=1, source_target_pairs={{0,8},{4,12},{8,0},{12,4},{16,24},{20,28},{24,16},{28,20},{1,9},{5... | collective-permute-start | bytes 491528 | tf_op jit(solution)/shard_map/ppermute | solution.py:923
  64.7 2.8 %collective-permute-start.10 = (bf16[576,128]{1,0:T(8,128)(2,1)S(1)}, bf16[576,128]{1,0:T(8,128)(2,1)S(1)}, u32[]{:S(2)}, u32[]{:S(2)}) collective-permute-start(bf16[576,128]{1,0:T(8,128)(2,1)S(1)} %get-tuple-element.126), channel_id=1, source_target_pairs={{0,4},{4,0},{8,12},{12,8},{16,20},{20,16},{24,28},{28,24},{1,5},{5... | collective-permute-start | bytes 442376 | tf_op jit(solution)/shard_map/ppermute | solution.py:733
  65.7 1.8 %collective-permute-start.11 = (bf16[576,128]{1,0:T(8,128)(2,1)S(1)}, bf16[576,128]{1,0:T(8,128)(2,1)S(1)}, u32[]{:S(2)}, u32[]{:S(2)}) collective-permute-start(bf16[576,128]{1,0:T(8,128)(2,1)S(1)} %get-tuple-element.127), channel_id=1, source_target_pairs={{0,4},{4,0},{8,12},{12,8},{16,20},{20,16},{24,28},{28,24},{1,5},{5... | collective-permute-start | bytes 442376 | tf_op jit(solution)/shard_map/ppermute | solution.py:733
  65.8 1.7 %collective-permute-start.12 = (bf16[576,128]{1,0:T(8,128)(2,1)S(1)}, bf16[576,128]{1,0:T(8,128)(2,1)S(1)}, u32[]{:S(2)}, u32[]{:S(2)}) collective-permute-start(bf16[576,128]{1,0:T(8,128)(2,1)S(1)} %get-tuple-element.128), channel_id=1, source_target_pairs={{0,4},{4,0},{8,12},{12,8},{16,20},{20,16},{24,28},{28,24},{1,5},{5... | collective-permute-start | bytes 442376 | tf_op jit(solution)/shard_map/ppermute | solution.py:733
  66.2 1.4 %collective-permute-start.13 = (bf16[576,128]{1,0:T(8,128)(2,1)S(1)}, bf16[576,128]{1,0:T(8,128)(2,1)S(1)}, u32[]{:S(2)}, u32[]{:S(2)}) collective-permute-start(bf16[576,128]{1,0:T(8,128)(2,1)S(1)} %get-tuple-element.129), channel_id=1, source_target_pairs={{0,4},{4,0},{8,12},{12,8},{16,20},{20,16},{24,28},{28,24},{1,5},{5... | collective-permute-start | bytes 442376 | tf_op jit(solution)/shard_map/ppermute | solution.py:733
  68.6 13.5 %copy-start.5 = (s32[4,8,40]{2,1,0:T(8,128)S(1)}, s32[4,8,40]{2,1,0:T(8,128)}, u32[]{:S(2)}) copy-start(s32[4,8,40]{2,1,0:T(8,128)} %occ.1) | copy-start | bytes 15364
  68.6 24.8 %all-to-all-start.3 = ((bf16[32,96,128]{2,1,0:T(8,128)(2,1)}), bf16[32,96,128]{2,1,0:T(8,128)(2,1)S(1)}, u32[]{:S(2)}, u32[]{:S(2)}) async-start(bf16[32,96,128]{2,1,0:T(8,128)(2,1)} %shard_map.182), calls=%async_computation.3 | async-start | bytes 1572864 | tf_op jit(solution)/shard_map/all_to_all | solution.py:761
  72.4 4.6 %collective-permute-start.8 = (bf16[4,1,48,256]{3,2,1,0:T(8,128)(2,1)S(1)}, bf16[4,1,48,256]{3,2,1,0:T(8,128)(2,1)S(1)}, u32[]{:S(2)}, u32[]{:S(2)}) collective-permute-start(bf16[4,1,48,256]{3,2,1,0:T(8,128)(2,1)S(1)} %get-tuple-element.123), channel_id=1, source_target_pairs={{0,4},{4,0},{8,12},{12,8},{16,20},{20,16},{24,28},{28,24},{1,5},{5... | collective-permute-start | bytes 294920 | tf_op jit(solution)/shard_map/ppermute | solution.py:733
  72.9 9.2 %collective-permute-start.9 = (bf16[4,1,48,256]{3,2,1,0:T(8,128)(2,1)S(1)}, bf16[4,1,48,256]{3,2,1,0:T(8,128)(2,1)S(1)}, u32[]{:S(2)}, u32[]{:S(2)}) collective-permute-start(bf16[4,1,48,256]{3,2,1,0:T(8,128)(2,1)S(1)} %get-tuple-element.124), channel_id=1, source_target_pairs={{4,8},{8,4},{12,16},{16,12},{20,24},{24,20},{5,9},{9,5},{13,17},{1... | collective-permute-start | bytes 294920 | tf_op jit(solution)/shard_map/ppermute | solution.py:733
  82.1 11.3 %copy-start.2 = (f32[2,18432]{1,0:T(2,128)S(1)}, f32[2,18432]{1,0:T(2,128)}, u32[]{:S(2)}) copy-start(f32[2,18432]{1,0:T(2,128)} %param.13) | copy-start | bytes 442372
  82.1 11.3 %copy-start.3 = (f32[2,18432]{1,0:T(2,128)S(1)}, f32[2,18432]{1,0:T(2,128)}, u32[]{:S(2)}) copy-start(f32[2,18432]{1,0:T(2,128)} %param.14) | copy-start | bytes 442372
  82.1 11.3 %copy-start.6 = (f32[4,256]{1,0:T(4,128)S(1)}, f32[4,256]{1,0:T(4,128)}, u32[]{:S(2)}) copy-start(f32[4,256]{1,0:T(4,128)} %n_first.1) | copy-start | bytes 12292
  82.1 11.3 %copy-start.7 = (f32[4,256]{1,0:T(4,128)S(1)}, f32[4,256]{1,0:T(4,128)}, u32[]{:S(2)}) copy-start(f32[4,256]{1,0:T(4,128)} %n_second.1) | copy-start | bytes 12292

commit v11 on v10

--- a/solution.py
+++ b/solution.py
@@ -635,31 +635,56 @@
         sent_ref[j] = jnp.concatenate([large, small], axis=0).astype(BF16)
 
 
+def whole_tiles(share):
+    return share // 16 * 16
+
+
+def write_parts(block_of, first_row, out_far, buffer, sems):
+    devices, rows, _ = buffer.shape
+    count = sems.shape[0]
+    per = devices // count
+    copies = []
+    for part in range(count):
+        mine = pl.ds(part * per, per)
+        for i in range(part * per, (part + 1) * per):
+            buffer[i] = block_of(i).astype(BF16)
+        there = out_far.at[mine, pl.ds(first_row, rows)]
+        copies.append(pltpu.make_async_copy(buffer.at[mine], there, sems.at[part]))
+        copies[-1].start()
+    for copy in copies:
+        copy.wait()
+
+
+def first_rows(keep, got, share, i, rows):
+    piece, at = divmod(i * share, got[0].shape[0])
+    mine = keep[i * share + rows.start : i * share + rows.stop, :]
+    return mine + wide(got[piece], slice(at + rows.start, at + rows.stop))
+
+
+def early_message_kernel(keep, *refs):
+    *got, out_far, buffer, sems = refs
+    devices, rows, _ = buffer.shape
+    share = keep.shape[0] // devices
+    write_parts(lambda i: first_rows(keep, got, share, i, slice(0, rows)), 0, out_far, buffer, sems)
+
+
 def message_kernel(keep, *refs):
-    *got, kept, came, out_far, out_ref, sems = refs
+    *got, kept, came, _, out_far, buffer, sems = refs
     devices = kept.shape[0]
     share = keep.shape[0] // devices
-    copies = []
-    count = sems.shape[0]
     rows = kept.shape[1]
     spare = came.shape[1] - rows
     third = Place().third
     none = jnp.zeros((rows - spare, kept.shape[2]), F32)
-    for part in range(count):
-        per = devices // count
-        mine = pl.ds(part * per, per)
-        for k in range(per):
-            i = part * per + k
-            first = keep[i * share : (i + 1) * share, :]
-            first = first + wide(got[part], slice(k * share, (k + 1) * share))
-            others = wide(came, i // 2)
-            small = [others[rows:], none] if i % 2 else [none, others[rows:]]
-            second = kept[i] + jnp.where(third == i % 2, others[:rows], jnp.concatenate(small, axis=0))
-            out_ref[i] = jnp.concatenate([first, second], axis=0).astype(BF16)
-        copies.append(pltpu.make_async_copy(out_ref.at[mine], out_far.at[mine], sems.at[part]))
-        copies[-1].start()
-    for copy in copies:
-        copy.wait()
+
+    def block_of(i):
+        others = wide(came, i // 2)
+        small = [others[rows:], none] if i % 2 else [none, others[rows:]]
+        second = kept[i] + jnp.where(third == i % 2, others[:rows], jnp.concatenate(small, axis=0))
+        last = first_rows(keep, got, share, i, slice(whole_tiles(share), share))
+        return jnp.concatenate([last, second], axis=0)
+
+    write_parts(block_of, whole_tiles(share), out_far, buffer, sems)
 
 
 def adamw(weight, grad, first, second, rate):
@@ -941,13 +966,27 @@
     share_rows = taps // devices
     if cut_again:
         rows = share_rows + kept.shape[1]
+        parts_shape = stored((devices, rows, chans // 2), BF16)
+        ready = whole_tiles(share_rows)
+        (parts,) = kernel_call(
+            early_message_kernel,
+            [parts_shape],
+            0,
+            size=1024,
+            far_out=(0,),
+            scratch=[pltpu.VMEM((devices, ready, chans // 2), BF16), dma((4,))],
+        )(keep1, *got1)
+        operands = (keep1, *got1, kept, came, parts)
+        at = len(operands) - 1
         (parts,) = kernel_call(
             message_kernel,
-            [stored((devices, rows, chans // 2), BF16)],
+            [parts_shape],
             1e9,
+            far=(at,),
             far_out=(0,),
-            scratch=[pltpu.VMEM((devices, rows, chans // 2), BF16), dma((4,))],
-        )(keep1, *got1, kept, came)
+            scratch=[pltpu.VMEM((devices, rows - ready, chans // 2), BF16), dma((4,))],
+            alias={at: 0},
+        )(*operands)
     else:
 
         def add_pair(lane, *operands, **options):

time: 94.9 us -> 94.7 us (level)
    pallas_call x16 -> x17, Pallas kernels: 25.1 us -> 25.8 us  [call(): pl.pallas_call(body, out_shape=out_shape, in_specs=specs, out_specs=[pl.B...]
  transfers between devices with their start and end apart: 16 -> 16, of which waited for: 4 -> 4; matrix products, arithmetic and copies ran while one was open for 2% -> 2% of each run, Pallas kernels for 15% -> 16%
where the time goes in v11:
time: 94.7 us; the launch traced here: 94.3 us
  blocking collectives  30.5 us (32%)
  Pallas kernels  25.8 us (27%)
  starting transfers between devices  24.2 us (26%)
  waiting for transfers between devices  11 us (12%)
  local copies, waits for them, and re-layouts  1.8 us (2%)
  between operations  0.98 us (1%)
    all_to_all x3, blocking collectives, exchange(): return lax.all_to_all(parts, BOTH, 0, 0, tiled=True)  30.5 us
    pallas_call x17, Pallas kernels, call(): pl.pallas_call(body, out_shape=out_shape, in_specs=specs, out_specs=[pl.B...  25.8 us
    ppermute x11, starting transfers between devices, swapped(): return lax.ppermute(block, axis, pairs)  13.3 us
    ppermute x2, starting transfers between devices, swapped_both(): return lax.ppermute(block, BOTH, pairs)  6.69 us
    all_to_all x1, waiting for transfers between devices, exchange(): return lax.all_to_all(parts, BOTH, 0, 0, tiled=True)  5.62 us
    ppermute x11, waiting for transfers between devices, swapped(): return lax.ppermute(block, axis, pairs)  5.32 us
    all_to_all x1, starting transfers between devices, exchange(): return lax.all_to_all(parts, BOTH, 0, 0, tiled=True)  2.92 us
  transfers between devices with their start and end apart: 16, of which 4 were waited for; matrix products, arithmetic and copies ran while one was open for 2% of the time, Pallas kernels for 16%

profile of v11, /device:TPU:1, one launch (start us, length us, event | category | flops | bytes accessed | tf_op | source)
XLA Modules:
  0.0 94.3 jit_solution(2642999815165806901)
XLA Ops:
  0.6 1.7 %shard_map.168 = (bf16[4,8,40,256]{3,2,1,0:T(8,128)(2,1)S(1)}, bf16[4,48,256]{2,1,0:T(8,128)(2,1)S(1)}, bf16[4,48,256]{2,1,0:T(8,128)(2,1)S(1)}, bf16[4,4,40,256...) custom-call(bf16[4,8,40,256]{3,2,1,0:T(8,128)(2,1)} %features.1, ...), custom_call_target="tpu_custom_call" | custom-call | flops 100000000 | bytes 4194304 | tf_op jit(solution)/shard_map/pallas_call | solution.py:41
  2.4 4.5 %collective-permute-start.2 = (bf16[4,4,40,256]{3,2,1,0:T(8,128)(2,1)S(1)}, bf16[4,4,40,256]{3,2,1,0:T(8,128)(2,1)S(1)}, u32[]{:S(2)}, u32[]{:S(2)}) collective-permute-start(bf16[4,4,40,256]{3,2,1,0:T(8,128)(2,1)S(1)} %get-tuple-element.81), channel_id=1, source_target_pairs={{4,8},{8,4},{12,16},{16,12},{20,24},{24,20},{5,9},{9,5},{13,17},{1... | collective-permute-start | bytes 983048 | tf_op jit(solution)/shard_map/ppermute | solution.py:758
  6.9 1.4 %collective-permute-start = (bf16[4,48,256]{2,1,0:T(8,128)(2,1)S(1)}, bf16[4,48,256]{2,1,0:T(8,128)(2,1)S(1)}, u32[]{:S(2)}, u32[]{:S(2)}) collective-permute-start(bf16[4,48,256]{2,1,0:T(8,128)(2,1)S(1)} %get-tuple-element.77), channel_id=1, source_target_pairs={{0,1},{1,0},{2,3},{3,2},{4,5},{5,4},{6,7},{7,6},{8,9},{9,8},{10,11... | collective-permute-start | bytes 294920 | tf_op jit(solution)/shard_map/ppermute | solution.py:758
  8.2 0.7 collective-permute-start.1
  8.9 6.0 %collective-permute-start.3 = (bf16[4,16,256]{2,1,0:T(8,128)(2,1)S(1)}, bf16[4,16,256]{2,1,0:T(8,128)(2,1)S(1)}, u32[]{:S(2)}, u32[]{:S(2)}) collective-permute-start(bf16[4,16,256]{2,1,0:T(8,128)(2,1)S(1)} %get-tuple-element.82), channel_id=1, source_target_pairs={{4,9},{5,8},{6,11},{7,10},{8,5},{9,4},{10,7},{11,6},{12,17},{13,16... | collective-permute-start | bytes 98312 | tf_op jit(solution)/shard_map/ppermute | solution.py:774
  14.9 0.7 collective-permute-start.4
  15.6 0.0 copy-start.1
  15.6 2.5 %shard_map.170 = (bf16[2304,256]{1,0:T(8,128)(2,1)S(1)}, bf16[2304,256]{1,0:T(8,128)(2,1)S(1)}) custom-call(f32[9216,128]{1,0:T(8,128)} %bitcast.37), custom_call_target="tpu_custom_call" | custom-call | bytes 1024 | tf_op jit(solution)/shard_map/pallas_call | solution.py:41
  18.1 0.0 collective-permute-done.rc
  18.2 0.2 shard_map.169
  18.4 0.0 collective-permute-done.4.rb_d
  18.4 0.0 collective-permute-done.2.rb
  18.4 0.1 collective-permute-start.5
  18.5 1.6 %shard_map.171 = (f32[2304,256]{1,0:T(8,128)S(1)}, f32[16,256]{1,0:T(8,128)S(1)}, bf16[1920,768]{1,0:T(8,128)(2,1)S(1)}) custom-call(bf16[4,8,48,256]{3,2,1,0:T(8,128)(2,1)S(1)} %get-tuple-element.79.ext, bf16[2304,256]{1,0:T(8,128)(2,1)S(1)} %get-tuple-element.89.w.w_far), custom_call_target="tpu_custom_call" | custom-call | bytes 1024 | tf_op jit(solution)/shard_map/pallas_call | solution.py:41
  20.1 0.1 collective-permute-done.5.ra
  20.2 1.6 %shard_map.172 = (f32[2304,256]{1,0:T(8,128)S(1)}, f32[32,2,256]{2,1,0:T(2,128)S(1)}, bf16[1920,768]{1,0:T(8,128)(2,1)S(1)}, bf16[4,2,48,256]{3,2,1,0:T(8,128)(2,1)S(1)}) custom-call(bf16[4,8,48,256]{3,2,1,0:T(8,128)(2,1)S(1)} %get-tuple-element.79.ext, ...), custom_call_target="tpu_custom_call", output_to_operand_aliasing={{0}: (7, {}), {2}: (8, {})} | custom-call | bytes 1024 | tf_op jit(solution)/shard_map/pallas_call | solution.py:41
  21.8 11.7 %all_to_all.20.st = f32[32,2,256]{2,1,0:T(2,128)S(1)} all-to-all(f32[32,2,256]{2,1,0:T(2,128)S(1)} %get-tuple-element.94), channel_id=1, replica_groups=mesh['rows'=8,'cols'=4] {'rows','cols'}, dimensions={0} | all-to-all | bytes 131072 | tf_op jit(solution)/shard_map/all_to_all | solution.py:786
  33.5 2.7 %shard_map.173 = (bf16[2304,768]{1,0:T(8,128)(2,1)S(1)}, f32[1920,256]{1,0:T(8,128)S(1)}, f32[32,4,256]{2,1,0:T(4,128)S(1)}, f32[8,256]{1,0:T(8,128)S(1)}) custom-call(f32[2304,256]{1,0:T(8,128)S(1)} %get-tuple-element.93.z1.z, f32[32,2,256]{2,1,0:T(2,128)S(1)} %all_to_all.20.st, f32[4,256]{1,0:T(4,128)S(1)} %copy-done.4, ...), custom_call_target="tpu_custom_call" | custom-call | flops 2264924160 | bytes 4194304 | tf_op jit(solution)/shard_map/pallas_call | solution.py:41
  36.2 9.7 %all_to_all.21.st.st2 = f32[32,4,256]{2,1,0:T(4,128)S(1)} all-to-all(f32[32,4,256]{2,1,0:T(4,128)S(1)} %get-tuple-element.98), channel_id=1, replica_groups=mesh['rows'=8,'cols'=4] {'rows','cols'}, dimensions={0} | all-to-all | bytes 262144 | tf_op jit(solution)/shard_map/all_to_all | solution.py:786
  45.8 2.5 %shard_map.174 = (bf16[1920,256]{1,0:T(8,128)(2,1)S(1)}, f32[2304,128]{1,0:T(8,128)S(1)}, bf16[2304,128]{1,0:T(8,128)(2,1)S(1)}) custom-call(f32[1920,256]{1,0:T(8,128)S(1)} %get-tuple-element.97.z2, f32[32,4,256]{2,1,0:T(4,128)S(1)} %all_to_all.21.st.st2, f32[8,256]{1,0:T(8,128)S(1)} %get-tuple-element.99.own, f32[4,256]{1,0:T(4,128)S(1)} %copy-done.4, ...), custom_call_target="tpu_custom_call" | custom-call | flops 1811939328 | bytes 4194304 | tf_op jit(solution)/shard_map/pallas_call | solution.py:41
  48.4 1.4 %collective-permute-start.6 = (bf16[2304,128]{1,0:T(8,128)(2,1)S(1)}, bf16[2304,128]{1,0:T(8,128)(2,1)S(1)}, u32[]{:S(2)}, u32[]{:S(2)}) collective-permute-start(bf16[2304,128]{1,0:T(8,128)(2,1)S(1)} %get-tuple-element.105), channel_id=1, source_target_pairs={{0,4},{4,0},{8,12},{12,8},{16,20},{20,16},{24,28},{28,24},{1,5},{5... | collective-permute-start | bytes 1769480 | tf_op jit(solution)/shard_map/ppermute | solution.py:758
  49.8 1.9 %shard_map.175 = (f32[1536,256]{1,0:T(8,128)S(1)}, f32[16,256]{1,0:T(8,128)S(1)}, bf16[4,8,40,256]{3,2,1,0:T(8,128)(2,1)S(1)}) custom-call(bf16[1920,256]{1,0:T(8,128)(2,1)S(1)} %get-tuple-element.102.d, bf16[2304,256]{1,0:T(8,128)(2,1)S(1)} %get-tuple-element.95.w, f32[2304,256]{1,0:T(8,128)S(1)} %get-tuple-element.93.z1.z, ...), custom_call_target="tpu_custom_call" | custom-call | bytes 1024 | tf_op jit(solution)/shard_map/pallas_call | solution.py:41
  51.7 0.2 shard_map.176
  51.9 0.6 collective-permute-start.7
  52.5 0.8 shard_map.177
  53.3 9.1 %all_to_all.22.st3 = f32[32,2,256]{2,1,0:T(2,128)S(1)} all-to-all(f32[32,2,256]{2,1,0:T(2,128)S(1)} %get-tuple-element.115), channel_id=1, replica_groups=mesh['rows'=8,'cols'=4] {'rows','cols'}, dimensions={0} | all-to-all | bytes 131072 | tf_op jit(solution)/shard_map/all_to_all | solution.py:786
  62.4 0.1 shard_map.178
  62.5 0.7 collective-permute-start.14
  63.2 1.5 %shard_map.179 = (bf16[1536,256]{1,0:T(8,128)(2,1)S(1)}, bf16[4,1,48,256]{3,2,1,0:T(8,128)(2,1)S(1)}, bf16[4,1,48,256]{3,2,1,0:T(8,128)(2,1)S(1)}, bf16[576,128]...) custom-call(f32[1536,256]{1,0:T(8,128)S(1)} %get-tuple-element.119.d, ...), custom_call_target="tpu_custom_call" | custom-call | bytes 1024 | tf_op jit(solution)/shard_map/pallas_call | solution.py:41
  64.7 1.0 %collective-permute-start.10 = (bf16[576,128]{1,0:T(8,128)(2,1)S(1)}, bf16[576,128]{1,0:T(8,128)(2,1)S(1)}, u32[]{:S(2)}, u32[]{:S(2)}) collective-permute-start(bf16[576,128]{1,0:T(8,128)(2,1)S(1)} %get-tuple-element.126), channel_id=1, source_target_pairs={{0,4},{4,0},{8,12},{12,8},{16,20},{20,16},{24,28},{28,24},{1,5},{5... | collective-permute-start | bytes 442376 | tf_op jit(solution)/shard_map/ppermute | solution.py:758
  65.7 0.1 collective-permute-start.11
  65.8 0.4 collective-permute-start.12
  66.2 0.1 collective-permute-start.13
  66.3 1.2 %shard_map.181.keep = f32[2304,128]{1,0:T(8,128)S(1)} custom-call(bf16[1920,768]{1,0:T(8,128)(2,1)S(1)} %get-tuple-element.121.x, bf16[256,1536]{1,0:T(8,128)(2,1)S(1)} %get-tuple-element.125.dt_ref), custom_call_target="tpu_custom_call" | custom-call | bytes 1024 | tf_op jit(solution)/shard_map/pallas_call | solution.py:41
  67.5 0.1 collective-permute-done.13.refs_3_
  67.6 0.9 shard_map.182.refs_6_
  68.5 0.8 shard_map.183
  69.3 0.0 copy-start.5
  69.3 2.9 %all-to-all-start.3 = ((bf16[32,96,128]{2,1,0:T(8,128)(2,1)}), bf16[32,96,128]{2,1,0:T(8,128)(2,1)S(1)}, u32[]{:S(2)}, u32[]{:S(2)}) async-start(bf16[32,96,128]{2,1,0:T(8,128)(2,1)} %shard_map.183), calls=%async_computation.3 | async-start | bytes 1572864 | tf_op jit(solution)/shard_map/all_to_all | solution.py:786
  72.3 0.5 collective-permute-start.8
  72.7 3.3 %collective-permute-start.9 = (bf16[4,1,48,256]{3,2,1,0:T(8,128)(2,1)S(1)}, bf16[4,1,48,256]{3,2,1,0:T(8,128)(2,1)S(1)}, u32[]{:S(2)}, u32[]{:S(2)}) collective-permute-start(bf16[4,1,48,256]{3,2,1,0:T(8,128)(2,1)S(1)} %get-tuple-element.124), channel_id=1, source_target_pairs={{4,8},{8,4},{12,16},{16,12},{20,24},{24,20},{5,9},{9,5},{13,17},{1... | collective-permute-start | bytes 294920 | tf_op jit(solution)/shard_map/ppermute | solution.py:758
  76.0 0.8 copy.36
  76.9 5.1 %collective-permute-done.9.rb = bf16[4,1,48,256]{3,2,1,0:T(8,128)(2,1)S(1)} collective-permute-done((bf16[4,1,48,256]{3,2,1,0:T(8,128)(2,1)S(1)}, bf16[4,1,48,256]{3,2,1,0:T(8,128)(2,1)S(1)}, u32[]{:S(2)}, u32[]{:S(2)}) %collective-permute-start.9) | collective-permute-done | bytes 98336 | tf_op jit(solution)/shard_map/ppermute | solution.py:758
  82.0 0.0 copy-start.7
  82.0 4.7 %shard_map.180 = f32[4,8,40,256]{3,2,1,0:T(8,128)} custom-call(bf16[1536,256]{1,0:T(8,128)(2,1)S(1)} %get-tuple-element.122.e, bf16[4,1,48,256]{3,2,1,0:T(8,128)(2,1)S(1)} %collective-permute-done.8.ra, bf16[4,1,48,256]{3,2,1,0:T(8,128)(2,1)S(1)} %collective-permute-done.9.rb, bf16[2304,256]{1,0:T(8,128)(2,1)} %copy-done, bf16[4,8,40,256]{3,2,1,0:T(8,128)(2,1)} %cot_far.1, ...), custom_call_target="tpu_custom_call" | custom-call | flops 1811939328 | bytes 4194304 | tf_op jit(solution)/shard_map/pallas_call | solution.py:41
  86.7 0.9 constant_dynamic-slice_fusion.w
  87.6 5.6 %all-to-all-done.3.parts = bf16[32,96,128]{2,1,0:T(8,128)(2,1)S(1)} async-done(((bf16[32,96,128]{2,1,0:T(8,128)(2,1)}), bf16[32,96,128]{2,1,0:T(8,128)(2,1)S(1)}, u32[]{:S(2)}, u32[]{:S(2)}) %all-to-all-start.3) | async-done | bytes 786464 | tf_op jit(solution)/shard_map/all_to_all | solution.py:786
  93.2 1.0 %shard_map.184 = (f32[288,128]{1,0:T(8,128)}, f32[288,128]{1,0:T(8,128)}, f32[288,128]{1,0:T(8,128)}, f32[288,128]{1,0:T(8,128)}, f32[4,256]{1,0:T(4,128)}, /*in...) custom-call(bf16[32,96,128]{2,1,0:T(8,128)(2,1)S(1)} %all-to-all-done.3.parts, ...), custom_call_target="tpu_custom_call" | custom-call | flops 100000000 | bytes 4194304 | tf_op jit(solution)/shard_map/pallas_call | solution.py:41
  (22 shorter events, 0.0 us)
Async XLA Ops:
  2.4 16.0 %collective-permute-start.2 = (bf16[4,4,40,256]{3,2,1,0:T(8,128)(2,1)S(1)}, bf16[4,4,40,256]{3,2,1,0:T(8,128)(2,1)S(1)}, u32[]{:S(2)}, u32[]{:S(2)}) collective-permute-start(bf16[4,4,40,256]{3,2,1,0:T(8,128)(2,1)S(1)} %get-tuple-element.81), channel_id=1, source_target_pairs={{4,8},{8,4},{12,16},{16,12},{20,24},{24,20},{5,9},{9,5},{13,17},{1... | collective-permute-start | bytes 983048 | tf_op jit(solution)/shard_map/ppermute | solution.py:758
  6.9 11.3 %collective-permute-start = (bf16[4,48,256]{2,1,0:T(8,128)(2,1)S(1)}, bf16[4,48,256]{2,1,0:T(8,128)(2,1)S(1)}, u32[]{:S(2)}, u32[]{:S(2)}) collective-permute-start(bf16[4,48,256]{2,1,0:T(8,128)(2,1)S(1)} %get-tuple-element.77), channel_id=1, source_target_pairs={{0,1},{1,0},{2,3},{3,2},{4,5},{5,4},{6,7},{7,6},{8,9},{9,8},{10,11... | collective-permute-start | bytes 294920 | tf_op jit(solution)/shard_map/ppermute | solution.py:758
  8.2 9.9 %collective-permute-start.1 = (bf16[4,48,256]{2,1,0:T(8,128)(2,1)S(1)}, bf16[4,48,256]{2,1,0:T(8,128)(2,1)S(1)}, u32[]{:S(2)}, u32[]{:S(2)}) collective-permute-start(bf16[4,48,256]{2,1,0:T(8,128)(2,1)S(1)} %get-tuple-element.78), channel_id=1, source_target_pairs={{1,2},{2,1},{5,6},{6,5},{9,10},{10,9},{13,14},{14,13},{17,18},{18,... | collective-permute-start | bytes 294920 | tf_op jit(solution)/shard_map/ppermute | solution.py:758
  8.9 9.5 %collective-permute-start.3 = (bf16[4,16,256]{2,1,0:T(8,128)(2,1)S(1)}, bf16[4,16,256]{2,1,0:T(8,128)(2,1)S(1)}, u32[]{:S(2)}, u32[]{:S(2)}) collective-permute-start(bf16[4,16,256]{2,1,0:T(8,128)(2,1)S(1)} %get-tuple-element.82), channel_id=1, source_target_pairs={{4,9},{5,8},{6,11},{7,10},{8,5},{9,4},{10,7},{11,6},{12,17},{13,16... | collective-permute-start | bytes 98312 | tf_op jit(solution)/shard_map/ppermute | solution.py:774
  14.9 3.4 %collective-permute-start.4 = (bf16[4,16,256]{2,1,0:T(8,128)(2,1)S(1)}, bf16[4,16,256]{2,1,0:T(8,128)(2,1)S(1)}, u32[]{:S(2)}, u32[]{:S(2)}) collective-permute-start(bf16[4,16,256]{2,1,0:T(8,128)(2,1)S(1)} %get-tuple-element.83), channel_id=1, source_target_pairs={{5,10},{6,9},{9,6},{10,5},{13,18},{14,17},{17,14},{18,13},{21,26},... | collective-permute-start | bytes 98312 | tf_op jit(solution)/shard_map/ppermute | solution.py:774
  15.6 2.5 %copy-start.1 = (bf16[4,8,40,256]{3,2,1,0:T(8,128)(2,1)S(1)}, bf16[4,8,40,256]{3,2,1,0:T(8,128)(2,1)}, u32[]{:S(2)}) copy-start(bf16[4,8,40,256]{3,2,1,0:T(8,128)(2,1)} %cot_far.1) | copy-start | bytes 1966084
  18.1 3.7 %copy-start = (bf16[2304,256]{1,0:T(8,128)(2,1)}, bf16[2304,256]{1,0:T(8,128)(2,1)S(1)}, u32[]{:S(2)}) copy-start(bf16[2304,256]{1,0:T(8,128)(2,1)S(1)} %get-tuple-element.89.w.w_far) | copy-start | bytes 3538948
  18.4 1.8 %collective-permute-start.5 = (bf16[4,4,48,256]{3,2,1,0:T(8,128)(2,1)S(1)}, bf16[4,4,48,256]{3,2,1,0:T(8,128)(2,1)S(1)}, u32[]{:S(2)}, u32[]{:S(2)}) collective-permute-start(bf16[4,4,48,256]{3,2,1,0:T(8,128)(2,1)S(1)} %get-tuple-element.85), channel_id=1, source_target_pairs={{0,4},{4,0},{8,12},{12,8},{16,20},{20,16},{24,28},{28,24},{1,5},{5... | collective-permute-start | bytes 1179656 | tf_op jit(solution)/shard_map/ppermute | solution.py:758
  20.2 13.3 %copy-start.4 = (f32[4,256]{1,0:T(4,128)S(1)}, f32[4,256]{1,0:T(4,128)}, u32[]{:S(2)}) copy-start(f32[4,256]{1,0:T(4,128)} %params.11) | copy-start | bytes 12292
  48.4 3.3 %collective-permute-start.6 = (bf16[2304,128]{1,0:T(8,128)(2,1)S(1)}, bf16[2304,128]{1,0:T(8,128)(2,1)S(1)}, u32[]{:S(2)}, u32[]{:S(2)}) collective-permute-start(bf16[2304,128]{1,0:T(8,128)(2,1)S(1)} %get-tuple-element.105), channel_id=1, source_target_pairs={{0,4},{4,0},{8,12},{12,8},{16,20},{20,16},{24,28},{28,24},{1,5},{5... | collective-permute-start | bytes 1769480 | tf_op jit(solution)/shard_map/ppermute | solution.py:758
  51.9 10.5 %collective-permute-start.7 = (bf16[32,40,128]{2,1,0:T(8,128)(2,1)S(1)}, bf16[32,40,128]{2,1,0:T(8,128)(2,1)S(1)}, u32[]{:S(2)}, u32[]{:S(2)}) collective-permute-start(bf16[32,40,128]{2,1,0:T(8,128)(2,1)S(1)} %get-tuple-element.117), channel_id=1, source_target_pairs={{0,16},{4,20},{8,24},{12,28},{16,0},{20,4},{24,8},{28,12},{1,17},{... | collective-permute-start | bytes 983048 | tf_op jit(solution)/shard_map/ppermute | solution.py:927
  62.5 6.0 %collective-permute-start.14 = (bf16[16,40,128]{2,1,0:T(8,128)(2,1)S(1)}, bf16[16,40,128]{2,1,0:T(8,128)(2,1)S(1)}, u32[]{:S(2)}, u32[]{:S(2)}) collective-permute-start(bf16[16,40,128]{2,1,0:T(8,128)(2,1)S(1)} %get-tuple-element.131), channel_id=1, source_target_pairs={{0,8},{4,12},{8,0},{12,4},{16,24},{20,28},{24,16},{28,20},{1,9},{5... | collective-permute-start | bytes 491528 | tf_op jit(solution)/shard_map/ppermute | solution.py:948
  64.7 2.8 %collective-permute-start.10 = (bf16[576,128]{1,0:T(8,128)(2,1)S(1)}, bf16[576,128]{1,0:T(8,128)(2,1)S(1)}, u32[]{:S(2)}, u32[]{:S(2)}) collective-permute-start(bf16[576,128]{1,0:T(8,128)(2,1)S(1)} %get-tuple-element.126), channel_id=1, source_target_pairs={{0,4},{4,0},{8,12},{12,8},{16,20},{20,16},{24,28},{28,24},{1,5},{5... | collective-permute-start | bytes 442376 | tf_op jit(solution)/shard_map/ppermute | solution.py:758
  65.7 1.8 %collective-permute-start.11 = (bf16[576,128]{1,0:T(8,128)(2,1)S(1)}, bf16[576,128]{1,0:T(8,128)(2,1)S(1)}, u32[]{:S(2)}, u32[]{:S(2)}) collective-permute-start(bf16[576,128]{1,0:T(8,128)(2,1)S(1)} %get-tuple-element.127), channel_id=1, source_target_pairs={{0,4},{4,0},{8,12},{12,8},{16,20},{20,16},{24,28},{28,24},{1,5},{5... | collective-permute-start | bytes 442376 | tf_op jit(solution)/shard_map/ppermute | solution.py:758
  65.8 1.7 %collective-permute-start.12 = (bf16[576,128]{1,0:T(8,128)(2,1)S(1)}, bf16[576,128]{1,0:T(8,128)(2,1)S(1)}, u32[]{:S(2)}, u32[]{:S(2)}) collective-permute-start(bf16[576,128]{1,0:T(8,128)(2,1)S(1)} %get-tuple-element.128), channel_id=1, source_target_pairs={{0,4},{4,0},{8,12},{12,8},{16,20},{20,16},{24,28},{28,24},{1,5},{5... | collective-permute-start | bytes 442376 | tf_op jit(solution)/shard_map/ppermute | solution.py:758
  66.2 1.4 %collective-permute-start.13 = (bf16[576,128]{1,0:T(8,128)(2,1)S(1)}, bf16[576,128]{1,0:T(8,128)(2,1)S(1)}, u32[]{:S(2)}, u32[]{:S(2)}) collective-permute-start(bf16[576,128]{1,0:T(8,128)(2,1)S(1)} %get-tuple-element.129), channel_id=1, source_target_pairs={{0,4},{4,0},{8,12},{12,8},{16,20},{20,16},{24,28},{28,24},{1,5},{5... | collective-permute-start | bytes 442376 | tf_op jit(solution)/shard_map/ppermute | solution.py:758
  69.3 12.7 %copy-start.5 = (s32[4,8,40]{2,1,0:T(8,128)S(1)}, s32[4,8,40]{2,1,0:T(8,128)}, u32[]{:S(2)}) copy-start(s32[4,8,40]{2,1,0:T(8,128)} %occ.1) | copy-start | bytes 15364
  69.3 23.9 %all-to-all-start.3 = ((bf16[32,96,128]{2,1,0:T(8,128)(2,1)}), bf16[32,96,128]{2,1,0:T(8,128)(2,1)S(1)}, u32[]{:S(2)}, u32[]{:S(2)}) async-start(bf16[32,96,128]{2,1,0:T(8,128)(2,1)} %shard_map.183), calls=%async_computation.3 | async-start | bytes 1572864 | tf_op jit(solution)/shard_map/all_to_all | solution.py:786
  72.3 4.6 %collective-permute-start.8 = (bf16[4,1,48,256]{3,2,1,0:T(8,128)(2,1)S(1)}, bf16[4,1,48,256]{3,2,1,0:T(8,128)(2,1)S(1)}, u32[]{:S(2)}, u32[]{:S(2)}) collective-permute-start(bf16[4,1,48,256]{3,2,1,0:T(8,128)(2,1)S(1)} %get-tuple-element.123), channel_id=1, source_target_pairs={{0,4},{4,0},{8,12},{12,8},{16,20},{20,16},{24,28},{28,24},{1,5},{5... | collective-permute-start | bytes 294920 | tf_op jit(solution)/shard_map/ppermute | solution.py:758
  72.7 9.2 %collective-permute-start.9 = (bf16[4,1,48,256]{3,2,1,0:T(8,128)(2,1)S(1)}, bf16[4,1,48,256]{3,2,1,0:T(8,128)(2,1)S(1)}, u32[]{:S(2)}, u32[]{:S(2)}) collective-permute-start(bf16[4,1,48,256]{3,2,1,0:T(8,128)(2,1)S(1)} %get-tuple-element.124), channel_id=1, source_target_pairs={{4,8},{8,4},{12,16},{16,12},{20,24},{24,20},{5,9},{9,5},{13,17},{1... | collective-permute-start | bytes 294920 | tf_op jit(solution)/shard_map/ppermute | solution.py:758
  82.0 11.3 %copy-start.2 = (f32[2,18432]{1,0:T(2,128)S(1)}, f32[2,18432]{1,0:T(2,128)}, u32[]{:S(2)}) copy-start(f32[2,18432]{1,0:T(2,128)} %param.13) | copy-start | bytes 442372
  82.0 11.3 %copy-start.3 = (f32[2,18432]{1,0:T(2,128)S(1)}, f32[2,18432]{1,0:T(2,128)}, u32[]{:S(2)}) copy-start(f32[2,18432]{1,0:T(2,128)} %param.14) | copy-start | bytes 442372
  82.0 11.3 %copy-start.6 = (f32[4,256]{1,0:T(4,128)S(1)}, f32[4,256]{1,0:T(4,128)}, u32[]{:S(2)}) copy-start(f32[4,256]{1,0:T(4,128)} %n_first.1) | copy-start | bytes 12292
  82.0 11.3 %copy-start.7 = (f32[4,256]{1,0:T(4,128)S(1)}, f32[4,256]{1,0:T(4,128)}, u32[]{:S(2)}) copy-start(f32[4,256]{1,0:T(4,128)} %n_second.1) | copy-start | bytes 12292

commit v12 on v11

--- a/solution.py
+++ b/solution.py
@@ -981,7 +981,8 @@
         (parts,) = kernel_call(
             message_kernel,
             [parts_shape],
-            1e9,
+            0,
+            size=1024,
             far=(at,),
             far_out=(0,),
             scratch=[pltpu.VMEM((devices, rows - ready, chans // 2), BF16), dma((4,))],

time: 94.7 us -> 94.7 us (level)
  no operation moved by 1% of the time
where the time goes in v12:
time: 94.7 us; the launch traced here: 94.3 us
  blocking collectives  30.5 us (32%)
  Pallas kernels  25.8 us (27%)
  starting transfers between devices  24.2 us (26%)
  waiting for transfers between devices  11 us (12%)
  local copies, waits for them, and re-layouts  1.8 us (2%)
  between operations  0.98 us (1%)
    all_to_all x3, blocking collectives, exchange(): return lax.all_to_all(parts, BOTH, 0, 0, tiled=True)  30.5 us
    pallas_call x17, Pallas kernels, call(): pl.pallas_call(body, out_shape=out_shape, in_specs=specs, out_specs=[pl.B...  25.8 us
    ppermute x11, starting transfers between devices, swapped(): return lax.ppermute(block, axis, pairs)  13.3 us
    ppermute x2, starting transfers between devices, swapped_both(): return lax.ppermute(block, BOTH, pairs)  6.69 us
    all_to_all x1, waiting for transfers between devices, exchange(): return lax.all_to_all(parts, BOTH, 0, 0, tiled=True)  5.62 us
    ppermute x11, waiting for transfers between devices, swapped(): return lax.ppermute(block, axis, pairs)  5.32 us
    all_to_all x1, starting transfers between devices, exchange(): return lax.all_to_all(parts, BOTH, 0, 0, tiled=True)  2.92 us
  transfers between devices with their start and end apart: 16, of which 4 were waited for; matrix products, arithmetic and copies ran while one was open for 2% of the time, Pallas kernels for 16%

profile of v12, /device:TPU:1, one launch (start us, length us, event | category | flops | bytes accessed | tf_op | source)
XLA Modules:
  0.0 94.3 jit_solution(2642999815165806901)
XLA Ops:
  0.6 1.7 %shard_map.168 = (bf16[4,8,40,256]{3,2,1,0:T(8,128)(2,1)S(1)}, bf16[4,48,256]{2,1,0:T(8,128)(2,1)S(1)}, bf16[4,48,256]{2,1,0:T(8,128)(2,1)S(1)}, bf16[4,4,40,256...) custom-call(bf16[4,8,40,256]{3,2,1,0:T(8,128)(2,1)} %features.1, ...), custom_call_target="tpu_custom_call" | custom-call | flops 100000000 | bytes 4194304 | tf_op jit(solution)/shard_map/pallas_call | solution.py:41
  2.4 4.5 %collective-permute-start.2 = (bf16[4,4,40,256]{3,2,1,0:T(8,128)(2,1)S(1)}, bf16[4,4,40,256]{3,2,1,0:T(8,128)(2,1)S(1)}, u32[]{:S(2)}, u32[]{:S(2)}) collective-permute-start(bf16[4,4,40,256]{3,2,1,0:T(8,128)(2,1)S(1)} %get-tuple-element.81), channel_id=1, source_target_pairs={{4,8},{8,4},{12,16},{16,12},{20,24},{24,20},{5,9},{9,5},{13,17},{1... | collective-permute-start | bytes 983048 | tf_op jit(solution)/shard_map/ppermute | solution.py:758
  6.9 1.4 %collective-permute-start = (bf16[4,48,256]{2,1,0:T(8,128)(2,1)S(1)}, bf16[4,48,256]{2,1,0:T(8,128)(2,1)S(1)}, u32[]{:S(2)}, u32[]{:S(2)}) collective-permute-start(bf16[4,48,256]{2,1,0:T(8,128)(2,1)S(1)} %get-tuple-element.77), channel_id=1, source_target_pairs={{0,1},{1,0},{2,3},{3,2},{4,5},{5,4},{6,7},{7,6},{8,9},{9,8},{10,11... | collective-permute-start | bytes 294920 | tf_op jit(solution)/shard_map/ppermute | solution.py:758
  8.2 0.7 collective-permute-start.1
  8.9 6.0 %collective-permute-start.3 = (bf16[4,16,256]{2,1,0:T(8,128)(2,1)S(1)}, bf16[4,16,256]{2,1,0:T(8,128)(2,1)S(1)}, u32[]{:S(2)}, u32[]{:S(2)}) collective-permute-start(bf16[4,16,256]{2,1,0:T(8,128)(2,1)S(1)} %get-tuple-element.82), channel_id=1, source_target_pairs={{4,9},{5,8},{6,11},{7,10},{8,5},{9,4},{10,7},{11,6},{12,17},{13,16... | collective-permute-start | bytes 98312 | tf_op jit(solution)/shard_map/ppermute | solution.py:774
  14.9 0.7 collective-permute-start.4
  15.6 0.0 copy-start.1
  15.6 2.5 %shard_map.170 = (bf16[2304,256]{1,0:T(8,128)(2,1)S(1)}, bf16[2304,256]{1,0:T(8,128)(2,1)S(1)}) custom-call(f32[9216,128]{1,0:T(8,128)} %bitcast.37), custom_call_target="tpu_custom_call" | custom-call | bytes 1024 | tf_op jit(solution)/shard_map/pallas_call | solution.py:41
  18.1 0.0 collective-permute-done.rc
  18.2 0.2 shard_map.169
  18.4 0.0 collective-permute-done.4.rb_d
  18.4 0.0 collective-permute-done.2.rb
  18.4 0.1 collective-permute-start.5
  18.5 1.6 %shard_map.171 = (f32[2304,256]{1,0:T(8,128)S(1)}, f32[16,256]{1,0:T(8,128)S(1)}, bf16[1920,768]{1,0:T(8,128)(2,1)S(1)}) custom-call(bf16[4,8,48,256]{3,2,1,0:T(8,128)(2,1)S(1)} %get-tuple-element.79.ext, bf16[2304,256]{1,0:T(8,128)(2,1)S(1)} %get-tuple-element.89.w.w_far), custom_call_target="tpu_custom_call" | custom-call | bytes 1024 | tf_op jit(solution)/shard_map/pallas_call | solution.py:41
  20.1 0.1 collective-permute-done.5.ra
  20.2 1.6 %shard_map.172 = (f32[2304,256]{1,0:T(8,128)S(1)}, f32[32,2,256]{2,1,0:T(2,128)S(1)}, bf16[1920,768]{1,0:T(8,128)(2,1)S(1)}, bf16[4,2,48,256]{3,2,1,0:T(8,128)(2,1)S(1)}) custom-call(bf16[4,8,48,256]{3,2,1,0:T(8,128)(2,1)S(1)} %get-tuple-element.79.ext, ...), custom_call_target="tpu_custom_call", output_to_operand_aliasing={{0}: (7, {}), {2}: (8, {})} | custom-call | bytes 1024 | tf_op jit(solution)/shard_map/pallas_call | solution.py:41
  21.8 11.7 %all_to_all.20.st = f32[32,2,256]{2,1,0:T(2,128)S(1)} all-to-all(f32[32,2,256]{2,1,0:T(2,128)S(1)} %get-tuple-element.94), channel_id=1, replica_groups=mesh['rows'=8,'cols'=4] {'rows','cols'}, dimensions={0} | all-to-all | bytes 131072 | tf_op jit(solution)/shard_map/all_to_all | solution.py:786
  33.5 2.7 %shard_map.173 = (bf16[2304,768]{1,0:T(8,128)(2,1)S(1)}, f32[1920,256]{1,0:T(8,128)S(1)}, f32[32,4,256]{2,1,0:T(4,128)S(1)}, f32[8,256]{1,0:T(8,128)S(1)}) custom-call(f32[2304,256]{1,0:T(8,128)S(1)} %get-tuple-element.93.z1.z, f32[32,2,256]{2,1,0:T(2,128)S(1)} %all_to_all.20.st, f32[4,256]{1,0:T(4,128)S(1)} %copy-done.4, ...), custom_call_target="tpu_custom_call" | custom-call | flops 2264924160 | bytes 4194304 | tf_op jit(solution)/shard_map/pallas_call | solution.py:41
  36.2 9.7 %all_to_all.21.st.st2 = f32[32,4,256]{2,1,0:T(4,128)S(1)} all-to-all(f32[32,4,256]{2,1,0:T(4,128)S(1)} %get-tuple-element.98), channel_id=1, replica_groups=mesh['rows'=8,'cols'=4] {'rows','cols'}, dimensions={0} | all-to-all | bytes 262144 | tf_op jit(solution)/shard_map/all_to_all | solution.py:786
  45.8 2.5 %shard_map.174 = (bf16[1920,256]{1,0:T(8,128)(2,1)S(1)}, f32[2304,128]{1,0:T(8,128)S(1)}, bf16[2304,128]{1,0:T(8,128)(2,1)S(1)}) custom-call(f32[1920,256]{1,0:T(8,128)S(1)} %get-tuple-element.97.z2, f32[32,4,256]{2,1,0:T(4,128)S(1)} %all_to_all.21.st.st2, f32[8,256]{1,0:T(8,128)S(1)} %get-tuple-element.99.own, f32[4,256]{1,0:T(4,128)S(1)} %copy-done.4, ...), custom_call_target="tpu_custom_call" | custom-call | flops 1811939328 | bytes 4194304 | tf_op jit(solution)/shard_map/pallas_call | solution.py:41
  48.4 1.4 %collective-permute-start.6 = (bf16[2304,128]{1,0:T(8,128)(2,1)S(1)}, bf16[2304,128]{1,0:T(8,128)(2,1)S(1)}, u32[]{:S(2)}, u32[]{:S(2)}) collective-permute-start(bf16[2304,128]{1,0:T(8,128)(2,1)S(1)} %get-tuple-element.105), channel_id=1, source_target_pairs={{0,4},{4,0},{8,12},{12,8},{16,20},{20,16},{24,28},{28,24},{1,5},{5... | collective-permute-start | bytes 1769480 | tf_op jit(solution)/shard_map/ppermute | solution.py:758
  49.8 1.9 %shard_map.175 = (f32[1536,256]{1,0:T(8,128)S(1)}, f32[16,256]{1,0:T(8,128)S(1)}, bf16[4,8,40,256]{3,2,1,0:T(8,128)(2,1)S(1)}) custom-call(bf16[1920,256]{1,0:T(8,128)(2,1)S(1)} %get-tuple-element.102.d, bf16[2304,256]{1,0:T(8,128)(2,1)S(1)} %get-tuple-element.95.w, f32[2304,256]{1,0:T(8,128)S(1)} %get-tuple-element.93.z1.z, ...), custom_call_target="tpu_custom_call" | custom-call | bytes 1024 | tf_op jit(solution)/shard_map/pallas_call | solution.py:41
  51.7 0.2 shard_map.176
  51.9 0.6 collective-permute-start.7
  52.5 0.8 shard_map.177
  53.3 9.1 %all_to_all.22.st3 = f32[32,2,256]{2,1,0:T(2,128)S(1)} all-to-all(f32[32,2,256]{2,1,0:T(2,128)S(1)} %get-tuple-element.115), channel_id=1, replica_groups=mesh['rows'=8,'cols'=4] {'rows','cols'}, dimensions={0} | all-to-all | bytes 131072 | tf_op jit(solution)/shard_map/all_to_all | solution.py:786
  62.4 0.1 shard_map.178
  62.5 0.7 collective-permute-start.14
  63.2 1.5 %shard_map.179 = (bf16[1536,256]{1,0:T(8,128)(2,1)S(1)}, bf16[4,1,48,256]{3,2,1,0:T(8,128)(2,1)S(1)}, bf16[4,1,48,256]{3,2,1,0:T(8,128)(2,1)S(1)}, bf16[576,128]...) custom-call(f32[1536,256]{1,0:T(8,128)S(1)} %get-tuple-element.119.d, ...), custom_call_target="tpu_custom_call" | custom-call | bytes 1024 | tf_op jit(solution)/shard_map/pallas_call | solution.py:41
  64.7 1.0 %collective-permute-start.10 = (bf16[576,128]{1,0:T(8,128)(2,1)S(1)}, bf16[576,128]{1,0:T(8,128)(2,1)S(1)}, u32[]{:S(2)}, u32[]{:S(2)}) collective-permute-start(bf16[576,128]{1,0:T(8,128)(2,1)S(1)} %get-tuple-element.126), channel_id=1, source_target_pairs={{0,4},{4,0},{8,12},{12,8},{16,20},{20,16},{24,28},{28,24},{1,5},{5... | collective-permute-start | bytes 442376 | tf_op jit(solution)/shard_map/ppermute | solution.py:758
  65.7 0.1 collective-permute-start.11
  65.8 0.4 collective-permute-start.12
  66.2 0.1 collective-permute-start.13
  66.3 1.2 %shard_map.181.keep = f32[2304,128]{1,0:T(8,128)S(1)} custom-call(bf16[1920,768]{1,0:T(8,128)(2,1)S(1)} %get-tuple-element.121.x, bf16[256,1536]{1,0:T(8,128)(2,1)S(1)} %get-tuple-element.125.dt_ref), custom_call_target="tpu_custom_call" | custom-call | bytes 1024 | tf_op jit(solution)/shard_map/pallas_call | solution.py:41
  67.5 0.1 collective-permute-done.13.refs_3_
  67.6 0.9 shard_map.182.refs_6_
  68.5 0.8 shard_map.183
  69.3 0.0 copy-start.5
  69.3 2.9 %all-to-all-start.3 = ((bf16[32,96,128]{2,1,0:T(8,128)(2,1)}), bf16[32,96,128]{2,1,0:T(8,128)(2,1)S(1)}, u32[]{:S(2)}, u32[]{:S(2)}) async-start(bf16[32,96,128]{2,1,0:T(8,128)(2,1)} %shard_map.183), calls=%async_computation.3 | async-start | bytes 1572864 | tf_op jit(solution)/shard_map/all_to_all | solution.py:786
  72.3 0.5 collective-permute-start.8
  72.7 3.3 %collective-permute-start.9 = (bf16[4,1,48,256]{3,2,1,0:T(8,128)(2,1)S(1)}, bf16[4,1,48,256]{3,2,1,0:T(8,128)(2,1)S(1)}, u32[]{:S(2)}, u32[]{:S(2)}) collective-permute-start(bf16[4,1,48,256]{3,2,1,0:T(8,128)(2,1)S(1)} %get-tuple-element.124), channel_id=1, source_target_pairs={{4,8},{8,4},{12,16},{16,12},{20,24},{24,20},{5,9},{9,5},{13,17},{1... | collective-permute-start | bytes 294920 | tf_op jit(solution)/shard_map/ppermute | solution.py:758
  76.0 0.8 copy.36
  76.9 5.1 %collective-permute-done.9.rb = bf16[4,1,48,256]{3,2,1,0:T(8,128)(2,1)S(1)} collective-permute-done((bf16[4,1,48,256]{3,2,1,0:T(8,128)(2,1)S(1)}, bf16[4,1,48,256]{3,2,1,0:T(8,128)(2,1)S(1)}, u32[]{:S(2)}, u32[]{:S(2)}) %collective-permute-start.9) | collective-permute-done | bytes 98336 | tf_op jit(solution)/shard_map/ppermute | solution.py:758
  82.0 0.0 copy-start.7
  82.0 4.7 %shard_map.180 = f32[4,8,40,256]{3,2,1,0:T(8,128)} custom-call(bf16[1536,256]{1,0:T(8,128)(2,1)S(1)} %get-tuple-element.122.e, bf16[4,1,48,256]{3,2,1,0:T(8,128)(2,1)S(1)} %collective-permute-done.8.ra, bf16[4,1,48,256]{3,2,1,0:T(8,128)(2,1)S(1)} %collective-permute-done.9.rb, bf16[2304,256]{1,0:T(8,128)(2,1)} %copy-done, bf16[4,8,40,256]{3,2,1,0:T(8,128)(2,1)} %cot_far.1, ...), custom_call_target="tpu_custom_call" | custom-call | flops 1811939328 | bytes 4194304 | tf_op jit(solution)/shard_map/pallas_call | solution.py:41
  86.7 0.9 constant_dynamic-slice_fusion.w
  87.6 5.6 %all-to-all-done.3.parts = bf16[32,96,128]{2,1,0:T(8,128)(2,1)S(1)} async-done(((bf16[32,96,128]{2,1,0:T(8,128)(2,1)}), bf16[32,96,128]{2,1,0:T(8,128)(2,1)S(1)}, u32[]{:S(2)}, u32[]{:S(2)}) %all-to-all-start.3) | async-done | bytes 786464 | tf_op jit(solution)/shard_map/all_to_all | solution.py:786
  93.2 1.0 %shard_map.184 = (f32[288,128]{1,0:T(8,128)}, f32[288,128]{1,0:T(8,128)}, f32[288,128]{1,0:T(8,128)}, f32[288,128]{1,0:T(8,128)}, f32[4,256]{1,0:T(4,128)}, /*in...) custom-call(bf16[32,96,128]{2,1,0:T(8,128)(2,1)S(1)} %all-to-all-done.3.parts, ...), custom_call_target="tpu_custom_call" | custom-call | flops 100000000 | bytes 4194304 | tf_op jit(solution)/shard_map/pallas_call | solution.py:41
  (22 shorter events, 0.0 us)
Async XLA Ops:
  2.4 16.0 %collective-permute-start.2 = (bf16[4,4,40,256]{3,2,1,0:T(8,128)(2,1)S(1)}, bf16[4,4,40,256]{3,2,1,0:T(8,128)(2,1)S(1)}, u32[]{:S(2)}, u32[]{:S(2)}) collective-permute-start(bf16[4,4,40,256]{3,2,1,0:T(8,128)(2,1)S(1)} %get-tuple-element.81), channel_id=1, source_target_pairs={{4,8},{8,4},{12,16},{16,12},{20,24},{24,20},{5,9},{9,5},{13,17},{1... | collective-permute-start | bytes 983048 | tf_op jit(solution)/shard_map/ppermute | solution.py:758
  6.9 11.3 %collective-permute-start = (bf16[4,48,256]{2,1,0:T(8,128)(2,1)S(1)}, bf16[4,48,256]{2,1,0:T(8,128)(2,1)S(1)}, u32[]{:S(2)}, u32[]{:S(2)}) collective-permute-start(bf16[4,48,256]{2,1,0:T(8,128)(2,1)S(1)} %get-tuple-element.77), channel_id=1, source_target_pairs={{0,1},{1,0},{2,3},{3,2},{4,5},{5,4},{6,7},{7,6},{8,9},{9,8},{10,11... | collective-permute-start | bytes 294920 | tf_op jit(solution)/shard_map/ppermute | solution.py:758
  8.2 9.9 %collective-permute-start.1 = (bf16[4,48,256]{2,1,0:T(8,128)(2,1)S(1)}, bf16[4,48,256]{2,1,0:T(8,128)(2,1)S(1)}, u32[]{:S(2)}, u32[]{:S(2)}) collective-permute-start(bf16[4,48,256]{2,1,0:T(8,128)(2,1)S(1)} %get-tuple-element.78), channel_id=1, source_target_pairs={{1,2},{2,1},{5,6},{6,5},{9,10},{10,9},{13,14},{14,13},{17,18},{18,... | collective-permute-start | bytes 294920 | tf_op jit(solution)/shard_map/ppermute | solution.py:758
  8.9 9.5 %collective-permute-start.3 = (bf16[4,16,256]{2,1,0:T(8,128)(2,1)S(1)}, bf16[4,16,256]{2,1,0:T(8,128)(2,1)S(1)}, u32[]{:S(2)}, u32[]{:S(2)}) collective-permute-start(bf16[4,16,256]{2,1,0:T(8,128)(2,1)S(1)} %get-tuple-element.82), channel_id=1, source_target_pairs={{4,9},{5,8},{6,11},{7,10},{8,5},{9,4},{10,7},{11,6},{12,17},{13,16... | collective-permute-start | bytes 98312 | tf_op jit(solution)/shard_map/ppermute | solution.py:774
  14.9 3.4 %collective-permute-start.4 = (bf16[4,16,256]{2,1,0:T(8,128)(2,1)S(1)}, bf16[4,16,256]{2,1,0:T(8,128)(2,1)S(1)}, u32[]{:S(2)}, u32[]{:S(2)}) collective-permute-start(bf16[4,16,256]{2,1,0:T(8,128)(2,1)S(1)} %get-tuple-element.83), channel_id=1, source_target_pairs={{5,10},{6,9},{9,6},{10,5},{13,18},{14,17},{17,14},{18,13},{21,26},... | collective-permute-start | bytes 98312 | tf_op jit(solution)/shard_map/ppermute | solution.py:774
  15.6 2.5 %copy-start.1 = (bf16[4,8,40,256]{3,2,1,0:T(8,128)(2,1)S(1)}, bf16[4,8,40,256]{3,2,1,0:T(8,128)(2,1)}, u32[]{:S(2)}) copy-start(bf16[4,8,40,256]{3,2,1,0:T(8,128)(2,1)} %cot_far.1) | copy-start | bytes 1966084
  18.1 3.7 %copy-start = (bf16[2304,256]{1,0:T(8,128)(2,1)}, bf16[2304,256]{1,0:T(8,128)(2,1)S(1)}, u32[]{:S(2)}) copy-start(bf16[2304,256]{1,0:T(8,128)(2,1)S(1)} %get-tuple-element.89.w.w_far) | copy-start | bytes 3538948
  18.4 1.8 %collective-permute-start.5 = (bf16[4,4,48,256]{3,2,1,0:T(8,128)(2,1)S(1)}, bf16[4,4,48,256]{3,2,1,0:T(8,128)(2,1)S(1)}, u32[]{:S(2)}, u32[]{:S(2)}) collective-permute-start(bf16[4,4,48,256]{3,2,1,0:T(8,128)(2,1)S(1)} %get-tuple-element.85), channel_id=1, source_target_pairs={{0,4},{4,0},{8,12},{12,8},{16,20},{20,16},{24,28},{28,24},{1,5},{5... | collective-permute-start | bytes 1179656 | tf_op jit(solution)/shard_map/ppermute | solution.py:758
  20.2 13.3 %copy-start.4 = (f32[4,256]{1,0:T(4,128)S(1)}, f32[4,256]{1,0:T(4,128)}, u32[]{:S(2)}) copy-start(f32[4,256]{1,0:T(4,128)} %params.11) | copy-start | bytes 12292
  48.4 3.3 %collective-permute-start.6 = (bf16[2304,128]{1,0:T(8,128)(2,1)S(1)}, bf16[2304,128]{1,0:T(8,128)(2,1)S(1)}, u32[]{:S(2)}, u32[]{:S(2)}) collective-permute-start(bf16[2304,128]{1,0:T(8,128)(2,1)S(1)} %get-tuple-element.105), channel_id=1, source_target_pairs={{0,4},{4,0},{8,12},{12,8},{16,20},{20,16},{24,28},{28,24},{1,5},{5... | collective-permute-start | bytes 1769480 | tf_op jit(solution)/shard_map/ppermute | solution.py:758
  51.9 10.5 %collective-permute-start.7 = (bf16[32,40,128]{2,1,0:T(8,128)(2,1)S(1)}, bf16[32,40,128]{2,1,0:T(8,128)(2,1)S(1)}, u32[]{:S(2)}, u32[]{:S(2)}) collective-permute-start(bf16[32,40,128]{2,1,0:T(8,128)(2,1)S(1)} %get-tuple-element.117), channel_id=1, source_target_pairs={{0,16},{4,20},{8,24},{12,28},{16,0},{20,4},{24,8},{28,12},{1,17},{... | collective-permute-start | bytes 983048 | tf_op jit(solution)/shard_map/ppermute | solution.py:927
  62.5 6.0 %collective-permute-start.14 = (bf16[16,40,128]{2,1,0:T(8,128)(2,1)S(1)}, bf16[16,40,128]{2,1,0:T(8,128)(2,1)S(1)}, u32[]{:S(2)}, u32[]{:S(2)}) collective-permute-start(bf16[16,40,128]{2,1,0:T(8,128)(2,1)S(1)} %get-tuple-element.131), channel_id=1, source_target_pairs={{0,8},{4,12},{8,0},{12,4},{16,24},{20,28},{24,16},{28,20},{1,9},{5... | collective-permute-start | bytes 491528 | tf_op jit(solution)/shard_map/ppermute | solution.py:948
  64.7 2.8 %collective-permute-start.10 = (bf16[576,128]{1,0:T(8,128)(2,1)S(1)}, bf16[576,128]{1,0:T(8,128)(2,1)S(1)}, u32[]{:S(2)}, u32[]{:S(2)}) collective-permute-start(bf16[576,128]{1,0:T(8,128)(2,1)S(1)} %get-tuple-element.126), channel_id=1, source_target_pairs={{0,4},{4,0},{8,12},{12,8},{16,20},{20,16},{24,28},{28,24},{1,5},{5... | collective-permute-start | bytes 442376 | tf_op jit(solution)/shard_map/ppermute | solution.py:758
  65.7 1.8 %collective-permute-start.11 = (bf16[576,128]{1,0:T(8,128)(2,1)S(1)}, bf16[576,128]{1,0:T(8,128)(2,1)S(1)}, u32[]{:S(2)}, u32[]{:S(2)}) collective-permute-start(bf16[576,128]{1,0:T(8,128)(2,1)S(1)} %get-tuple-element.127), channel_id=1, source_target_pairs={{0,4},{4,0},{8,12},{12,8},{16,20},{20,16},{24,28},{28,24},{1,5},{5... | collective-permute-start | bytes 442376 | tf_op jit(solution)/shard_map/ppermute | solution.py:758
  65.8 1.7 %collective-permute-start.12 = (bf16[576,128]{1,0:T(8,128)(2,1)S(1)}, bf16[576,128]{1,0:T(8,128)(2,1)S(1)}, u32[]{:S(2)}, u32[]{:S(2)}) collective-permute-start(bf16[576,128]{1,0:T(8,128)(2,1)S(1)} %get-tuple-element.128), channel_id=1, source_target_pairs={{0,4},{4,0},{8,12},{12,8},{16,20},{20,16},{24,28},{28,24},{1,5},{5... | collective-permute-start | bytes 442376 | tf_op jit(solution)/shard_map/ppermute | solution.py:758
  66.2 1.4 %collective-permute-start.13 = (bf16[576,128]{1,0:T(8,128)(2,1)S(1)}, bf16[576,128]{1,0:T(8,128)(2,1)S(1)}, u32[]{:S(2)}, u32[]{:S(2)}) collective-permute-start(bf16[576,128]{1,0:T(8,128)(2,1)S(1)} %get-tuple-element.129), channel_id=1, source_target_pairs={{0,4},{4,0},{8,12},{12,8},{16,20},{20,16},{24,28},{28,24},{1,5},{5... | collective-permute-start | bytes 442376 | tf_op jit(solution)/shard_map/ppermute | solution.py:758
  69.3 12.7 %copy-start.5 = (s32[4,8,40]{2,1,0:T(8,128)S(1)}, s32[4,8,40]{2,1,0:T(8,128)}, u32[]{:S(2)}) copy-start(s32[4,8,40]{2,1,0:T(8,128)} %occ.1) | copy-start | bytes 15364
  69.3 23.9 %all-to-all-start.3 = ((bf16[32,96,128]{2,1,0:T(8,128)(2,1)}), bf16[32,96,128]{2,1,0:T(8,128)(2,1)S(1)}, u32[]{:S(2)}, u32[]{:S(2)}) async-start(bf16[32,96,128]{2,1,0:T(8,128)(2,1)} %shard_map.183), calls=%async_computation.3 | async-start | bytes 1572864 | tf_op jit(solution)/shard_map/all_to_all | solution.py:786
  72.3 4.6 %collective-permute-start.8 = (bf16[4,1,48,256]{3,2,1,0:T(8,128)(2,1)S(1)}, bf16[4,1,48,256]{3,2,1,0:T(8,128)(2,1)S(1)}, u32[]{:S(2)}, u32[]{:S(2)}) collective-permute-start(bf16[4,1,48,256]{3,2,1,0:T(8,128)(2,1)S(1)} %get-tuple-element.123), channel_id=1, source_target_pairs={{0,4},{4,0},{8,12},{12,8},{16,20},{20,16},{24,28},{28,24},{1,5},{5... | collective-permute-start | bytes 294920 | tf_op jit(solution)/shard_map/ppermute | solution.py:758
  72.7 9.2 %collective-permute-start.9 = (bf16[4,1,48,256]{3,2,1,0:T(8,128)(2,1)S(1)}, bf16[4,1,48,256]{3,2,1,0:T(8,128)(2,1)S(1)}, u32[]{:S(2)}, u32[]{:S(2)}) collective-permute-start(bf16[4,1,48,256]{3,2,1,0:T(8,128)(2,1)S(1)} %get-tuple-element.124), channel_id=1, source_target_pairs={{4,8},{8,4},{12,16},{16,12},{20,24},{24,20},{5,9},{9,5},{13,17},{1... | collective-permute-start | bytes 294920 | tf_op jit(solution)/shard_map/ppermute | solution.py:758
  82.0 11.3 %copy-start.2 = (f32[2,18432]{1,0:T(2,128)S(1)}, f32[2,18432]{1,0:T(2,128)}, u32[]{:S(2)}) copy-start(f32[2,18432]{1,0:T(2,128)} %param.13) | copy-start | bytes 442372
  82.0 11.3 %copy-start.3 = (f32[2,18432]{1,0:T(2,128)S(1)}, f32[2,18432]{1,0:T(2,128)}, u32[]{:S(2)}) copy-start(f32[2,18432]{1,0:T(2,128)} %param.14) | copy-start | bytes 442372
  82.0 11.3 %copy-start.6 = (f32[4,256]{1,0:T(4,128)S(1)}, f32[4,256]{1,0:T(4,128)}, u32[]{:S(2)}) copy-start(f32[4,256]{1,0:T(4,128)} %n_first.1) | copy-start | bytes 12292
  82.0 11.3 %copy-start.7 = (f32[4,256]{1,0:T(4,128)S(1)}, f32[4,256]{1,0:T(4,128)}, u32[]{:S(2)}) copy-start(f32[4,256]{1,0:T(4,128)} %n_second.1) | copy-start | bytes 12292
